TPU v7x, 256 devices: a whole 4x4x8 slice. The times are simulated.
256 devices in a mesh: az: 16 (over z, x_hi), ax: 8 (over y, core), rad: 2 (over x_lo).
Axes of the slice: x: 4 (x_hi: 2, x_lo: 2; x = x_hi * 2 + x_lo), y: 4, z: 8, core: 2. Of those that a mesh axis runs over, the one named last changes fastest.
Arguments:
- fields: float32 [5, 64, 1024, 256], P(None, 'ax', 'az', 'rad'), may hold values from -6 to 6
- coeffs: float32 [5, 6], replicated, may hold values from 0.05 to 0.4
- parcels: float32 [4, 256, 16, 256], P(None, 'ax', 'az', 'rad'), may hold values from -6 to 6, as said below
- cells: int32 [256, 16, 256], P('ax', 'az', 'rad'), may hold values from 0 to 65535
- counts: int32 [8, 16, 2], P('ax', 'az', 'rad'), may hold values from 1024 to 4096, as said below
- moves: int32 [256, 16, 2], P('ax', 'az', 'rad'), may hold values from -1 to 1, as said below
- widths: int32 [16], replicated, may hold values from 2 to 65
Outputs:
- gas_out: float32 [5, 64, 1024, 256], P(None, 'ax', 'az', 'rad')
- parcels_out: float32 [4, 320, 16, 256], P(None, 'ax', 'az', 'rad')
Inputs may be any that keep to these rules, and one draw needn't show every extreme that they name: `parcels`: squared diameters (property 3) lie between 0.25 and 2; velocities lie within the range. `counts`: some device holds exactly 4096 live parcels. `moves`: every device sends exactly 4 blocks to the next axial device and 4 to the previous one, except that nothing leaves the first or last axial device across the end.
All inputs are finite; a program needn't handle non-finite values.
Results may differ from a plain program's by a relative error of at most 0.00005.
Values sent between devices are 32-bit elements; how exact they have to be, the bound alone decides.
No kernel may reach another device: no remote copies, remote signals or barrier semaphores. Data moves between devices by JAX's collectives and lax.ppermute only.
A program may use at most 256 MiB of HBM per device.

v0:
```python
import math

import jax
import jax.numpy as jnp
from jax import lax
from jax.sharding import PartitionSpec as P

FIELDS = 5
CYCLES = 16
MODES = 128
BLK = 128
BLK_DEV = 32
MOVEB = 4


STEP_SIZE = 0.5
EVAP_RATE = 0.5
COUPLING = 0.5


def with_halo(block, sides, width, periodic):
    for axis, dim in sides:
        count = lax.axis_size(axis)
        forward = [(i, i + 1) for i in range(count - 1)]
        if periodic:
            forward.append((count - 1, 0))
        backward = [(target, source) for source, target in forward]
        low = lax.ppermute(
            lax.slice_in_dim(block, block.shape[dim] - width, None, axis=dim), axis, forward
        )
        high = lax.ppermute(lax.slice_in_dim(block, 0, width, axis=dim), axis, backward)
        block = jnp.concatenate([low, block, high], axis=dim)
    return block


def passed_along(value, axis, steps):
    count = lax.axis_size(axis)
    leading, last = (max(0, -steps), min(count, count - steps))
    return lax.ppermute(value, axis, [(source, source + steps) for source in range(leading, last)])


def basis_table(positions, total_cells):
    column = jnp.arange(MODES, dtype=jnp.int32)
    half_modes = MODES // 2
    mode_number = jnp.where(column < half_modes, column, column - half_modes + 1)
    phases = positions[:, None] * mode_number[None, :] % total_cells
    angles = phases.astype(jnp.float32) * jnp.float32(2.0 * math.pi / total_cells)
    table = jnp.where(column[None, :] < half_modes, jnp.cos(angles), jnp.sin(angles))
    weight = jnp.where(mode_number == 0, 1.0 / total_cells, 2.0 / total_cells).astype(jnp.float32)
    return (table, mode_number, weight)


def parcel_step(state, gas_vel):
    drop_vel = state[0:3]
    diam_sq = state[3]
    slip = gas_vel - drop_vel
    slip_sq = jnp.sum(slip * slip, axis=0)
    new_vel = (drop_vel * diam_sq + STEP_SIZE * gas_vel) / (diam_sq + STEP_SIZE)
    new_diam = diam_sq / (1.0 + STEP_SIZE * EVAP_RATE * (1.0 + slip_sq))
    mass_loss = diam_sq - new_diam
    momentum = diam_sq * (new_vel - drop_vel)
    sources = jnp.concatenate([mass_loss[None], -momentum, mass_loss[None]], axis=0) * COUPLING
    return (jnp.concatenate([new_vel, new_diam[None]], axis=0), sources)


def pick_blocks(state, chosen):
    flags = chosen.astype(jnp.int32)
    ranks = jnp.cumsum(flags) - 1
    slots = jnp.arange(MOVEB, dtype=jnp.int32)[:, None]
    select = ((ranks[None, :] == slots) & (flags[None, :] == 1)).astype(jnp.float32)
    return jnp.einsum("sb,pbzl->pszl", select, state, precision=lax.Precision.HIGHEST)


def shards(fields, coeffs, parcels, cells, counts, moves, widths):
    ax_cells, az_cells, rad_cells = (fields.shape[1], fields.shape[2], fields.shape[3])
    rad_index = lax.axis_index("rad")
    az_index = lax.axis_index("az")
    az_count = lax.axis_size("az")
    total_az = az_cells * az_count
    sector_padded = with_halo(fields, (("az", 2),), 1, True)
    slab_padded = with_halo(fields, (("ax", 1), ("rad", 3)), 1, False)
    gas_vel = fields[1:4].reshape(3, -1)[:, cells]
    new_state, sources = parcel_step(parcels, gas_vel)
    slot_index = (
        jnp.arange(BLK_DEV, dtype=jnp.int32)[:, None, None] * BLK
        + jnp.arange(BLK, dtype=jnp.int32)[None, None, :]
    )
    alive = slot_index < counts[0, 0, 0]
    new_state = jnp.where(alive[None], new_state, 0.0)
    sources = jnp.where(alive[None], sources, 0.0)
    block_move = moves[:, 0, 0]
    sent_up = pick_blocks(new_state, block_move == 1)
    sent_down = pick_blocks(new_state, block_move == -1)
    from_below = passed_along(sent_up, "ax", 1)
    from_above = passed_along(sent_down, "ax", -1)
    staying = jnp.where((block_move == 0)[None, :, None, None], new_state, 0.0)
    parcels_out = jnp.concatenate([staying, from_below, from_above], axis=1)
    coeff_cols = [coeffs[:, index][:, None, None, None] for index in range(6)]
    metric = 4.0 / (
        (rad_index * rad_cells + jnp.arange(rad_cells, dtype=jnp.int32)).astype(jnp.float32) + 4.0
    )
    ahead_ax = slab_padded[:, 2:, :, 1:-1]
    behind_ax = slab_padded[:, :-2, :, 1:-1]
    ahead_rad = slab_padded[:, 1:-1, :, 2:]
    behind_rad = slab_padded[:, 1:-1, :, :-2]
    ahead_az = sector_padded[:, :, 2:, :]
    behind_az = sector_padded[:, :, :-2, :]
    twice = 2.0 * fields
    rhs_terms = coeff_cols[0] * (ahead_ax - behind_ax) + coeff_cols[1] * (
        ahead_ax + behind_ax - twice
    )
    rhs_terms = rhs_terms + metric * (
        coeff_cols[2] * (ahead_az - behind_az) + coeff_cols[3] * (ahead_az + behind_az - twice)
    )
    rhs_terms = (
        rhs_terms
        + coeff_cols[4] * (ahead_rad - behind_rad)
        + coeff_cols[5] * (ahead_rad + behind_rad - twice)
    )
    sectioned = fields + STEP_SIZE * rhs_terms
    sectioned = (
        sectioned.reshape(FIELDS, -1).at[:, cells.reshape(-1)].add(sources.reshape(FIELDS, -1))
    )
    sectioned = sectioned.reshape(FIELDS, ax_cells, az_cells, rad_cells)
    near_cycles = sectioned[..., :CYCLES]
    positions = az_index * az_cells + jnp.arange(az_cells, dtype=jnp.int32)
    table_local, mode_number, weight = basis_table(positions, total_az)
    scale = jnp.where(mode_number[None, :] < widths[:, None], weight[None, :], 0.0)
    partial_coeff = jnp.einsum(
        "fxzr,zk->fxrk", near_cycles, table_local, precision=lax.Precision.HIGHEST
    )
    coefficients = lax.psum(partial_coeff, "az")
    filtered = jnp.einsum(
        "fxrk,zk->fxzr",
        coefficients * scale[None, None],
        table_local,
        precision=lax.Precision.HIGHEST,
    )
    inner_final = jnp.where(rad_index == 0, filtered, near_cycles)
    gas_out = jnp.concatenate([inner_final, sectioned[..., CYCLES:]], axis=3)
    return (gas_out, parcels_out)


def solution(mesh):
    return jax.shard_map(
        shards,
        mesh=mesh,
        in_specs=(
            P(None, "ax", "az", "rad"),
            P(),
            P(None, "ax", "az", "rad"),
            P("ax", "az", "rad"),
            P("ax", "az", "rad"),
            P("ax", "az", "rad"),
            P(),
        ),
        out_specs=(P(None, "ax", "az", "rad"), P(None, "ax", "az", "rad")),
        check_vma=False,
    )
```

profile of v0, /device:TPU:8, one launch (start us, length us, event | category | flops | bytes accessed | tf_op | source)
XLA Modules:
  0.0 336.8 jit_solution(4432422655409617930)
XLA Ops:
  7.2 0.0 slice-start
  7.2 0.0 all-reduce.2.cloned.1.call-start
  7.2 1.8 fusion.43
  9.0 1.9 collective-permute-start.1
  11.0 3.6 %collective-permute-start = (f32[5,1,64,128]{3,2,1,0:T(8,128)}, f32[5,1,64,128]{3,2,1,0:T(8,128)S(1)}, u32[]{:S(2)}, u32[]{:S(2)}) collective-permute-start(f32[5,1,64,128]{3,2,1,0:T(8,128)} %get-tuple-element.19), channel_id=1, source_target_pairs={{2,0},{4,2},{6,4},{8,6},{10,8},{12,10},{14,12},{3,1},{5,3},{7,5},{... | collective-permute-start | bytes 491528 | tf_op jit(solution)/shard_map/ppermute | solution.py:31
  14.6 1.6 fusion.42
  16.2 8.3 %collective-permute-start.2 = (f32[5,8,1,128]{3,1,2,0:T(8,128)}, f32[5,8,1,128]{3,1,2,0:T(8,128)S(1)}, u32[]{:S(2)}, u32[]{:S(2)}) collective-permute-start(f32[5,8,1,128]{3,1,2,0:T(8,128)} %bitcast.41), channel_id=1, source_target_pairs={{16,0},{32,16},{48,32},{64,48},{80,64},{96,80},{112,96},{128,112},... | collective-permute-start | bytes 61448 | tf_op jit(solution)/shard_map/ppermute | solution.py:31
  24.6 0.0 collective-permute-start.3
  24.6 0.0 copy-start.3
  24.6 16.6 %copy.64 = f32[3,8,64,128]{0,3,2,1:T(8,128)} copy(f32[3,8,64,128]{3,2,1,0:T(8,128)S(1)} %slice-done) | data formatting | bytes 1572864 | tf_op jit(solution)/shard_map/slice | solution.py:82
  41.3 21.3 %gather_fusion = f32[4096,3]{1,0:T(8,128)S(1)} fusion(f32[3,65536]{0,1:T(8,128)} %bitcast.74, s32[4096]{0:T(1024)S(1)} %broadcast_clamp_fusion), kind=kCustom, calls=%fused_computation | custom fusion | bytes 114688 | tf_op jit(solution)/shard_map/gather | solution.py:82
  62.6 0.0 copy-start.15
  62.6 0.0 copy-start.1
  62.6 0.6 copy.65
  63.2 0.3 negate_reduce_fusion
  64.3 0.1 copy.70
  64.4 0.1 reduce-window.16
  64.5 0.1 add_reduce_fusion.1
  64.6 0.1 add_compare_fusion
  64.7 0.8 convolution_bitcast_fusion.2
  65.4 1.9 collective-permute-start.6
  67.4 0.5 iota_compare_fusion.2
  67.9 0.5 compare_select_fusion.3
  68.4 0.8 slice_reduce_fusion.5
  69.3 0.1 copy.71
  69.4 0.1 reduce-window.17
  69.5 0.1 add_reduce_fusion
  69.6 0.1 broadcast_select_fusion
  69.7 0.1 add.210
  69.8 0.1 fusion.6
  69.9 0.6 add_divide_fusion.1
  70.5 0.7 convolution_bitcast_fusion.1
  71.3 0.0 collective-permute-done.1
  71.3 0.1 constant_dynamic-update-slice_fusion.1
  71.5 2.3 fusion.41
  73.7 2.9 copy.79
  76.6 1.3 collective-permute-start.4
  77.9 2.9 copy.80
  80.8 5.2 %collective-permute-start.5 = (f32[5,10,64,1]{2,1,3,0:T(8,128)}, f32[5,10,64,1]{2,1,3,0:T(8,128)}, u32[]{:S(2)}, u32[]{:S(2)}) collective-permute-start(f32[5,10,64,1]{2,1,3,0:T(8,128)} %copy.80), channel_id=1, source_target_pairs={{0,1},{2,3},{4,5},{6,7},{8,9},{10,11},{12,13},{14,15},{16,17},{18,... | collective-permute-start | bytes 38408 | tf_op jit(solution)/shard_map/ppermute | solution.py:28
  86.0 0.6 iota_add_fusion
  86.5 2.0 copy.66
  88.5 0.0 collective-permute-done.4
  88.5 3.1 collective-permute-start.7
  91.6 1.8 copy.60
  93.4 0.0 collective-permute-done.5
  93.4 2.5 copy.62
  95.9 0.0 collective-permute-done.2
  96.0 4.5 %multiply_add_fusion = f32[5,8,64,128]{3,2,1,0:T(8,128)} fusion(f32[5,8,64,128]{3,2,1,0:T(8,128)S(1)} %copy-done, f32[5,10,64,1]{3,2,1,0:T(8,128)} %copy.60, f32[5,10,64,128]{3,2,1,0:T(8,128)S(1)} %constant_dynamic-update-slice_fusion, f32[5,10,64,1]{3,2,1,0:T(8,128)} %copy.62, f32[5,8,1,128]{3,2,1,0:T(1,128)S(1)} %bitcast.90, f32[5,8,1,128]{3,2,1,0:T(1,128)} %bitcast.3, ...), kind=kLoop, calls=%fused_computation.9 | loop fusion | flops 9830400 | bytes 4654712 | tf_op jit(solution)/shard_map/add | solution.py:120
  100.4 18.0 %copy.63 = f32[5,8,64,128]{0,3,2,1:T(8,128)} copy(f32[5,8,64,128]{3,2,1,0:T(8,128)} %multiply_add_fusion) | data formatting | bytes 2621440 | tf_op jit(solution)/shard_map/add | solution.py:120
  118.4 42.0 %scatter_fusion = f32[5,65536]{0,1:T(8,128)} fusion(f32[5,65536]{0,1:T(8,128)} %bitcast.71, s32[4096]{0:T(1024)S(1)} %bitcast.81, f32[4096,5]{1,0:T(8,128)} %copy.66), kind=kCustom, calls=%fused_computation.1 | custom fusion | flops 20480 | bytes 262144 | tf_op jit(solution)/shard_map/scatter-add | solution.py:122
  160.4 4.6 %slice.102 = f32[5,8,64,16]{0,3,2,1:T(8,128)} slice(f32[5,8,64,128]{0,3,2,1:T(8,128)} %bitcast.72), slice={[0:5], [0:8], [0:64], [0:16]} | slice | bytes 327680 | tf_op jit(solution)/shard_map/slice | solution.py:125
  165.0 3.3 copy.81
  168.3 1.3 fusion.11
  169.7 0.0 all-reduce.2.cloned.1.call-update
  169.7 0.1 compare_select_fusion.2
  169.8 0.0 collective-permute-done.6
  169.8 0.0 collective-permute-done.7
  169.8 1.4 pad_maximum_fusion.7
  171.2 21.5 %slice.103 = f32[5,8,64,112]{0,3,2,1:T(8,128)} slice(f32[5,8,64,128]{0,3,2,1:T(8,128)} %bitcast.73), slice={[0:5], [0:8], [0:64], [16:128]} | slice | bytes 2293760 | tf_op jit(solution)/shard_map/slice | solution.py:140
  192.7 16.8 %copy.82 = f32[5,8,64,112]{3,2,1,0:T(8,128)S(1)} copy(f32[5,8,64,112]{0,3,2,1:T(8,128)} %slice.103) | data formatting | bytes 2293760
  209.6 116.9 %all-reduce.2.cloned.1.call-done = f32[5,8,16,128]{3,2,1,0:T(8,128)} async-done(((f32[5,8,16,128]{3,2,1,0:T(8,128)}), f32[5,8,16,128]{3,2,1,0:T(8,128)}) %all-reduce.2.cloned.1.call-update) | async-done | bytes 327696 | tf_op jit(solution)/shard_map/psum | solution.py:132
  326.4 1.6 fusion.2
  328.0 0.4 copy.69
  328.5 1.5 pad_maximum_fusion.6
  (46 shorter events, 0.3 us)
Async XLA Ops:
  7.2 17.4 %slice-start = ((f32[5,8,64,128]{3,2,1,0:T(8,128)}), f32[3,8,64,128]{3,2,1,0:T(8,128)S(1)}, s32[]{:S(2)}) async-start(f32[5,8,64,128]{3,2,1,0:T(8,128)} %param.7), calls=%async_computation.1 | async-start | bytes 1572864 | tf_op jit(solution)/shard_map/slice | solution.py:82
  7.2 17.4 %copy-start.2 = (f32[4,32,1,128]{3,2,1,0:T(1,128)S(1)}, f32[4,32,1,128]{3,2,1,0:T(1,128)}, u32[]{:S(2)}) copy-start(f32[4,32,1,128]{3,2,1,0:T(1,128)} %param.9) | copy-start | bytes 196612
  7.2 319.3 %all-reduce.2.cloned.1.call-start = ((), (), s32[]{:S(2)}) async-start(), calls=%async_computation | async-start | bytes 655360 | tf_op jit(solution)/shard_map/psum | solution.py:132
  9.0 62.2 %collective-permute-start.1 = (f32[5,1,64,128]{3,2,1,0:T(8,128)}, f32[5,1,64,128]{3,2,1,0:T(8,128)S(1)}, u32[]{:S(2)}, u32[]{:S(2)}) collective-permute-start(f32[5,1,64,128]{3,2,1,0:T(8,128)} %get-tuple-element.20), channel_id=1, source_target_pairs={{0,2},{2,4},{4,6},{6,8},{8,10},{10,12},{12,14},{1,3},{3,5},{5,7},{... | collective-permute-start | bytes 491528 | tf_op jit(solution)/shard_map/ppermute | solution.py:28
  11.0 60.5 %collective-permute-start = (f32[5,1,64,128]{3,2,1,0:T(8,128)}, f32[5,1,64,128]{3,2,1,0:T(8,128)S(1)}, u32[]{:S(2)}, u32[]{:S(2)}) collective-permute-start(f32[5,1,64,128]{3,2,1,0:T(8,128)} %get-tuple-element.19), channel_id=1, source_target_pairs={{2,0},{4,2},{6,4},{8,6},{10,8},{12,10},{14,12},{3,1},{5,3},{7,5},{... | collective-permute-start | bytes 491528 | tf_op jit(solution)/shard_map/ppermute | solution.py:31
  16.2 79.7 %collective-permute-start.2 = (f32[5,8,1,128]{3,1,2,0:T(8,128)}, f32[5,8,1,128]{3,1,2,0:T(8,128)S(1)}, u32[]{:S(2)}, u32[]{:S(2)}) collective-permute-start(f32[5,8,1,128]{3,1,2,0:T(8,128)} %bitcast.41), channel_id=1, source_target_pairs={{16,0},{32,16},{48,32},{64,48},{80,64},{96,80},{112,96},{128,112},... | collective-permute-start | bytes 61448 | tf_op jit(solution)/shard_map/ppermute | solution.py:31
  24.6 71.4 %collective-permute-start.3 = (f32[5,8,1,128]{3,1,2,0:T(8,128)}, f32[5,8,1,128]{3,1,2,0:T(8,128)}, u32[]{:S(2)}, u32[]{:S(2)}) collective-permute-start(f32[5,8,1,128]{3,1,2,0:T(8,128)} %bitcast.42), channel_id=1, source_target_pairs={{0,16},{16,32},{32,48},{48,64},{64,80},{80,96},{96,112},{112,128},... | collective-permute-start | bytes 61448 | tf_op jit(solution)/shard_map/ppermute | solution.py:28
  24.6 16.6 %copy-start.3 = (s32[32,1,128]{2,1,0:T(1,128)S(1)}, s32[32,1,128]{2,1,0:T(1,128)}, u32[]{:S(2)}) copy-start(s32[32,1,128]{2,1,0:T(1,128)} %param.10) | copy-start | bytes 49156
  62.6 1.7 copy-start.15
  62.6 5.8 %copy-start.1 = (f32[5,6]{1,0:T(8,128)S(1)}, f32[5,6]{1,0:T(8,128)}, u32[]{:S(2)}) copy-start(f32[5,6]{1,0:T(8,128)} %param.8) | copy-start | bytes 364
  63.2 8.0 %copy-start = (f32[5,8,64,128]{3,2,1,0:T(8,128)S(1)}, f32[5,8,64,128]{3,2,1,0:T(8,128)}, u32[]{:S(2)}) copy-start(f32[5,8,64,128]{3,2,1,0:T(8,128)} %param.7) | copy-start | bytes 3932164
  65.4 104.4 %collective-permute-start.6 = (f32[4,4,1,128]{3,1,0,2:T(4,128)}, f32[4,4,1,128]{3,1,0,2:T(4,128)}, u32[]{:S(2)}, u32[]{:S(2)}) collective-permute-start(f32[4,4,1,128]{3,1,0,2:T(4,128)} %convolution_bitcast_fusion.2), channel_id=1, source_target_pairs={{0,2},{2,4},{4,6},{6,8},{8,10},{10,12},{12,14},{1,3},{3,5},{5,7},{... | collective-permute-start | bytes 24584 | tf_op jit(solution)/shard_map/ppermute | solution.py:39
  76.6 11.9 %collective-permute-start.4 = (f32[5,10,64,1]{2,1,3,0:T(8,128)}, f32[5,10,64,1]{2,1,3,0:T(8,128)S(1)}, u32[]{:S(2)}, u32[]{:S(2)}) collective-permute-start(f32[5,10,64,1]{2,1,3,0:T(8,128)} %copy.79), channel_id=1, source_target_pairs={{1,0},{3,2},{5,4},{7,6},{9,8},{11,10},{13,12},{15,14},{17,16},{19,... | collective-permute-start | bytes 38408 | tf_op jit(solution)/shard_map/ppermute | solution.py:31
  80.8 12.6 %collective-permute-start.5 = (f32[5,10,64,1]{2,1,3,0:T(8,128)}, f32[5,10,64,1]{2,1,3,0:T(8,128)}, u32[]{:S(2)}, u32[]{:S(2)}) collective-permute-start(f32[5,10,64,1]{2,1,3,0:T(8,128)} %copy.80), channel_id=1, source_target_pairs={{0,1},{2,3},{4,5},{6,7},{8,9},{10,11},{12,13},{14,15},{16,17},{18,... | collective-permute-start | bytes 38408 | tf_op jit(solution)/shard_map/ppermute | solution.py:28
  88.5 7.4 %copy-start.4 = (f32[5]{0:T(128)S(1)}, f32[5]{0:T(128)}, u32[]{:S(2)}) copy-start(f32[5]{0:T(128)} %get-tuple-element.6) | copy-start | bytes 64
  88.5 7.4 %copy-start.5 = (f32[5]{0:T(128)S(1)}, f32[5]{0:T(128)}, u32[]{:S(2)}) copy-start(f32[5]{0:T(128)} %get-tuple-element.7) | copy-start | bytes 64
  88.5 7.4 %copy-start.6 = (f32[5]{0:T(128)S(1)}, f32[5]{0:T(128)}, u32[]{:S(2)}) copy-start(f32[5]{0:T(128)} %get-tuple-element.8) | copy-start | bytes 64
  88.5 7.4 %copy-start.7 = (f32[5]{0:T(128)S(1)}, f32[5]{0:T(128)}, u32[]{:S(2)}) copy-start(f32[5]{0:T(128)} %get-tuple-element.9) | copy-start | bytes 64
  88.5 7.5 %copy-start.8 = (f32[5]{0:T(128)S(1)}, f32[5]{0:T(128)}, u32[]{:S(2)}) copy-start(f32[5]{0:T(128)} %get-tuple-element.10) | copy-start | bytes 64
  88.5 7.5 %copy-start.9 = (f32[5]{0:T(128)S(1)}, f32[5]{0:T(128)}, u32[]{:S(2)}) copy-start(f32[5]{0:T(128)} %get-tuple-element.11) | copy-start | bytes 64
  88.5 7.5 %copy-start.12 = (f32[128]{0:T(128)S(1)}, f32[128]{0:T(128)}, u32[]{:S(2)}) copy-start(f32[128]{0:T(128)} %add_divide_fusion.1) | copy-start | bytes 1540
  88.5 81.2 %collective-permute-start.7 = (f32[4,4,1,128]{3,1,0,2:T(4,128)}, f32[4,4,1,128]{3,1,0,2:T(4,128)S(1)}, u32[]{:S(2)}, u32[]{:S(2)}) collective-permute-start(f32[4,4,1,128]{3,1,0,2:T(4,128)} %convolution_bitcast_fusion.1), channel_id=1, source_target_pairs={{2,0},{4,2},{6,4},{8,6},{10,8},{12,10},{14,12},{3,1},{5,3},{7,5},{... | collective-permute-start | bytes 24584 | tf_op jit(solution)/shard_map/ppermute | solution.py:39
  165.0 3.3 copy-start.10
  165.0 3.3 copy-start.11
  165.0 4.7 %copy-start.13 = (s32[16]{0:T(128)S(1)}, s32[16]{0:T(128)}, u32[]{:S(2)}) copy-start(s32[16]{0:T(128)} %param.13) | copy-start | bytes 196
  165.0 4.7 %copy-start.14 = (f32[128]{0:T(128)S(1)}, f32[128]{0:T(128)}, u32[]{:S(2)}) copy-start(f32[128]{0:T(128)} %compare_select_fusion.3) | copy-start | bytes 1540
Sparse Core Ops, SparseCore 0:
  169.8 156.5 all-reduce.1
where the time goes:
time: 338 us; the launch traced here: 337 us
  local copies, waits for them, and re-layouts  122 us (36%)
  waiting for transfers between devices  117 us (35%)
  other arithmetic  52.7 us (16%)
  starting transfers between devices  25.3 us (7%)
  between operations  15.2 us (4%)
  matrix products  4.42 us (1%)
    psum x1, waiting for transfers between devices, shards(): coefficients = lax.psum(partial_coeff, 'az')  117 us
    scatter-add x1, other arithmetic, shards(): sectioned.reshape(FIELDS, -1).at[:, cells.reshape(-1)]  42 us
    unnamed x39, local copies, waits for them, and re-layouts  26.2 us
    gather x2, local copies, waits for them, and re-layouts, shards(): gas_vel = fields[1:4].reshape(3, -1)[:, cells]  21.9 us
    slice x1, local copies, waits for them, and re-layouts, shards(): gas_out = jnp.concatenate([inner_final, sectioned[..., CYCLES:]], axis=3)  21.5 us
    add x1, local copies, waits for them, and re-layouts, shards(): sectioned = fields + STEP_SIZE * rhs_terms  18 us
    slice x3, local copies, waits for them, and re-layouts, shards(): gas_vel = fields[1:4].reshape(3, -1)[:, cells]  16.6 us
    ppermute x3, starting transfers between devices, with_halo(): lax.ppermute(lax.slice_in_dim(block, 0, width, axis=dim), axis, backward)  13.2 us
  transfers between devices with their start and end apart: 9, of which 1 were waited for; matrix products, arithmetic and copies ran while one was open for 52% of the time, Pallas kernels for 0%

commit v1 on v0

v1 whole, which is shorter than its diff:
```python
import math

import jax
import jax.numpy as jnp
import numpy as np
from jax import lax
from jax.experimental import pallas as pl
from jax.experimental.pallas import tpu as pltpu
from jax.sharding import PartitionSpec as P

FIELDS = 5
CYCLES = 16
MODES = 128
HALF = MODES // 2
BLK = 128
BLK_DEV = 32
MOVEB = 4
CAX, CAZ, CR = 8, 64, 128
ROWS = CAX * CAZ
PARCELS = BLK * BLK_DEV
NAZ = 1024
N_AZ = 16
PAIRS = CAX // 2
QUADS = CYCLES // 4
LINES = FIELDS * 4

STEP_SIZE = 0.5
EVAP_RATE = 0.5
COUPLING = 0.5

F32 = jnp.float32
BF16 = jnp.bfloat16
HIGHEST = lax.Precision.HIGHEST
VMEM = pl.BlockSpec(memory_space=pltpu.VMEM)
SMEM = pl.BlockSpec(memory_space=pltpu.SMEM)
NT = (((1,), (1,)), ((), ()))


def basis_rows():
    column = np.arange(MODES)
    mode = np.where(column < HALF, column, column - HALF + 1)
    phases = (mode[:, None] * np.arange(NAZ)[None, :]) % NAZ
    angles = phases.astype(np.float32) * np.float32(2.0 * math.pi / NAZ)
    return np.where(column[:, None] < HALF, np.cos(angles), np.sin(angles)).astype(np.float32)


def iota(shape, axis):
    return lax.broadcasted_iota(jnp.int32, shape, axis)


def halves(value):
    high = value.astype(BF16)
    return high, (value - high.astype(F32)).astype(BF16)


def call(body, out_shape, in_specs, flops, nbytes, scratch=(), mib=24):
    return pl.pallas_call(
        body,
        out_shape=[jax.ShapeDtypeStruct(shape, F32) for shape in out_shape],
        in_specs=in_specs,
        out_specs=[VMEM] * len(out_shape),
        scratch_shapes=list(scratch),
        compiler_params=pltpu.CompilerParams(vmem_limit_bytes=mib * 2**20),
        cost_estimate=pl.CostEstimate(flops=flops, bytes_accessed=nbytes, transcendentals=0),
    )


def edges_body(rad_ref, q_ref, ax_lo, ax_hi, az_lo, az_hi, rad_out):
    ax_lo[...] = q_ref[:, 0]
    ax_hi[...] = q_ref[:, CAX - 1]
    az_lo[...] = q_ref[:, :, 0, :]
    az_hi[...] = q_ref[:, :, CAZ - 1, :]
    extra = jnp.where(rad_ref[0] == 0, 1, 0)
    lane = iota((32, CR), 1)
    packed = jnp.zeros((32, CR), F32)
    for f in range(FIELDS):
        for g in range(16):
            part = q_ref[f, g // 2, (g % 2) * 32 : (g % 2) * 32 + 32, :]
            spot = g * 8 + f
            packed = jnp.where(lane == spot, pltpu.roll(part, spot + extra, 1), packed)
    rad_out[...] = packed


def one_hot_rows(cells_ref, first, blocks):
    cells = jnp.concatenate([cells_ref[first + i : first + i + 1, :] for i in range(blocks)], axis=1)
    width = blocks * BLK
    hit = iota((ROWS, width), 0) == (cells >> 7)
    return jnp.where(hit, 1.0, 0.0).astype(BF16), cells & (CR - 1)


def parcels_body(
    count_ref, move_ref, q_ref, parcel_ref, cells_ref,
    src_out, stay_out, up_out, down_out, near_out,
    hot_ref, gas_ref, state_ref, spread_ref,
):
    parts = [[], [], []]
    for f in range(3):
        table = q_ref[f + 1].reshape(ROWS, CR).T
        high = table.astype(BF16)
        rest = table - high.astype(F32)
        mid = rest.astype(BF16)
        parts[0].append(high)
        parts[1].append(mid)
        parts[2].append((rest - mid.astype(F32)).astype(BF16))
    parts = [jnp.concatenate(part, axis=0) for part in parts]
    for first in range(0, BLK_DEV, 4):
        width = 4 * BLK
        hot, lanes = one_hot_rows(cells_ref, first, 4)
        hot_ref[:, first * BLK : first * BLK + width] = hot
        rows = sum(jnp.dot(part, hot, preferred_element_type=F32) for part in parts)
        mask = iota((CR, width), 0) == lanes
        for f in range(3):
            found = jnp.sum(jnp.where(mask, rows[f * CR : (f + 1) * CR], 0.0), axis=0, keepdims=True)
            for i in range(4):
                gas_ref[f, first + i : first + i + 1, :] = found[:, i * BLK : (i + 1) * BLK]
    slot = iota((BLK_DEV, BLK), 0) * BLK + iota((BLK_DEV, BLK), 1)
    alive = slot < count_ref[0]
    diam = parcel_ref[3]
    vel = [parcel_ref[i] for i in range(3)]
    gas = [gas_ref[i] for i in range(3)]
    slip = [g - u for g, u in zip(gas, vel)]
    slip_sq = slip[0] * slip[0] + slip[1] * slip[1] + slip[2] * slip[2]
    new_vel = [(u * diam + STEP_SIZE * g) / (diam + STEP_SIZE) for u, g in zip(vel, gas)]
    new_diam = diam / (1.0 + STEP_SIZE * EVAP_RATE * (1.0 + slip_sq))
    sources = [(diam - new_diam) * COUPLING] + [
        -(diam * (v - u)) * COUPLING for v, u in zip(new_vel, vel)
    ]
    sources = [jnp.where(alive, s, 0.0) for s in sources]
    for i in range(4):
        src_out[i] = sources[i]
        state_ref[i] = jnp.where(alive, (new_vel + [new_diam])[i], 0.0)
    up_out[...] = jnp.zeros_like(up_out)
    down_out[...] = jnp.zeros_like(down_out)

    def place(block, ranks):
        up, down = ranks
        move = move_ref[block]
        row = state_ref[:, pl.ds(block, 1), :]
        stay_out[:, pl.ds(block, 1), :] = jnp.where(move == 0, row, 0.0)

        @pl.when(move == 1)
        def _():
            up_out[:, pl.ds(jnp.minimum(up, MOVEB - 1), 1), :] = row

        @pl.when(move == -1)
        def _():
            down_out[:, pl.ds(jnp.minimum(down, MOVEB - 1), 1), :] = row

        return up + (move == 1).astype(jnp.int32), down + (move == -1).astype(jnp.int32)

    lax.fori_loop(0, BLK_DEV, place, (jnp.int32(0), jnp.int32(0)))
    split = []
    for s in sources:
        high = s.astype(BF16).astype(F32)
        split.append((high, s - high))
    for block in range(BLK_DEV):
        mask = iota((CYCLES, BLK), 0) == (cells_ref[block : block + 1, :] & (CR - 1))
        for i in range(4):
            for half in range(2):
                row = split[i][half][block : block + 1, :]
                first = (half * 4 + i) * CYCLES
                spread_ref[first : first + CYCLES, block * BLK : (block + 1) * BLK] = jnp.where(
                    mask, row, 0.0
                ).astype(BF16)
    total = lax.dot_general(spread_ref[...], hot_ref[...], NT, preferred_element_type=F32)
    near_out[...] = total[: 4 * CYCLES] + total[4 * CYCLES :]


SOURCE_OF = (0, 1, 2, 3, 0)


def section_body(
    rad_ref, coef_ref, q_ref, ax_prev, ax_next, az_prev, az_next, rad_in, near_ref, sect_out, send_out
):
    rad = rad_ref[0]
    lane = iota((CAZ, CR), 1)
    row = iota((CAZ, CR), 0)
    metric = 4.0 / ((rad * CR + lane).astype(F32) + 4.0)
    last = (lane == CR - 1) & (rad == 0)
    first = (lane == 0) & (rad == 1)
    ends = (lane == CR - 1) | (lane == 0)
    for f in range(FIELDS):
        c = [coef_ref[f, i] for i in range(6)]
        mid = (1.0 - c[1] - c[5]) - c[3] * metric
        az_up = (0.5 * (c[2] + c[3])) * metric
        az_down = (0.5 * (c[3] - c[2])) * metric
        ax_up, ax_down = 0.5 * (c[0] + c[1]), 0.5 * (c[1] - c[0])
        rad_up, rad_down = 0.5 * (c[4] + c[5]), 0.5 * (c[5] - c[4])
        for a in range(CAX):
            q = q_ref[f, a]
            ahead = q_ref[f, a + 1] if a + 1 < CAX else ax_next[f]
            behind = q_ref[f, a - 1] if a else ax_prev[f]
            az_a = jnp.where(row == CAZ - 1, az_next[f, a : a + 1, :], pltpu.roll(q, CAZ - 1, 0))
            az_b = jnp.where(row == 0, az_prev[f, a : a + 1, :], pltpu.roll(q, 1, 0))
            edge = jnp.concatenate(
                [rad_in[:, (2 * a + h) * 8 + f : (2 * a + h) * 8 + f + 1] for h in range(2)], axis=0
            )
            edge = jnp.broadcast_to(edge, (CAZ, CR))
            r_a = jnp.where(last, edge, jnp.where(lane == CR - 1, 0.0, pltpu.roll(q, CR - 1, 1)))
            r_b = jnp.where(first, edge, jnp.where(lane == 0, 0.0, pltpu.roll(q, 1, 1)))
            out = (
                mid * q + ax_up * ahead + ax_down * behind + az_up * az_a + az_down * az_b
                + rad_up * r_a + rad_down * r_b
            )
            sect_out[f, a] = out
        for pair in range(PAIRS):
            block = sect_out[f, 2 * pair : 2 * pair + 2].reshape(2 * CAZ, CR).T[:CYCLES]
            s = SOURCE_OF[f] * CYCLES
            block = block + near_ref[s : s + CYCLES, pair * 2 * CAZ : (pair + 1) * 2 * CAZ]
            for quad in range(QUADS):
                send_out[pair * QUADS + quad, f * 4 : f * 4 + 4, :] = block[quad * 4 : quad * 4 + 4]


def scatter_body(sect_ref, src_ref, cells_ref, sect_out, acc_ref):
    step = 8
    for first in range(0, BLK_DEV, step):
        hot, lanes = one_hot_rows(cells_ref, first, step)
        mask = iota((CR, step * BLK), 0) == lanes
        spread = [[], []]
        for i in range(4):
            row = jnp.concatenate([src_ref[i, first + j : first + j + 1, :] for j in range(step)], axis=1)
            high = row.astype(BF16).astype(F32)
            spread[0].append(jnp.where(mask, high, 0.0).astype(BF16))
            spread[1].append(jnp.where(mask, row - high, 0.0).astype(BF16))
        total = sum(
            lax.dot_general(hot, jnp.concatenate(part, axis=0), NT, preferred_element_type=F32)
            for part in spread
        )
        if first == 0:
            acc_ref[...] = total
        else:
            acc_ref[...] += total
    for f in range(FIELDS):
        s = SOURCE_OF[f] * CR
        added = acc_ref[:, s : s + CR].reshape(CAX, CAZ, CR)
        sect_out[f] = sect_ref[f] + added


def filter_body(az_ref, width_ref, basis_ref, got_ref, send_out, line_ref):
    quad = az_ref[0] % QUADS
    lane = iota((LINES, 2 * CAZ), 1)
    low = lane < CAZ
    line_ref[...] = jnp.zeros_like(line_ref)
    for i in range(N_AZ // 2):
        t0, t1 = got_ref[2 * i], got_ref[2 * i + 1]
        cols = slice(i * 2 * CAZ, (i + 1) * 2 * CAZ)
        line_ref[0:LINES, cols] = jnp.where(low, t0, pltpu.roll(t1, CAZ, 1))
        line_ref[24 : 24 + LINES, cols] = jnp.where(low, pltpu.roll(t0, CAZ, 1), t1)
    basis = basis_ref[...]
    coefs = lax.dot_general(line_ref[...], basis, NT, precision=HIGHEST, preferred_element_type=F32)
    column = iota((48, MODES), 1)
    row = iota((48, MODES), 0) % 4
    mode = jnp.where(column < HALF, column, column - HALF + 1)
    width = jnp.zeros((48, MODES), jnp.int32)
    for i in range(4):
        width = jnp.where(row == i, width_ref[quad * 4 + i], width)
    weight = jnp.where(mode == 0, 1.0 / NAZ, 2.0 / NAZ)
    coefs = coefs * jnp.where(mode < width, weight, 0.0)
    line_ref[...] = jnp.dot(coefs, basis, precision=HIGHEST, preferred_element_type=F32)
    for i in range(N_AZ // 2):
        cols = slice(i * 2 * CAZ, (i + 1) * 2 * CAZ)
        t0, t1 = line_ref[0:LINES, cols], line_ref[24 : 24 + LINES, cols]
        send_out[2 * i] = jnp.where(low, t0, pltpu.roll(t1, CAZ, 1))
        send_out[2 * i + 1] = jnp.where(low, pltpu.roll(t0, CAZ, 1), t1)


def merge_body(rad_ref, sect_ref, got_ref, stay_ref, below_ref, above_ref, gas_out, parcels_out, flip_ref):
    near = (iota((2 * CAZ, CR), 1) < CYCLES) & (rad_ref[0] == 0)
    flip_ref[...] = jnp.zeros_like(flip_ref)
    for pair in range(PAIRS):
        for f in range(FIELDS):
            for quad in range(QUADS):
                first = f * CYCLES + quad * 4
                flip_ref[first : first + 4, :] = got_ref[pair * QUADS + quad, f * 4 : f * 4 + 4, :]
        turned = flip_ref[...].T
        for f in range(FIELDS):
            moved = pltpu.roll(turned, (CR - f * CYCLES) % CR, 1) if f else turned
            kept = sect_ref[f, 2 * pair : 2 * pair + 2].reshape(2 * CAZ, CR)
            gas_out[f, 2 * pair : 2 * pair + 2] = jnp.where(near, moved, kept).reshape(2, CAZ, CR)
    parcels_out[:, 0:BLK_DEV, :] = stay_ref[...]
    parcels_out[:, BLK_DEV : BLK_DEV + MOVEB, :] = below_ref[...]
    parcels_out[:, BLK_DEV + MOVEB :, :] = above_ref[...]


def shards(fields, coeffs, parcels, cells, counts, moves, widths):
    rad_index = lax.axis_index("rad").astype(jnp.int32).reshape(1)
    az_index = lax.axis_index("az").astype(jnp.int32).reshape(1)
    n_ax, n_az, n_rad = (lax.axis_size(axis) for axis in ("ax", "az", "rad"))
    parcels = parcels.reshape(4, BLK_DEV, BLK)
    cells = cells.reshape(BLK_DEV, BLK)
    counts = counts.reshape(1)
    moves = moves.reshape(BLK_DEV)
    up = [(i, i + 1) for i in range(n_ax - 1)]
    down = [(i + 1, i) for i in range(n_ax - 1)]
    ahead = [(i, (i + 1) % n_az) for i in range(n_az)]
    back = [((i + 1) % n_az, i) for i in range(n_az)]
    across = [(i, i ^ 1) for i in range(n_rad)]

    ax_lo, ax_hi, az_lo, az_hi, rad_edge = call(
        edges_body,
        [(FIELDS, CAZ, CR)] * 2 + [(FIELDS, CAX, CR)] * 2 + [(32, CR)],
        [SMEM, VMEM], 10**6, 2 * 10**6,
    )(rad_index, fields)
    ax_prev = lax.ppermute(ax_hi, "ax", up)
    ax_next = lax.ppermute(ax_lo, "ax", down)
    az_prev = lax.ppermute(az_hi, "az", ahead)
    az_next = lax.ppermute(az_lo, "az", back)
    rad_got = lax.ppermute(rad_edge, "rad", across)

    src, stay, sent_up, sent_down, near = call(
        parcels_body,
        [(4, BLK_DEV, BLK), (4, BLK_DEV, BLK), (4, MOVEB, BLK), (4, MOVEB, BLK), (4 * CYCLES, ROWS)],
        [SMEM, SMEM, VMEM, VMEM, VMEM], 6 * 10**9, 2 * 10**6,
        [
            pltpu.VMEM((ROWS, PARCELS), BF16),
            pltpu.VMEM((3, BLK_DEV, BLK), F32),
            pltpu.VMEM((4, BLK_DEV, BLK), F32),
            pltpu.VMEM((8 * CYCLES, PARCELS), BF16),
        ],
    )(counts, moves, fields, parcels, cells)
    from_below = lax.ppermute(sent_up, "ax", up)
    from_above = lax.ppermute(sent_down, "ax", down)

    sect, to_owner = call(
        section_body,
        [(FIELDS, CAX, CAZ, CR), (N_AZ, LINES, 2 * CAZ)],
        [SMEM, SMEM] + [VMEM] * 7, 10**7, 4 * 10**6,
    )(rad_index, coeffs, fields, ax_prev, ax_next, az_prev, az_next, rad_got, near)
    lines = lax.all_to_all(to_owner, "az", 0, 0, tiled=True)

    (sect,) = call(
        scatter_body,
        [(FIELDS, CAX, CAZ, CR)],
        [VMEM] * 3, 8 * 10**9, 4 * 10**6,
        [pltpu.VMEM((ROWS, 4 * CR), F32)],
    )(sect, src, cells)

    (to_home,) = call(
        filter_body,
        [(N_AZ, LINES, 2 * CAZ)],
        [SMEM, SMEM, VMEM, VMEM], 10**8, 10**6,
        [pltpu.VMEM((48, NAZ), F32)],
    )(az_index, widths, jnp.asarray(basis_rows()), lines)
    filtered = lax.all_to_all(to_home, "az", 0, 0, tiled=True)

    gas_out, parcels_out = call(
        merge_body,
        [(FIELDS, CAX, CAZ, CR), (4, BLK_DEV + 2 * MOVEB, BLK)],
        [SMEM] + [VMEM] * 5, 10**6, 4 * 10**6,
        [pltpu.VMEM((CR, CR), F32)],
    )(rad_index, sect, filtered, stay, from_below, from_above)
    return gas_out, parcels_out.reshape(4, BLK_DEV + 2 * MOVEB, 1, BLK)


def solution(mesh):
    block = P(None, "ax", "az", "rad")
    flat = P("ax", "az", "rad")
    return jax.shard_map(
        shards,
        mesh=mesh,
        in_specs=(block, P(), block, flat, flat, flat, P()),
        out_specs=(block, block),
        check_vma=False,
    )
```

time: 338 us -> 71.5 us (0.21)
  local copies, waits for them, and re-layouts: 122 us -> 2.17 us
  waiting for transfers between devices: 117 us -> 13.9 us
  other arithmetic: 52.7 us -> 0 us
  Pallas kernels: 0 us -> 22.7 us
  between operations: 15.2 us -> 1.49 us
  starting transfers between devices: 25.3 us -> 30.7 us
  matrix products: 4.42 us -> 0 us
    psum x1 -> x0, waiting for transfers between devices: 117 us -> none  [shards(): coefficients = lax.psum(partial_coeff, 'az')]
    slice x9 -> x0, local copies, waits for them, and re-layouts: 49.2 us -> none  [the longest x1 21.5 us: shards(): gas_out = jnp.concatenate([inner_final, sectioned[..., CYCLES:]], axis=3)]
    scatter-add x1 -> x0, other arithmetic: 42 us -> none  [shards(): sectioned.reshape(FIELDS, -1).at[:, cells.reshape(-1)]]
    unnamed x39 -> x16, local copies, waits for them, and re-layouts: 26.2 us -> 2.17 us
    pallas_call x0 -> x6, Pallas kernels: none -> 22.7 us  [the longest x1 8.44 us: shards(): call(parcels_body, [(4, BLK_DEV, BLK), (4, BLK_DEV, BLK), (4, MOVEB, BLK)...]
    gather x2 -> x0, local copies, waits for them, and re-layouts: 21.9 us -> none  [shards(): gas_vel = fields[1:4].reshape(3, -1)[:, cells]]
    add x3 -> x0, local copies, waits for them, and re-layouts: 18.1 us -> none  [the longest x1 18 us: shards(): sectioned = fields + STEP_SIZE * rhs_terms]
    all_to_all x0 -> x2, waiting for transfers between devices: none -> 13.9 us  [the longest x1 6.99 us: shards(): filtered = lax.all_to_all(to_home, 'az', 0, 0, tiled=True)]
  transfers between devices with their start and end apart: 9 -> 9, of which waited for: 1 -> 2; matrix products, arithmetic and copies ran while one was open for 52% -> 0% of each run, Pallas kernels for 0% -> 22%
where the time goes in v1:
time: 71.5 us; the launch traced here: 71 us
  starting transfers between devices  30.7 us (43%)
  Pallas kernels  22.7 us (32%)
  waiting for transfers between devices  13.9 us (19%)
  local copies, waits for them, and re-layouts  2.17 us (3%)
  between operations  1.49 us (2%)
    pallas_call x1, Pallas kernels, shards(): call(parcels_body, [(4, BLK_DEV, BLK), (4, BLK_DEV, BLK), (4, MOVEB, BLK)...  8.44 us
    all_to_all x1, waiting for transfers between devices, shards(): filtered = lax.all_to_all(to_home, 'az', 0, 0, tiled=True)  6.99 us
    all_to_all x1, waiting for transfers between devices, shards(): lines = lax.all_to_all(to_owner, 'az', 0, 0, tiled=True)  6.93 us
    all_to_all x1, starting transfers between devices, shards(): lines = lax.all_to_all(to_owner, 'az', 0, 0, tiled=True)  6.26 us
    ppermute x1, starting transfers between devices, shards(): az_next = lax.ppermute(az_lo, 'az', back)  5.29 us
    pallas_call x1, Pallas kernels, shards(): call(section_body, [(FIELDS, CAX, CAZ, CR), (N_AZ, LINES, 2 * CAZ)], [SME...  5.19 us
    pallas_call x1, Pallas kernels, shards(): call(scatter_body, [(FIELDS, CAX, CAZ, CR)], [VMEM] * 3, 8 * 10 ** 9, 4 *...  4.52 us
    all_to_all x1, starting transfers between devices, shards(): filtered = lax.all_to_all(to_home, 'az', 0, 0, tiled=True)  3.7 us
  transfers between devices with their start and end apart: 9, of which 2 were waited for; matrix products, arithmetic and copies ran while one was open for 0% of the time, Pallas kernels for 22%

profile of v1, /device:TPU:8, one launch (start us, length us, event | category | flops | bytes accessed | tf_op | source)
XLA Modules:
  0.0 71.0 jit_solution(18113724916868397198)
XLA Ops:
  0.6 0.0 copy-start.7
  0.6 0.0 copy-start
  0.7 1.3 %copy-done = f32[5,8,64,128]{3,2,1,0:T(8,128)S(1)} copy-done((f32[5,8,64,128]{3,2,1,0:T(8,128)S(1)}, f32[5,8,64,128]{3,2,1,0:T(8,128)}, u32[]{:S(2)}) %copy-start) | copy-done | bytes 1310744
  2.0 0.0 copy-start.1
  2.0 0.0 copy-start.6
  2.0 0.4 shard_map.95
  2.4 1.6 %collective-permute-start.4 = (f32[32,128]{1,0:T(8,128)S(1)}, f32[32,128]{1,0:T(8,128)S(1)}, u32[]{:S(2)}, u32[]{:S(2)}) collective-permute-start(f32[32,128]{1,0:T(8,128)S(1)} %get-tuple-element.20), channel_id=1, source_target_pairs={{0,1},{1,0},{2,3},{3,2},{4,5},{5,4},{6,7},{7,6},{8,9},{9,8},{10,11... | collective-permute-start | bytes 49160 | tf_op jit(solution)/shard_map/ppermute | solution.py:308
  4.0 2.7 %collective-permute-start.2 = (f32[5,8,128]{2,1,0:T(8,128)S(1)}, f32[5,8,128]{2,1,0:T(8,128)S(1)}, u32[]{:S(2)}, u32[]{:S(2)}) collective-permute-start(f32[5,8,128]{2,1,0:T(8,128)S(1)} %get-tuple-element.18), channel_id=1, source_target_pairs={{0,16},{16,32},{32,48},{48,64},{64,80},{80,96},{96,112},{112,128},... | collective-permute-start | bytes 61448 | tf_op jit(solution)/shard_map/ppermute | solution.py:306
  6.7 5.3 %collective-permute-start.3 = (f32[5,8,128]{2,1,0:T(8,128)S(1)}, f32[5,8,128]{2,1,0:T(8,128)S(1)}, u32[]{:S(2)}, u32[]{:S(2)}) collective-permute-start(f32[5,8,128]{2,1,0:T(8,128)S(1)} %get-tuple-element.19), channel_id=1, source_target_pairs={{16,0},{32,16},{48,32},{64,48},{80,64},{96,80},{112,96},{128,112},... | collective-permute-start | bytes 61448 | tf_op jit(solution)/shard_map/ppermute | solution.py:307
  12.0 1.9 %collective-permute-start = (f32[5,64,128]{2,1,0:T(8,128)S(1)}, f32[5,64,128]{2,1,0:T(8,128)S(1)}, u32[]{:S(2)}, u32[]{:S(2)}) collective-permute-start(f32[5,64,128]{2,1,0:T(8,128)S(1)} %get-tuple-element.16), channel_id=1, source_target_pairs={{0,2},{2,4},{4,6},{6,8},{8,10},{10,12},{12,14},{1,3},{3,5},{5,7},{... | collective-permute-start | bytes 491528 | tf_op jit(solution)/shard_map/ppermute | solution.py:304
  13.9 3.6 %collective-permute-start.1 = (f32[5,64,128]{2,1,0:T(8,128)S(1)}, f32[5,64,128]{2,1,0:T(8,128)S(1)}, u32[]{:S(2)}, u32[]{:S(2)}) collective-permute-start(f32[5,64,128]{2,1,0:T(8,128)S(1)} %get-tuple-element.17), channel_id=1, source_target_pairs={{2,0},{4,2},{6,4},{8,6},{10,8},{12,10},{14,12},{3,1},{5,3},{7,5},{... | collective-permute-start | bytes 491528 | tf_op jit(solution)/shard_map/ppermute | solution.py:305
  18.2 0.0 copy-done.7
  18.2 0.0 copy-done.1
  18.2 0.0 copy-done.6
  18.2 0.0 copy-start.5
  18.2 0.8 %copy-done.5 = f32[4,32,1,128]{3,2,1,0:T(1,128)S(1)} copy-done((f32[4,32,1,128]{3,2,1,0:T(1,128)S(1)}, f32[4,32,1,128]{3,2,1,0:T(1,128)}, u32[]{:S(2)}) %copy-start.5) | copy-done | bytes 65560
  19.1 0.0 copy-start.3
  19.1 8.4 %shard_map.96 = (f32[4,32,128]{2,1,0:T(8,128)S(1)}, f32[4,32,128]{2,1,0:T(8,128)S(1)}, f32[4,4,128]{2,1,0:T(4,128)S(1)}, f32[4,4,128]{2,1,0:T(4,128)S(1)}, f32[64,512]{1,0:T(8,128)S(1)}) custom-call(s32[1]{0:T(128)} %bitcast.9.count_ref, s32[32]{0:T(128)S(1)} %bitcast.13, f32[5,8,64,128]{3,2,1,0:T(8,128)S(1)} %copy-done.1, f32[4,32,128]{2,1,0:T(8,128)S(1)} %bitcast.10, ...), custom_call_target="tpu_custom_call" | custom-call | flops 6000000000 | bytes 2000000 | tf_op jit(solution)/shard_map/pallas_call | solution.py:310
  27.5 0.0 copy-start.2
  27.5 0.0 copy-start.4
  27.5 0.0 collective-permute-done.4.rad_in
  27.6 0.0 collective-permute-done.2.az_prev
  27.6 0.0 collective-permute-done.3.az_next
  27.6 0.0 collective-permute-done.ax_prev
  27.6 0.0 collective-permute-done.1.ax_next
  27.6 0.0 copy-done.3
  27.6 5.2 %shard_map.97 = (f32[5,8,64,128]{3,2,1,0:T(8,128)S(1)}, f32[16,20,128]{2,1,0:T(8,128)}) custom-call(s32[1]{0:T(128)} %bitcast.rad_ref, f32[5,6]{1,0:T(8,128)S(1)} %copy-done.3, f32[5,8,64,128]{3,2,1,0:T(8,128)S(1)} %copy-done.1, f32[5,64,128]{2,1,0:T(8,128)S(1)} %collective-permute-done.ax_prev, f32[5,64,128]{2,1,0:T(8,128)S(1)} %collective-permute-done.1.ax_next, ...), custom_call_target="tpu_custom_call" | custom-call | flops 10000000 | bytes 4000000 | tf_op jit(solution)/shard_map/pallas_call | solution.py:324
  32.8 6.3 %all-to-all-start = ((f32[16,20,128]{2,1,0:T(8,128)}), f32[16,20,128]{2,1,0:T(8,128)S(1)}, u32[]{:S(2)}, u32[]{:S(2)}) async-start(f32[16,20,128]{2,1,0:T(8,128)} %get-tuple-element.24), calls=%async_computation | async-start | bytes 393216 | tf_op jit(solution)/shard_map/all_to_all | solution.py:329
  39.1 1.9 %collective-permute-start.5 = (f32[4,4,128]{2,1,0:T(4,128)S(1)}, f32[4,4,128]{2,1,0:T(4,128)S(1)}, u32[]{:S(2)}, u32[]{:S(2)}) collective-permute-start(f32[4,4,128]{2,1,0:T(4,128)S(1)} %get-tuple-element.26), channel_id=1, source_target_pairs={{0,2},{2,4},{4,6},{6,8},{8,10},{10,12},{12,14},{1,3},{3,5},{5,7},{... | collective-permute-start | bytes 24584 | tf_op jit(solution)/shard_map/ppermute | solution.py:321
  41.0 3.6 %collective-permute-start.6 = (f32[4,4,128]{2,1,0:T(4,128)S(1)}, f32[4,4,128]{2,1,0:T(4,128)S(1)}, u32[]{:S(2)}, u32[]{:S(2)}) collective-permute-start(f32[4,4,128]{2,1,0:T(4,128)S(1)} %get-tuple-element.27), channel_id=1, source_target_pairs={{2,0},{4,2},{6,4},{8,6},{10,8},{12,10},{14,12},{3,1},{5,3},{7,5},{... | collective-permute-start | bytes 24584 | tf_op jit(solution)/shard_map/ppermute | solution.py:322
  44.6 6.9 %all-to-all-done.got_ref = f32[16,20,128]{2,1,0:T(8,128)S(1)} async-done(((f32[16,20,128]{2,1,0:T(8,128)}), f32[16,20,128]{2,1,0:T(8,128)S(1)}, u32[]{:S(2)}, u32[]{:S(2)}) %all-to-all-start) | async-done | bytes 163872 | tf_op jit(solution)/shard_map/all_to_all | solution.py:329
  51.6 0.0 copy-done.2
  51.6 0.0 copy-done.4
  51.6 2.6 %shard_map.99 = f32[16,20,128]{2,1,0:T(8,128)} custom-call(s32[1]{0:T(128)} %bitcast.5.az_ref, s32[16]{0:T(128)S(1)} %copy-done.4, f32[128,1024]{1,0:T(8,128)S(1)} %copy-done.2, f32[16,20,128]{2,1,0:T(8,128)S(1)} %all-to-all-done.got_ref), custom_call_target="tpu_custom_call" | custom-call | flops 100000000 | bytes 1000000 | tf_op jit(solution)/shard_map/pallas_call | solution.py:338
  54.2 3.7 %all-to-all-start.1 = ((f32[16,20,128]{2,1,0:T(8,128)}), f32[16,20,128]{2,1,0:T(8,128)S(1)}, u32[]{:S(2)}, u32[]{:S(2)}) async-start(f32[16,20,128]{2,1,0:T(8,128)} %shard_map.99), calls=%async_computation.1 | async-start | bytes 393216 | tf_op jit(solution)/shard_map/all_to_all | solution.py:344
  57.9 4.5 %shard_map.98.sect_ref = f32[5,8,64,128]{3,2,1,0:T(8,128)S(1)} custom-call(f32[5,8,64,128]{3,2,1,0:T(8,128)S(1)} %get-tuple-element.22.sect_ref, f32[4,32,128]{2,1,0:T(8,128)S(1)} %get-tuple-element.23.src_ref, s32[32,128]{1,0:T(8,128)S(1)} %bitcast.12), custom_call_target="tpu_custom_call" | custom-call | flops 8000000000 | bytes 4000000 | tf_op jit(solution)/shard_map/pallas_call | solution.py:331
  62.5 0.0 collective-permute-done.5.below_ref
  62.5 0.0 collective-permute-done.6.above_ref
  62.5 7.0 %all-to-all-done.1.got_ref = f32[16,20,128]{2,1,0:T(8,128)S(1)} async-done(((f32[16,20,128]{2,1,0:T(8,128)}), f32[16,20,128]{2,1,0:T(8,128)S(1)}, u32[]{:S(2)}, u32[]{:S(2)}) %all-to-all-start.1) | async-done | bytes 163872 | tf_op jit(solution)/shard_map/all_to_all | solution.py:344
  69.5 1.5 %shard_map.100 = (f32[5,8,64,128]{3,2,1,0:T(8,128)}, f32[4,40,128]{2,1,0:T(8,128)}) custom-call(s32[1]{0:T(128)} %bitcast.rad_ref, f32[5,8,64,128]{3,2,1,0:T(8,128)S(1)} %shard_map.98.sect_ref, f32[16,20,128]{2,1,0:T(8,128)S(1)} %all-to-all-done.1.got_ref, f32[4,32,128]{2,1,0:T(8,128)S(1)} %get-tuple-element.25.stay_ref, ...), custom_call_target="tpu_custom_call" | custom-call | flops 1000000 | bytes 4000000 | tf_op jit(solution)/shard_map/pallas_call | solution.py:346
Async XLA Ops:
  0.6 17.6 %copy-start.7 = (s32[32,1,1]{0,2,1:T(1,128)S(1)}, s32[32,1,1]{0,2,1:T(1,128)}, u32[]{:S(2)}) copy-start(s32[32,1,1]{0,2,1:T(1,128)} %param.13) | copy-start | bytes 388
  0.6 1.3 %copy-start = (f32[5,8,64,128]{3,2,1,0:T(8,128)S(1)}, f32[5,8,64,128]{3,2,1,0:T(8,128)}, u32[]{:S(2)}) copy-start(f32[5,8,64,128]{3,2,1,0:T(8,128)} %q_ref.5) | copy-start | bytes 3932164
  2.0 16.3 %copy-start.1 = (f32[5,8,64,128]{3,2,1,0:T(8,128)S(1)}, f32[5,8,64,128]{3,2,1,0:T(8,128)}, u32[]{:S(2)}) copy-start(f32[5,8,64,128]{3,2,1,0:T(8,128)} %q_ref.5) | copy-start | bytes 3932164
  2.0 16.3 %copy-start.6 = (s32[32,1,128]{2,1,0:T(1,128)S(1)}, s32[32,1,128]{2,1,0:T(1,128)}, u32[]{:S(2)}) copy-start(s32[32,1,128]{2,1,0:T(1,128)} %param.11) | copy-start | bytes 49156
  2.4 25.2 %collective-permute-start.4 = (f32[32,128]{1,0:T(8,128)S(1)}, f32[32,128]{1,0:T(8,128)S(1)}, u32[]{:S(2)}, u32[]{:S(2)}) collective-permute-start(f32[32,128]{1,0:T(8,128)S(1)} %get-tuple-element.20), channel_id=1, source_target_pairs={{0,1},{1,0},{2,3},{3,2},{4,5},{5,4},{6,7},{7,6},{8,9},{9,8},{10,11... | collective-permute-start | bytes 49160 | tf_op jit(solution)/shard_map/ppermute | solution.py:308
  4.0 23.6 %collective-permute-start.2 = (f32[5,8,128]{2,1,0:T(8,128)S(1)}, f32[5,8,128]{2,1,0:T(8,128)S(1)}, u32[]{:S(2)}, u32[]{:S(2)}) collective-permute-start(f32[5,8,128]{2,1,0:T(8,128)S(1)} %get-tuple-element.18), channel_id=1, source_target_pairs={{0,16},{16,32},{32,48},{48,64},{64,80},{80,96},{96,112},{112,128},... | collective-permute-start | bytes 61448 | tf_op jit(solution)/shard_map/ppermute | solution.py:306
  6.7 20.9 %collective-permute-start.3 = (f32[5,8,128]{2,1,0:T(8,128)S(1)}, f32[5,8,128]{2,1,0:T(8,128)S(1)}, u32[]{:S(2)}, u32[]{:S(2)}) collective-permute-start(f32[5,8,128]{2,1,0:T(8,128)S(1)} %get-tuple-element.19), channel_id=1, source_target_pairs={{16,0},{32,16},{48,32},{64,48},{80,64},{96,80},{112,96},{128,112},... | collective-permute-start | bytes 61448 | tf_op jit(solution)/shard_map/ppermute | solution.py:307
  12.0 15.6 %collective-permute-start = (f32[5,64,128]{2,1,0:T(8,128)S(1)}, f32[5,64,128]{2,1,0:T(8,128)S(1)}, u32[]{:S(2)}, u32[]{:S(2)}) collective-permute-start(f32[5,64,128]{2,1,0:T(8,128)S(1)} %get-tuple-element.16), channel_id=1, source_target_pairs={{0,2},{2,4},{4,6},{6,8},{8,10},{10,12},{12,14},{1,3},{3,5},{5,7},{... | collective-permute-start | bytes 491528 | tf_op jit(solution)/shard_map/ppermute | solution.py:304
  13.9 13.7 %collective-permute-start.1 = (f32[5,64,128]{2,1,0:T(8,128)S(1)}, f32[5,64,128]{2,1,0:T(8,128)S(1)}, u32[]{:S(2)}, u32[]{:S(2)}) collective-permute-start(f32[5,64,128]{2,1,0:T(8,128)S(1)} %get-tuple-element.17), channel_id=1, source_target_pairs={{2,0},{4,2},{6,4},{8,6},{10,8},{12,10},{14,12},{3,1},{5,3},{7,5},{... | collective-permute-start | bytes 491528 | tf_op jit(solution)/shard_map/ppermute | solution.py:305
  18.2 0.8 %copy-start.5 = (f32[4,32,1,128]{3,2,1,0:T(1,128)S(1)}, f32[4,32,1,128]{3,2,1,0:T(1,128)}, u32[]{:S(2)}) copy-start(f32[4,32,1,128]{3,2,1,0:T(1,128)} %param.10) | copy-start | bytes 196612
  19.1 8.5 %copy-start.3 = (f32[5,6]{1,0:T(8,128)S(1)}, f32[5,6]{1,0:T(8,128)}, u32[]{:S(2)}) copy-start(f32[5,6]{1,0:T(8,128)} %coef_ref.1) | copy-start | bytes 364
  27.5 24.1 %copy-start.2 = (f32[128,1024]{1,0:T(8,128)S(1)}, f32[128,1024]{1,0:T(8,128)}, u32[]{:S(2)}) copy-start(f32[128,1024]{1,0:T(8,128)} %constant.11.clone.basis_ref) | copy-start | bytes 1572868
  27.5 24.0 %copy-start.4 = (s32[16]{0:T(128)S(1)}, s32[16]{0:T(128)}, u32[]{:S(2)}) copy-start(s32[16]{0:T(128)} %width_ref.1) | copy-start | bytes 196
  32.8 18.8 %all-to-all-start = ((f32[16,20,128]{2,1,0:T(8,128)}), f32[16,20,128]{2,1,0:T(8,128)S(1)}, u32[]{:S(2)}, u32[]{:S(2)}) async-start(f32[16,20,128]{2,1,0:T(8,128)} %get-tuple-element.24), calls=%async_computation | async-start | bytes 393216 | tf_op jit(solution)/shard_map/all_to_all | solution.py:329
  39.1 23.4 %collective-permute-start.5 = (f32[4,4,128]{2,1,0:T(4,128)S(1)}, f32[4,4,128]{2,1,0:T(4,128)S(1)}, u32[]{:S(2)}, u32[]{:S(2)}) collective-permute-start(f32[4,4,128]{2,1,0:T(4,128)S(1)} %get-tuple-element.26), channel_id=1, source_target_pairs={{0,2},{2,4},{4,6},{6,8},{8,10},{10,12},{12,14},{1,3},{3,5},{5,7},{... | collective-permute-start | bytes 24584 | tf_op jit(solution)/shard_map/ppermute | solution.py:321
  41.0 21.5 %collective-permute-start.6 = (f32[4,4,128]{2,1,0:T(4,128)S(1)}, f32[4,4,128]{2,1,0:T(4,128)S(1)}, u32[]{:S(2)}, u32[]{:S(2)}) collective-permute-start(f32[4,4,128]{2,1,0:T(4,128)S(1)} %get-tuple-element.27), channel_id=1, source_target_pairs={{2,0},{4,2},{6,4},{8,6},{10,8},{12,10},{14,12},{3,1},{5,3},{7,5},{... | collective-permute-start | bytes 24584 | tf_op jit(solution)/shard_map/ppermute | solution.py:322
  54.2 15.2 %all-to-all-start.1 = ((f32[16,20,128]{2,1,0:T(8,128)}), f32[16,20,128]{2,1,0:T(8,128)S(1)}, u32[]{:S(2)}, u32[]{:S(2)}) async-start(f32[16,20,128]{2,1,0:T(8,128)} %shard_map.99), calls=%async_computation.1 | async-start | bytes 393216 | tf_op jit(solution)/shard_map/all_to_all | solution.py:344

commit v2 on v1

--- a/solution.py
+++ b/solution.py
@@ -2,6 +2,7 @@
 
 import jax
 import jax.numpy as jnp
+import ml_dtypes
 import numpy as np
 from jax import lax
 from jax.experimental import pallas as pl
@@ -41,7 +42,10 @@
     mode = np.where(column < HALF, column, column - HALF + 1)
     phases = (mode[:, None] * np.arange(NAZ)[None, :]) % NAZ
     angles = phases.astype(np.float32) * np.float32(2.0 * math.pi / NAZ)
-    return np.where(column[:, None] < HALF, np.cos(angles), np.sin(angles)).astype(np.float32)
+    table = np.where(column[:, None] < HALF, np.cos(angles), np.sin(angles)).astype(np.float32)
+    high = table.astype(ml_dtypes.bfloat16)
+    low = (table - high.astype(np.float32)).astype(ml_dtypes.bfloat16)
+    return np.concatenate([high, low])
 
 
 def iota(shape, axis):
@@ -65,20 +69,11 @@
     )
 
 
-def edges_body(rad_ref, q_ref, ax_lo, ax_hi, az_lo, az_hi, rad_out):
-    ax_lo[...] = q_ref[:, 0]
-    ax_hi[...] = q_ref[:, CAX - 1]
-    az_lo[...] = q_ref[:, :, 0, :]
-    az_hi[...] = q_ref[:, :, CAZ - 1, :]
-    extra = jnp.where(rad_ref[0] == 0, 1, 0)
-    lane = iota((32, CR), 1)
-    packed = jnp.zeros((32, CR), F32)
-    for f in range(FIELDS):
-        for g in range(16):
-            part = q_ref[f, g // 2, (g % 2) * 32 : (g % 2) * 32 + 32, :]
-            spot = g * 8 + f
-            packed = jnp.where(lane == spot, pltpu.roll(part, spot + extra, 1), packed)
-    rad_out[...] = packed
+def edges_body(odd_ref, q_ref, first_out, second_out):
+    odd = odd_ref[0] == 1
+    low, high = q_ref[:, 0], q_ref[:, CAX - 1]
+    first_out[...] = jnp.where(odd, low, high)
+    second_out[...] = jnp.where(odd, high, low)
 
 
 def one_hot_rows(cells_ref, first, blocks):
@@ -93,15 +88,12 @@
     src_out, stay_out, up_out, down_out, near_out,
     hot_ref, gas_ref, state_ref, spread_ref,
 ):
-    parts = [[], [], []]
+    parts = [[], []]
     for f in range(3):
         table = q_ref[f + 1].reshape(ROWS, CR).T
-        high = table.astype(BF16)
-        rest = table - high.astype(F32)
-        mid = rest.astype(BF16)
+        high, low = halves(table)
         parts[0].append(high)
-        parts[1].append(mid)
-        parts[2].append((rest - mid.astype(F32)).astype(BF16))
+        parts[1].append(low)
     parts = [jnp.concatenate(part, axis=0) for part in parts]
     for first in range(0, BLK_DEV, 4):
         width = 4 * BLK
@@ -169,49 +161,92 @@
 SOURCE_OF = (0, 1, 2, 3, 0)
 
 
-def section_body(
-    rad_ref, coef_ref, q_ref, ax_prev, ax_next, az_prev, az_next, rad_in, near_ref, sect_out, send_out
+BAND = 24
+
+
+def near_body(
+    rad_ref, odd_ref, coef_ref, q_ref, first_ref, second_ref, near_ref,
+    send_out, az_lo, az_hi, rad_out,
 ):
-    rad = rad_ref[0]
-    lane = iota((CAZ, CR), 1)
-    row = iota((CAZ, CR), 0)
-    metric = 4.0 / ((rad * CR + lane).astype(F32) + 4.0)
-    last = (lane == CR - 1) & (rad == 0)
-    first = (lane == 0) & (rad == 1)
-    ends = (lane == CR - 1) | (lane == 0)
+    lane = iota((CR, 2 * CAZ), 1)
+    row = iota((CR, 2 * CAZ), 0)
+    z = lane % CAZ
+
+    def turned(parts):
+        packed = jnp.zeros((2 * CAZ, CR), F32)
+        for f, part in enumerate(parts):
+            moved = pltpu.roll(part, f * BAND, 1) if f else part
+            packed = jnp.where((lane >= f * BAND) & (lane < (f + 1) * BAND), moved, packed)
+        return packed.T
+
+    tiles = [
+        turned([q_ref[f, 2 * p : 2 * p + 2].reshape(2 * CAZ, CR) for f in range(FIELDS)])
+        for p in range(PAIRS)
+    ]
+    odd = odd_ref[0] == 1
+    first, second = first_ref[...], second_ref[...]
+    before, after = jnp.where(odd, first, second), jnp.where(odd, second, first)
+    halo = turned([jnp.concatenate([before[f], after[f]], axis=0) for f in range(FIELDS)])
+
+    column = iota((CR, 1), 0)
+    radius = column
+    c = [jnp.zeros((CR, 1), F32) for _ in range(6)]
     for f in range(FIELDS):
-        c = [coef_ref[f, i] for i in range(6)]
-        mid = (1.0 - c[1] - c[5]) - c[3] * metric
-        az_up = (0.5 * (c[2] + c[3])) * metric
-        az_down = (0.5 * (c[3] - c[2])) * metric
-        ax_up, ax_down = 0.5 * (c[0] + c[1]), 0.5 * (c[1] - c[0])
-        rad_up, rad_down = 0.5 * (c[4] + c[5]), 0.5 * (c[5] - c[4])
-        for a in range(CAX):
-            q = q_ref[f, a]
-            ahead = q_ref[f, a + 1] if a + 1 < CAX else ax_next[f]
-            behind = q_ref[f, a - 1] if a else ax_prev[f]
-            az_a = jnp.where(row == CAZ - 1, az_next[f, a : a + 1, :], pltpu.roll(q, CAZ - 1, 0))
-            az_b = jnp.where(row == 0, az_prev[f, a : a + 1, :], pltpu.roll(q, 1, 0))
-            edge = jnp.concatenate(
-                [rad_in[:, (2 * a + h) * 8 + f : (2 * a + h) * 8 + f + 1] for h in range(2)], axis=0
-            )
-            edge = jnp.broadcast_to(edge, (CAZ, CR))
-            r_a = jnp.where(last, edge, jnp.where(lane == CR - 1, 0.0, pltpu.roll(q, CR - 1, 1)))
-            r_b = jnp.where(first, edge, jnp.where(lane == 0, 0.0, pltpu.roll(q, 1, 1)))
-            out = (
-                mid * q + ax_up * ahead + ax_down * behind + az_up * az_a + az_down * az_b
-                + rad_up * r_a + rad_down * r_b
-            )
-            sect_out[f, a] = out
-        for pair in range(PAIRS):
-            block = sect_out[f, 2 * pair : 2 * pair + 2].reshape(2 * CAZ, CR).T[:CYCLES]
+        here = (column >= f * BAND) & (column < (f + 1) * BAND)
+        radius = jnp.where(here, column - f * BAND, radius)
+        c = [jnp.where(here, coef_ref[f, i], c[i]) for i in range(6)]
+    metric = 4.0 / (radius.astype(F32) + 4.0)
+    mid = (1.0 - c[1] - c[5]) - c[3] * metric
+    az_up, az_down = (0.5 * (c[2] + c[3])) * metric, (0.5 * (c[3] - c[2])) * metric
+    ax_up, ax_down = 0.5 * (c[0] + c[1]), 0.5 * (c[1] - c[0])
+    rad_up = 0.5 * (c[4] + c[5])
+    rad_down = jnp.where(radius == 0, 0.0, 0.5 * (c[5] - c[4]))
+    low = lane < CAZ
+    swapped = [pltpu.roll(t, CAZ, 1) for t in tiles]
+    for p in range(PAIRS):
+        q = tiles[p]
+        ahead = jnp.where(low, swapped[p], swapped[p + 1] if p + 1 < PAIRS else halo)
+        behind = jnp.where(low, swapped[p - 1] if p else halo, swapped[p])
+        az_a = jnp.where(z == CAZ - 1, 0.0, pltpu.roll(q, 2 * CAZ - 1, 1))
+        az_b = jnp.where(z == 0, 0.0, pltpu.roll(q, 1, 1))
+        r_a = pltpu.roll(q, CR - 1, 0)
+        r_b = pltpu.roll(q, 1, 0)
+        out = (
+            mid * q + ax_up * ahead + ax_down * behind + az_up * az_a + az_down * az_b
+            + rad_up * r_a + rad_down * r_b
+        )
+        ends = jnp.where(z == 0, az_up * q, jnp.where(z == CAZ - 1, az_down * q, 0.0))
+        ends = sum(
+            pltpu.roll(ends[f * BAND : f * BAND + CYCLES], 2 * f, 1) if f else ends[:CYCLES]
+            for f in range(FIELDS)
+        )
+        for f in range(FIELDS):
             s = SOURCE_OF[f] * CYCLES
-            block = block + near_ref[s : s + CYCLES, pair * 2 * CAZ : (pair + 1) * 2 * CAZ]
+            block = out[f * BAND : f * BAND + CYCLES] + near_ref[
+                s : s + CYCLES, p * 2 * CAZ : (p + 1) * 2 * CAZ
+            ]
             for quad in range(QUADS):
-                send_out[pair * QUADS + quad, f * 4 : f * 4 + 4, :] = block[quad * 4 : quad * 4 + 4]
-
-
-def scatter_body(sect_ref, src_ref, cells_ref, sect_out, acc_ref):
+                send_out[p * QUADS + quad, f * 4 : f * 4 + 4, :] = block[quad * 4 : quad * 4 + 4]
+        for quad in range(QUADS):
+            send_out[p * QUADS + quad, LINES : LINES + 4, :] = ends[quad * 4 : quad * 4 + 4]
+    az_lo[...] = q_ref[:, :, 0, :]
+    az_hi[...] = q_ref[:, :, CAZ - 1, :]
+    rad_edges(rad_ref[0], q_ref, rad_out)
+
+
+def rad_edges(rad, q_ref, rad_out):
+    extra = jnp.where(rad == 0, 1, 0)
+    lane = iota((32, CR), 1)
+    packed = jnp.zeros((32, CR), F32)
+    for f in range(FIELDS):
+        for g in range(16):
+            part = q_ref[f, g // 2, (g % 2) * 32 : (g % 2) * 32 + 32, :]
+            spot = g * 8 + f
+            packed = jnp.where(lane == spot, pltpu.roll(part, spot + extra, 1), packed)
+    rad_out[...] = packed
+
+
+def scatter_body(src_ref, cells_ref, acc_ref):
     step = 8
     for first in range(0, BLK_DEV, step):
         hot, lanes = one_hot_rows(cells_ref, first, step)
@@ -230,36 +265,103 @@
             acc_ref[...] = total
         else:
             acc_ref[...] += total
+
+
+def section_body(
+    rad_ref, odd_ref, coef_ref, q_ref, first_ref, second_ref, az_prev, az_next, rad_in, acc_ref, sect_out
+):
+    rad = rad_ref[0]
+    odd = odd_ref[0] == 1
+    lane = iota((CAZ, CR), 1)
+    row = iota((CAZ, CR), 0)
+    metric = 4.0 / ((rad * CR + iota((1, CR), 1)).astype(F32) + 4.0)
+    target = jnp.where(rad == 0, CR - 1, 0)
     for f in range(FIELDS):
+        c = [coef_ref[f, i] for i in range(6)]
+        mid = (1.0 - c[1] - c[5]) - c[3] * metric
+        az_up = (0.5 * (c[2] + c[3])) * metric
+        az_down = (0.5 * (c[3] - c[2])) * metric
+        az_up_in = jnp.where(row == CAZ - 1, 0.0, az_up)
+        az_down_in = jnp.where(row == 0, 0.0, az_down)
+        ax_up, ax_down = 0.5 * (c[0] + c[1]), 0.5 * (c[1] - c[0])
+        rad_up, rad_down = 0.5 * (c[4] + c[5]), 0.5 * (c[5] - c[4])
+        rad_up_in = jnp.where(iota((1, CR), 1) == CR - 1, 0.0, rad_up)
+        rad_down_in = jnp.where(iota((1, CR), 1) == 0, 0.0, rad_down)
+        rad_edge = jnp.where(rad == 0, rad_up, rad_down)
         s = SOURCE_OF[f] * CR
-        added = acc_ref[:, s : s + CR].reshape(CAX, CAZ, CR)
-        sect_out[f] = sect_ref[f] + added
-
-
-def filter_body(az_ref, width_ref, basis_ref, got_ref, send_out, line_ref):
-    quad = az_ref[0] % QUADS
-    lane = iota((LINES, 2 * CAZ), 1)
-    low = lane < CAZ
-    line_ref[...] = jnp.zeros_like(line_ref)
+        for a in range(CAX):
+            q = q_ref[f, a]
+            ahead = q_ref[f, a + 1] if a + 1 < CAX else jnp.where(odd, second_ref[f], first_ref[f])
+            behind = q_ref[f, a - 1] if a else jnp.where(odd, first_ref[f], second_ref[f])
+            out = (
+                mid * q + ax_up * ahead + ax_down * behind
+                + az_up_in * pltpu.roll(q, CAZ - 1, 0) + az_down_in * pltpu.roll(q, 1, 0)
+                + rad_up_in * pltpu.roll(q, CR - 1, 1) + rad_down_in * pltpu.roll(q, 1, 1)
+                + acc_ref[a * CAZ : (a + 1) * CAZ, s : s + CR]
+            )
+            edge = jnp.concatenate(
+                [pltpu.roll(rad_in[...], (target + (2 * CR - ((2 * a + h) * 8 + f))) % CR, 1) for h in range(2)],
+                axis=0,
+            )
+            sect_out[f, a] = out + jnp.where(lane == target, rad_edge * edge, 0.0)
+            sect_out[f, a, 0:1] += az_down * az_prev[f, a : a + 1]
+            sect_out[f, a, CAZ - 1 : CAZ] += az_up * az_next[f, a : a + 1]
+
+
+def lined(pieces, line_ref):
+    low = iota((LINES, 2 * CAZ), 1) < CAZ
     for i in range(N_AZ // 2):
-        t0, t1 = got_ref[2 * i], got_ref[2 * i + 1]
+        t0, t1 = pieces(2 * i), pieces(2 * i + 1)
         cols = slice(i * 2 * CAZ, (i + 1) * 2 * CAZ)
         line_ref[0:LINES, cols] = jnp.where(low, t0, pltpu.roll(t1, CAZ, 1))
-        line_ref[24 : 24 + LINES, cols] = jnp.where(low, pltpu.roll(t0, CAZ, 1), t1)
-    basis = basis_ref[...]
-    coefs = lax.dot_general(line_ref[...], basis, NT, precision=HIGHEST, preferred_element_type=F32)
-    column = iota((48, MODES), 1)
-    row = iota((48, MODES), 0) % 4
+        line_ref[BAND : BAND + LINES, cols] = jnp.where(low, pltpu.roll(t0, CAZ, 1), t1)
+
+
+def filter_body(
+    az_ref, width_ref, basis_ref, got_ref, up_ref, down_ref,
+    send_out, up_out, down_out, line_ref, ends_ref, piece_ref,
+):
+    up_out[...] = up_ref[...]
+    down_out[...] = down_ref[...]
+    quad = az_ref[0] % QUADS
+    low = iota((LINES, 2 * CAZ), 1) < CAZ
+    line_ref[...] = jnp.zeros_like(line_ref)
+    ends_ref[...] = jnp.zeros_like(ends_ref)
+    for s in range(N_AZ):
+        packed = got_ref[s, LINES : LINES + 4, :]
+        for f in range(FIELDS):
+            piece_ref[s, f * 4 : f * 4 + 4, :] = pltpu.roll(packed, 2 * CAZ - 2 * f, 1) if f else packed
+    lined(lambda s: got_ref[s, 0:LINES, :], line_ref)
+    lined(lambda s: piece_ref[s], ends_ref)
+    z = iota((2 * BAND, NAZ), 1) % CAZ
+    ends = ends_ref[...]
+    lines = (
+        line_ref[...]
+        + jnp.where(z == CAZ - 1, pltpu.roll(ends, NAZ - 1, 1), 0.0)
+        + jnp.where(z == 0, pltpu.roll(ends, 1, 1), 0.0)
+    )
+    rows = 2 * BAND
+    high, rest = halves(lines)
+    both = jnp.concatenate([high, rest], axis=0)
+    whole = lax.dot_general(both, basis_ref[:MODES], NT, preferred_element_type=F32)
+    part = lax.dot_general(high, basis_ref[MODES:], NT, preferred_element_type=F32)
+    coefs = whole[:rows] + whole[rows:] + part
+    column = iota((rows, MODES), 1)
+    cycle = iota((rows, MODES), 0) % 4
     mode = jnp.where(column < HALF, column, column - HALF + 1)
-    width = jnp.zeros((48, MODES), jnp.int32)
+    width = jnp.zeros((rows, MODES), jnp.int32)
     for i in range(4):
-        width = jnp.where(row == i, width_ref[quad * 4 + i], width)
+        width = jnp.where(cycle == i, width_ref[quad * 4 + i], width)
     weight = jnp.where(mode == 0, 1.0 / NAZ, 2.0 / NAZ)
     coefs = coefs * jnp.where(mode < width, weight, 0.0)
-    line_ref[...] = jnp.dot(coefs, basis, precision=HIGHEST, preferred_element_type=F32)
+    high, rest = halves(coefs)
+    both = jnp.concatenate([high, rest], axis=0)
+    whole = jnp.dot(both, basis_ref[:MODES], preferred_element_type=F32)
+    part = jnp.dot(high, basis_ref[MODES:], preferred_element_type=F32)
+    line_ref[...] = whole[:rows] + whole[rows:] + part
     for i in range(N_AZ // 2):
         cols = slice(i * 2 * CAZ, (i + 1) * 2 * CAZ)
-        t0, t1 = line_ref[0:LINES, cols], line_ref[24 : 24 + LINES, cols]
+        t0, t1 = line_ref[0:LINES, cols], line_ref[BAND : BAND + LINES, cols]
         send_out[2 * i] = jnp.where(low, t0, pltpu.roll(t1, CAZ, 1))
         send_out[2 * i + 1] = jnp.where(low, pltpu.roll(t0, CAZ, 1), t1)
 
@@ -285,6 +387,7 @@
 def shards(fields, coeffs, parcels, cells, counts, moves, widths):
     rad_index = lax.axis_index("rad").astype(jnp.int32).reshape(1)
     az_index = lax.axis_index("az").astype(jnp.int32).reshape(1)
+    odd = (lax.axis_index("ax").astype(jnp.int32) % 2).reshape(1)
     n_ax, n_az, n_rad = (lax.axis_size(axis) for axis in ("ax", "az", "rad"))
     parcels = parcels.reshape(4, BLK_DEV, BLK)
     cells = cells.reshape(BLK_DEV, BLK)
@@ -292,20 +395,17 @@
     moves = moves.reshape(BLK_DEV)
     up = [(i, i + 1) for i in range(n_ax - 1)]
     down = [(i + 1, i) for i in range(n_ax - 1)]
+    inner = [(i, i ^ 1) for i in range(n_ax)]
+    outer = [(i, ((i + 1) ^ 1) - 1) for i in range(1, n_ax - 1)]
     ahead = [(i, (i + 1) % n_az) for i in range(n_az)]
     back = [((i + 1) % n_az, i) for i in range(n_az)]
     across = [(i, i ^ 1) for i in range(n_rad)]
 
-    ax_lo, ax_hi, az_lo, az_hi, rad_edge = call(
-        edges_body,
-        [(FIELDS, CAZ, CR)] * 2 + [(FIELDS, CAX, CR)] * 2 + [(32, CR)],
-        [SMEM, VMEM], 10**6, 2 * 10**6,
-    )(rad_index, fields)
-    ax_prev = lax.ppermute(ax_hi, "ax", up)
-    ax_next = lax.ppermute(ax_lo, "ax", down)
-    az_prev = lax.ppermute(az_hi, "az", ahead)
-    az_next = lax.ppermute(az_lo, "az", back)
-    rad_got = lax.ppermute(rad_edge, "rad", across)
+    first, second = call(
+        edges_body, [(FIELDS, CAZ, CR)] * 2, [SMEM, VMEM], 10**6, 2 * 10**6, mib=4
+    )(odd, fields)
+    first = lax.ppermute(first, "ax", inner)
+    second = lax.ppermute(second, "ax", outer)
 
     src, stay, sent_up, sent_down, near = call(
         parcels_body,
@@ -318,36 +418,46 @@
             pltpu.VMEM((8 * CYCLES, PARCELS), BF16),
         ],
     )(counts, moves, fields, parcels, cells)
+
+    to_owner, az_lo, az_hi, rad_edge = call(
+        near_body,
+        [(N_AZ, LINES + 4, 2 * CAZ), (FIELDS, CAX, CR), (FIELDS, CAX, CR), (32, CR)],
+        [SMEM, SMEM, SMEM] + [VMEM] * 4, 10**7, 4 * 10**6, mib=8,
+    )(rad_index, odd, coeffs, fields, first, second, near)
+    lines = lax.all_to_all(to_owner, "az", 0, 0, tiled=True)
+    az_prev = lax.ppermute(az_hi, "az", ahead)
+    az_next = lax.ppermute(az_lo, "az", back)
+    rad_got = lax.ppermute(rad_edge, "rad", across)
+
+    (added,) = call(
+        scatter_body, [(ROWS, 4 * CR)], [VMEM] * 2, 8 * 10**9, 10**6, mib=16
+    )(src, cells)
+
+    to_home, sent_up, sent_down = call(
+        filter_body,
+        [(N_AZ, LINES, 2 * CAZ), (4, MOVEB, BLK), (4, MOVEB, BLK)],
+        [SMEM, SMEM] + [VMEM] * 4, 10**8, 10**6,
+        [
+            pltpu.VMEM((2 * BAND, NAZ), F32),
+            pltpu.VMEM((2 * BAND, NAZ), F32),
+            pltpu.VMEM((N_AZ, LINES, 2 * CAZ), F32),
+        ],
+        mib=6,
+    )(az_index, widths, jnp.asarray(basis_rows()), lines, sent_up, sent_down)
+    filtered = lax.all_to_all(to_home, "az", 0, 0, tiled=True)
     from_below = lax.ppermute(sent_up, "ax", up)
     from_above = lax.ppermute(sent_down, "ax", down)
 
-    sect, to_owner = call(
-        section_body,
-        [(FIELDS, CAX, CAZ, CR), (N_AZ, LINES, 2 * CAZ)],
-        [SMEM, SMEM] + [VMEM] * 7, 10**7, 4 * 10**6,
-    )(rad_index, coeffs, fields, ax_prev, ax_next, az_prev, az_next, rad_got, near)
-    lines = lax.all_to_all(to_owner, "az", 0, 0, tiled=True)
-
     (sect,) = call(
-        scatter_body,
-        [(FIELDS, CAX, CAZ, CR)],
-        [VMEM] * 3, 8 * 10**9, 4 * 10**6,
-        [pltpu.VMEM((ROWS, 4 * CR), F32)],
-    )(sect, src, cells)
-
-    (to_home,) = call(
-        filter_body,
-        [(N_AZ, LINES, 2 * CAZ)],
-        [SMEM, SMEM, VMEM, VMEM], 10**8, 10**6,
-        [pltpu.VMEM((48, NAZ), F32)],
-    )(az_index, widths, jnp.asarray(basis_rows()), lines)
-    filtered = lax.all_to_all(to_home, "az", 0, 0, tiled=True)
+        section_body, [(FIELDS, CAX, CAZ, CR)], [SMEM, SMEM, SMEM] + [VMEM] * 7, 4 * 10**9, 4 * 10**6, mib=8
+    )(rad_index, odd, coeffs, fields, first, second, az_prev, az_next, rad_got, added)
 
     gas_out, parcels_out = call(
         merge_body,
         [(FIELDS, CAX, CAZ, CR), (4, BLK_DEV + 2 * MOVEB, BLK)],
         [SMEM] + [VMEM] * 5, 10**6, 4 * 10**6,
         [pltpu.VMEM((CR, CR), F32)],
+        mib=8,
     )(rad_index, sect, filtered, stay, from_below, from_above)
     return gas_out, parcels_out.reshape(4, BLK_DEV + 2 * MOVEB, 1, BLK)
 

time: 71.5 us -> 63.6 us (0.89)
  waiting for transfers between devices: 13.9 us -> 4.92 us
  Pallas kernels: 22.7 us -> 19.4 us
  local copies, waits for them, and re-layouts: 2.17 us -> 4.35 us
  starting transfers between devices: 30.7 us -> 32.4 us
    all_to_all x1, waiting for transfers between devices: 6.93 us -> 1.13 us  [shards(): lines = lax.all_to_all(to_owner, 'az', 0, 0, tiled=True)]
    all_to_all x1, waiting for transfers between devices: 6.99 us -> 3.77 us  [shards(): filtered = lax.all_to_all(to_home, 'az', 0, 0, tiled=True)]
    ppermute x1, starting transfers between devices: 5.29 us -> 2.12 us  [shards(): az_next = lax.ppermute(az_lo, 'az', back)]
    all_to_all x1, starting transfers between devices: 6.26 us -> 9.31 us  [shards(): lines = lax.all_to_all(to_owner, 'az', 0, 0, tiled=True)]
    all_to_all x1, starting transfers between devices: 3.7 us -> 6.47 us  [shards(): filtered = lax.all_to_all(to_home, 'az', 0, 0, tiled=True)]
    unnamed x16 -> x20, local copies, waits for them, and re-layouts: 2.17 us -> 4.35 us
    pallas_call x4 -> x5, Pallas kernels: 12.8 us -> 10.9 us  [the longest x1 4.52 us: shards(): call(scatter_body, [(ROWS, 4 * CR)], [VMEM] * 2, 8 * 10 ** 9, 10 ** 6, mi...]
    pallas_call x1, Pallas kernels: 8.44 us -> 6.93 us  [shards(): call(parcels_body, [(4, BLK_DEV, BLK), (4, BLK_DEV, BLK), (4, MOVEB, BLK)...]
  transfers between devices with their start and end apart: 9 -> 9, of which waited for: 2 -> 2; matrix products, arithmetic and copies ran while one was open for 0% -> 0% of each run, Pallas kernels for 22% -> 25%
where the time goes in v2:
time: 63.6 us; the launch traced here: 62.5 us
  starting transfers between devices  32.4 us (51%)
  Pallas kernels  19.4 us (31%)
  waiting for transfers between devices  4.92 us (8%)
  local copies, waits for them, and re-layouts  4.35 us (7%)
  between operations  1.51 us (2%)
    all_to_all x1, starting transfers between devices, shards(): lines = lax.all_to_all(to_owner, 'az', 0, 0, tiled=True)  9.31 us
    pallas_call x1, Pallas kernels, shards(): call(parcels_body, [(4, BLK_DEV, BLK), (4, BLK_DEV, BLK), (4, MOVEB, BLK)...  6.93 us
    all_to_all x1, starting transfers between devices, shards(): filtered = lax.all_to_all(to_home, 'az', 0, 0, tiled=True)  6.47 us
    pallas_call x1, Pallas kernels, shards(): call(scatter_body, [(ROWS, 4 * CR)], [VMEM] * 2, 8 * 10 ** 9, 10 ** 6, mi...  4.52 us
    unnamed x20, local copies, waits for them, and re-layouts  4.35 us
    ppermute x1, starting transfers between devices, shards(): second = lax.ppermute(second, 'ax', outer)  4.18 us
    ppermute x1, starting transfers between devices, shards(): az_prev = lax.ppermute(az_hi, 'az', ahead)  3.95 us
    all_to_all x1, waiting for transfers between devices, shards(): filtered = lax.all_to_all(to_home, 'az', 0, 0, tiled=True)  3.77 us
  transfers between devices with their start and end apart: 9, of which 2 were waited for; matrix products, arithmetic and copies ran while one was open for 0% of the time, Pallas kernels for 25%

profile of v2, /device:TPU:8, one launch (start us, length us, event | category | flops | bytes accessed | tf_op | source)
XLA Modules:
  0.0 62.5 jit_solution(10595433755866954806)
XLA Ops:
  0.6 0.0 copy-start.7
  0.6 0.0 copy-start.6
  0.7 0.0 copy-start
  0.7 1.3 %copy-done = f32[5,8,64,128]{3,2,1,0:T(8,128)S(1)} copy-done((f32[5,8,64,128]{3,2,1,0:T(8,128)S(1)}, f32[5,8,64,128]{3,2,1,0:T(8,128)}, u32[]{:S(2)}) %copy-start) | copy-done | bytes 1310744
  2.0 0.0 copy-start.1
  2.0 0.1 collective-permute-start
  2.1 4.2 %collective-permute-start.1 = (f32[5,64,128]{2,1,0:T(8,128)S(1)}, f32[5,64,128]{2,1,0:T(8,128)S(1)}, u32[]{:S(2)}, u32[]{:S(2)}) collective-permute-start(f32[5,64,128]{2,1,0:T(8,128)S(1)} %get-tuple-element.19), channel_id=1, source_target_pairs={{2,4},{4,2},{6,8},{8,6},{10,12},{12,10},{3,5},{5,3},{7,9},{9,7},{1... | collective-permute-start | bytes 491528 | tf_op jit(solution)/shard_map/ppermute | solution.py:408
  6.9 0.0 copy-done.7
  7.0 0.0 copy-done.6
  7.0 0.0 copy-done.1
  7.0 0.0 copy-start.5
  7.0 0.8 %copy-done.5 = f32[4,32,1,128]{3,2,1,0:T(1,128)S(1)} copy-done((f32[4,32,1,128]{3,2,1,0:T(1,128)S(1)}, f32[4,32,1,128]{3,2,1,0:T(1,128)}, u32[]{:S(2)}) %copy-start.5) | copy-done | bytes 65560
  7.8 0.0 copy-start.3
  7.8 6.9 %shard_map.96 = (f32[4,32,128]{2,1,0:T(8,128)S(1)}, f32[4,32,128]{2,1,0:T(8,128)S(1)}, f32[4,4,128]{2,1,0:T(4,128)S(1)}, f32[4,4,128]{2,1,0:T(4,128)S(1)}, f32[64,512]{1,0:T(8,128)S(1)}) custom-call(s32[1]{0:T(128)} %bitcast.10.count_ref, s32[32]{0:T(128)S(1)} %bitcast.14, f32[5,8,64,128]{3,2,1,0:T(8,128)S(1)} %copy-done.1, f32[4,32,128]{2,1,0:T(8,128)S(1)} %bitcast.11, ...), custom_call_target="tpu_custom_call" | custom-call | flops 6000000000 | bytes 2000000 | tf_op jit(solution)/shard_map/pallas_call | solution.py:410
  14.8 0.0 collective-permute-done.first_ref
  14.8 0.0 collective-permute-done.1.second_ref
  14.8 0.0 copy-done.3
  14.8 2.3 %shard_map.97 = (f32[16,24,128]{2,1,0:T(8,128)}, f32[5,8,128]{2,1,0:T(8,128)S(1)}, f32[5,8,128]{2,1,0:T(8,128)S(1)}, f32[32,128]{1,0:T(8,128)S(1)}) custom-call(s32[1]{0:T(128)} %bitcast.rad_ref, s32[1]{0:T(128)} %bitcast.1.odd_ref, f32[5,6]{1,0:T(8,128)S(1)} %copy-done.3, f32[5,8,64,128]{3,2,1,0:T(8,128)S(1)} %copy-done.1, ...), custom_call_target="tpu_custom_call" | custom-call | flops 10000000 | bytes 4000000 | tf_op jit(solution)/shard_map/pallas_call | solution.py:422
  17.1 9.3 %all-to-all-start = ((f32[16,24,128]{2,1,0:T(8,128)}), f32[16,24,128]{2,1,0:T(8,128)S(1)}, u32[]{:S(2)}, u32[]{:S(2)}) async-start(f32[16,24,128]{2,1,0:T(8,128)} %get-tuple-element.25), calls=%async_computation | async-start | bytes 393216 | tf_op jit(solution)/shard_map/all_to_all | solution.py:427
  26.4 0.7 %collective-permute-start.4 = (f32[32,128]{1,0:T(8,128)S(1)}, f32[32,128]{1,0:T(8,128)S(1)}, u32[]{:S(2)}, u32[]{:S(2)}) collective-permute-start(f32[32,128]{1,0:T(8,128)S(1)} %get-tuple-element.23), channel_id=1, source_target_pairs={{0,1},{1,0},{2,3},{3,2},{4,5},{5,4},{6,7},{7,6},{8,9},{9,8},{10,11... | collective-permute-start | bytes 49160 | tf_op jit(solution)/shard_map/ppermute | solution.py:430
  27.1 3.9 %collective-permute-start.2 = (f32[5,8,128]{2,1,0:T(8,128)S(1)}, f32[5,8,128]{2,1,0:T(8,128)S(1)}, u32[]{:S(2)}, u32[]{:S(2)}) collective-permute-start(f32[5,8,128]{2,1,0:T(8,128)S(1)} %get-tuple-element.21), channel_id=1, source_target_pairs={{0,16},{16,32},{32,48},{48,64},{64,80},{80,96},{96,112},{112,128},... | collective-permute-start | bytes 61448 | tf_op jit(solution)/shard_map/ppermute | solution.py:428
  31.0 2.1 %collective-permute-start.3 = (f32[5,8,128]{2,1,0:T(8,128)S(1)}, f32[5,8,128]{2,1,0:T(8,128)S(1)}, u32[]{:S(2)}, u32[]{:S(2)}) collective-permute-start(f32[5,8,128]{2,1,0:T(8,128)S(1)} %get-tuple-element.22), channel_id=1, source_target_pairs={{16,0},{32,16},{48,32},{64,48},{80,64},{96,80},{112,96},{128,112},... | collective-permute-start | bytes 61448 | tf_op jit(solution)/shard_map/ppermute | solution.py:429
  33.2 0.0 copy-start.2
  33.2 0.0 copy-start.4
  33.2 4.5 %shard_map.98.acc_ref = f32[512,512]{1,0:T(8,128)S(1)} custom-call(f32[4,32,128]{2,1,0:T(8,128)S(1)} %get-tuple-element.24.src_ref, s32[32,128]{1,0:T(8,128)S(1)} %bitcast.13), custom_call_target="tpu_custom_call" | custom-call | flops 8000000000 | bytes 1000000 | tf_op jit(solution)/shard_map/pallas_call | solution.py:432
  37.7 0.0 copy-start.8
  37.7 1.0 %copy-done.8 = f32[512,512]{1,0:T(8,128)} copy-done((f32[512,512]{1,0:T(8,128)}, f32[512,512]{1,0:T(8,128)S(1)}, u32[]{:S(2)}) %copy-start.8) | copy-done | bytes 1048600
  38.7 1.1 %all-to-all-done.got_ref = f32[16,24,128]{2,1,0:T(8,128)S(1)} async-done(((f32[16,24,128]{2,1,0:T(8,128)}), f32[16,24,128]{2,1,0:T(8,128)S(1)}, u32[]{:S(2)}, u32[]{:S(2)}) %all-to-all-start) | async-done | bytes 196640 | tf_op jit(solution)/shard_map/all_to_all | solution.py:427
  39.8 0.0 copy-done.2
  39.8 0.0 copy-done.4
  39.8 2.2 %shard_map.100 = (f32[16,20,128]{2,1,0:T(8,128)}, f32[4,4,128]{2,1,0:T(4,128)S(1)}, f32[4,4,128]{2,1,0:T(4,128)S(1)}) custom-call(s32[1]{0:T(128)} %bitcast.6.az_ref, s32[16]{0:T(128)S(1)} %copy-done.4, bf16[256,1024]{1,0:T(8,128)(2,1)S(1)} %copy-done.2, f32[16,24,128]{2,1,0:T(8,128)S(1)} %all-to-all-done.got_ref, ...), custom_call_target="tpu_custom_call" | custom-call | flops 100000000 | bytes 1000000 | tf_op jit(solution)/shard_map/pallas_call | solution.py:436
  42.0 6.5 %all-to-all-start.1 = ((f32[16,20,128]{2,1,0:T(8,128)}), f32[16,20,128]{2,1,0:T(8,128)S(1)}, u32[]{:S(2)}, u32[]{:S(2)}) async-start(f32[16,20,128]{2,1,0:T(8,128)} %get-tuple-element.28), calls=%async_computation.1 | async-start | bytes 393216 | tf_op jit(solution)/shard_map/all_to_all | solution.py:447
  48.5 1.9 %collective-permute-start.5 = (f32[4,4,128]{2,1,0:T(4,128)S(1)}, f32[4,4,128]{2,1,0:T(4,128)S(1)}, u32[]{:S(2)}, u32[]{:S(2)}) collective-permute-start(f32[4,4,128]{2,1,0:T(4,128)S(1)} %get-tuple-element.30), channel_id=1, source_target_pairs={{0,2},{2,4},{4,6},{6,8},{8,10},{10,12},{12,14},{1,3},{3,5},{5,7},{... | collective-permute-start | bytes 24584 | tf_op jit(solution)/shard_map/ppermute | solution.py:448
  50.4 3.6 %collective-permute-start.6 = (f32[4,4,128]{2,1,0:T(4,128)S(1)}, f32[4,4,128]{2,1,0:T(4,128)S(1)}, u32[]{:S(2)}, u32[]{:S(2)}) collective-permute-start(f32[4,4,128]{2,1,0:T(4,128)S(1)} %get-tuple-element.31), channel_id=1, source_target_pairs={{2,0},{4,2},{6,4},{8,6},{10,8},{12,10},{14,12},{3,1},{5,3},{7,5},{... | collective-permute-start | bytes 24584 | tf_op jit(solution)/shard_map/ppermute | solution.py:449
  54.1 0.0 collective-permute-done.4.rad_in
  54.1 0.0 collective-permute-done.2.az_prev
  54.1 0.0 collective-permute-done.3.az_next
  54.1 0.0 copy-start.9
  54.1 1.2 %copy-done.9 = f32[512,512]{1,0:T(8,128)S(1)} copy-done((f32[512,512]{1,0:T(8,128)S(1)}, f32[512,512]{1,0:T(8,128)}, u32[]{:S(2)}) %copy-start.9) | copy-done | bytes 1048600
  55.3 1.8 %shard_map.99.sect_ref = f32[5,8,64,128]{3,2,1,0:T(8,128)S(1)} custom-call(s32[1]{0:T(128)} %bitcast.rad_ref, s32[1]{0:T(128)} %bitcast.1.odd_ref, f32[5,6]{1,0:T(8,128)S(1)} %copy-done.3, f32[5,8,64,128]{3,2,1,0:T(8,128)S(1)} %copy-done.1, f32[5,64,128]{2,1,0:T(8,128)S(1)} %collective-permute-done.first_ref, ...), custom_call_target="tpu_custom_call" | custom-call | flops 4000000000 | bytes 4000000 | tf_op jit(solution)/shard_map/pallas_call | solution.py:451
  57.2 0.0 collective-permute-done.5.below_ref
  57.2 0.0 collective-permute-done.6.above_ref
  57.2 3.8 %all-to-all-done.1.got_ref = f32[16,20,128]{2,1,0:T(8,128)S(1)} async-done(((f32[16,20,128]{2,1,0:T(8,128)}), f32[16,20,128]{2,1,0:T(8,128)S(1)}, u32[]{:S(2)}, u32[]{:S(2)}) %all-to-all-start.1) | async-done | bytes 163872 | tf_op jit(solution)/shard_map/all_to_all | solution.py:447
  61.0 1.5 %shard_map.101 = (f32[5,8,64,128]{3,2,1,0:T(8,128)}, f32[4,40,128]{2,1,0:T(8,128)}) custom-call(s32[1]{0:T(128)} %bitcast.rad_ref, f32[5,8,64,128]{3,2,1,0:T(8,128)S(1)} %shard_map.99.sect_ref, f32[16,20,128]{2,1,0:T(8,128)S(1)} %all-to-all-done.1.got_ref, f32[4,32,128]{2,1,0:T(8,128)S(1)} %get-tuple-element.29.stay_ref, ...), custom_call_target="tpu_custom_call" | custom-call | flops 1000000 | bytes 4000000 | tf_op jit(solution)/shard_map/pallas_call | solution.py:455
  (1 shorter events, 0.0 us)
Async XLA Ops:
  0.6 6.3 %copy-start.7 = (s32[32,1,1]{0,2,1:T(1,128)S(1)}, s32[32,1,1]{0,2,1:T(1,128)}, u32[]{:S(2)}) copy-start(s32[32,1,1]{0,2,1:T(1,128)} %param.13) | copy-start | bytes 388
  0.6 6.3 %copy-start.6 = (s32[32,1,128]{2,1,0:T(1,128)S(1)}, s32[32,1,128]{2,1,0:T(1,128)}, u32[]{:S(2)}) copy-start(s32[32,1,128]{2,1,0:T(1,128)} %param.11) | copy-start | bytes 49156
  0.7 1.3 %copy-start = (f32[5,8,64,128]{3,2,1,0:T(8,128)S(1)}, f32[5,8,64,128]{3,2,1,0:T(8,128)}, u32[]{:S(2)}) copy-start(f32[5,8,64,128]{3,2,1,0:T(8,128)} %q_ref.7) | copy-start | bytes 3932164
  2.0 5.0 %copy-start.1 = (f32[5,8,64,128]{3,2,1,0:T(8,128)S(1)}, f32[5,8,64,128]{3,2,1,0:T(8,128)}, u32[]{:S(2)}) copy-start(f32[5,8,64,128]{3,2,1,0:T(8,128)} %q_ref.7) | copy-start | bytes 3932164
  2.0 12.8 %collective-permute-start = (f32[5,64,128]{2,1,0:T(8,128)S(1)}, f32[5,64,128]{2,1,0:T(8,128)S(1)}, u32[]{:S(2)}, u32[]{:S(2)}) collective-permute-start(f32[5,64,128]{2,1,0:T(8,128)S(1)} %get-tuple-element.18), channel_id=1, source_target_pairs={{0,2},{2,0},{4,6},{6,4},{8,10},{10,8},{12,14},{14,12},{1,3},{3,1},... | collective-permute-start | bytes 491528 | tf_op jit(solution)/shard_map/ppermute | solution.py:407
  2.1 12.7 %collective-permute-start.1 = (f32[5,64,128]{2,1,0:T(8,128)S(1)}, f32[5,64,128]{2,1,0:T(8,128)S(1)}, u32[]{:S(2)}, u32[]{:S(2)}) collective-permute-start(f32[5,64,128]{2,1,0:T(8,128)S(1)} %get-tuple-element.19), channel_id=1, source_target_pairs={{2,4},{4,2},{6,8},{8,6},{10,12},{12,10},{3,5},{5,3},{7,9},{9,7},{1... | collective-permute-start | bytes 491528 | tf_op jit(solution)/shard_map/ppermute | solution.py:408
  7.0 0.8 %copy-start.5 = (f32[4,32,1,128]{3,2,1,0:T(1,128)S(1)}, f32[4,32,1,128]{3,2,1,0:T(1,128)}, u32[]{:S(2)}) copy-start(f32[4,32,1,128]{3,2,1,0:T(1,128)} %param.10) | copy-start | bytes 196612
  7.8 7.0 %copy-start.3 = (f32[5,6]{1,0:T(8,128)S(1)}, f32[5,6]{1,0:T(8,128)}, u32[]{:S(2)}) copy-start(f32[5,6]{1,0:T(8,128)} %coef_ref.3) | copy-start | bytes 364
  17.1 22.7 %all-to-all-start = ((f32[16,24,128]{2,1,0:T(8,128)}), f32[16,24,128]{2,1,0:T(8,128)S(1)}, u32[]{:S(2)}, u32[]{:S(2)}) async-start(f32[16,24,128]{2,1,0:T(8,128)} %get-tuple-element.25), calls=%async_computation | async-start | bytes 393216 | tf_op jit(solution)/shard_map/all_to_all | solution.py:427
  26.4 27.7 %collective-permute-start.4 = (f32[32,128]{1,0:T(8,128)S(1)}, f32[32,128]{1,0:T(8,128)S(1)}, u32[]{:S(2)}, u32[]{:S(2)}) collective-permute-start(f32[32,128]{1,0:T(8,128)S(1)} %get-tuple-element.23), channel_id=1, source_target_pairs={{0,1},{1,0},{2,3},{3,2},{4,5},{5,4},{6,7},{7,6},{8,9},{9,8},{10,11... | collective-permute-start | bytes 49160 | tf_op jit(solution)/shard_map/ppermute | solution.py:430
  27.1 27.0 %collective-permute-start.2 = (f32[5,8,128]{2,1,0:T(8,128)S(1)}, f32[5,8,128]{2,1,0:T(8,128)S(1)}, u32[]{:S(2)}, u32[]{:S(2)}) collective-permute-start(f32[5,8,128]{2,1,0:T(8,128)S(1)} %get-tuple-element.21), channel_id=1, source_target_pairs={{0,16},{16,32},{32,48},{48,64},{64,80},{80,96},{96,112},{112,128},... | collective-permute-start | bytes 61448 | tf_op jit(solution)/shard_map/ppermute | solution.py:428
  31.0 23.1 %collective-permute-start.3 = (f32[5,8,128]{2,1,0:T(8,128)S(1)}, f32[5,8,128]{2,1,0:T(8,128)S(1)}, u32[]{:S(2)}, u32[]{:S(2)}) collective-permute-start(f32[5,8,128]{2,1,0:T(8,128)S(1)} %get-tuple-element.22), channel_id=1, source_target_pairs={{16,0},{32,16},{48,32},{64,48},{80,64},{96,80},{112,96},{128,112},... | collective-permute-start | bytes 61448 | tf_op jit(solution)/shard_map/ppermute | solution.py:429
  33.2 6.6 %copy-start.2 = (bf16[256,1024]{1,0:T(8,128)(2,1)S(1)}, bf16[256,1024]{1,0:T(8,128)(2,1)}, u32[]{:S(2)}) copy-start(bf16[256,1024]{1,0:T(8,128)(2,1)} %constant.28.clone.basis_ref) | copy-start | bytes 1572868
  33.2 6.6 %copy-start.4 = (s32[16]{0:T(128)S(1)}, s32[16]{0:T(128)}, u32[]{:S(2)}) copy-start(s32[16]{0:T(128)} %width_ref.1) | copy-start | bytes 196
  37.7 1.0 %copy-start.8 = (f32[512,512]{1,0:T(8,128)}, f32[512,512]{1,0:T(8,128)S(1)}, u32[]{:S(2)}) copy-start(f32[512,512]{1,0:T(8,128)S(1)} %shard_map.98.acc_ref) | copy-start | bytes 3145732
  42.0 18.9 %all-to-all-start.1 = ((f32[16,20,128]{2,1,0:T(8,128)}), f32[16,20,128]{2,1,0:T(8,128)S(1)}, u32[]{:S(2)}, u32[]{:S(2)}) async-start(f32[16,20,128]{2,1,0:T(8,128)} %get-tuple-element.28), calls=%async_computation.1 | async-start | bytes 393216 | tf_op jit(solution)/shard_map/all_to_all | solution.py:447
  48.5 8.7 %collective-permute-start.5 = (f32[4,4,128]{2,1,0:T(4,128)S(1)}, f32[4,4,128]{2,1,0:T(4,128)S(1)}, u32[]{:S(2)}, u32[]{:S(2)}) collective-permute-start(f32[4,4,128]{2,1,0:T(4,128)S(1)} %get-tuple-element.30), channel_id=1, source_target_pairs={{0,2},{2,4},{4,6},{6,8},{8,10},{10,12},{12,14},{1,3},{3,5},{5,7},{... | collective-permute-start | bytes 24584 | tf_op jit(solution)/shard_map/ppermute | solution.py:448
  50.4 6.7 %collective-permute-start.6 = (f32[4,4,128]{2,1,0:T(4,128)S(1)}, f32[4,4,128]{2,1,0:T(4,128)S(1)}, u32[]{:S(2)}, u32[]{:S(2)}) collective-permute-start(f32[4,4,128]{2,1,0:T(4,128)S(1)} %get-tuple-element.31), channel_id=1, source_target_pairs={{2,0},{4,2},{6,4},{8,6},{10,8},{12,10},{14,12},{3,1},{5,3},{7,5},{... | collective-permute-start | bytes 24584 | tf_op jit(solution)/shard_map/ppermute | solution.py:449
  54.1 1.2 %copy-start.9 = (f32[512,512]{1,0:T(8,128)S(1)}, f32[512,512]{1,0:T(8,128)}, u32[]{:S(2)}) copy-start(f32[512,512]{1,0:T(8,128)} %copy-done.8) | copy-start | bytes 3145732

commit v3 on v2

--- a/solution.py
+++ b/solution.py
@@ -34,6 +34,8 @@
 HIGHEST = lax.Precision.HIGHEST
 VMEM = pl.BlockSpec(memory_space=pltpu.VMEM)
 SMEM = pl.BlockSpec(memory_space=pltpu.SMEM)
+ANY = pl.BlockSpec(memory_space=pl.ANY)
+HBM = pl.BlockSpec(memory_space=pltpu.HBM)
 NT = (((1,), (1,)), ((), ()))
 
 
@@ -69,13 +71,6 @@
     )
 
 
-def edges_body(odd_ref, q_ref, first_out, second_out):
-    odd = odd_ref[0] == 1
-    low, high = q_ref[:, 0], q_ref[:, CAX - 1]
-    first_out[...] = jnp.where(odd, low, high)
-    second_out[...] = jnp.where(odd, high, low)
-
-
 def one_hot_rows(cells_ref, first, blocks):
     cells = jnp.concatenate([cells_ref[first + i : first + i + 1, :] for i in range(blocks)], axis=1)
     width = blocks * BLK
@@ -84,21 +79,36 @@
 
 
 def parcels_body(
-    count_ref, move_ref, q_ref, parcel_ref, cells_ref,
-    src_out, stay_out, up_out, down_out, near_out,
-    hot_ref, gas_ref, state_ref, spread_ref,
+    odd_ref, count_ref, move_ref, q_hbm, parcel_ref, cells_ref,
+    src_out, stay_out, first_out, second_out,
+    q_ref, hot_ref, gas_ref, state_ref, leave_ref, sems,
 ):
+    odd = odd_ref[0]
+    last = CAX - 1
+    copies = [
+        pltpu.make_async_copy(q_hbm.at[pl.ds(1, 3)], q_ref, sems.at[0]),
+        pltpu.make_async_copy(
+            q_hbm.at[:, last * (1 - odd)], first_out.at[pl.ds(0, FIELDS)], sems.at[1]
+        ),
+        pltpu.make_async_copy(q_hbm.at[:, last * odd], second_out.at[pl.ds(0, FIELDS)], sems.at[2]),
+    ]
+    for copy in copies:
+        copy.start()
+    for first in range(0, BLK_DEV, 4):
+        hot_ref[:, first * BLK : (first + 4) * BLK] = one_hot_rows(cells_ref, first, 4)[0]
+    copies[0].wait()
     parts = [[], []]
     for f in range(3):
-        table = q_ref[f + 1].reshape(ROWS, CR).T
+        table = q_ref[f].reshape(ROWS, CR).T
         high, low = halves(table)
         parts[0].append(high)
         parts[1].append(low)
     parts = [jnp.concatenate(part, axis=0) for part in parts]
     for first in range(0, BLK_DEV, 4):
         width = 4 * BLK
-        hot, lanes = one_hot_rows(cells_ref, first, 4)
-        hot_ref[:, first * BLK : first * BLK + width] = hot
+        hot = hot_ref[:, first * BLK : first * BLK + width]
+        lanes = jnp.concatenate([cells_ref[first + i : first + i + 1, :] for i in range(4)], axis=1)
+        lanes = lanes & (CR - 1)
         rows = sum(jnp.dot(part, hot, preferred_element_type=F32) for part in parts)
         mask = iota((CR, width), 0) == lanes
         for f in range(3):
@@ -121,8 +131,7 @@
     for i in range(4):
         src_out[i] = sources[i]
         state_ref[i] = jnp.where(alive, (new_vel + [new_diam])[i], 0.0)
-    up_out[...] = jnp.zeros_like(up_out)
-    down_out[...] = jnp.zeros_like(down_out)
+    leave_ref[...] = jnp.zeros_like(leave_ref)
 
     def place(block, ranks):
         up, down = ranks
@@ -132,41 +141,33 @@
 
         @pl.when(move == 1)
         def _():
-            up_out[:, pl.ds(jnp.minimum(up, MOVEB - 1), 1), :] = row
+            leave_ref[0, :, pl.ds(jnp.minimum(up, MOVEB - 1), 1), :] = row
 
         @pl.when(move == -1)
         def _():
-            down_out[:, pl.ds(jnp.minimum(down, MOVEB - 1), 1), :] = row
+            leave_ref[1, :, pl.ds(jnp.minimum(down, MOVEB - 1), 1), :] = row
 
         return up + (move == 1).astype(jnp.int32), down + (move == -1).astype(jnp.int32)
 
     lax.fori_loop(0, BLK_DEV, place, (jnp.int32(0), jnp.int32(0)))
-    split = []
-    for s in sources:
-        high = s.astype(BF16).astype(F32)
-        split.append((high, s - high))
-    for block in range(BLK_DEV):
-        mask = iota((CYCLES, BLK), 0) == (cells_ref[block : block + 1, :] & (CR - 1))
+    for out, flag in ((first_out, 0), (second_out, 1)):
+        out[FIELDS] = jnp.zeros((CAZ, CR), F32)
         for i in range(4):
-            for half in range(2):
-                row = split[i][half][block : block + 1, :]
-                first = (half * 4 + i) * CYCLES
-                spread_ref[first : first + CYCLES, block * BLK : (block + 1) * BLK] = jnp.where(
-                    mask, row, 0.0
-                ).astype(BF16)
-    total = lax.dot_general(spread_ref[...], hot_ref[...], NT, preferred_element_type=F32)
-    near_out[...] = total[: 4 * CYCLES] + total[4 * CYCLES :]
+            out[FIELDS, 4 * i : 4 * i + 4, :] = jnp.where(odd == flag, leave_ref[0, i], leave_ref[1, i])
+    copies[1].wait()
+    copies[2].wait()
 
 
 SOURCE_OF = (0, 1, 2, 3, 0)
 
 
 BAND = 24
+SHARE = 2 * FIELDS * CAX // N_AZ
 
 
 def near_body(
     rad_ref, odd_ref, coef_ref, q_ref, first_ref, second_ref, near_ref,
-    send_out, az_lo, az_hi, rad_out,
+    send_out, rad_out, az_ref,
 ):
     lane = iota((CR, 2 * CAZ), 1)
     row = iota((CR, 2 * CAZ), 0)
@@ -184,7 +185,7 @@
         for p in range(PAIRS)
     ]
     odd = odd_ref[0] == 1
-    first, second = first_ref[...], second_ref[...]
+    first, second = first_ref[0:FIELDS], second_ref[0:FIELDS]
     before, after = jnp.where(odd, first, second), jnp.where(odd, second, first)
     halo = turned([jnp.concatenate([before[f], after[f]], axis=0) for f in range(FIELDS)])
 
@@ -229,8 +230,11 @@
                 send_out[p * QUADS + quad, f * 4 : f * 4 + 4, :] = block[quad * 4 : quad * 4 + 4]
         for quad in range(QUADS):
             send_out[p * QUADS + quad, LINES : LINES + 4, :] = ends[quad * 4 : quad * 4 + 4]
-    az_lo[...] = q_ref[:, :, 0, :]
-    az_hi[...] = q_ref[:, :, CAZ - 1, :]
+    for f in range(FIELDS):
+        az_ref[f * CAX : (f + 1) * CAX] = q_ref[f, :, 0, :]
+        az_ref[(FIELDS + f) * CAX : (FIELDS + f + 1) * CAX] = q_ref[f, :, CAZ - 1, :]
+    for owner in range(N_AZ):
+        send_out[owner, LINES + 4 :, :] = az_ref[owner * SHARE : (owner + 1) * SHARE]
     rad_edges(rad_ref[0], q_ref, rad_out)
 
 
@@ -246,66 +250,92 @@
     rad_out[...] = packed
 
 
-def scatter_body(src_ref, cells_ref, acc_ref):
+def scattered(src_ref, cells_ref, acc_ref, start, stop, near_ref=None):
     step = 8
-    for first in range(0, BLK_DEV, step):
+    for first in range(0 if near_ref is not None else start, BLK_DEV if near_ref is not None else stop, step):
         hot, lanes = one_hot_rows(cells_ref, first, step)
-        mask = iota((CR, step * BLK), 0) == lanes
-        spread = [[], []]
+        rows = [[], []]
         for i in range(4):
             row = jnp.concatenate([src_ref[i, first + j : first + j + 1, :] for j in range(step)], axis=1)
             high = row.astype(BF16).astype(F32)
-            spread[0].append(jnp.where(mask, high, 0.0).astype(BF16))
-            spread[1].append(jnp.where(mask, row - high, 0.0).astype(BF16))
+            rows[0].append(high)
+            rows[1].append(row - high)
+        if near_ref is not None:
+            mask = iota((CYCLES, step * BLK), 0) == lanes
+            spread = jnp.concatenate(
+                [jnp.where(mask, row, 0.0).astype(BF16) for row in rows[0] + rows[1]], axis=0
+            )
+            total = lax.dot_general(spread, hot, NT, preferred_element_type=F32)
+            total = total[: 4 * CYCLES] + total[4 * CYCLES :]
+            if first == 0:
+                near_ref[...] = total
+            else:
+                near_ref[...] += total
+        if not start <= first < stop:
+            continue
+        mask = iota((CR, step * BLK), 0) == lanes
         total = sum(
-            lax.dot_general(hot, jnp.concatenate(part, axis=0), NT, preferred_element_type=F32)
-            for part in spread
+            lax.dot_general(
+                hot,
+                jnp.concatenate([jnp.where(mask, row, 0.0).astype(BF16) for row in part], axis=0),
+                NT,
+                preferred_element_type=F32,
+            )
+            for part in rows
         )
-        if first == 0:
+        if first == start:
             acc_ref[...] = total
         else:
             acc_ref[...] += total
 
 
-def section_body(
-    rad_ref, odd_ref, coef_ref, q_ref, first_ref, second_ref, az_prev, az_next, rad_in, acc_ref, sect_out
-):
+def first_half_body(src_ref, cells_ref, acc_out, near_out):
+    scattered(src_ref, cells_ref, acc_out, 0, BLK_DEV // 2, near_out)
+
+
+def section_body(rad_ref, odd_ref, coef_ref, q_ref, first_ref, second_ref, acc_ref, sect_out):
     rad = rad_ref[0]
     odd = odd_ref[0] == 1
-    lane = iota((CAZ, CR), 1)
     row = iota((CAZ, CR), 0)
-    metric = 4.0 / ((rad * CR + iota((1, CR), 1)).astype(F32) + 4.0)
-    target = jnp.where(rad == 0, CR - 1, 0)
+    lane = iota((1, CR), 1)
+    metric = 4.0 / ((rad * CR + lane).astype(F32) + 4.0)
     for f in range(FIELDS):
         c = [coef_ref[f, i] for i in range(6)]
         mid = (1.0 - c[1] - c[5]) - c[3] * metric
-        az_up = (0.5 * (c[2] + c[3])) * metric
-        az_down = (0.5 * (c[3] - c[2])) * metric
-        az_up_in = jnp.where(row == CAZ - 1, 0.0, az_up)
-        az_down_in = jnp.where(row == 0, 0.0, az_down)
+        az_up = jnp.where(row == CAZ - 1, 0.0, (0.5 * (c[2] + c[3])) * metric)
+        az_down = jnp.where(row == 0, 0.0, (0.5 * (c[3] - c[2])) * metric)
         ax_up, ax_down = 0.5 * (c[0] + c[1]), 0.5 * (c[1] - c[0])
-        rad_up, rad_down = 0.5 * (c[4] + c[5]), 0.5 * (c[5] - c[4])
-        rad_up_in = jnp.where(iota((1, CR), 1) == CR - 1, 0.0, rad_up)
-        rad_down_in = jnp.where(iota((1, CR), 1) == 0, 0.0, rad_down)
-        rad_edge = jnp.where(rad == 0, rad_up, rad_down)
+        rad_up = jnp.where(lane == CR - 1, 0.0, 0.5 * (c[4] + c[5]))
+        rad_down = jnp.where(lane == 0, 0.0, 0.5 * (c[5] - c[4]))
         s = SOURCE_OF[f] * CR
         for a in range(CAX):
             q = q_ref[f, a]
             ahead = q_ref[f, a + 1] if a + 1 < CAX else jnp.where(odd, second_ref[f], first_ref[f])
             behind = q_ref[f, a - 1] if a else jnp.where(odd, first_ref[f], second_ref[f])
-            out = (
+            sect_out[f, a] = (
                 mid * q + ax_up * ahead + ax_down * behind
-                + az_up_in * pltpu.roll(q, CAZ - 1, 0) + az_down_in * pltpu.roll(q, 1, 0)
-                + rad_up_in * pltpu.roll(q, CR - 1, 1) + rad_down_in * pltpu.roll(q, 1, 1)
+                + az_up * pltpu.roll(q, CAZ - 1, 0) + az_down * pltpu.roll(q, 1, 0)
+                + rad_up * pltpu.roll(q, CR - 1, 1) + rad_down * pltpu.roll(q, 1, 1)
                 + acc_ref[a * CAZ : (a + 1) * CAZ, s : s + CR]
             )
+
+
+def second_half_body(rad_ref, coef_ref, sect_ref, src_ref, cells_ref, rad_in, sect_out, acc_ref):
+    scattered(src_ref, cells_ref, acc_ref, BLK_DEV // 2, BLK_DEV)
+    rad = rad_ref[0]
+    lane = iota((CAZ, CR), 1)
+    target = jnp.where(rad == 0, CR - 1, 0)
+    for f in range(FIELDS):
+        c4, c5 = coef_ref[f, 4], coef_ref[f, 5]
+        weight = 0.5 * jnp.where(rad == 0, c4 + c5, c5 - c4)
+        weight = jnp.where(lane == target, weight, 0.0)
+        s = SOURCE_OF[f] * CR
+        for a in range(CAX):
             edge = jnp.concatenate(
                 [pltpu.roll(rad_in[...], (target + (2 * CR - ((2 * a + h) * 8 + f))) % CR, 1) for h in range(2)],
                 axis=0,
             )
-            sect_out[f, a] = out + jnp.where(lane == target, rad_edge * edge, 0.0)
-            sect_out[f, a, 0:1] += az_down * az_prev[f, a : a + 1]
-            sect_out[f, a, CAZ - 1 : CAZ] += az_up * az_next[f, a : a + 1]
+            sect_out[f, a] = sect_ref[f, a] + acc_ref[a * CAZ : (a + 1) * CAZ, s : s + CR] + weight * edge
 
 
 def lined(pieces, line_ref):
@@ -318,11 +348,14 @@
 
 
 def filter_body(
-    az_ref, width_ref, basis_ref, got_ref, up_ref, down_ref,
-    send_out, up_out, down_out, line_ref, ends_ref, piece_ref,
+    az_ref, width_ref, basis_ref, got_ref, _, send_out, line_ref, ends_ref, piece_ref
 ):
-    up_out[...] = up_ref[...]
-    down_out[...] = down_ref[...]
+    for home in range(N_AZ):
+        send_out[home, LINES:, :] = jnp.where(
+            az_ref[0] < N_AZ // 2,
+            got_ref[(home + 1) % N_AZ, LINES + 4 :, :],
+            got_ref[(home - 1) % N_AZ, LINES + 4 :, :],
+        )
     quad = az_ref[0] % QUADS
     low = iota((LINES, 2 * CAZ), 1) < CAZ
     line_ref[...] = jnp.zeros_like(line_ref)
@@ -362,13 +395,18 @@
     for i in range(N_AZ // 2):
         cols = slice(i * 2 * CAZ, (i + 1) * 2 * CAZ)
         t0, t1 = line_ref[0:LINES, cols], line_ref[BAND : BAND + LINES, cols]
-        send_out[2 * i] = jnp.where(low, t0, pltpu.roll(t1, CAZ, 1))
-        send_out[2 * i + 1] = jnp.where(low, pltpu.roll(t0, CAZ, 1), t1)
-
-
-def merge_body(rad_ref, sect_ref, got_ref, stay_ref, below_ref, above_ref, gas_out, parcels_out, flip_ref):
+        send_out[2 * i, 0:LINES] = jnp.where(low, t0, pltpu.roll(t1, CAZ, 1))
+        send_out[2 * i + 1, 0:LINES] = jnp.where(low, pltpu.roll(t0, CAZ, 1), t1)
+
+
+def merge_body(
+    rad_ref, odd_ref, coef_ref, sect_ref, got_ref, stay_ref, first_ref, second_ref,
+    gas_out, parcels_out, flip_ref, az_ref,
+):
     near = (iota((2 * CAZ, CR), 1) < CYCLES) & (rad_ref[0] == 0)
     flip_ref[...] = jnp.zeros_like(flip_ref)
+    for owner in range(N_AZ):
+        az_ref[owner * SHARE : (owner + 1) * SHARE] = got_ref[owner, LINES:, :]
     for pair in range(PAIRS):
         for f in range(FIELDS):
             for quad in range(QUADS):
@@ -379,86 +417,100 @@
             moved = pltpu.roll(turned, (CR - f * CYCLES) % CR, 1) if f else turned
             kept = sect_ref[f, 2 * pair : 2 * pair + 2].reshape(2 * CAZ, CR)
             gas_out[f, 2 * pair : 2 * pair + 2] = jnp.where(near, moved, kept).reshape(2, CAZ, CR)
+    lane = iota((1, CR), 1)
+    metric = 4.0 / ((rad_ref[0] * CR + lane).astype(F32) + 4.0)
+    metric = jnp.where((lane < CYCLES) & (rad_ref[0] == 0), 0.0, metric)
+    for f in range(FIELDS):
+        az_up = (0.5 * (coef_ref[f, 2] + coef_ref[f, 3])) * metric
+        az_down = (0.5 * (coef_ref[f, 3] - coef_ref[f, 2])) * metric
+        after = az_up * az_ref[f * CAX : (f + 1) * CAX]
+        before = az_down * az_ref[(FIELDS + f) * CAX : (FIELDS + f + 1) * CAX]
+        for a in range(CAX):
+            gas_out[f, a, 0:1] += before[a : a + 1]
+            gas_out[f, a, CAZ - 1 : CAZ] += after[a : a + 1]
+    odd = odd_ref[0] == 1
     parcels_out[:, 0:BLK_DEV, :] = stay_ref[...]
-    parcels_out[:, BLK_DEV : BLK_DEV + MOVEB, :] = below_ref[...]
-    parcels_out[:, BLK_DEV + MOVEB :, :] = above_ref[...]
+    for i in range(4):
+        first, second = first_ref[FIELDS, 4 * i : 4 * i + 4, :], second_ref[FIELDS, 4 * i : 4 * i + 4, :]
+        parcels_out[i, BLK_DEV : BLK_DEV + MOVEB, :] = jnp.where(odd, first, second)
+        parcels_out[i, BLK_DEV + MOVEB :, :] = jnp.where(odd, second, first)
 
 
 def shards(fields, coeffs, parcels, cells, counts, moves, widths):
     rad_index = lax.axis_index("rad").astype(jnp.int32).reshape(1)
     az_index = lax.axis_index("az").astype(jnp.int32).reshape(1)
     odd = (lax.axis_index("ax").astype(jnp.int32) % 2).reshape(1)
-    n_ax, n_az, n_rad = (lax.axis_size(axis) for axis in ("ax", "az", "rad"))
+    n_ax, n_rad = lax.axis_size("ax"), lax.axis_size("rad")
     parcels = parcels.reshape(4, BLK_DEV, BLK)
     cells = cells.reshape(BLK_DEV, BLK)
     counts = counts.reshape(1)
     moves = moves.reshape(BLK_DEV)
-    up = [(i, i + 1) for i in range(n_ax - 1)]
-    down = [(i + 1, i) for i in range(n_ax - 1)]
     inner = [(i, i ^ 1) for i in range(n_ax)]
     outer = [(i, ((i + 1) ^ 1) - 1) for i in range(1, n_ax - 1)]
-    ahead = [(i, (i + 1) % n_az) for i in range(n_az)]
-    back = [((i + 1) % n_az, i) for i in range(n_az)]
     across = [(i, i ^ 1) for i in range(n_rad)]
-
-    first, second = call(
-        edges_body, [(FIELDS, CAZ, CR)] * 2, [SMEM, VMEM], 10**6, 2 * 10**6, mib=4
-    )(odd, fields)
-    first = lax.ppermute(first, "ax", inner)
-    second = lax.ppermute(second, "ax", outer)
-
-    src, stay, sent_up, sent_down, near = call(
+    gas_shape = (FIELDS, CAX, CAZ, CR)
+
+    src, stay, first, second = call(
         parcels_body,
-        [(4, BLK_DEV, BLK), (4, BLK_DEV, BLK), (4, MOVEB, BLK), (4, MOVEB, BLK), (4 * CYCLES, ROWS)],
-        [SMEM, SMEM, VMEM, VMEM, VMEM], 6 * 10**9, 2 * 10**6,
+        [(4, BLK_DEV, BLK), (4, BLK_DEV, BLK)] + [(FIELDS + 1, CAZ, CR)] * 2,
+        [SMEM, SMEM, SMEM, HBM, VMEM, VMEM], 6 * 10**9, 2 * 10**6,
         [
+            pltpu.VMEM((3, CAX, CAZ, CR), F32),
             pltpu.VMEM((ROWS, PARCELS), BF16),
             pltpu.VMEM((3, BLK_DEV, BLK), F32),
             pltpu.VMEM((4, BLK_DEV, BLK), F32),
-            pltpu.VMEM((8 * CYCLES, PARCELS), BF16),
+            pltpu.VMEM((2, 4, MOVEB, BLK), F32),
+            pltpu.SemaphoreType.DMA((3,)),
         ],
-    )(counts, moves, fields, parcels, cells)
-
-    to_owner, az_lo, az_hi, rad_edge = call(
+        mib=62,
+    )(odd, counts, moves, fields, parcels, cells)
+    first = lax.ppermute(first, "ax", inner)
+    second = lax.ppermute(second, "ax", outer)
+
+    added, near = call(
+        first_half_body, [(ROWS, 4 * CR), (4 * CYCLES, ROWS)], [VMEM] * 2, 4 * 10**9, 10**6, mib=16
+    )(src, cells)
+
+    to_owner, rad_edge = call(
         near_body,
-        [(N_AZ, LINES + 4, 2 * CAZ), (FIELDS, CAX, CR), (FIELDS, CAX, CR), (32, CR)],
-        [SMEM, SMEM, SMEM] + [VMEM] * 4, 10**7, 4 * 10**6, mib=8,
+        [(N_AZ, LINES + 4 + SHARE, 2 * CAZ), (32, CR)],
+        [SMEM, SMEM, SMEM] + [VMEM] * 4, 10**7, 4 * 10**6,
+        [pltpu.VMEM((2 * FIELDS * CAX, CR), F32)],
+        mib=8,
     )(rad_index, odd, coeffs, fields, first, second, near)
     lines = lax.all_to_all(to_owner, "az", 0, 0, tiled=True)
-    az_prev = lax.ppermute(az_hi, "az", ahead)
-    az_next = lax.ppermute(az_lo, "az", back)
     rad_got = lax.ppermute(rad_edge, "rad", across)
 
-    (added,) = call(
-        scatter_body, [(ROWS, 4 * CR)], [VMEM] * 2, 8 * 10**9, 10**6, mib=16
-    )(src, cells)
-
-    to_home, sent_up, sent_down = call(
+    (sect,) = call(
+        section_body, [gas_shape], [SMEM, SMEM, SMEM] + [VMEM] * 4, 2 * 10**9, 4 * 10**6, mib=8
+    )(rad_index, odd, coeffs, fields, first, second, added)
+
+    (to_home,) = call(
         filter_body,
-        [(N_AZ, LINES, 2 * CAZ), (4, MOVEB, BLK), (4, MOVEB, BLK)],
-        [SMEM, SMEM] + [VMEM] * 4, 10**8, 10**6,
+        [(N_AZ, LINES + SHARE, 2 * CAZ)],
+        [SMEM, SMEM] + [VMEM] * 2 + [ANY], 10**8, 10**6,
         [
             pltpu.VMEM((2 * BAND, NAZ), F32),
             pltpu.VMEM((2 * BAND, NAZ), F32),
             pltpu.VMEM((N_AZ, LINES, 2 * CAZ), F32),
         ],
         mib=6,
-    )(az_index, widths, jnp.asarray(basis_rows()), lines, sent_up, sent_down)
+    )(az_index, widths, jnp.asarray(basis_rows()), lines, sect)
     filtered = lax.all_to_all(to_home, "az", 0, 0, tiled=True)
-    from_below = lax.ppermute(sent_up, "ax", up)
-    from_above = lax.ppermute(sent_down, "ax", down)
 
     (sect,) = call(
-        section_body, [(FIELDS, CAX, CAZ, CR)], [SMEM, SMEM, SMEM] + [VMEM] * 7, 4 * 10**9, 4 * 10**6, mib=8
-    )(rad_index, odd, coeffs, fields, first, second, az_prev, az_next, rad_got, added)
+        second_half_body, [gas_shape], [SMEM, SMEM] + [VMEM] * 4, 4 * 10**9, 4 * 10**6,
+        [pltpu.VMEM((ROWS, 4 * CR), F32)],
+        mib=16,
+    )(rad_index, coeffs, sect, src, cells, rad_got)
 
     gas_out, parcels_out = call(
         merge_body,
-        [(FIELDS, CAX, CAZ, CR), (4, BLK_DEV + 2 * MOVEB, BLK)],
-        [SMEM] + [VMEM] * 5, 10**6, 4 * 10**6,
-        [pltpu.VMEM((CR, CR), F32)],
+        [gas_shape, (4, BLK_DEV + 2 * MOVEB, BLK)],
+        [SMEM, SMEM, SMEM] + [VMEM] * 5, 10**6, 4 * 10**6,
+        [pltpu.VMEM((CR, CR), F32), pltpu.VMEM((2 * FIELDS * CAX, CR), F32)],
         mib=8,
-    )(rad_index, sect, filtered, stay, from_below, from_above)
+    )(rad_index, odd, coeffs, sect, filtered, stay, first, second)
     return gas_out, parcels_out.reshape(4, BLK_DEV + 2 * MOVEB, 1, BLK)
 
 

time: 63.6 us -> 66.8 us (1.050)
  waiting for transfers between devices: 4.92 us -> 21.4 us
  starting transfers between devices: 32.4 us -> 18.1 us
  Pallas kernels: 19.4 us -> 22.2 us
  local copies, waits for them, and re-layouts: 4.35 us -> 3.13 us
    ppermute x4 -> x0, starting transfers between devices: 11.6 us -> none  [the longest x1 3.95 us: shards(): az_prev = lax.ppermute(az_hi, 'az', ahead)]
    all_to_all x1, waiting for transfers between devices: 1.13 us -> 11.7 us  [shards(): lines = lax.all_to_all(to_owner, 'az', 0, 0, tiled=True)]
    all_to_all x1, waiting for transfers between devices: 3.77 us -> 9.68 us  [shards(): filtered = lax.all_to_all(to_home, 'az', 0, 0, tiled=True)]
    pallas_call x7, Pallas kernels: 19.4 us -> 22.2 us  [the longest x1 7.18 us: shards(): call(parcels_body, [(4, BLK_DEV, BLK), (4, BLK_DEV, BLK)] + [(FIELDS + 1,...]
    all_to_all x1, starting transfers between devices: 6.47 us -> 3.71 us  [shards(): filtered = lax.all_to_all(to_home, 'az', 0, 0, tiled=True)]
    unnamed x20, local copies, waits for them, and re-layouts: 4.35 us -> 3.13 us
  transfers between devices with their start and end apart: 9 -> 5, of which waited for: 2 -> 2; matrix products, arithmetic and copies ran while one was open for 0% -> 0% of each run, Pallas kernels for 25% -> 16%
where the time goes in v3:
time: 66.8 us; the launch traced here: 66.3 us
  Pallas kernels  22.2 us (33%)
  waiting for transfers between devices  21.4 us (32%)
  starting transfers between devices  18.1 us (27%)
  local copies, waits for them, and re-layouts  3.13 us (5%)
  between operations  1.45 us (2%)
    all_to_all x1, waiting for transfers between devices, shards(): lines = lax.all_to_all(to_owner, 'az', 0, 0, tiled=True)  11.7 us
    all_to_all x1, waiting for transfers between devices, shards(): filtered = lax.all_to_all(to_home, 'az', 0, 0, tiled=True)  9.68 us
    all_to_all x1, starting transfers between devices, shards(): lines = lax.all_to_all(to_owner, 'az', 0, 0, tiled=True)  9.44 us
    pallas_call x1, Pallas kernels, shards(): call(parcels_body, [(4, BLK_DEV, BLK), (4, BLK_DEV, BLK)] + [(FIELDS + 1,...  7.18 us
    ppermute x1, starting transfers between devices, shards(): second = lax.ppermute(second, 'ax', outer)  4.18 us
    all_to_all x1, starting transfers between devices, shards(): filtered = lax.all_to_all(to_home, 'az', 0, 0, tiled=True)  3.71 us
    pallas_call x1, Pallas kernels, shards(): call(first_half_body, [(ROWS, 4 * CR), (4 * CYCLES, ROWS)], [VMEM] * 2, 4...  3.68 us
    unnamed x20, local copies, waits for them, and re-layouts  3.13 us
  transfers between devices with their start and end apart: 5, of which 2 were waited for; matrix products, arithmetic and copies ran while one was open for 0% of the time, Pallas kernels for 16%

profile of v3, /device:TPU:8, one launch (start us, length us, event | category | flops | bytes accessed | tf_op | source)
XLA Modules:
  0.0 66.3 jit_solution(9059655036527362505)
XLA Ops:
  1.3 0.0 copy-start.5
  1.3 7.2 %shard_map.95 = (f32[4,32,128]{2,1,0:T(8,128)}, f32[4,32,128]{2,1,0:T(8,128)}, f32[6,64,128]{2,1,0:T(8,128)}, f32[6,64,128]{2,1,0:T(8,128)}) custom-call(s32[1]{0:T(128)} %bitcast.1.odd_ref, s32[1]{0:T(128)} %bitcast.10.count_ref, s32[32]{0:T(128)} %bitcast.16, f32[5,8,64,128]{3,2,1,0:T(8,128)} %q_ref.3, f32[4,32,128]{2,1,0:T(8,128)} %bitcast.15, ...), custom_call_target="tpu_custom_call" | custom-call | flops 6000000000 | bytes 2000000 | tf_op jit(solution)/shard_map/pallas_call | solution.py:453
  8.5 0.1 collective-permute-start
  8.6 4.2 %collective-permute-start.1 = (f32[6,64,128]{2,1,0:T(8,128)}, f32[6,64,128]{2,1,0:T(8,128)S(1)}, u32[]{:S(2)}, u32[]{:S(2)}) collective-permute-start(f32[6,64,128]{2,1,0:T(8,128)} %get-tuple-element.13), channel_id=1, source_target_pairs={{2,4},{4,2},{6,8},{8,6},{10,12},{12,10},{3,5},{5,3},{7,9},{9,7},{1... | collective-permute-start | bytes 589832 | tf_op jit(solution)/shard_map/ppermute | solution.py:468
  12.8 0.0 copy-done.5
  12.8 0.0 copy-start.8
  12.8 0.8 %copy-done.8 = f32[4,32,128]{2,1,0:T(8,128)S(1)} copy-done((f32[4,32,128]{2,1,0:T(8,128)S(1)}, f32[4,32,128]{2,1,0:T(8,128)}, u32[]{:S(2)}) %copy-start.8) | copy-done | bytes 65560
  13.6 0.0 copy-start
  13.6 0.0 copy-start.3
  13.6 3.7 %shard_map.96 = (f32[512,512]{1,0:T(8,128)S(1)}, f32[64,512]{1,0:T(8,128)S(1)}) custom-call(f32[4,32,128]{2,1,0:T(8,128)S(1)} %copy-done.8, s32[32,128]{1,0:T(8,128)S(1)} %bitcast.12), custom_call_target="tpu_custom_call" | custom-call | flops 4000000000 | bytes 1000000 | tf_op jit(solution)/shard_map/pallas_call | solution.py:470
  17.3 0.0 copy-start.6
  17.3 0.0 collective-permute-done.first_ref
  17.3 0.0 collective-permute-done.1.second_ref
  17.4 0.0 copy-done
  17.4 0.0 copy-done.3
  17.4 2.4 %shard_map.98 = (f32[16,29,128]{2,1,0:T(8,128)}, f32[32,128]{1,0:T(8,128)S(1)}) custom-call(s32[1]{0:T(128)} %bitcast.rad_ref, s32[1]{0:T(128)} %bitcast.1.odd_ref, f32[5,6]{1,0:T(8,128)S(1)} %copy-done.3, f32[5,8,64,128]{3,2,1,0:T(8,128)S(1)} %copy-done, f32[6,64,128]{2,1,0:T(8,128)S(1)} %collective-permute-done.first_ref, ...), custom_call_target="tpu_custom_call" | custom-call | flops 10000000 | bytes 4000000 | tf_op jit(solution)/shard_map/pallas_call | solution.py:474
  19.8 9.4 %all-to-all-start = ((f32[16,29,128]{2,1,0:T(8,128)}), f32[16,29,128]{2,1,0:T(8,128)S(1)}, u32[]{:S(2)}, u32[]{:S(2)}) async-start(f32[16,29,128]{2,1,0:T(8,128)} %get-tuple-element.18), calls=%async_computation | async-start | bytes 524288 | tf_op jit(solution)/shard_map/all_to_all | solution.py:481
  29.3 0.7 %collective-permute-start.2 = (f32[32,128]{1,0:T(8,128)S(1)}, f32[32,128]{1,0:T(8,128)S(1)}, u32[]{:S(2)}, u32[]{:S(2)}) collective-permute-start(f32[32,128]{1,0:T(8,128)S(1)} %get-tuple-element.17), channel_id=1, source_target_pairs={{0,1},{1,0},{2,3},{3,2},{4,5},{5,4},{6,7},{7,6},{8,9},{9,8},{10,11... | collective-permute-start | bytes 49160 | tf_op jit(solution)/shard_map/ppermute | solution.py:482
  29.9 0.0 copy-done.6
  29.9 0.0 copy-start.7
  29.9 1.2 %copy-done.7 = f32[512,512]{1,0:T(8,128)S(1)} copy-done((f32[512,512]{1,0:T(8,128)S(1)}, f32[512,512]{1,0:T(8,128)}, u32[]{:S(2)}) %copy-start.7) | copy-done | bytes 1048600
  31.2 0.0 copy-start.4
  31.2 1.5 %shard_map.97.sect_ref._ = f32[5,8,64,128]{3,2,1,0:T(8,128)S(1)} custom-call(s32[1]{0:T(128)} %bitcast.rad_ref, s32[1]{0:T(128)} %bitcast.1.odd_ref, f32[5,6]{1,0:T(8,128)S(1)} %copy-done.3, f32[5,8,64,128]{3,2,1,0:T(8,128)S(1)} %copy-done, f32[6,64,128]{2,1,0:T(8,128)S(1)} %collective-permute-done.first_ref, ...), custom_call_target="tpu_custom_call" | custom-call | flops 2000000000 | bytes 4000000 | tf_op jit(solution)/shard_map/pallas_call | solution.py:484
  32.7 11.7 %all-to-all-done.got_ref = f32[16,29,128]{2,1,0:T(8,128)S(1)} async-done(((f32[16,29,128]{2,1,0:T(8,128)}), f32[16,29,128]{2,1,0:T(8,128)S(1)}, u32[]{:S(2)}, u32[]{:S(2)}) %all-to-all-start) | async-done | bytes 237600 | tf_op jit(solution)/shard_map/all_to_all | solution.py:481
  44.4 0.0 copy-done.4
  44.4 0.0 copy-start.1
  44.4 1.0 %copy-done.1 = bf16[256,1024]{1,0:T(8,128)(2,1)S(1)} copy-done((bf16[256,1024]{1,0:T(8,128)(2,1)S(1)}, bf16[256,1024]{1,0:T(8,128)(2,1)}, u32[]{:S(2)}) %copy-start.1) | copy-done | bytes 524312
  45.4 0.0 copy-start.9
  45.4 2.3 %shard_map.100 = f32[16,25,128]{2,1,0:T(8,128)} custom-call(s32[1]{0:T(128)} %bitcast.6.az_ref, s32[16]{0:T(128)S(1)} %copy-done.4, bf16[256,1024]{1,0:T(8,128)(2,1)S(1)} %copy-done.1, f32[16,29,128]{2,1,0:T(8,128)S(1)} %all-to-all-done.got_ref, f32[5,8,64,128]{3,2,1,0:T(8,128)S(1)} %shard_map.97.sect_ref._), custom_call_target="tpu_custom_call" | custom-call | flops 100000000 | bytes 1000000 | tf_op jit(solution)/shard_map/pallas_call | solution.py:488
  47.7 3.7 %all-to-all-start.1 = ((f32[16,25,128]{2,1,0:T(8,128)}), f32[16,25,128]{2,1,0:T(8,128)S(1)}, u32[]{:S(2)}, u32[]{:S(2)}) async-start(f32[16,25,128]{2,1,0:T(8,128)} %shard_map.100), calls=%async_computation.1 | async-start | bytes 524288 | tf_op jit(solution)/shard_map/all_to_all | solution.py:499
  51.4 0.0 copy-start.2
  51.4 0.0 collective-permute-done.2.rad_in
  51.4 0.0 copy-done.9
  51.4 3.0 %shard_map.99.sect_ref = f32[5,8,64,128]{3,2,1,0:T(8,128)S(1)} custom-call(s32[1]{0:T(128)} %bitcast.rad_ref, f32[5,6]{1,0:T(8,128)S(1)} %copy-done.3, f32[5,8,64,128]{3,2,1,0:T(8,128)S(1)} %shard_map.97.sect_ref._, f32[4,32,128]{2,1,0:T(8,128)S(1)} %copy-done.9, s32[32,128]{1,0:T(8,128)S(1)} %bitcast.13, f32[32,128]{1,0:T(8,128)S(1)} %collective-permute-done.2.rad_in), custom_call_target="tpu_custom_call" | custom-call | flops 4000000000 | bytes 4000000 | tf_op jit(solution)/shard_map/pallas_call | solution.py:501
  54.4 9.7 %all-to-all-done.1.got_ref = f32[16,25,128]{2,1,0:T(8,128)S(1)} async-done(((f32[16,25,128]{2,1,0:T(8,128)}), f32[16,25,128]{2,1,0:T(8,128)S(1)}, u32[]{:S(2)}, u32[]{:S(2)}) %all-to-all-start.1) | async-done | bytes 204832 | tf_op jit(solution)/shard_map/all_to_all | solution.py:499
  64.1 0.0 copy-done.2
  64.1 2.2 %shard_map.101 = (f32[5,8,64,128]{3,2,1,0:T(8,128)}, f32[4,40,128]{2,1,0:T(8,128)}) custom-call(s32[1]{0:T(128)} %bitcast.rad_ref, s32[1]{0:T(128)} %bitcast.1.odd_ref, f32[5,6]{1,0:T(8,128)S(1)} %copy-done.3, f32[5,8,64,128]{3,2,1,0:T(8,128)S(1)} %shard_map.99.sect_ref, f32[16,25,128]{2,1,0:T(8,128)S(1)} %all-to-all-done.1.got_ref, ...), custom_call_target="tpu_custom_call" | custom-call | flops 1000000 | bytes 4000000 | tf_op jit(solution)/shard_map/pallas_call | solution.py:507
Async XLA Ops:
  1.3 11.5 %copy-start.5 = (s32[32,1,128]{2,1,0:T(1,128)S(1)}, s32[32,1,128]{2,1,0:T(1,128)}, u32[]{:S(2)}) copy-start(s32[32,1,128]{2,1,0:T(1,128)} %param.11) | copy-start | bytes 49156
  8.5 8.8 %collective-permute-start = (f32[6,64,128]{2,1,0:T(8,128)}, f32[6,64,128]{2,1,0:T(8,128)S(1)}, u32[]{:S(2)}, u32[]{:S(2)}) collective-permute-start(f32[6,64,128]{2,1,0:T(8,128)} %get-tuple-element.12), channel_id=1, source_target_pairs={{0,2},{2,0},{4,6},{6,4},{8,10},{10,8},{12,14},{14,12},{1,3},{3,1},... | collective-permute-start | bytes 589832 | tf_op jit(solution)/shard_map/ppermute | solution.py:467
  8.6 8.8 %collective-permute-start.1 = (f32[6,64,128]{2,1,0:T(8,128)}, f32[6,64,128]{2,1,0:T(8,128)S(1)}, u32[]{:S(2)}, u32[]{:S(2)}) collective-permute-start(f32[6,64,128]{2,1,0:T(8,128)} %get-tuple-element.13), channel_id=1, source_target_pairs={{2,4},{4,2},{6,8},{8,6},{10,12},{12,10},{3,5},{5,3},{7,9},{9,7},{1... | collective-permute-start | bytes 589832 | tf_op jit(solution)/shard_map/ppermute | solution.py:468
  12.8 0.8 %copy-start.8 = (f32[4,32,128]{2,1,0:T(8,128)S(1)}, f32[4,32,128]{2,1,0:T(8,128)}, u32[]{:S(2)}) copy-start(f32[4,32,128]{2,1,0:T(8,128)} %get-tuple-element.14.src_ref) | copy-start | bytes 196612
  13.6 3.7 %copy-start = (f32[5,8,64,128]{3,2,1,0:T(8,128)S(1)}, f32[5,8,64,128]{3,2,1,0:T(8,128)}, u32[]{:S(2)}) copy-start(f32[5,8,64,128]{3,2,1,0:T(8,128)} %q_ref.3) | copy-start | bytes 3932164
  13.6 3.7 %copy-start.3 = (f32[5,6]{1,0:T(8,128)S(1)}, f32[5,6]{1,0:T(8,128)}, u32[]{:S(2)}) copy-start(f32[5,6]{1,0:T(8,128)} %coef_ref.7) | copy-start | bytes 364
  17.3 12.6 %copy-start.6 = (f32[512,512]{1,0:T(8,128)}, f32[512,512]{1,0:T(8,128)S(1)}, u32[]{:S(2)}) copy-start(f32[512,512]{1,0:T(8,128)S(1)} %get-tuple-element.15.acc_ref) | copy-start | bytes 3145732
  19.8 24.6 %all-to-all-start = ((f32[16,29,128]{2,1,0:T(8,128)}), f32[16,29,128]{2,1,0:T(8,128)S(1)}, u32[]{:S(2)}, u32[]{:S(2)}) async-start(f32[16,29,128]{2,1,0:T(8,128)} %get-tuple-element.18), calls=%async_computation | async-start | bytes 524288 | tf_op jit(solution)/shard_map/all_to_all | solution.py:481
  29.3 22.2 %collective-permute-start.2 = (f32[32,128]{1,0:T(8,128)S(1)}, f32[32,128]{1,0:T(8,128)S(1)}, u32[]{:S(2)}, u32[]{:S(2)}) collective-permute-start(f32[32,128]{1,0:T(8,128)S(1)} %get-tuple-element.17), channel_id=1, source_target_pairs={{0,1},{1,0},{2,3},{3,2},{4,5},{5,4},{6,7},{7,6},{8,9},{9,8},{10,11... | collective-permute-start | bytes 49160 | tf_op jit(solution)/shard_map/ppermute | solution.py:482
  29.9 1.2 %copy-start.7 = (f32[512,512]{1,0:T(8,128)S(1)}, f32[512,512]{1,0:T(8,128)}, u32[]{:S(2)}) copy-start(f32[512,512]{1,0:T(8,128)} %copy-done.6) | copy-start | bytes 3145732
  31.2 13.2 %copy-start.4 = (s32[16]{0:T(128)S(1)}, s32[16]{0:T(128)}, u32[]{:S(2)}) copy-start(s32[16]{0:T(128)} %width_ref.1) | copy-start | bytes 196
  44.4 1.0 %copy-start.1 = (bf16[256,1024]{1,0:T(8,128)(2,1)S(1)}, bf16[256,1024]{1,0:T(8,128)(2,1)}, u32[]{:S(2)}) copy-start(bf16[256,1024]{1,0:T(8,128)(2,1)} %constant.28.clone.basis_ref) | copy-start | bytes 1572868
  45.4 6.0 %copy-start.9 = (f32[4,32,128]{2,1,0:T(8,128)S(1)}, f32[4,32,128]{2,1,0:T(8,128)}, u32[]{:S(2)}) copy-start(f32[4,32,128]{2,1,0:T(8,128)} %get-tuple-element.14.src_ref) | copy-start | bytes 196612
  47.7 16.4 %all-to-all-start.1 = ((f32[16,25,128]{2,1,0:T(8,128)}), f32[16,25,128]{2,1,0:T(8,128)S(1)}, u32[]{:S(2)}, u32[]{:S(2)}) async-start(f32[16,25,128]{2,1,0:T(8,128)} %shard_map.100), calls=%async_computation.1 | async-start | bytes 524288 | tf_op jit(solution)/shard_map/all_to_all | solution.py:499
  51.4 12.7 %copy-start.2 = (f32[4,32,128]{2,1,0:T(8,128)S(1)}, f32[4,32,128]{2,1,0:T(8,128)}, u32[]{:S(2)}) copy-start(f32[4,32,128]{2,1,0:T(8,128)} %get-tuple-element.19.stay_ref) | copy-start | bytes 196612

commit v4 on v3

--- a/solution.py
+++ b/solution.py
@@ -71,6 +71,18 @@
     )
 
 
+def edges_body(odd_ref, q_hbm, first_out, second_out, sems):
+    odd, last = odd_ref[0], CAX - 1
+    copies = [
+        pltpu.make_async_copy(q_hbm.at[:, last * (1 - odd)], first_out, sems.at[0]),
+        pltpu.make_async_copy(q_hbm.at[:, last * odd], second_out, sems.at[1]),
+    ]
+    for copy in copies:
+        copy.start()
+    for copy in copies:
+        copy.wait()
+
+
 def one_hot_rows(cells_ref, first, blocks):
     cells = jnp.concatenate([cells_ref[first + i : first + i + 1, :] for i in range(blocks)], axis=1)
     width = blocks * BLK
@@ -78,43 +90,11 @@
     return jnp.where(hit, 1.0, 0.0).astype(BF16), cells & (CR - 1)
 
 
-def parcels_body(
-    odd_ref, count_ref, move_ref, q_hbm, parcel_ref, cells_ref,
-    src_out, stay_out, first_out, second_out,
-    q_ref, hot_ref, gas_ref, state_ref, leave_ref, sems,
-):
-    odd = odd_ref[0]
-    last = CAX - 1
-    copies = [
-        pltpu.make_async_copy(q_hbm.at[pl.ds(1, 3)], q_ref, sems.at[0]),
-        pltpu.make_async_copy(
-            q_hbm.at[:, last * (1 - odd)], first_out.at[pl.ds(0, FIELDS)], sems.at[1]
-        ),
-        pltpu.make_async_copy(q_hbm.at[:, last * odd], second_out.at[pl.ds(0, FIELDS)], sems.at[2]),
-    ]
-    for copy in copies:
-        copy.start()
-    for first in range(0, BLK_DEV, 4):
-        hot_ref[:, first * BLK : (first + 4) * BLK] = one_hot_rows(cells_ref, first, 4)[0]
-    copies[0].wait()
-    parts = [[], []]
-    for f in range(3):
-        table = q_ref[f].reshape(ROWS, CR).T
-        high, low = halves(table)
-        parts[0].append(high)
-        parts[1].append(low)
-    parts = [jnp.concatenate(part, axis=0) for part in parts]
-    for first in range(0, BLK_DEV, 4):
-        width = 4 * BLK
-        hot = hot_ref[:, first * BLK : first * BLK + width]
-        lanes = jnp.concatenate([cells_ref[first + i : first + i + 1, :] for i in range(4)], axis=1)
-        lanes = lanes & (CR - 1)
-        rows = sum(jnp.dot(part, hot, preferred_element_type=F32) for part in parts)
-        mask = iota((CR, width), 0) == lanes
-        for f in range(3):
-            found = jnp.sum(jnp.where(mask, rows[f * CR : (f + 1) * CR], 0.0), axis=0, keepdims=True)
-            for i in range(4):
-                gas_ref[f, first + i : first + i + 1, :] = found[:, i * BLK : (i + 1) * BLK]
+def lane_row(cells_ref, first, blocks):
+    return jnp.concatenate([cells_ref[first + i : first + i + 1, :] for i in range(blocks)], axis=1) & (CR - 1)
+
+
+def step(count_ref, parcel_ref, gas_ref):
     slot = iota((BLK_DEV, BLK), 0) * BLK + iota((BLK_DEV, BLK), 1)
     alive = slot < count_ref[0]
     diam = parcel_ref[3]
@@ -127,10 +107,36 @@
     sources = [(diam - new_diam) * COUPLING] + [
         -(diam * (v - u)) * COUPLING for v, u in zip(new_vel, vel)
     ]
-    sources = [jnp.where(alive, s, 0.0) for s in sources]
+    state = [jnp.where(alive, s, 0.0) for s in new_vel + [new_diam]]
+    return state, [jnp.where(alive, s, 0.0) for s in sources]
+
+
+def pick(rows, first, spans, mask, gas_ref):
+    for f, (start, stop) in enumerate(spans):
+        found = jnp.sum(jnp.where(mask, rows[start:stop], 0.0), axis=0, keepdims=True)
+        for i in range(4):
+            gas_ref[f, first + i : first + i + 1, :] = found[:, i * BLK : (i + 1) * BLK]
+
+
+def parcels_body(
+    odd_ref, count_ref, move_ref, q_ref, parcel_ref, cells_ref,
+    src_out, stay_out, first_out, second_out, gas_ref, state_ref, leave_ref,
+):
+    parts = [[], []]
+    for f in range(3):
+        high, low = halves(q_ref[f + 1].reshape(ROWS, CR).T)
+        parts[0].append(high)
+        parts[1].append(low)
+    parts = [jnp.concatenate(part, axis=0) for part in parts]
+    spans = [(f * CR, (f + 1) * CR) for f in range(3)]
+    for first in range(0, BLK_DEV, 4):
+        hot, lanes = one_hot_rows(cells_ref, first, 4)
+        rows = sum(jnp.dot(part, hot, preferred_element_type=F32) for part in parts)
+        pick(rows, first, spans, iota((CR, 4 * BLK), 0) == lanes, gas_ref)
+    state, sources = step(count_ref, parcel_ref, gas_ref)
     for i in range(4):
         src_out[i] = sources[i]
-        state_ref[i] = jnp.where(alive, (new_vel + [new_diam])[i], 0.0)
+        state_ref[i] = state[i]
     leave_ref[...] = jnp.zeros_like(leave_ref)
 
     def place(block, ranks):
@@ -150,12 +156,10 @@
         return up + (move == 1).astype(jnp.int32), down + (move == -1).astype(jnp.int32)
 
     lax.fori_loop(0, BLK_DEV, place, (jnp.int32(0), jnp.int32(0)))
-    for out, flag in ((first_out, 0), (second_out, 1)):
-        out[FIELDS] = jnp.zeros((CAZ, CR), F32)
-        for i in range(4):
-            out[FIELDS, 4 * i : 4 * i + 4, :] = jnp.where(odd == flag, leave_ref[0, i], leave_ref[1, i])
-    copies[1].wait()
-    copies[2].wait()
+    odd = odd_ref[0] == 1
+    up, down = leave_ref[0], leave_ref[1]
+    first_out[...] = jnp.where(odd, down, up)
+    second_out[...] = jnp.where(odd, up, down)
 
 
 SOURCE_OF = (0, 1, 2, 3, 0)
@@ -165,27 +169,50 @@
 SHARE = 2 * FIELDS * CAX // N_AZ
 
 
+def turned(parts):
+    lane = iota((2 * CAZ, CR), 1)
+    packed = jnp.zeros((2 * CAZ, CR), F32)
+    for f, part in enumerate(parts):
+        moved = pltpu.roll(part, f * BAND, 1) if f else part
+        packed = jnp.where((lane >= f * BAND) & (lane < (f + 1) * BAND), moved, packed)
+    return packed.T
+
+
+def near_parcels_body(count_ref, q_ref, parcel_ref, cells_ref, tiles_out, near_out, gas_ref, hot_ref, spread_ref):
+    for p in range(PAIRS):
+        tiles_out[:, p * 2 * CAZ : (p + 1) * 2 * CAZ] = turned(
+            [q_ref[f, 2 * p : 2 * p + 2].reshape(2 * CAZ, CR) for f in range(FIELDS)]
+        )
+    start = 16
+    high, low = halves(tiles_out[start : 4 * BAND])
+    spans = [((f + 1) * BAND - start, (f + 1) * BAND - start + CYCLES) for f in range(3)]
+    for first in range(0, BLK_DEV, 4):
+        hot, lanes = one_hot_rows(cells_ref, first, 4)
+        hot_ref[:, first * BLK : (first + 4) * BLK] = hot
+        rows = jnp.dot(high, hot, preferred_element_type=F32) + jnp.dot(low, hot, preferred_element_type=F32)
+        pick(rows, first, spans, iota((CYCLES, 4 * BLK), 0) == lanes, gas_ref)
+    _, sources = step(count_ref, parcel_ref, gas_ref)
+    rows = [s.astype(BF16).astype(F32) for s in sources]
+    rows = rows + [s - r for s, r in zip(sources, rows)]
+    for block in range(BLK_DEV):
+        mask = iota((CYCLES, BLK), 0) == (cells_ref[block : block + 1, :] & (CR - 1))
+        for i, row in enumerate(rows):
+            spread_ref[i * CYCLES : (i + 1) * CYCLES, block * BLK : (block + 1) * BLK] = jnp.where(
+                mask, row[block : block + 1, :], 0.0
+            ).astype(BF16)
+    total = lax.dot_general(spread_ref[...], hot_ref[...], NT, preferred_element_type=F32)
+    near_out[...] = total[: 4 * CYCLES] + total[4 * CYCLES :]
+
+
 def near_body(
-    rad_ref, odd_ref, coef_ref, q_ref, first_ref, second_ref, near_ref,
+    rad_ref, odd_ref, coef_ref, q_ref, first_ref, second_ref, tiles_ref, near_ref,
     send_out, rad_out, az_ref,
 ):
     lane = iota((CR, 2 * CAZ), 1)
-    row = iota((CR, 2 * CAZ), 0)
     z = lane % CAZ
-
-    def turned(parts):
-        packed = jnp.zeros((2 * CAZ, CR), F32)
-        for f, part in enumerate(parts):
-            moved = pltpu.roll(part, f * BAND, 1) if f else part
-            packed = jnp.where((lane >= f * BAND) & (lane < (f + 1) * BAND), moved, packed)
-        return packed.T
-
-    tiles = [
-        turned([q_ref[f, 2 * p : 2 * p + 2].reshape(2 * CAZ, CR) for f in range(FIELDS)])
-        for p in range(PAIRS)
-    ]
+    tiles = [tiles_ref[:, p * 2 * CAZ : (p + 1) * 2 * CAZ] for p in range(PAIRS)]
     odd = odd_ref[0] == 1
-    first, second = first_ref[0:FIELDS], second_ref[0:FIELDS]
+    first, second = first_ref[...], second_ref[...]
     before, after = jnp.where(odd, first, second), jnp.where(odd, second, first)
     halo = turned([jnp.concatenate([before[f], after[f]], axis=0) for f in range(FIELDS)])
 
@@ -250,55 +277,33 @@
     rad_out[...] = packed
 
 
-def scattered(src_ref, cells_ref, acc_ref, start, stop, near_ref=None):
-    step = 8
-    for first in range(0 if near_ref is not None else start, BLK_DEV if near_ref is not None else stop, step):
-        hot, lanes = one_hot_rows(cells_ref, first, step)
-        rows = [[], []]
+def gas_body(
+    rad_ref, odd_ref, coef_ref, q_ref, first_ref, second_ref, rad_in, src_ref, cells_ref, _, sect_out, acc_ref
+):
+    width = 8
+    for first in range(0, BLK_DEV, width):
+        hot, lanes = one_hot_rows(cells_ref, first, width)
+        mask = iota((CR, width * BLK), 0) == lanes
+        spread = [[], []]
         for i in range(4):
-            row = jnp.concatenate([src_ref[i, first + j : first + j + 1, :] for j in range(step)], axis=1)
+            row = jnp.concatenate([src_ref[i, first + j : first + j + 1, :] for j in range(width)], axis=1)
             high = row.astype(BF16).astype(F32)
-            rows[0].append(high)
-            rows[1].append(row - high)
-        if near_ref is not None:
-            mask = iota((CYCLES, step * BLK), 0) == lanes
-            spread = jnp.concatenate(
-                [jnp.where(mask, row, 0.0).astype(BF16) for row in rows[0] + rows[1]], axis=0
-            )
-            total = lax.dot_general(spread, hot, NT, preferred_element_type=F32)
-            total = total[: 4 * CYCLES] + total[4 * CYCLES :]
-            if first == 0:
-                near_ref[...] = total
-            else:
-                near_ref[...] += total
-        if not start <= first < stop:
-            continue
-        mask = iota((CR, step * BLK), 0) == lanes
+            spread[0].append(jnp.where(mask, high, 0.0).astype(BF16))
+            spread[1].append(jnp.where(mask, row - high, 0.0).astype(BF16))
         total = sum(
-            lax.dot_general(
-                hot,
-                jnp.concatenate([jnp.where(mask, row, 0.0).astype(BF16) for row in part], axis=0),
-                NT,
-                preferred_element_type=F32,
-            )
-            for part in rows
+            lax.dot_general(hot, jnp.concatenate(part, axis=0), NT, preferred_element_type=F32)
+            for part in spread
         )
-        if first == start:
+        if first == 0:
             acc_ref[...] = total
         else:
             acc_ref[...] += total
-
-
-def first_half_body(src_ref, cells_ref, acc_out, near_out):
-    scattered(src_ref, cells_ref, acc_out, 0, BLK_DEV // 2, near_out)
-
-
-def section_body(rad_ref, odd_ref, coef_ref, q_ref, first_ref, second_ref, acc_ref, sect_out):
     rad = rad_ref[0]
     odd = odd_ref[0] == 1
     row = iota((CAZ, CR), 0)
     lane = iota((1, CR), 1)
     metric = 4.0 / ((rad * CR + lane).astype(F32) + 4.0)
+    target = jnp.where(rad == 0, CR - 1, 0)
     for f in range(FIELDS):
         c = [coef_ref[f, i] for i in range(6)]
         mid = (1.0 - c[1] - c[5]) - c[3] * metric
@@ -307,35 +312,24 @@
         ax_up, ax_down = 0.5 * (c[0] + c[1]), 0.5 * (c[1] - c[0])
         rad_up = jnp.where(lane == CR - 1, 0.0, 0.5 * (c[4] + c[5]))
         rad_down = jnp.where(lane == 0, 0.0, 0.5 * (c[5] - c[4]))
+        across = 0.5 * jnp.where(rad == 0, c[4] + c[5], c[5] - c[4])
+        across = jnp.where(lane == target, across, 0.0)
         s = SOURCE_OF[f] * CR
         for a in range(CAX):
             q = q_ref[f, a]
             ahead = q_ref[f, a + 1] if a + 1 < CAX else jnp.where(odd, second_ref[f], first_ref[f])
             behind = q_ref[f, a - 1] if a else jnp.where(odd, first_ref[f], second_ref[f])
+            edge = jnp.concatenate(
+                [pltpu.roll(rad_in[...], (target + (2 * CR - ((2 * a + h) * 8 + f))) % CR, 1) for h in range(2)],
+                axis=0,
+            )
             sect_out[f, a] = (
                 mid * q + ax_up * ahead + ax_down * behind
                 + az_up * pltpu.roll(q, CAZ - 1, 0) + az_down * pltpu.roll(q, 1, 0)
                 + rad_up * pltpu.roll(q, CR - 1, 1) + rad_down * pltpu.roll(q, 1, 1)
+                + across * edge
                 + acc_ref[a * CAZ : (a + 1) * CAZ, s : s + CR]
             )
-
-
-def second_half_body(rad_ref, coef_ref, sect_ref, src_ref, cells_ref, rad_in, sect_out, acc_ref):
-    scattered(src_ref, cells_ref, acc_ref, BLK_DEV // 2, BLK_DEV)
-    rad = rad_ref[0]
-    lane = iota((CAZ, CR), 1)
-    target = jnp.where(rad == 0, CR - 1, 0)
-    for f in range(FIELDS):
-        c4, c5 = coef_ref[f, 4], coef_ref[f, 5]
-        weight = 0.5 * jnp.where(rad == 0, c4 + c5, c5 - c4)
-        weight = jnp.where(lane == target, weight, 0.0)
-        s = SOURCE_OF[f] * CR
-        for a in range(CAX):
-            edge = jnp.concatenate(
-                [pltpu.roll(rad_in[...], (target + (2 * CR - ((2 * a + h) * 8 + f))) % CR, 1) for h in range(2)],
-                axis=0,
-            )
-            sect_out[f, a] = sect_ref[f, a] + acc_ref[a * CAZ : (a + 1) * CAZ, s : s + CR] + weight * edge
 
 
 def lined(pieces, line_ref):
@@ -348,8 +342,11 @@
 
 
 def filter_body(
-    az_ref, width_ref, basis_ref, got_ref, _, send_out, line_ref, ends_ref, piece_ref
+    az_ref, width_ref, basis_ref, got_ref, first_ref, second_ref,
+    send_out, first_out, second_out, line_ref, ends_ref, piece_ref,
 ):
+    first_out[...] = first_ref[...]
+    second_out[...] = second_ref[...]
     for home in range(N_AZ):
         send_out[home, LINES:, :] = jnp.where(
             az_ref[0] < N_AZ // 2,
@@ -430,10 +427,9 @@
             gas_out[f, a, CAZ - 1 : CAZ] += after[a : a + 1]
     odd = odd_ref[0] == 1
     parcels_out[:, 0:BLK_DEV, :] = stay_ref[...]
-    for i in range(4):
-        first, second = first_ref[FIELDS, 4 * i : 4 * i + 4, :], second_ref[FIELDS, 4 * i : 4 * i + 4, :]
-        parcels_out[i, BLK_DEV : BLK_DEV + MOVEB, :] = jnp.where(odd, first, second)
-        parcels_out[i, BLK_DEV + MOVEB :, :] = jnp.where(odd, second, first)
+    first, second = first_ref[...], second_ref[...]
+    parcels_out[:, BLK_DEV : BLK_DEV + MOVEB, :] = jnp.where(odd, first, second)
+    parcels_out[:, BLK_DEV + MOVEB :, :] = jnp.where(odd, second, first)
 
 
 def shards(fields, coeffs, parcels, cells, counts, moves, widths):
@@ -450,59 +446,67 @@
     across = [(i, i ^ 1) for i in range(n_rad)]
     gas_shape = (FIELDS, CAX, CAZ, CR)
 
-    src, stay, first, second = call(
+    first, second = call(
+        edges_body, [(FIELDS, CAZ, CR)] * 2, [SMEM, HBM], 10**6, 10**6,
+        [pltpu.SemaphoreType.DMA((2,))], mib=62,
+    )(odd, fields)
+    first = lax.ppermute(first, "ax", inner)
+    second = lax.ppermute(second, "ax", outer)
+
+    tiles, near = call(
+        near_parcels_body,
+        [(CR, ROWS), (4 * CYCLES, ROWS)],
+        [SMEM] + [VMEM] * 3, 3 * 10**9, 2 * 10**6,
+        [
+            pltpu.VMEM((3, BLK_DEV, BLK), F32),
+            pltpu.VMEM((ROWS, PARCELS), BF16),
+            pltpu.VMEM((8 * CYCLES, PARCELS), BF16),
+        ],
+        mib=16,
+    )(counts, fields, parcels, cells)
+
+    to_owner, rad_edge = call(
+        near_body,
+        [(N_AZ, LINES + 4 + SHARE, 2 * CAZ), (32, CR)],
+        [SMEM, SMEM, SMEM] + [VMEM] * 5, 10**7, 4 * 10**6,
+        [pltpu.VMEM((2 * FIELDS * CAX, CR), F32)],
+        mib=8,
+    )(rad_index, odd, coeffs, fields, first, second, tiles, near)
+    lines = lax.all_to_all(to_owner, "az", 0, 0, tiled=True)
+    rad_got = lax.ppermute(rad_edge, "rad", across)
+
+    src, stay, first_moved, second_moved = call(
         parcels_body,
-        [(4, BLK_DEV, BLK), (4, BLK_DEV, BLK)] + [(FIELDS + 1, CAZ, CR)] * 2,
-        [SMEM, SMEM, SMEM, HBM, VMEM, VMEM], 6 * 10**9, 2 * 10**6,
+        [(4, BLK_DEV, BLK), (4, BLK_DEV, BLK), (4, MOVEB, BLK), (4, MOVEB, BLK)],
+        [SMEM, SMEM, SMEM] + [VMEM] * 3 , 6 * 10**9, 2 * 10**6,
         [
-            pltpu.VMEM((3, CAX, CAZ, CR), F32),
-            pltpu.VMEM((ROWS, PARCELS), BF16),
             pltpu.VMEM((3, BLK_DEV, BLK), F32),
             pltpu.VMEM((4, BLK_DEV, BLK), F32),
             pltpu.VMEM((2, 4, MOVEB, BLK), F32),
-            pltpu.SemaphoreType.DMA((3,)),
         ],
-        mib=62,
+        mib=16,
     )(odd, counts, moves, fields, parcels, cells)
-    first = lax.ppermute(first, "ax", inner)
-    second = lax.ppermute(second, "ax", outer)
-
-    added, near = call(
-        first_half_body, [(ROWS, 4 * CR), (4 * CYCLES, ROWS)], [VMEM] * 2, 4 * 10**9, 10**6, mib=16
-    )(src, cells)
-
-    to_owner, rad_edge = call(
-        near_body,
-        [(N_AZ, LINES + 4 + SHARE, 2 * CAZ), (32, CR)],
-        [SMEM, SMEM, SMEM] + [VMEM] * 4, 10**7, 4 * 10**6,
-        [pltpu.VMEM((2 * FIELDS * CAX, CR), F32)],
-        mib=8,
-    )(rad_index, odd, coeffs, fields, first, second, near)
-    lines = lax.all_to_all(to_owner, "az", 0, 0, tiled=True)
-    rad_got = lax.ppermute(rad_edge, "rad", across)
-
-    (sect,) = call(
-        section_body, [gas_shape], [SMEM, SMEM, SMEM] + [VMEM] * 4, 2 * 10**9, 4 * 10**6, mib=8
-    )(rad_index, odd, coeffs, fields, first, second, added)
-
-    (to_home,) = call(
+
+    to_home, first_moved, second_moved = call(
         filter_body,
-        [(N_AZ, LINES + SHARE, 2 * CAZ)],
-        [SMEM, SMEM] + [VMEM] * 2 + [ANY], 10**8, 10**6,
+        [(N_AZ, LINES + SHARE, 2 * CAZ), (4, MOVEB, BLK), (4, MOVEB, BLK)],
+        [SMEM, SMEM] + [VMEM] * 4, 10**8, 10**6,
         [
             pltpu.VMEM((2 * BAND, NAZ), F32),
             pltpu.VMEM((2 * BAND, NAZ), F32),
             pltpu.VMEM((N_AZ, LINES, 2 * CAZ), F32),
         ],
         mib=6,
-    )(az_index, widths, jnp.asarray(basis_rows()), lines, sect)
+    )(az_index, widths, jnp.asarray(basis_rows()), lines, first_moved, second_moved)
     filtered = lax.all_to_all(to_home, "az", 0, 0, tiled=True)
+    first_moved = lax.ppermute(first_moved, "ax", inner)
+    second_moved = lax.ppermute(second_moved, "ax", outer)
 
     (sect,) = call(
-        second_half_body, [gas_shape], [SMEM, SMEM] + [VMEM] * 4, 4 * 10**9, 4 * 10**6,
+        gas_body, [gas_shape], [SMEM, SMEM, SMEM] + [VMEM] * 6 + [ANY], 8 * 10**9, 4 * 10**6,
         [pltpu.VMEM((ROWS, 4 * CR), F32)],
         mib=16,
-    )(rad_index, coeffs, sect, src, cells, rad_got)
+    )(rad_index, odd, coeffs, fields, first, second, rad_got, src, cells, to_home)
 
     gas_out, parcels_out = call(
         merge_body,
@@ -510,7 +514,7 @@
         [SMEM, SMEM, SMEM] + [VMEM] * 5, 10**6, 4 * 10**6,
         [pltpu.VMEM((CR, CR), F32), pltpu.VMEM((2 * FIELDS * CAX, CR), F32)],
         mib=8,
-    )(rad_index, odd, coeffs, sect, filtered, stay, first, second)
+    )(rad_index, odd, coeffs, sect, filtered, stay, first_moved, second_moved)
     return gas_out, parcels_out.reshape(4, BLK_DEV + 2 * MOVEB, 1, BLK)
 
 

time: 66.8 us -> 60.5 us (0.906)
  waiting for transfers between devices: 21.4 us -> 14.8 us
  local copies, waits for them, and re-layouts: 3.13 us -> 0.86 us
  starting transfers between devices: 18.1 us -> 20 us
  Pallas kernels: 22.2 us -> 23 us
    all_to_all x1, waiting for transfers between devices: 9.68 us -> 5.73 us  [shards(): filtered = lax.all_to_all(to_home, 'az', 0, 0, tiled=True)]
    all_to_all x1, waiting for transfers between devices: 11.7 us -> 9.02 us  [shards(): lines = lax.all_to_all(to_owner, 'az', 0, 0, tiled=True)]
    unnamed x20 -> x14, local copies, waits for them, and re-layouts: 3.13 us -> 0.86 us
    ppermute x0 -> x2, starting transfers between devices: none -> 2.19 us  [the longest x1 2.1 us: shards(): second_moved = lax.ppermute(second_moved, 'ax', outer)]
    pallas_call x5, Pallas kernels: 17.6 us -> 18.8 us  [the longest x1 5.52 us: shards(): call(parcels_body, [(4, BLK_DEV, BLK), (4, BLK_DEV, BLK), (4, MOVEB, BLK)...]
  transfers between devices with their start and end apart: 5 -> 7, of which waited for: 2 -> 2; matrix products, arithmetic and copies ran while one was open for 0% -> 0% of each run, Pallas kernels for 16% -> 28%
where the time goes in v4:
time: 60.5 us; the launch traced here: 60 us
  Pallas kernels  23 us (38%)
  starting transfers between devices  20 us (33%)
  waiting for transfers between devices  14.8 us (24%)
  between operations  1.48 us (2%)
  local copies, waits for them, and re-layouts  0.86 us (1%)
    all_to_all x1, starting transfers between devices, shards(): lines = lax.all_to_all(to_owner, 'az', 0, 0, tiled=True)  9.3 us
    all_to_all x1, waiting for transfers between devices, shards(): lines = lax.all_to_all(to_owner, 'az', 0, 0, tiled=True)  9.02 us
    all_to_all x1, waiting for transfers between devices, shards(): filtered = lax.all_to_all(to_home, 'az', 0, 0, tiled=True)  5.73 us
    pallas_call x1, Pallas kernels, shards(): call(parcels_body, [(4, BLK_DEV, BLK), (4, BLK_DEV, BLK), (4, MOVEB, BLK)...  5.52 us
    pallas_call x1, Pallas kernels, shards(): call(gas_body, [gas_shape], [SMEM, SMEM, SMEM] + [VMEM] * 6 + [ANY], 8 *...  5.43 us
    ppermute x1, starting transfers between devices, shards(): second = lax.ppermute(second, 'ax', outer)  4.18 us
    pallas_call x1, Pallas kernels, shards(): call(near_parcels_body, [(CR, ROWS), (4 * CYCLES, ROWS)], [SMEM] + [VMEM]...  3.72 us
    all_to_all x1, starting transfers between devices, shards(): filtered = lax.all_to_all(to_home, 'az', 0, 0, tiled=True)  3.53 us
  transfers between devices with their start and end apart: 7, of which 2 were waited for; matrix products, arithmetic and copies ran while one was open for 0% of the time, Pallas kernels for 28%

profile of v4, /device:TPU:8, one launch (start us, length us, event | category | flops | bytes accessed | tf_op | source)
XLA Modules:
  0.0 60.0 jit_solution(1567130408403370399)
XLA Ops:
  0.6 0.0 copy-start
  0.6 0.0 copy-start.5
  0.7 1.8 %shard_map.95 = (f32[5,64,128]{2,1,0:T(8,128)}, f32[5,64,128]{2,1,0:T(8,128)}) custom-call(s32[1]{0:T(128)} %bitcast.1.odd_ref, f32[5,8,64,128]{3,2,1,0:T(8,128)} %q_ref.7), custom_call_target="tpu_custom_call" | custom-call | flops 1000000 | bytes 1000000 | tf_op jit(solution)/shard_map/pallas_call | solution.py:449
  2.5 0.1 collective-permute-start
  2.6 4.2 %collective-permute-start.1 = (f32[5,64,128]{2,1,0:T(8,128)}, f32[5,64,128]{2,1,0:T(8,128)S(1)}, u32[]{:S(2)}, u32[]{:S(2)}) collective-permute-start(f32[5,64,128]{2,1,0:T(8,128)} %get-tuple-element.18), channel_id=1, source_target_pairs={{2,4},{4,2},{6,8},{8,6},{10,12},{12,10},{3,5},{5,3},{7,9},{9,7},{1... | collective-permute-start | bytes 491528 | tf_op jit(solution)/shard_map/ppermute | solution.py:454
  7.4 0.0 copy-done
  7.4 0.0 copy-done.5
  7.5 0.0 copy-start.4
  7.5 0.8 %copy-done.4 = f32[4,32,1,128]{3,2,1,0:T(1,128)S(1)} copy-done((f32[4,32,1,128]{3,2,1,0:T(1,128)S(1)}, f32[4,32,1,128]{3,2,1,0:T(1,128)}, u32[]{:S(2)}) %copy-start.4) | copy-done | bytes 65560
  8.3 0.0 copy-start.2
  8.3 3.7 %shard_map.96 = (f32[128,512]{1,0:T(8,128)S(1)}, f32[64,512]{1,0:T(8,128)S(1)}) custom-call(s32[1]{0:T(128)} %bitcast.10.count_ref, f32[5,8,64,128]{3,2,1,0:T(8,128)S(1)} %copy-done, f32[4,32,128]{2,1,0:T(8,128)S(1)} %bitcast.12, s32[32,128]{1,0:T(8,128)S(1)} %bitcast.14), custom_call_target="tpu_custom_call" | custom-call | flops 3000000000 | bytes 2000000 | tf_op jit(solution)/shard_map/pallas_call | solution.py:456
  12.0 0.0 copy-start.6
  12.0 0.0 collective-permute-done.first_ref
  12.1 0.0 collective-permute-done.1.second_ref
  12.1 0.0 copy-done.2
  12.1 2.0 %shard_map.97 = (f32[16,29,128]{2,1,0:T(8,128)}, f32[32,128]{1,0:T(8,128)S(1)}) custom-call(s32[1]{0:T(128)} %bitcast.rad_ref, s32[1]{0:T(128)} %bitcast.1.odd_ref, f32[5,6]{1,0:T(8,128)S(1)} %copy-done.2, f32[5,8,64,128]{3,2,1,0:T(8,128)S(1)} %copy-done, f32[5,64,128]{2,1,0:T(8,128)S(1)} %collective-permute-done.first_ref, ...), custom_call_target="tpu_custom_call" | custom-call | flops 10000000 | bytes 4000000 | tf_op jit(solution)/shard_map/pallas_call | solution.py:468
  14.1 9.3 %all-to-all-start = ((f32[16,29,128]{2,1,0:T(8,128)}), f32[16,29,128]{2,1,0:T(8,128)S(1)}, u32[]{:S(2)}, u32[]{:S(2)}) async-start(f32[16,29,128]{2,1,0:T(8,128)} %get-tuple-element.23), calls=%async_computation | async-start | bytes 524288 | tf_op jit(solution)/shard_map/all_to_all | solution.py:475
  23.4 0.7 %collective-permute-start.2 = (f32[32,128]{1,0:T(8,128)S(1)}, f32[32,128]{1,0:T(8,128)S(1)}, u32[]{:S(2)}, u32[]{:S(2)}) collective-permute-start(f32[32,128]{1,0:T(8,128)S(1)} %get-tuple-element.21), channel_id=1, source_target_pairs={{0,1},{1,0},{2,3},{3,2},{4,5},{5,4},{6,7},{7,6},{8,9},{9,8},{10,11... | collective-permute-start | bytes 49160 | tf_op jit(solution)/shard_map/ppermute | solution.py:476
  24.1 0.0 copy-done.6
  24.1 0.0 copy-start.1
  24.1 0.0 copy-start.3
  24.1 5.5 %shard_map.98 = (f32[4,32,128]{2,1,0:T(8,128)S(1)}, f32[4,32,128]{2,1,0:T(8,128)S(1)}, f32[4,4,128]{2,1,0:T(4,128)S(1)}, f32[4,4,128]{2,1,0:T(4,128)S(1)}) custom-call(s32[1]{0:T(128)} %bitcast.1.odd_ref, s32[1]{0:T(128)} %bitcast.11.count_ref, s32[32]{0:T(128)S(1)} %bitcast.17, f32[5,8,64,128]{3,2,1,0:T(8,128)S(1)} %copy-done, f32[4,32,128]{2,1,0:T(8,128)S(1)} %bitcast.13, ...), custom_call_target="tpu_custom_call" | custom-call | flops 6000000000 | bytes 2000000 | tf_op jit(solution)/shard_map/pallas_call | solution.py:478
  29.6 9.0 %all-to-all-done.got_ref = f32[16,29,128]{2,1,0:T(8,128)S(1)} async-done(((f32[16,29,128]{2,1,0:T(8,128)}), f32[16,29,128]{2,1,0:T(8,128)S(1)}, u32[]{:S(2)}, u32[]{:S(2)}) %all-to-all-start) | async-done | bytes 237600 | tf_op jit(solution)/shard_map/all_to_all | solution.py:475
  38.6 0.0 copy-done.1
  38.6 0.0 copy-done.3
  38.6 2.2 %shard_map.99 = (f32[16,25,128]{2,1,0:T(8,128)}, f32[4,4,128]{2,1,0:T(4,128)S(1)}, f32[4,4,128]{2,1,0:T(4,128)S(1)}) custom-call(s32[1]{0:T(128)} %bitcast.6.az_ref, s32[16]{0:T(128)S(1)} %copy-done.3, bf16[256,1024]{1,0:T(8,128)(2,1)S(1)} %copy-done.1, f32[16,29,128]{2,1,0:T(8,128)S(1)} %all-to-all-done.got_ref, ...), custom_call_target="tpu_custom_call" | custom-call | flops 100000000 | bytes 1000000 | tf_op jit(solution)/shard_map/pallas_call | solution.py:490
  40.9 3.5 %all-to-all-start.1 = ((f32[16,25,128]{2,1,0:T(8,128)}), f32[16,25,128]{2,1,0:T(8,128)S(1)}, u32[]{:S(2)}, u32[]{:S(2)}) async-start(f32[16,25,128]{2,1,0:T(8,128)} %get-tuple-element.26._), calls=%async_computation.1 | async-start | bytes 524288 | tf_op jit(solution)/shard_map/all_to_all | solution.py:501
  44.4 0.1 collective-permute-start.3
  44.5 2.1 %collective-permute-start.4 = (f32[4,4,128]{2,1,0:T(4,128)S(1)}, f32[4,4,128]{2,1,0:T(4,128)S(1)}, u32[]{:S(2)}, u32[]{:S(2)}) collective-permute-start(f32[4,4,128]{2,1,0:T(4,128)S(1)} %get-tuple-element.29), channel_id=1, source_target_pairs={{2,4},{4,2},{6,8},{8,6},{10,12},{12,10},{3,5},{5,3},{7,9},{9,7},{1... | collective-permute-start | bytes 24584 | tf_op jit(solution)/shard_map/ppermute | solution.py:503
  46.6 0.0 collective-permute-done.2.rad_in
  46.6 5.4 %shard_map.100.sect_ref = f32[5,8,64,128]{3,2,1,0:T(8,128)S(1)} custom-call(s32[1]{0:T(128)} %bitcast.rad_ref, s32[1]{0:T(128)} %bitcast.1.odd_ref, f32[5,6]{1,0:T(8,128)S(1)} %copy-done.2, f32[5,8,64,128]{3,2,1,0:T(8,128)S(1)} %copy-done, f32[5,64,128]{2,1,0:T(8,128)S(1)} %collective-permute-done.first_ref, ...), custom_call_target="tpu_custom_call" | custom-call | flops 8000000000 | bytes 4000000 | tf_op jit(solution)/shard_map/pallas_call | solution.py:505
  52.1 0.0 collective-permute-done.3.first_ref
  52.1 0.0 collective-permute-done.4.second_ref
  52.1 5.7 %all-to-all-done.1.got_ref = f32[16,25,128]{2,1,0:T(8,128)S(1)} async-done(((f32[16,25,128]{2,1,0:T(8,128)}), f32[16,25,128]{2,1,0:T(8,128)S(1)}, u32[]{:S(2)}, u32[]{:S(2)}) %all-to-all-start.1) | async-done | bytes 204832 | tf_op jit(solution)/shard_map/all_to_all | solution.py:501
  57.8 2.2 %shard_map.101 = (f32[5,8,64,128]{3,2,1,0:T(8,128)}, f32[4,40,128]{2,1,0:T(8,128)}) custom-call(s32[1]{0:T(128)} %bitcast.rad_ref, s32[1]{0:T(128)} %bitcast.1.odd_ref, f32[5,6]{1,0:T(8,128)S(1)} %copy-done.2, f32[5,8,64,128]{3,2,1,0:T(8,128)S(1)} %shard_map.100.sect_ref, f32[16,25,128]{2,1,0:T(8,128)S(1)} %all-to-all-done.1.got_ref, ...), custom_call_target="tpu_custom_call" | custom-call | flops 1000000 | bytes 4000000 | tf_op jit(solution)/shard_map/pallas_call | solution.py:511
Async XLA Ops:
  0.6 6.8 %copy-start = (f32[5,8,64,128]{3,2,1,0:T(8,128)S(1)}, f32[5,8,64,128]{3,2,1,0:T(8,128)}, u32[]{:S(2)}) copy-start(f32[5,8,64,128]{3,2,1,0:T(8,128)} %q_ref.7) | copy-start | bytes 3932164
  0.6 6.8 %copy-start.5 = (s32[32,1,128]{2,1,0:T(1,128)S(1)}, s32[32,1,128]{2,1,0:T(1,128)}, u32[]{:S(2)}) copy-start(s32[32,1,128]{2,1,0:T(1,128)} %param.11) | copy-start | bytes 49156
  2.5 9.5 %collective-permute-start = (f32[5,64,128]{2,1,0:T(8,128)}, f32[5,64,128]{2,1,0:T(8,128)S(1)}, u32[]{:S(2)}, u32[]{:S(2)}) collective-permute-start(f32[5,64,128]{2,1,0:T(8,128)} %get-tuple-element.17), channel_id=1, source_target_pairs={{0,2},{2,0},{4,6},{6,4},{8,10},{10,8},{12,14},{14,12},{1,3},{3,1},... | collective-permute-start | bytes 491528 | tf_op jit(solution)/shard_map/ppermute | solution.py:453
  2.6 9.5 %collective-permute-start.1 = (f32[5,64,128]{2,1,0:T(8,128)}, f32[5,64,128]{2,1,0:T(8,128)S(1)}, u32[]{:S(2)}, u32[]{:S(2)}) collective-permute-start(f32[5,64,128]{2,1,0:T(8,128)} %get-tuple-element.18), channel_id=1, source_target_pairs={{2,4},{4,2},{6,8},{8,6},{10,12},{12,10},{3,5},{5,3},{7,9},{9,7},{1... | collective-permute-start | bytes 491528 | tf_op jit(solution)/shard_map/ppermute | solution.py:454
  7.5 0.8 %copy-start.4 = (f32[4,32,1,128]{3,2,1,0:T(1,128)S(1)}, f32[4,32,1,128]{3,2,1,0:T(1,128)}, u32[]{:S(2)}) copy-start(f32[4,32,1,128]{3,2,1,0:T(1,128)} %param.10) | copy-start | bytes 196612
  8.3 3.8 %copy-start.2 = (f32[5,6]{1,0:T(8,128)S(1)}, f32[5,6]{1,0:T(8,128)}, u32[]{:S(2)}) copy-start(f32[5,6]{1,0:T(8,128)} %coef_ref.5) | copy-start | bytes 364
  12.0 12.0 %copy-start.6 = (s32[32,1,1]{0,2,1:T(1,128)S(1)}, s32[32,1,1]{0,2,1:T(1,128)}, u32[]{:S(2)}) copy-start(s32[32,1,1]{0,2,1:T(1,128)} %param.13) | copy-start | bytes 388
  14.1 24.5 %all-to-all-start = ((f32[16,29,128]{2,1,0:T(8,128)}), f32[16,29,128]{2,1,0:T(8,128)S(1)}, u32[]{:S(2)}, u32[]{:S(2)}) async-start(f32[16,29,128]{2,1,0:T(8,128)} %get-tuple-element.23), calls=%async_computation | async-start | bytes 524288 | tf_op jit(solution)/shard_map/all_to_all | solution.py:475
  23.4 23.2 %collective-permute-start.2 = (f32[32,128]{1,0:T(8,128)S(1)}, f32[32,128]{1,0:T(8,128)S(1)}, u32[]{:S(2)}, u32[]{:S(2)}) collective-permute-start(f32[32,128]{1,0:T(8,128)S(1)} %get-tuple-element.21), channel_id=1, source_target_pairs={{0,1},{1,0},{2,3},{3,2},{4,5},{5,4},{6,7},{7,6},{8,9},{9,8},{10,11... | collective-permute-start | bytes 49160 | tf_op jit(solution)/shard_map/ppermute | solution.py:476
  24.1 14.6 %copy-start.1 = (bf16[256,1024]{1,0:T(8,128)(2,1)S(1)}, bf16[256,1024]{1,0:T(8,128)(2,1)}, u32[]{:S(2)}) copy-start(bf16[256,1024]{1,0:T(8,128)(2,1)} %constant.28.clone.basis_ref) | copy-start | bytes 1572868
  24.1 14.6 %copy-start.3 = (s32[16]{0:T(128)S(1)}, s32[16]{0:T(128)}, u32[]{:S(2)}) copy-start(s32[16]{0:T(128)} %width_ref.1) | copy-start | bytes 196
  40.9 17.0 %all-to-all-start.1 = ((f32[16,25,128]{2,1,0:T(8,128)}), f32[16,25,128]{2,1,0:T(8,128)S(1)}, u32[]{:S(2)}, u32[]{:S(2)}) async-start(f32[16,25,128]{2,1,0:T(8,128)} %get-tuple-element.26._), calls=%async_computation.1 | async-start | bytes 524288 | tf_op jit(solution)/shard_map/all_to_all | solution.py:501
  44.4 7.7 %collective-permute-start.3 = (f32[4,4,128]{2,1,0:T(4,128)S(1)}, f32[4,4,128]{2,1,0:T(4,128)S(1)}, u32[]{:S(2)}, u32[]{:S(2)}) collective-permute-start(f32[4,4,128]{2,1,0:T(4,128)S(1)} %get-tuple-element.28), channel_id=1, source_target_pairs={{0,2},{2,0},{4,6},{6,4},{8,10},{10,8},{12,14},{14,12},{1,3},{3,1},... | collective-permute-start | bytes 24584 | tf_op jit(solution)/shard_map/ppermute | solution.py:502
  44.5 7.6 %collective-permute-start.4 = (f32[4,4,128]{2,1,0:T(4,128)S(1)}, f32[4,4,128]{2,1,0:T(4,128)S(1)}, u32[]{:S(2)}, u32[]{:S(2)}) collective-permute-start(f32[4,4,128]{2,1,0:T(4,128)S(1)} %get-tuple-element.29), channel_id=1, source_target_pairs={{2,4},{4,2},{6,8},{8,6},{10,12},{12,10},{3,5},{5,3},{7,9},{9,7},{1... | collective-permute-start | bytes 24584 | tf_op jit(solution)/shard_map/ppermute | solution.py:503

commit v5 on v4

--- a/solution.py
+++ b/solution.py
@@ -59,28 +59,23 @@
     return high, (value - high.astype(F32)).astype(BF16)
 
 
-def call(body, out_shape, in_specs, flops, nbytes, scratch=(), mib=24):
+def call(body, out_shape, in_specs, flops, nbytes, scratch=(), mib=24, hbm_first=False):
     return pl.pallas_call(
         body,
         out_shape=[jax.ShapeDtypeStruct(shape, F32) for shape in out_shape],
         in_specs=in_specs,
-        out_specs=[VMEM] * len(out_shape),
+        out_specs=[HBM if hbm_first and i == 0 else VMEM for i in range(len(out_shape))],
         scratch_shapes=list(scratch),
         compiler_params=pltpu.CompilerParams(vmem_limit_bytes=mib * 2**20),
         cost_estimate=pl.CostEstimate(flops=flops, bytes_accessed=nbytes, transcendentals=0),
     )
 
 
-def edges_body(odd_ref, q_hbm, first_out, second_out, sems):
-    odd, last = odd_ref[0], CAX - 1
-    copies = [
-        pltpu.make_async_copy(q_hbm.at[:, last * (1 - odd)], first_out, sems.at[0]),
-        pltpu.make_async_copy(q_hbm.at[:, last * odd], second_out, sems.at[1]),
-    ]
-    for copy in copies:
-        copy.start()
-    for copy in copies:
-        copy.wait()
+def edges_body(odd_ref, q_ref, first_out, second_out):
+    odd = odd_ref[0] == 1
+    low, high = q_ref[:, 0], q_ref[:, CAX - 1]
+    first_out[...] = jnp.where(odd, low, high)
+    second_out[...] = jnp.where(odd, high, low)
 
 
 def one_hot_rows(cells_ref, first, blocks):
@@ -119,9 +114,10 @@
 
 
 def parcels_body(
-    odd_ref, count_ref, move_ref, q_ref, parcel_ref, cells_ref,
-    src_out, stay_out, first_out, second_out, gas_ref, state_ref, leave_ref,
+    rad_ref, odd_ref, count_ref, move_ref, q_ref, parcel_ref, cells_ref,
+    src_out, stay_out, first_out, second_out, rad_out, gas_ref, state_ref, leave_ref,
 ):
+    rad_edges(rad_ref[0], q_ref, rad_out)
     parts = [[], []]
     for f in range(3):
         high, low = halves(q_ref[f + 1].reshape(ROWS, CR).T)
@@ -184,12 +180,14 @@
             [q_ref[f, 2 * p : 2 * p + 2].reshape(2 * CAZ, CR) for f in range(FIELDS)]
         )
     start = 16
-    high, low = halves(tiles_out[start : 4 * BAND])
+    table = jnp.concatenate(halves(tiles_out[start : 4 * BAND]), axis=0)
+    depth = 4 * BAND - start
     spans = [((f + 1) * BAND - start, (f + 1) * BAND - start + CYCLES) for f in range(3)]
     for first in range(0, BLK_DEV, 4):
         hot, lanes = one_hot_rows(cells_ref, first, 4)
         hot_ref[:, first * BLK : (first + 4) * BLK] = hot
-        rows = jnp.dot(high, hot, preferred_element_type=F32) + jnp.dot(low, hot, preferred_element_type=F32)
+        rows = jnp.dot(table, hot, preferred_element_type=F32)
+        rows = rows[:depth] + rows[depth:]
         pick(rows, first, spans, iota((CYCLES, 4 * BLK), 0) == lanes, gas_ref)
     _, sources = step(count_ref, parcel_ref, gas_ref)
     rows = [s.astype(BF16).astype(F32) for s in sources]
@@ -205,9 +203,14 @@
 
 
 def near_body(
-    rad_ref, odd_ref, coef_ref, q_ref, first_ref, second_ref, tiles_ref, near_ref,
-    send_out, rad_out, az_ref,
+    odd_ref, coef_ref, q_ref, first_ref, second_ref, tiles_ref, near_ref, send_hbm, az_ref, send_out, sems
 ):
+    for f in range(FIELDS):
+        az_ref[f * CAX : (f + 1) * CAX] = q_ref[f, :, 0, :]
+        az_ref[(FIELDS + f) * CAX : (FIELDS + f + 1) * CAX] = q_ref[f, :, CAZ - 1, :]
+    for owner in range(N_AZ):
+        send_out[owner, LINES + 4 :, :] = az_ref[owner * SHARE : (owner + 1) * SHARE]
+    copies = []
     lane = iota((CR, 2 * CAZ), 1)
     z = lane % CAZ
     tiles = [tiles_ref[:, p * 2 * CAZ : (p + 1) * 2 * CAZ] for p in range(PAIRS)]
@@ -257,12 +260,11 @@
                 send_out[p * QUADS + quad, f * 4 : f * 4 + 4, :] = block[quad * 4 : quad * 4 + 4]
         for quad in range(QUADS):
             send_out[p * QUADS + quad, LINES : LINES + 4, :] = ends[quad * 4 : quad * 4 + 4]
-    for f in range(FIELDS):
-        az_ref[f * CAX : (f + 1) * CAX] = q_ref[f, :, 0, :]
-        az_ref[(FIELDS + f) * CAX : (FIELDS + f + 1) * CAX] = q_ref[f, :, CAZ - 1, :]
-    for owner in range(N_AZ):
-        send_out[owner, LINES + 4 :, :] = az_ref[owner * SHARE : (owner + 1) * SHARE]
-    rad_edges(rad_ref[0], q_ref, rad_out)
+        span = pl.ds(p * QUADS, QUADS)
+        copies.append(pltpu.make_async_copy(send_out.at[span], send_hbm.at[span], sems.at[p]))
+        copies[p].start()
+    for copy in copies:
+        copy.wait()
 
 
 def rad_edges(rad, q_ref, rad_out):
@@ -343,7 +345,7 @@
 
 def filter_body(
     az_ref, width_ref, basis_ref, got_ref, first_ref, second_ref,
-    send_out, first_out, second_out, line_ref, ends_ref, piece_ref,
+    send_hbm, first_out, second_out, line_ref, ends_ref, piece_ref, send_out, sems,
 ):
     first_out[...] = first_ref[...]
     second_out[...] = second_ref[...]
@@ -389,35 +391,49 @@
     whole = jnp.dot(both, basis_ref[:MODES], preferred_element_type=F32)
     part = jnp.dot(high, basis_ref[MODES:], preferred_element_type=F32)
     line_ref[...] = whole[:rows] + whole[rows:] + part
+    copies = []
     for i in range(N_AZ // 2):
         cols = slice(i * 2 * CAZ, (i + 1) * 2 * CAZ)
         t0, t1 = line_ref[0:LINES, cols], line_ref[BAND : BAND + LINES, cols]
         send_out[2 * i, 0:LINES] = jnp.where(low, t0, pltpu.roll(t1, CAZ, 1))
         send_out[2 * i + 1, 0:LINES] = jnp.where(low, pltpu.roll(t0, CAZ, 1), t1)
+        if i % 2:
+            span = pl.ds(2 * i - 2, 4)
+            copies.append(pltpu.make_async_copy(send_out.at[span], send_hbm.at[span], sems.at[i // 2]))
+            copies[-1].start()
+    for copy in copies:
+        copy.wait()
 
 
 def merge_body(
     rad_ref, odd_ref, coef_ref, sect_ref, got_ref, stay_ref, first_ref, second_ref,
-    gas_out, parcels_out, flip_ref, az_ref,
+    gas_hbm, parcels_out, flip_ref, az_ref, gas_out, sems,
 ):
+    odd = odd_ref[0] == 1
+    parcels_out[:, 0:BLK_DEV, :] = stay_ref[...]
+    first, second = first_ref[...], second_ref[...]
+    parcels_out[:, BLK_DEV : BLK_DEV + MOVEB, :] = jnp.where(odd, first, second)
+    parcels_out[:, BLK_DEV + MOVEB :, :] = jnp.where(odd, second, first)
     near = (iota((2 * CAZ, CR), 1) < CYCLES) & (rad_ref[0] == 0)
-    flip_ref[...] = jnp.zeros_like(flip_ref)
     for owner in range(N_AZ):
         az_ref[owner * SHARE : (owner + 1) * SHARE] = got_ref[owner, LINES:, :]
+    tiles = []
     for pair in range(PAIRS):
+        flip_ref[pair, FIELDS * CYCLES :, :] = jnp.zeros((CR - FIELDS * CYCLES, CR), F32)
         for f in range(FIELDS):
             for quad in range(QUADS):
                 first = f * CYCLES + quad * 4
-                flip_ref[first : first + 4, :] = got_ref[pair * QUADS + quad, f * 4 : f * 4 + 4, :]
-        turned = flip_ref[...].T
-        for f in range(FIELDS):
-            moved = pltpu.roll(turned, (CR - f * CYCLES) % CR, 1) if f else turned
-            kept = sect_ref[f, 2 * pair : 2 * pair + 2].reshape(2 * CAZ, CR)
-            gas_out[f, 2 * pair : 2 * pair + 2] = jnp.where(near, moved, kept).reshape(2, CAZ, CR)
+                flip_ref[pair, first : first + 4, :] = got_ref[pair * QUADS + quad, f * 4 : f * 4 + 4, :]
+        tiles.append(flip_ref[pair].T)
     lane = iota((1, CR), 1)
     metric = 4.0 / ((rad_ref[0] * CR + lane).astype(F32) + 4.0)
     metric = jnp.where((lane < CYCLES) & (rad_ref[0] == 0), 0.0, metric)
+    copies = []
     for f in range(FIELDS):
+        for pair in range(PAIRS):
+            moved = pltpu.roll(tiles[pair], CR - f * CYCLES, 1) if f else tiles[pair]
+            kept = sect_ref[f, 2 * pair : 2 * pair + 2].reshape(2 * CAZ, CR)
+            gas_out[f, 2 * pair : 2 * pair + 2] = jnp.where(near, moved, kept).reshape(2, CAZ, CR)
         az_up = (0.5 * (coef_ref[f, 2] + coef_ref[f, 3])) * metric
         az_down = (0.5 * (coef_ref[f, 3] - coef_ref[f, 2])) * metric
         after = az_up * az_ref[f * CAX : (f + 1) * CAX]
@@ -425,11 +441,10 @@
         for a in range(CAX):
             gas_out[f, a, 0:1] += before[a : a + 1]
             gas_out[f, a, CAZ - 1 : CAZ] += after[a : a + 1]
-    odd = odd_ref[0] == 1
-    parcels_out[:, 0:BLK_DEV, :] = stay_ref[...]
-    first, second = first_ref[...], second_ref[...]
-    parcels_out[:, BLK_DEV : BLK_DEV + MOVEB, :] = jnp.where(odd, first, second)
-    parcels_out[:, BLK_DEV + MOVEB :, :] = jnp.where(odd, second, first)
+        copies.append(pltpu.make_async_copy(gas_out.at[f], gas_hbm.at[f], sems.at[f]))
+        copies[f].start()
+    for copy in copies:
+        copy.wait()
 
 
 def shards(fields, coeffs, parcels, cells, counts, moves, widths):
@@ -447,8 +462,7 @@
     gas_shape = (FIELDS, CAX, CAZ, CR)
 
     first, second = call(
-        edges_body, [(FIELDS, CAZ, CR)] * 2, [SMEM, HBM], 10**6, 10**6,
-        [pltpu.SemaphoreType.DMA((2,))], mib=62,
+        edges_body, [(FIELDS, CAZ, CR)] * 2, [SMEM, VMEM], 10**6, 10**6, mib=4
     )(odd, fields)
     first = lax.ppermute(first, "ax", inner)
     second = lax.ppermute(second, "ax", outer)
@@ -465,27 +479,32 @@
         mib=16,
     )(counts, fields, parcels, cells)
 
-    to_owner, rad_edge = call(
+    (to_owner,) = call(
         near_body,
-        [(N_AZ, LINES + 4 + SHARE, 2 * CAZ), (32, CR)],
-        [SMEM, SMEM, SMEM] + [VMEM] * 5, 10**7, 4 * 10**6,
-        [pltpu.VMEM((2 * FIELDS * CAX, CR), F32)],
+        [(N_AZ, LINES + 4 + SHARE, 2 * CAZ)],
+        [SMEM, SMEM] + [VMEM] * 5, 10**7, 4 * 10**6,
+        [
+            pltpu.VMEM((2 * FIELDS * CAX, CR), F32),
+            pltpu.VMEM((N_AZ, LINES + 4 + SHARE, 2 * CAZ), F32),
+            pltpu.SemaphoreType.DMA((PAIRS,)),
+        ],
         mib=8,
-    )(rad_index, odd, coeffs, fields, first, second, tiles, near)
+        hbm_first=True,
+    )(odd, coeffs, fields, first, second, tiles, near)
     lines = lax.all_to_all(to_owner, "az", 0, 0, tiled=True)
-    rad_got = lax.ppermute(rad_edge, "rad", across)
-
-    src, stay, first_moved, second_moved = call(
+
+    src, stay, first_moved, second_moved, rad_edge = call(
         parcels_body,
-        [(4, BLK_DEV, BLK), (4, BLK_DEV, BLK), (4, MOVEB, BLK), (4, MOVEB, BLK)],
-        [SMEM, SMEM, SMEM] + [VMEM] * 3 , 6 * 10**9, 2 * 10**6,
+        [(4, BLK_DEV, BLK), (4, BLK_DEV, BLK), (4, MOVEB, BLK), (4, MOVEB, BLK), (32, CR)],
+        [SMEM] * 4 + [VMEM] * 3, 6 * 10**9, 2 * 10**6,
         [
             pltpu.VMEM((3, BLK_DEV, BLK), F32),
             pltpu.VMEM((4, BLK_DEV, BLK), F32),
             pltpu.VMEM((2, 4, MOVEB, BLK), F32),
         ],
         mib=16,
-    )(odd, counts, moves, fields, parcels, cells)
+    )(rad_index, odd, counts, moves, fields, parcels, cells)
+    rad_got = lax.ppermute(rad_edge, "rad", across)
 
     to_home, first_moved, second_moved = call(
         filter_body,
@@ -495,8 +514,11 @@
             pltpu.VMEM((2 * BAND, NAZ), F32),
             pltpu.VMEM((2 * BAND, NAZ), F32),
             pltpu.VMEM((N_AZ, LINES, 2 * CAZ), F32),
+            pltpu.VMEM((N_AZ, LINES + SHARE, 2 * CAZ), F32),
+            pltpu.SemaphoreType.DMA((4,)),
         ],
         mib=6,
+        hbm_first=True,
     )(az_index, widths, jnp.asarray(basis_rows()), lines, first_moved, second_moved)
     filtered = lax.all_to_all(to_home, "az", 0, 0, tiled=True)
     first_moved = lax.ppermute(first_moved, "ax", inner)
@@ -512,8 +534,14 @@
         merge_body,
         [gas_shape, (4, BLK_DEV + 2 * MOVEB, BLK)],
         [SMEM, SMEM, SMEM] + [VMEM] * 5, 10**6, 4 * 10**6,
-        [pltpu.VMEM((CR, CR), F32), pltpu.VMEM((2 * FIELDS * CAX, CR), F32)],
+        [
+            pltpu.VMEM((PAIRS, CR, CR), F32),
+            pltpu.VMEM((2 * FIELDS * CAX, CR), F32),
+            pltpu.VMEM(gas_shape, F32),
+            pltpu.SemaphoreType.DMA((FIELDS,)),
+        ],
         mib=8,
+        hbm_first=True,
     )(rad_index, odd, coeffs, sect, filtered, stay, first_moved, second_moved)
     return gas_out, parcels_out.reshape(4, BLK_DEV + 2 * MOVEB, 1, BLK)
 

time: 60.5 us -> 60.3 us (level)
  Pallas kernels: 23 us -> 20.9 us
  local copies, waits for them, and re-layouts: 0.86 us -> 2.18 us
    pallas_call x2, Pallas kernels: 3.84 us -> 1.7 us  [the longest x1 1.68 us: shards(): call(near_body, [(N_AZ, LINES + 4 + SHARE, 2 * CAZ)], [SMEM, SMEM] + [VME...]
    unnamed x14 -> x18, local copies, waits for them, and re-layouts: 0.86 us -> 2.18 us
    all_to_all x1, waiting for transfers between devices: 5.73 us -> 6.71 us  [shards(): filtered = lax.all_to_all(to_home, 'az', 0, 0, tiled=True)]
    all_to_all x1, waiting for transfers between devices: 9.02 us -> 8.24 us  [shards(): lines = lax.all_to_all(to_owner, 'az', 0, 0, tiled=True)]
where the time goes in v5:
time: 60.3 us; the launch traced here: 59.9 us
  Pallas kernels  20.9 us (35%)
  starting transfers between devices  20.1 us (33%)
  waiting for transfers between devices  15 us (25%)
  local copies, waits for them, and re-layouts  2.18 us (4%)
  between operations  1.67 us (3%)
    all_to_all x1, starting transfers between devices, shards(): lines = lax.all_to_all(to_owner, 'az', 0, 0, tiled=True)  9.31 us
    all_to_all x1, waiting for transfers between devices, shards(): lines = lax.all_to_all(to_owner, 'az', 0, 0, tiled=True)  8.24 us
    all_to_all x1, waiting for transfers between devices, shards(): filtered = lax.all_to_all(to_home, 'az', 0, 0, tiled=True)  6.71 us
    pallas_call x1, Pallas kernels, shards(): call(parcels_body, [(4, BLK_DEV, BLK), (4, BLK_DEV, BLK), (4, MOVEB, BLK)...  5.56 us
    pallas_call x1, Pallas kernels, shards(): call(gas_body, [gas_shape], [SMEM, SMEM, SMEM] + [VMEM] * 6 + [ANY], 8 *...  5.45 us
    ppermute x1, starting transfers between devices, shards(): second = lax.ppermute(second, 'ax', outer)  4.18 us
    all_to_all x1, starting transfers between devices, shards(): filtered = lax.all_to_all(to_home, 'az', 0, 0, tiled=True)  3.55 us
    pallas_call x1, Pallas kernels, shards(): call(near_parcels_body, [(CR, ROWS), (4 * CYCLES, ROWS)], [SMEM] + [VMEM]...  3.53 us
  transfers between devices with their start and end apart: 7, of which 2 were waited for; matrix products, arithmetic and copies ran while one was open for 0% of the time, Pallas kernels for 28%

profile of v5, /device:TPU:8, one launch (start us, length us, event | category | flops | bytes accessed | tf_op | source)
XLA Modules:
  0.0 59.9 jit_solution(15564466632518228290)
XLA Ops:
  0.6 0.0 copy-start.7
  0.7 0.0 copy-start
  0.7 1.3 %copy-done = f32[5,8,64,128]{3,2,1,0:T(8,128)S(1)} copy-done((f32[5,8,64,128]{3,2,1,0:T(8,128)S(1)}, f32[5,8,64,128]{3,2,1,0:T(8,128)}, u32[]{:S(2)}) %copy-start) | copy-done | bytes 1310744
  2.0 0.0 copy-start.1
  2.0 0.1 collective-permute-start
  2.1 4.2 %collective-permute-start.1 = (f32[5,64,128]{2,1,0:T(8,128)S(1)}, f32[5,64,128]{2,1,0:T(8,128)S(1)}, u32[]{:S(2)}, u32[]{:S(2)}) collective-permute-start(f32[5,64,128]{2,1,0:T(8,128)S(1)} %get-tuple-element.17), channel_id=1, source_target_pairs={{2,4},{4,2},{6,8},{8,6},{10,12},{12,10},{3,5},{5,3},{7,9},{9,7},{1... | collective-permute-start | bytes 491528 | tf_op jit(solution)/shard_map/ppermute | solution.py:468
  6.9 0.0 copy-done.7
  7.0 0.0 copy-done.1
  7.0 0.0 copy-start.5
  7.0 0.8 %copy-done.5 = f32[4,32,1,128]{3,2,1,0:T(1,128)S(1)} copy-done((f32[4,32,1,128]{3,2,1,0:T(1,128)S(1)}, f32[4,32,1,128]{3,2,1,0:T(1,128)}, u32[]{:S(2)}) %copy-start.5) | copy-done | bytes 65560
  7.8 0.0 copy-start.3
  7.8 3.5 %shard_map.97 = (f32[128,512]{1,0:T(8,128)S(1)}, f32[64,512]{1,0:T(8,128)S(1)}) custom-call(s32[1]{0:T(128)} %bitcast.11.count_ref, f32[5,8,64,128]{3,2,1,0:T(8,128)S(1)} %copy-done.1, f32[4,32,128]{2,1,0:T(8,128)S(1)} %bitcast.12, s32[32,128]{1,0:T(8,128)S(1)} %bitcast.14), custom_call_target="tpu_custom_call" | custom-call | flops 3000000000 | bytes 2000000 | tf_op jit(solution)/shard_map/pallas_call | solution.py:470
  11.3 0.0 collective-permute-done.first_ref
  11.4 0.0 collective-permute-done.1.second_ref
  11.4 0.0 copy-done.3
  11.4 0.0 copy-start.6
  11.4 0.0 copy-start.8
  11.4 1.7 %shard_map.98 = f32[16,29,128]{2,1,0:T(8,128)} custom-call(s32[1]{0:T(128)} %bitcast.1.odd_ref, f32[5,6]{1,0:T(8,128)S(1)} %copy-done.3, f32[5,8,64,128]{3,2,1,0:T(8,128)S(1)} %copy-done.1, f32[5,64,128]{2,1,0:T(8,128)S(1)} %collective-permute-done.first_ref, f32[5,64,128]{2,1,0:T(8,128)S(1)} %collective-permute-done.1.second_ref, ...), custom_call_target="tpu_custom_call" | custom-call | flops 10000000 | bytes 4000000 | tf_op jit(solution)/shard_map/pallas_call | solution.py:482
  13.1 9.3 %all-to-all-start = ((f32[16,29,128]{2,1,0:T(8,128)}), f32[16,29,128]{2,1,0:T(8,128)S(1)}, u32[]{:S(2)}, u32[]{:S(2)}) async-start(f32[16,29,128]{2,1,0:T(8,128)} %shard_map.98), calls=%async_computation | async-start | bytes 524288 | tf_op jit(solution)/shard_map/all_to_all | solution.py:494
  22.4 0.0 copy-done.6
  22.4 0.0 copy-done.8
  22.4 0.0 copy-start.2
  22.4 0.0 copy-start.4
  22.4 5.6 %shard_map.96 = (f32[4,32,128]{2,1,0:T(8,128)S(1)}, f32[4,32,128]{2,1,0:T(8,128)S(1)}, f32[4,4,128]{2,1,0:T(4,128)S(1)}, f32[4,4,128]{2,1,0:T(4,128)S(1)}, f32[32,128]{1,0:T(8,128)S(1)}) custom-call(s32[1]{0:T(128)} %bitcast.rad_ref, s32[1]{0:T(128)} %bitcast.1.odd_ref, s32[1]{0:T(128)} %bitcast.10.count_ref, s32[32]{0:T(128)S(1)} %bitcast.17, ...), custom_call_target="tpu_custom_call" | custom-call | flops 6000000000 | bytes 2000000 | tf_op jit(solution)/shard_map/pallas_call | solution.py:496
  28.0 0.7 %collective-permute-start.2 = (f32[32,128]{1,0:T(8,128)S(1)}, f32[32,128]{1,0:T(8,128)S(1)}, u32[]{:S(2)}, u32[]{:S(2)}) collective-permute-start(f32[32,128]{1,0:T(8,128)S(1)} %get-tuple-element.18), channel_id=1, source_target_pairs={{0,1},{1,0},{2,3},{3,2},{4,5},{5,4},{6,7},{7,6},{8,9},{9,8},{10,11... | collective-permute-start | bytes 49160 | tf_op jit(solution)/shard_map/ppermute | solution.py:507
  28.7 8.2 %all-to-all-done.got_ref = f32[16,29,128]{2,1,0:T(8,128)S(1)} async-done(((f32[16,29,128]{2,1,0:T(8,128)}), f32[16,29,128]{2,1,0:T(8,128)S(1)}, u32[]{:S(2)}, u32[]{:S(2)}) %all-to-all-start) | async-done | bytes 237600 | tf_op jit(solution)/shard_map/all_to_all | solution.py:494
  36.9 0.0 copy-done.2
  36.9 0.0 copy-done.4
  36.9 2.2 %shard_map.99 = (f32[16,25,128]{2,1,0:T(8,128)}, f32[4,4,128]{2,1,0:T(4,128)S(1)}, f32[4,4,128]{2,1,0:T(4,128)S(1)}) custom-call(s32[1]{0:T(128)} %bitcast.6.az_ref, s32[16]{0:T(128)S(1)} %copy-done.4, bf16[256,1024]{1,0:T(8,128)(2,1)S(1)} %copy-done.2, f32[16,29,128]{2,1,0:T(8,128)S(1)} %all-to-all-done.got_ref, ...), custom_call_target="tpu_custom_call" | custom-call | flops 100000000 | bytes 1000000 | tf_op jit(solution)/shard_map/pallas_call | solution.py:509
  39.1 3.5 %all-to-all-start.1 = ((f32[16,25,128]{2,1,0:T(8,128)}), f32[16,25,128]{2,1,0:T(8,128)S(1)}, u32[]{:S(2)}, u32[]{:S(2)}) async-start(f32[16,25,128]{2,1,0:T(8,128)} %get-tuple-element.24._), calls=%async_computation.1 | async-start | bytes 524288 | tf_op jit(solution)/shard_map/all_to_all | solution.py:523
  42.7 0.2 collective-permute-start.3
  42.9 2.1 %collective-permute-start.4 = (f32[4,4,128]{2,1,0:T(4,128)S(1)}, f32[4,4,128]{2,1,0:T(4,128)S(1)}, u32[]{:S(2)}, u32[]{:S(2)}) collective-permute-start(f32[4,4,128]{2,1,0:T(4,128)S(1)} %get-tuple-element.27), channel_id=1, source_target_pairs={{2,4},{4,2},{6,8},{8,6},{10,12},{12,10},{3,5},{5,3},{7,9},{9,7},{1... | collective-permute-start | bytes 24584 | tf_op jit(solution)/shard_map/ppermute | solution.py:525
  45.0 0.0 collective-permute-done.2.rad_in
  45.0 5.5 %shard_map.100.sect_ref = f32[5,8,64,128]{3,2,1,0:T(8,128)S(1)} custom-call(s32[1]{0:T(128)} %bitcast.rad_ref, s32[1]{0:T(128)} %bitcast.1.odd_ref, f32[5,6]{1,0:T(8,128)S(1)} %copy-done.3, f32[5,8,64,128]{3,2,1,0:T(8,128)S(1)} %copy-done.1, f32[5,64,128]{2,1,0:T(8,128)S(1)} %collective-permute-done.first_ref, ...), custom_call_target="tpu_custom_call" | custom-call | flops 8000000000 | bytes 4000000 | tf_op jit(solution)/shard_map/pallas_call | solution.py:527
  50.5 0.0 collective-permute-done.3.first_ref
  50.5 0.0 collective-permute-done.4.second_ref
  50.5 6.7 %all-to-all-done.1.got_ref = f32[16,25,128]{2,1,0:T(8,128)S(1)} async-done(((f32[16,25,128]{2,1,0:T(8,128)}), f32[16,25,128]{2,1,0:T(8,128)S(1)}, u32[]{:S(2)}, u32[]{:S(2)}) %all-to-all-start.1) | async-done | bytes 204832 | tf_op jit(solution)/shard_map/all_to_all | solution.py:523
  57.2 2.5 %shard_map.101 = (f32[5,8,64,128]{3,2,1,0:T(8,128)}, f32[4,40,128]{2,1,0:T(8,128)}) custom-call(s32[1]{0:T(128)} %bitcast.rad_ref, s32[1]{0:T(128)} %bitcast.1.odd_ref, f32[5,6]{1,0:T(8,128)S(1)} %copy-done.3, f32[5,8,64,128]{3,2,1,0:T(8,128)S(1)} %shard_map.100.sect_ref, f32[16,25,128]{2,1,0:T(8,128)S(1)} %all-to-all-done.1.got_ref, ...), custom_call_target="tpu_custom_call" | custom-call | flops 1000000 | bytes 4000000 | tf_op jit(solution)/shard_map/pallas_call | solution.py:533
  (1 shorter events, 0.0 us)
Async XLA Ops:
  0.6 6.3 %copy-start.7 = (s32[32,1,128]{2,1,0:T(1,128)S(1)}, s32[32,1,128]{2,1,0:T(1,128)}, u32[]{:S(2)}) copy-start(s32[32,1,128]{2,1,0:T(1,128)} %param.11) | copy-start | bytes 49156
  0.7 1.3 %copy-start = (f32[5,8,64,128]{3,2,1,0:T(8,128)S(1)}, f32[5,8,64,128]{3,2,1,0:T(8,128)}, u32[]{:S(2)}) copy-start(f32[5,8,64,128]{3,2,1,0:T(8,128)} %q_ref.9) | copy-start | bytes 3932164
  2.0 5.0 %copy-start.1 = (f32[5,8,64,128]{3,2,1,0:T(8,128)S(1)}, f32[5,8,64,128]{3,2,1,0:T(8,128)}, u32[]{:S(2)}) copy-start(f32[5,8,64,128]{3,2,1,0:T(8,128)} %q_ref.9) | copy-start | bytes 3932164
  2.0 9.3 %collective-permute-start = (f32[5,64,128]{2,1,0:T(8,128)S(1)}, f32[5,64,128]{2,1,0:T(8,128)S(1)}, u32[]{:S(2)}, u32[]{:S(2)}) collective-permute-start(f32[5,64,128]{2,1,0:T(8,128)S(1)} %get-tuple-element.16), channel_id=1, source_target_pairs={{0,2},{2,0},{4,6},{6,4},{8,10},{10,8},{12,14},{14,12},{1,3},{3,1},... | collective-permute-start | bytes 491528 | tf_op jit(solution)/shard_map/ppermute | solution.py:467
  2.1 9.3 %collective-permute-start.1 = (f32[5,64,128]{2,1,0:T(8,128)S(1)}, f32[5,64,128]{2,1,0:T(8,128)S(1)}, u32[]{:S(2)}, u32[]{:S(2)}) collective-permute-start(f32[5,64,128]{2,1,0:T(8,128)S(1)} %get-tuple-element.17), channel_id=1, source_target_pairs={{2,4},{4,2},{6,8},{8,6},{10,12},{12,10},{3,5},{5,3},{7,9},{9,7},{1... | collective-permute-start | bytes 491528 | tf_op jit(solution)/shard_map/ppermute | solution.py:468
  7.0 0.8 %copy-start.5 = (f32[4,32,1,128]{3,2,1,0:T(1,128)S(1)}, f32[4,32,1,128]{3,2,1,0:T(1,128)}, u32[]{:S(2)}) copy-start(f32[4,32,1,128]{3,2,1,0:T(1,128)} %param.10) | copy-start | bytes 196612
  7.8 3.6 %copy-start.3 = (f32[5,6]{1,0:T(8,128)S(1)}, f32[5,6]{1,0:T(8,128)}, u32[]{:S(2)}) copy-start(f32[5,6]{1,0:T(8,128)} %coef_ref.5) | copy-start | bytes 364
  11.4 11.0 %copy-start.6 = (f32[4,32,1,128]{3,2,1,0:T(1,128)S(1)}, f32[4,32,1,128]{3,2,1,0:T(1,128)}, u32[]{:S(2)}) copy-start(f32[4,32,1,128]{3,2,1,0:T(1,128)} %param.10) | copy-start | bytes 196612
  11.4 11.0 %copy-start.8 = (s32[32,1,1]{0,2,1:T(1,128)S(1)}, s32[32,1,1]{0,2,1:T(1,128)}, u32[]{:S(2)}) copy-start(s32[32,1,1]{0,2,1:T(1,128)} %param.13) | copy-start | bytes 388
  13.1 23.8 %all-to-all-start = ((f32[16,29,128]{2,1,0:T(8,128)}), f32[16,29,128]{2,1,0:T(8,128)S(1)}, u32[]{:S(2)}, u32[]{:S(2)}) async-start(f32[16,29,128]{2,1,0:T(8,128)} %shard_map.98), calls=%async_computation | async-start | bytes 524288 | tf_op jit(solution)/shard_map/all_to_all | solution.py:494
  22.4 14.5 %copy-start.2 = (bf16[256,1024]{1,0:T(8,128)(2,1)S(1)}, bf16[256,1024]{1,0:T(8,128)(2,1)}, u32[]{:S(2)}) copy-start(bf16[256,1024]{1,0:T(8,128)(2,1)} %constant.28.clone.basis_ref) | copy-start | bytes 1572868
  22.4 14.5 %copy-start.4 = (s32[16]{0:T(128)S(1)}, s32[16]{0:T(128)}, u32[]{:S(2)}) copy-start(s32[16]{0:T(128)} %width_ref.1) | copy-start | bytes 196
  28.0 17.0 %collective-permute-start.2 = (f32[32,128]{1,0:T(8,128)S(1)}, f32[32,128]{1,0:T(8,128)S(1)}, u32[]{:S(2)}, u32[]{:S(2)}) collective-permute-start(f32[32,128]{1,0:T(8,128)S(1)} %get-tuple-element.18), channel_id=1, source_target_pairs={{0,1},{1,0},{2,3},{3,2},{4,5},{5,4},{6,7},{7,6},{8,9},{9,8},{10,11... | collective-permute-start | bytes 49160 | tf_op jit(solution)/shard_map/ppermute | solution.py:507
  39.1 18.1 %all-to-all-start.1 = ((f32[16,25,128]{2,1,0:T(8,128)}), f32[16,25,128]{2,1,0:T(8,128)S(1)}, u32[]{:S(2)}, u32[]{:S(2)}) async-start(f32[16,25,128]{2,1,0:T(8,128)} %get-tuple-element.24._), calls=%async_computation.1 | async-start | bytes 524288 | tf_op jit(solution)/shard_map/all_to_all | solution.py:523
  42.7 7.8 %collective-permute-start.3 = (f32[4,4,128]{2,1,0:T(4,128)S(1)}, f32[4,4,128]{2,1,0:T(4,128)S(1)}, u32[]{:S(2)}, u32[]{:S(2)}) collective-permute-start(f32[4,4,128]{2,1,0:T(4,128)S(1)} %get-tuple-element.26), channel_id=1, source_target_pairs={{0,2},{2,0},{4,6},{6,4},{8,10},{10,8},{12,14},{14,12},{1,3},{3,1},... | collective-permute-start | bytes 24584 | tf_op jit(solution)/shard_map/ppermute | solution.py:524
  42.9 7.6 %collective-permute-start.4 = (f32[4,4,128]{2,1,0:T(4,128)S(1)}, f32[4,4,128]{2,1,0:T(4,128)S(1)}, u32[]{:S(2)}, u32[]{:S(2)}) collective-permute-start(f32[4,4,128]{2,1,0:T(4,128)S(1)} %get-tuple-element.27), channel_id=1, source_target_pairs={{2,4},{4,2},{6,8},{8,6},{10,12},{12,10},{3,5},{5,3},{7,9},{9,7},{1... | collective-permute-start | bytes 24584 | tf_op jit(solution)/shard_map/ppermute | solution.py:525

commit v6 on v5

--- a/solution.py
+++ b/solution.py
@@ -39,7 +39,7 @@
 NT = (((1,), (1,)), ((), ()))
 
 
-def basis_rows():
+def basis_parts():
     column = np.arange(MODES)
     mode = np.where(column < HALF, column, column - HALF + 1)
     phases = (mode[:, None] * np.arange(NAZ)[None, :]) % NAZ
@@ -47,7 +47,8 @@
     table = np.where(column[:, None] < HALF, np.cos(angles), np.sin(angles)).astype(np.float32)
     high = table.astype(ml_dtypes.bfloat16)
     low = (table - high.astype(np.float32)).astype(ml_dtypes.bfloat16)
-    return np.concatenate([high, low])
+    parts = np.concatenate([high, low])
+    return jnp.asarray(parts), jnp.asarray(np.ascontiguousarray(parts.T))
 
 
 def iota(shape, axis):
@@ -115,7 +116,7 @@
 
 def parcels_body(
     rad_ref, odd_ref, count_ref, move_ref, q_ref, parcel_ref, cells_ref,
-    src_out, stay_out, first_out, second_out, rad_out, gas_ref, state_ref, leave_ref,
+    src_out, stay_out, leave_out, rad_out, gas_ref, state_ref, leave_ref,
 ):
     rad_edges(rad_ref[0], q_ref, rad_out)
     parts = [[], []]
@@ -154,8 +155,8 @@
     lax.fori_loop(0, BLK_DEV, place, (jnp.int32(0), jnp.int32(0)))
     odd = odd_ref[0] == 1
     up, down = leave_ref[0], leave_ref[1]
-    first_out[...] = jnp.where(odd, down, up)
-    second_out[...] = jnp.where(odd, up, down)
+    leave_out[0] = jnp.where(odd, down, up)
+    leave_out[1] = jnp.where(odd, up, down)
 
 
 SOURCE_OF = (0, 1, 2, 3, 0)
@@ -344,11 +345,10 @@
 
 
 def filter_body(
-    az_ref, width_ref, basis_ref, got_ref, first_ref, second_ref,
-    send_hbm, first_out, second_out, line_ref, ends_ref, piece_ref, send_out, sems,
+    az_ref, width_ref, basis_ref, turned_ref, got_ref, moved_ref,
+    send_out, onward_out, line_ref, ends_ref, piece_ref,
 ):
-    first_out[...] = first_ref[...]
-    second_out[...] = second_ref[...]
+    onward_out[...] = moved_ref[1]
     for home in range(N_AZ):
         send_out[home, LINES:, :] = jnp.where(
             az_ref[0] < N_AZ // 2,
@@ -373,11 +373,9 @@
         + jnp.where(z == 0, pltpu.roll(ends, 1, 1), 0.0)
     )
     rows = 2 * BAND
-    high, rest = halves(lines)
-    both = jnp.concatenate([high, rest], axis=0)
-    whole = lax.dot_general(both, basis_ref[:MODES], NT, preferred_element_type=F32)
-    part = lax.dot_general(high, basis_ref[MODES:], NT, preferred_element_type=F32)
-    coefs = whole[:rows] + whole[rows:] + part
+    both = jnp.concatenate(halves(lines), axis=0)
+    whole = jnp.dot(both, turned_ref[...], preferred_element_type=F32)
+    coefs = whole[:rows, :MODES] + whole[rows:, :MODES] + whole[:rows, MODES:]
     column = iota((rows, MODES), 1)
     cycle = iota((rows, MODES), 0) % 4
     mode = jnp.where(column < HALF, column, column - HALF + 1)
@@ -387,31 +385,23 @@
     weight = jnp.where(mode == 0, 1.0 / NAZ, 2.0 / NAZ)
     coefs = coefs * jnp.where(mode < width, weight, 0.0)
     high, rest = halves(coefs)
-    both = jnp.concatenate([high, rest], axis=0)
-    whole = jnp.dot(both, basis_ref[:MODES], preferred_element_type=F32)
-    part = jnp.dot(high, basis_ref[MODES:], preferred_element_type=F32)
-    line_ref[...] = whole[:rows] + whole[rows:] + part
-    copies = []
+    line_ref[...] = jnp.dot(
+        jnp.concatenate([high, high], axis=1), basis_ref[...], preferred_element_type=F32
+    ) + jnp.dot(rest, basis_ref[:MODES], preferred_element_type=F32)
     for i in range(N_AZ // 2):
         cols = slice(i * 2 * CAZ, (i + 1) * 2 * CAZ)
         t0, t1 = line_ref[0:LINES, cols], line_ref[BAND : BAND + LINES, cols]
         send_out[2 * i, 0:LINES] = jnp.where(low, t0, pltpu.roll(t1, CAZ, 1))
         send_out[2 * i + 1, 0:LINES] = jnp.where(low, pltpu.roll(t0, CAZ, 1), t1)
-        if i % 2:
-            span = pl.ds(2 * i - 2, 4)
-            copies.append(pltpu.make_async_copy(send_out.at[span], send_hbm.at[span], sems.at[i // 2]))
-            copies[-1].start()
-    for copy in copies:
-        copy.wait()
 
 
 def merge_body(
-    rad_ref, odd_ref, coef_ref, sect_ref, got_ref, stay_ref, first_ref, second_ref,
-    gas_hbm, parcels_out, flip_ref, az_ref, gas_out, sems,
+    rad_ref, odd_ref, coef_ref, sect_ref, got_ref, stay_ref, moved_ref, onward_ref,
+    gas_out, parcels_out, flip_ref, az_ref,
 ):
     odd = odd_ref[0] == 1
     parcels_out[:, 0:BLK_DEV, :] = stay_ref[...]
-    first, second = first_ref[...], second_ref[...]
+    first, second = moved_ref[0], onward_ref[...]
     parcels_out[:, BLK_DEV : BLK_DEV + MOVEB, :] = jnp.where(odd, first, second)
     parcels_out[:, BLK_DEV + MOVEB :, :] = jnp.where(odd, second, first)
     near = (iota((2 * CAZ, CR), 1) < CYCLES) & (rad_ref[0] == 0)
@@ -428,7 +418,6 @@
     lane = iota((1, CR), 1)
     metric = 4.0 / ((rad_ref[0] * CR + lane).astype(F32) + 4.0)
     metric = jnp.where((lane < CYCLES) & (rad_ref[0] == 0), 0.0, metric)
-    copies = []
     for f in range(FIELDS):
         for pair in range(PAIRS):
             moved = pltpu.roll(tiles[pair], CR - f * CYCLES, 1) if f else tiles[pair]
@@ -441,10 +430,6 @@
         for a in range(CAX):
             gas_out[f, a, 0:1] += before[a : a + 1]
             gas_out[f, a, CAZ - 1 : CAZ] += after[a : a + 1]
-        copies.append(pltpu.make_async_copy(gas_out.at[f], gas_hbm.at[f], sems.at[f]))
-        copies[f].start()
-    for copy in copies:
-        copy.wait()
 
 
 def shards(fields, coeffs, parcels, cells, counts, moves, widths):
@@ -458,6 +443,7 @@
     moves = moves.reshape(BLK_DEV)
     inner = [(i, i ^ 1) for i in range(n_ax)]
     outer = [(i, ((i + 1) ^ 1) - 1) for i in range(1, n_ax - 1)]
+    along = [(i, i + 2) for i in range(0, n_ax - 2, 2)] + [(i, i - 2) for i in range(3, n_ax, 2)]
     across = [(i, i ^ 1) for i in range(n_rad)]
     gas_shape = (FIELDS, CAX, CAZ, CR)
 
@@ -493,9 +479,9 @@
     )(odd, coeffs, fields, first, second, tiles, near)
     lines = lax.all_to_all(to_owner, "az", 0, 0, tiled=True)
 
-    src, stay, first_moved, second_moved, rad_edge = call(
+    src, stay, leaving, rad_edge = call(
         parcels_body,
-        [(4, BLK_DEV, BLK), (4, BLK_DEV, BLK), (4, MOVEB, BLK), (4, MOVEB, BLK), (32, CR)],
+        [(4, BLK_DEV, BLK), (4, BLK_DEV, BLK), (2, 4, MOVEB, BLK), (32, CR)],
         [SMEM] * 4 + [VMEM] * 3, 6 * 10**9, 2 * 10**6,
         [
             pltpu.VMEM((3, BLK_DEV, BLK), F32),
@@ -505,24 +491,22 @@
         mib=16,
     )(rad_index, odd, counts, moves, fields, parcels, cells)
     rad_got = lax.ppermute(rad_edge, "rad", across)
-
-    to_home, first_moved, second_moved = call(
+    moved = lax.ppermute(leaving, "ax", inner)
+
+    basis, basis_turned = basis_parts()
+    to_home, onward = call(
         filter_body,
-        [(N_AZ, LINES + SHARE, 2 * CAZ), (4, MOVEB, BLK), (4, MOVEB, BLK)],
+        [(N_AZ, LINES + SHARE, 2 * CAZ), (4, MOVEB, BLK)],
         [SMEM, SMEM] + [VMEM] * 4, 10**8, 10**6,
         [
             pltpu.VMEM((2 * BAND, NAZ), F32),
             pltpu.VMEM((2 * BAND, NAZ), F32),
             pltpu.VMEM((N_AZ, LINES, 2 * CAZ), F32),
-            pltpu.VMEM((N_AZ, LINES + SHARE, 2 * CAZ), F32),
-            pltpu.SemaphoreType.DMA((4,)),
         ],
         mib=6,
-        hbm_first=True,
-    )(az_index, widths, jnp.asarray(basis_rows()), lines, first_moved, second_moved)
+    )(az_index, widths, basis, basis_turned, lines, moved)
     filtered = lax.all_to_all(to_home, "az", 0, 0, tiled=True)
-    first_moved = lax.ppermute(first_moved, "ax", inner)
-    second_moved = lax.ppermute(second_moved, "ax", outer)
+    onward = lax.ppermute(onward, "ax", along)
 
     (sect,) = call(
         gas_body, [gas_shape], [SMEM, SMEM, SMEM] + [VMEM] * 6 + [ANY], 8 * 10**9, 4 * 10**6,
@@ -537,12 +521,9 @@
         [
             pltpu.VMEM((PAIRS, CR, CR), F32),
             pltpu.VMEM((2 * FIELDS * CAX, CR), F32),
-            pltpu.VMEM(gas_shape, F32),
-            pltpu.SemaphoreType.DMA((FIELDS,)),
         ],
         mib=8,
-        hbm_first=True,
-    )(rad_index, odd, coeffs, sect, filtered, stay, first_moved, second_moved)
+    )(rad_index, odd, coeffs, sect, filtered, stay, moved, onward)
     return gas_out, parcels_out.reshape(4, BLK_DEV + 2 * MOVEB, 1, BLK)
 
 

time: 60.3 us -> 59.7 us (0.990)
  starting transfers between devices: 20.1 us -> 23.1 us
  waiting for transfers between devices: 15 us -> 12 us
    ppermute x2, starting transfers between devices: 2.29 us -> 5.35 us  [the longest x1 4.25 us: shards(): onward = lax.ppermute(onward, 'ax', along)]
    all_to_all x1, waiting for transfers between devices: 6.71 us -> 4.76 us  [shards(): filtered = lax.all_to_all(to_home, 'az', 0, 0, tiled=True)]
    all_to_all x1, waiting for transfers between devices: 8.24 us -> 6.96 us  [shards(): lines = lax.all_to_all(to_owner, 'az', 0, 0, tiled=True)]
    unnamed x18 -> x20, local copies, waits for them, and re-layouts: 2.18 us -> 2.19 us
  transfers between devices with their start and end apart: 7 -> 7, of which waited for: 2 -> 3; matrix products, arithmetic and copies ran while one was open for 0% -> 0% of each run, Pallas kernels for 28% -> 28%
where the time goes in v6:
time: 59.7 us; the launch traced here: 59.3 us
  starting transfers between devices  23.1 us (39%)
  Pallas kernels  20.6 us (35%)
  waiting for transfers between devices  12 us (20%)
  local copies, waits for them, and re-layouts  2.19 us (4%)
  between operations  1.51 us (3%)
    all_to_all x1, starting transfers between devices, shards(): lines = lax.all_to_all(to_owner, 'az', 0, 0, tiled=True)  9.31 us
    all_to_all x1, waiting for transfers between devices, shards(): lines = lax.all_to_all(to_owner, 'az', 0, 0, tiled=True)  6.96 us
    pallas_call x1, Pallas kernels, shards(): call(parcels_body, [(4, BLK_DEV, BLK), (4, BLK_DEV, BLK), (2, 4, MOVEB, B...  5.55 us
    pallas_call x1, Pallas kernels, shards(): call(gas_body, [gas_shape], [SMEM, SMEM, SMEM] + [VMEM] * 6 + [ANY], 8 *...  5.45 us
    all_to_all x1, waiting for transfers between devices, shards(): filtered = lax.all_to_all(to_home, 'az', 0, 0, tiled=True)  4.76 us
    ppermute x1, starting transfers between devices, shards(): onward = lax.ppermute(onward, 'ax', along)  4.25 us
    ppermute x1, starting transfers between devices, shards(): second = lax.ppermute(second, 'ax', outer)  4.18 us
    all_to_all x1, starting transfers between devices, shards(): filtered = lax.all_to_all(to_home, 'az', 0, 0, tiled=True)  3.53 us
  transfers between devices with their start and end apart: 7, of which 3 were waited for; matrix products, arithmetic and copies ran while one was open for 0% of the time, Pallas kernels for 28%

profile of v6, /device:TPU:8, one launch (start us, length us, event | category | flops | bytes accessed | tf_op | source)
XLA Modules:
  0.0 59.3 jit_solution(4451823702040728915)
XLA Ops:
  0.6 0.0 copy-start.8
  0.7 0.0 copy-start
  0.7 1.3 %copy-done = f32[5,8,64,128]{3,2,1,0:T(8,128)S(1)} copy-done((f32[5,8,64,128]{3,2,1,0:T(8,128)S(1)}, f32[5,8,64,128]{3,2,1,0:T(8,128)}, u32[]{:S(2)}) %copy-start) | copy-done | bytes 1310744
  2.0 0.0 copy-start.1
  2.0 0.1 collective-permute-start
  2.1 4.2 %collective-permute-start.1 = (f32[5,64,128]{2,1,0:T(8,128)S(1)}, f32[5,64,128]{2,1,0:T(8,128)S(1)}, u32[]{:S(2)}, u32[]{:S(2)}) collective-permute-start(f32[5,64,128]{2,1,0:T(8,128)S(1)} %get-tuple-element.15), channel_id=1, source_target_pairs={{2,4},{4,2},{6,8},{8,6},{10,12},{12,10},{3,5},{5,3},{7,9},{9,7},{1... | collective-permute-start | bytes 491528 | tf_op jit(solution)/shard_map/ppermute | solution.py:454
  6.9 0.0 copy-done.8
  7.0 0.0 copy-done.1
  7.0 0.0 copy-start.6
  7.0 0.8 %copy-done.6 = f32[4,32,1,128]{3,2,1,0:T(1,128)S(1)} copy-done((f32[4,32,1,128]{3,2,1,0:T(1,128)S(1)}, f32[4,32,1,128]{3,2,1,0:T(1,128)}, u32[]{:S(2)}) %copy-start.6) | copy-done | bytes 65560
  7.8 0.0 copy-start.4
  7.8 3.5 %shard_map.106 = (f32[128,512]{1,0:T(8,128)S(1)}, f32[64,512]{1,0:T(8,128)S(1)}) custom-call(s32[1]{0:T(128)} %bitcast.11.count_ref, f32[5,8,64,128]{3,2,1,0:T(8,128)S(1)} %copy-done.1, f32[4,32,128]{2,1,0:T(8,128)S(1)} %bitcast.12, s32[32,128]{1,0:T(8,128)S(1)} %bitcast.14), custom_call_target="tpu_custom_call" | custom-call | flops 3000000000 | bytes 2000000 | tf_op jit(solution)/shard_map/pallas_call | solution.py:456
  11.3 0.0 collective-permute-done.first_ref
  11.3 0.0 collective-permute-done.1.second_ref
  11.4 0.0 copy-done.4
  11.4 0.0 copy-start.7
  11.4 0.0 copy-start.9
  11.4 1.7 %shard_map.107 = f32[16,29,128]{2,1,0:T(8,128)} custom-call(s32[1]{0:T(128)} %bitcast.1.odd_ref, f32[5,6]{1,0:T(8,128)S(1)} %copy-done.4, f32[5,8,64,128]{3,2,1,0:T(8,128)S(1)} %copy-done.1, f32[5,64,128]{2,1,0:T(8,128)S(1)} %collective-permute-done.first_ref, f32[5,64,128]{2,1,0:T(8,128)S(1)} %collective-permute-done.1.second_ref, ...), custom_call_target="tpu_custom_call" | custom-call | flops 10000000 | bytes 4000000 | tf_op jit(solution)/shard_map/pallas_call | solution.py:468
  13.1 9.3 %all-to-all-start = ((f32[16,29,128]{2,1,0:T(8,128)}), f32[16,29,128]{2,1,0:T(8,128)S(1)}, u32[]{:S(2)}, u32[]{:S(2)}) async-start(f32[16,29,128]{2,1,0:T(8,128)} %shard_map.107), calls=%async_computation | async-start | bytes 524288 | tf_op jit(solution)/shard_map/all_to_all | solution.py:480
  22.4 0.0 copy-done.7
  22.4 0.0 copy-done.9
  22.4 0.0 copy-start.2
  22.4 0.0 copy-start.3
  22.4 0.0 copy-start.5
  22.5 5.5 %shard_map.105 = (f32[4,32,128]{2,1,0:T(8,128)S(1)}, f32[4,32,128]{2,1,0:T(8,128)S(1)}, f32[2,4,4,128]{3,2,1,0:T(4,128)S(1)}, f32[32,128]{1,0:T(8,128)S(1)}) custom-call(s32[1]{0:T(128)} %bitcast.rad_ref, s32[1]{0:T(128)} %bitcast.1.odd_ref, s32[1]{0:T(128)} %bitcast.10.count_ref, s32[32]{0:T(128)S(1)} %bitcast.17, f32[5,8,64,128]{3,2,1,0:T(8,128)S(1)} %copy-done.1, ...), custom_call_target="tpu_custom_call" | custom-call | flops 6000000000 | bytes 2000000 | tf_op jit(solution)/shard_map/pallas_call | solution.py:482
  28.0 1.1 %collective-permute-start.3 = (f32[2,4,4,128]{3,2,1,0:T(4,128)S(1)}, f32[2,4,4,128]{3,2,1,0:T(4,128)S(1)}, u32[]{:S(2)}, u32[]{:S(2)}) collective-permute-start(f32[2,4,4,128]{3,2,1,0:T(4,128)S(1)} %get-tuple-element.20), channel_id=1, source_target_pairs={{0,2},{2,0},{4,6},{6,4},{8,10},{10,8},{12,14},{14,12},{1,3},{3,1},... | collective-permute-start | bytes 49160 | tf_op jit(solution)/shard_map/ppermute | solution.py:494
  29.1 0.6 collective-permute-start.2
  29.7 0.3 collective-permute-done.3.moved_ref
  29.9 7.0 %all-to-all-done.got_ref = f32[16,29,128]{2,1,0:T(8,128)S(1)} async-done(((f32[16,29,128]{2,1,0:T(8,128)}), f32[16,29,128]{2,1,0:T(8,128)S(1)}, u32[]{:S(2)}, u32[]{:S(2)}) %all-to-all-start) | async-done | bytes 237600 | tf_op jit(solution)/shard_map/all_to_all | solution.py:480
  36.9 0.0 copy-done.2
  36.9 0.0 copy-done.3
  36.9 0.0 copy-done.5
  36.9 2.2 %shard_map.108 = (f32[16,25,128]{2,1,0:T(8,128)}, f32[4,4,128]{2,1,0:T(4,128)S(1)}) custom-call(s32[1]{0:T(128)} %bitcast.6.az_ref, s32[16]{0:T(128)S(1)} %copy-done.5, bf16[256,1024]{1,0:T(8,128)(2,1)S(1)} %copy-done.3, bf16[1024,256]{1,0:T(8,128)(2,1)S(1)} %copy-done.2, f32[16,29,128]{2,1,0:T(8,128)S(1)} %all-to-all-done.got_ref, ...), custom_call_target="tpu_custom_call" | custom-call | flops 100000000 | bytes 1000000 | tf_op jit(solution)/shard_map/pallas_call | solution.py:497
  39.1 3.5 %all-to-all-start.1 = ((f32[16,25,128]{2,1,0:T(8,128)}), f32[16,25,128]{2,1,0:T(8,128)S(1)}, u32[]{:S(2)}, u32[]{:S(2)}) async-start(f32[16,25,128]{2,1,0:T(8,128)} %get-tuple-element.21._), calls=%async_computation.1 | async-start | bytes 524288 | tf_op jit(solution)/shard_map/all_to_all | solution.py:508
  42.6 4.3 %collective-permute-start.4 = (f32[4,4,128]{2,1,0:T(4,128)S(1)}, f32[4,4,128]{2,1,0:T(4,128)S(1)}, u32[]{:S(2)}, u32[]{:S(2)}) collective-permute-start(f32[4,4,128]{2,1,0:T(4,128)S(1)} %get-tuple-element.23), channel_id=1, source_target_pairs={{0,4},{4,8},{8,12},{6,2},{10,6},{14,10},{1,5},{5,9},{9,13},{7,3},{... | collective-permute-start | bytes 24584 | tf_op jit(solution)/shard_map/ppermute | solution.py:509
  46.9 0.0 collective-permute-done.2.rad_in
  46.9 5.5 %shard_map.109.sect_ref = f32[5,8,64,128]{3,2,1,0:T(8,128)S(1)} custom-call(s32[1]{0:T(128)} %bitcast.rad_ref, s32[1]{0:T(128)} %bitcast.1.odd_ref, f32[5,6]{1,0:T(8,128)S(1)} %copy-done.4, f32[5,8,64,128]{3,2,1,0:T(8,128)S(1)} %copy-done.1, f32[5,64,128]{2,1,0:T(8,128)S(1)} %collective-permute-done.first_ref, ...), custom_call_target="tpu_custom_call" | custom-call | flops 8000000000 | bytes 4000000 | tf_op jit(solution)/shard_map/pallas_call | solution.py:511
  52.4 0.0 collective-permute-done.4.onward_ref
  52.4 4.8 %all-to-all-done.1.got_ref = f32[16,25,128]{2,1,0:T(8,128)S(1)} async-done(((f32[16,25,128]{2,1,0:T(8,128)}), f32[16,25,128]{2,1,0:T(8,128)S(1)}, u32[]{:S(2)}, u32[]{:S(2)}) %all-to-all-start.1) | async-done | bytes 204832 | tf_op jit(solution)/shard_map/all_to_all | solution.py:508
  57.1 2.2 %shard_map.110 = (f32[5,8,64,128]{3,2,1,0:T(8,128)}, f32[4,40,128]{2,1,0:T(8,128)}) custom-call(s32[1]{0:T(128)} %bitcast.rad_ref, s32[1]{0:T(128)} %bitcast.1.odd_ref, f32[5,6]{1,0:T(8,128)S(1)} %copy-done.4, f32[5,8,64,128]{3,2,1,0:T(8,128)S(1)} %shard_map.109.sect_ref, f32[16,25,128]{2,1,0:T(8,128)S(1)} %all-to-all-done.1.got_ref, ...), custom_call_target="tpu_custom_call" | custom-call | flops 1000000 | bytes 4000000 | tf_op jit(solution)/shard_map/pallas_call | solution.py:517
  (1 shorter events, 0.0 us)
Async XLA Ops:
  0.6 6.3 %copy-start.8 = (s32[32,1,128]{2,1,0:T(1,128)S(1)}, s32[32,1,128]{2,1,0:T(1,128)}, u32[]{:S(2)}) copy-start(s32[32,1,128]{2,1,0:T(1,128)} %param.12) | copy-start | bytes 49156
  0.7 1.3 %copy-start = (f32[5,8,64,128]{3,2,1,0:T(8,128)S(1)}, f32[5,8,64,128]{3,2,1,0:T(8,128)}, u32[]{:S(2)}) copy-start(f32[5,8,64,128]{3,2,1,0:T(8,128)} %q_ref.9) | copy-start | bytes 3932164
  2.0 5.0 %copy-start.1 = (f32[5,8,64,128]{3,2,1,0:T(8,128)S(1)}, f32[5,8,64,128]{3,2,1,0:T(8,128)}, u32[]{:S(2)}) copy-start(f32[5,8,64,128]{3,2,1,0:T(8,128)} %q_ref.9) | copy-start | bytes 3932164
  2.0 9.3 %collective-permute-start = (f32[5,64,128]{2,1,0:T(8,128)S(1)}, f32[5,64,128]{2,1,0:T(8,128)S(1)}, u32[]{:S(2)}, u32[]{:S(2)}) collective-permute-start(f32[5,64,128]{2,1,0:T(8,128)S(1)} %get-tuple-element.14), channel_id=1, source_target_pairs={{0,2},{2,0},{4,6},{6,4},{8,10},{10,8},{12,14},{14,12},{1,3},{3,1},... | collective-permute-start | bytes 491528 | tf_op jit(solution)/shard_map/ppermute | solution.py:453
  2.1 9.2 %collective-permute-start.1 = (f32[5,64,128]{2,1,0:T(8,128)S(1)}, f32[5,64,128]{2,1,0:T(8,128)S(1)}, u32[]{:S(2)}, u32[]{:S(2)}) collective-permute-start(f32[5,64,128]{2,1,0:T(8,128)S(1)} %get-tuple-element.15), channel_id=1, source_target_pairs={{2,4},{4,2},{6,8},{8,6},{10,12},{12,10},{3,5},{5,3},{7,9},{9,7},{1... | collective-permute-start | bytes 491528 | tf_op jit(solution)/shard_map/ppermute | solution.py:454
  7.0 0.8 %copy-start.6 = (f32[4,32,1,128]{3,2,1,0:T(1,128)S(1)}, f32[4,32,1,128]{3,2,1,0:T(1,128)}, u32[]{:S(2)}) copy-start(f32[4,32,1,128]{3,2,1,0:T(1,128)} %param.11) | copy-start | bytes 196612
  7.8 3.6 %copy-start.4 = (f32[5,6]{1,0:T(8,128)S(1)}, f32[5,6]{1,0:T(8,128)}, u32[]{:S(2)}) copy-start(f32[5,6]{1,0:T(8,128)} %coef_ref.5) | copy-start | bytes 364
  11.4 11.0 %copy-start.7 = (f32[4,32,1,128]{3,2,1,0:T(1,128)S(1)}, f32[4,32,1,128]{3,2,1,0:T(1,128)}, u32[]{:S(2)}) copy-start(f32[4,32,1,128]{3,2,1,0:T(1,128)} %param.11) | copy-start | bytes 196612
  11.4 11.0 %copy-start.9 = (s32[32,1,1]{0,2,1:T(1,128)S(1)}, s32[32,1,1]{0,2,1:T(1,128)}, u32[]{:S(2)}) copy-start(s32[32,1,1]{0,2,1:T(1,128)} %param.14) | copy-start | bytes 388
  13.1 23.8 %all-to-all-start = ((f32[16,29,128]{2,1,0:T(8,128)}), f32[16,29,128]{2,1,0:T(8,128)S(1)}, u32[]{:S(2)}, u32[]{:S(2)}) async-start(f32[16,29,128]{2,1,0:T(8,128)} %shard_map.107), calls=%async_computation | async-start | bytes 524288 | tf_op jit(solution)/shard_map/all_to_all | solution.py:480
  22.4 14.5 %copy-start.2 = (bf16[1024,256]{1,0:T(8,128)(2,1)S(1)}, bf16[1024,256]{1,0:T(8,128)(2,1)}, u32[]{:S(2)}) copy-start(bf16[1024,256]{1,0:T(8,128)(2,1)} %constant.31.clone.turned_ref) | copy-start | bytes 1572868
  22.4 14.5 %copy-start.3 = (bf16[256,1024]{1,0:T(8,128)(2,1)S(1)}, bf16[256,1024]{1,0:T(8,128)(2,1)}, u32[]{:S(2)}) copy-start(bf16[256,1024]{1,0:T(8,128)(2,1)} %constant.30.clone.basis_ref) | copy-start | bytes 1572868
  22.4 14.5 %copy-start.5 = (s32[16]{0:T(128)S(1)}, s32[16]{0:T(128)}, u32[]{:S(2)}) copy-start(s32[16]{0:T(128)} %width_ref.1) | copy-start | bytes 196
  28.0 1.9 %collective-permute-start.3 = (f32[2,4,4,128]{3,2,1,0:T(4,128)S(1)}, f32[2,4,4,128]{3,2,1,0:T(4,128)S(1)}, u32[]{:S(2)}, u32[]{:S(2)}) collective-permute-start(f32[2,4,4,128]{3,2,1,0:T(4,128)S(1)} %get-tuple-element.20), channel_id=1, source_target_pairs={{0,2},{2,0},{4,6},{6,4},{8,10},{10,8},{12,14},{14,12},{1,3},{3,1},... | collective-permute-start | bytes 49160 | tf_op jit(solution)/shard_map/ppermute | solution.py:494
  29.1 17.8 %collective-permute-start.2 = (f32[32,128]{1,0:T(8,128)S(1)}, f32[32,128]{1,0:T(8,128)S(1)}, u32[]{:S(2)}, u32[]{:S(2)}) collective-permute-start(f32[32,128]{1,0:T(8,128)S(1)} %get-tuple-element.16), channel_id=1, source_target_pairs={{0,1},{1,0},{2,3},{3,2},{4,5},{5,4},{6,7},{7,6},{8,9},{9,8},{10,11... | collective-permute-start | bytes 49160 | tf_op jit(solution)/shard_map/ppermute | solution.py:493
  39.1 18.0 %all-to-all-start.1 = ((f32[16,25,128]{2,1,0:T(8,128)}), f32[16,25,128]{2,1,0:T(8,128)S(1)}, u32[]{:S(2)}, u32[]{:S(2)}) async-start(f32[16,25,128]{2,1,0:T(8,128)} %get-tuple-element.21._), calls=%async_computation.1 | async-start | bytes 524288 | tf_op jit(solution)/shard_map/all_to_all | solution.py:508
  42.6 9.7 %collective-permute-start.4 = (f32[4,4,128]{2,1,0:T(4,128)S(1)}, f32[4,4,128]{2,1,0:T(4,128)S(1)}, u32[]{:S(2)}, u32[]{:S(2)}) collective-permute-start(f32[4,4,128]{2,1,0:T(4,128)S(1)} %get-tuple-element.23), channel_id=1, source_target_pairs={{0,4},{4,8},{8,12},{6,2},{10,6},{14,10},{1,5},{5,9},{9,13},{7,3},{... | collective-permute-start | bytes 24584 | tf_op jit(solution)/shard_map/ppermute | solution.py:509

commit v7 on v6

--- a/solution.py
+++ b/solution.py
@@ -72,22 +72,30 @@
     )
 
 
-def edges_body(odd_ref, q_ref, first_out, second_out):
+def edges_body(odd_ref, q_ref, first_out, second_out, az_lo, az_hi):
     odd = odd_ref[0] == 1
     low, high = q_ref[:, 0], q_ref[:, CAX - 1]
     first_out[...] = jnp.where(odd, low, high)
     second_out[...] = jnp.where(odd, high, low)
+    az_lo[...] = q_ref[:, :, 0, :]
+    az_hi[...] = q_ref[:, :, CAZ - 1, :]
+
+
+def lane_row(cells_ref, first, blocks):
+    return jnp.concatenate([cells_ref[first + i : first + i + 1, :] for i in range(blocks)], axis=1)
+
+
+def equals(count, row):
+    numbers = iota((count, row.shape[1]), 0).astype(F32).astype(BF16)
+    return numbers == row.astype(F32).astype(BF16)
 
 
 def one_hot_rows(cells_ref, first, blocks):
-    cells = jnp.concatenate([cells_ref[first + i : first + i + 1, :] for i in range(blocks)], axis=1)
-    width = blocks * BLK
-    hit = iota((ROWS, width), 0) == (cells >> 7)
-    return jnp.where(hit, 1.0, 0.0).astype(BF16), cells & (CR - 1)
-
-
-def lane_row(cells_ref, first, blocks):
-    return jnp.concatenate([cells_ref[first + i : first + i + 1, :] for i in range(blocks)], axis=1) & (CR - 1)
+    cells = lane_row(cells_ref, first, blocks)
+    one, zero = jnp.ones((), BF16), jnp.zeros((), BF16)
+    half = ROWS // 2
+    parts = [jnp.where(equals(half, (cells >> 7) - half * i), one, zero) for i in range(2)]
+    return jnp.concatenate(parts, axis=0), cells & (CR - 1)
 
 
 def step(count_ref, parcel_ref, gas_ref):
@@ -119,16 +127,13 @@
     src_out, stay_out, leave_out, rad_out, gas_ref, state_ref, leave_ref,
 ):
     rad_edges(rad_ref[0], q_ref, rad_out)
-    parts = [[], []]
-    for f in range(3):
-        high, low = halves(q_ref[f + 1].reshape(ROWS, CR).T)
-        parts[0].append(high)
-        parts[1].append(low)
-    parts = [jnp.concatenate(part, axis=0) for part in parts]
+    table = jnp.concatenate(
+        [jnp.concatenate(halves(q_ref[f + 1].reshape(ROWS, CR).T), axis=1) for f in range(3)], axis=0
+    )
     spans = [(f * CR, (f + 1) * CR) for f in range(3)]
     for first in range(0, BLK_DEV, 4):
         hot, lanes = one_hot_rows(cells_ref, first, 4)
-        rows = sum(jnp.dot(part, hot, preferred_element_type=F32) for part in parts)
+        rows = jnp.dot(table, jnp.concatenate([hot, hot], axis=0), preferred_element_type=F32)
         pick(rows, first, spans, iota((CR, 4 * BLK), 0) == lanes, gas_ref)
     state, sources = step(count_ref, parcel_ref, gas_ref)
     for i in range(4):
@@ -163,7 +168,6 @@
 
 
 BAND = 24
-SHARE = 2 * FIELDS * CAX // N_AZ
 
 
 def turned(parts):
@@ -191,26 +195,21 @@
         rows = rows[:depth] + rows[depth:]
         pick(rows, first, spans, iota((CYCLES, 4 * BLK), 0) == lanes, gas_ref)
     _, sources = step(count_ref, parcel_ref, gas_ref)
-    rows = [s.astype(BF16).astype(F32) for s in sources]
-    rows = rows + [s - r for s, r in zip(sources, rows)]
-    for block in range(BLK_DEV):
-        mask = iota((CYCLES, BLK), 0) == (cells_ref[block : block + 1, :] & (CR - 1))
+    rows = [s.astype(BF16) for s in sources]
+    rows = [r.astype(F32) for r in rows] + [s - r.astype(F32) for s, r in zip(sources, rows)]
+    zero = jnp.zeros((), BF16)
+    for first in range(0, BLK_DEV, 4):
+        mask = equals(CYCLES, lane_row(cells_ref, first, 4) & (CR - 1))
         for i, row in enumerate(rows):
-            spread_ref[i * CYCLES : (i + 1) * CYCLES, block * BLK : (block + 1) * BLK] = jnp.where(
-                mask, row[block : block + 1, :], 0.0
-            ).astype(BF16)
+            row = jnp.concatenate([row[first + j : first + j + 1] for j in range(4)], axis=1).astype(BF16)
+            spread_ref[i * CYCLES : (i + 1) * CYCLES, first * BLK : (first + 4) * BLK] = jnp.where(mask, row, zero)
     total = lax.dot_general(spread_ref[...], hot_ref[...], NT, preferred_element_type=F32)
     near_out[...] = total[: 4 * CYCLES] + total[4 * CYCLES :]
 
 
 def near_body(
-    odd_ref, coef_ref, q_ref, first_ref, second_ref, tiles_ref, near_ref, send_hbm, az_ref, send_out, sems
+    odd_ref, coef_ref, first_ref, second_ref, tiles_ref, near_ref, _, __, send_hbm, send_out, sems
 ):
-    for f in range(FIELDS):
-        az_ref[f * CAX : (f + 1) * CAX] = q_ref[f, :, 0, :]
-        az_ref[(FIELDS + f) * CAX : (FIELDS + f + 1) * CAX] = q_ref[f, :, CAZ - 1, :]
-    for owner in range(N_AZ):
-        send_out[owner, LINES + 4 :, :] = az_ref[owner * SHARE : (owner + 1) * SHARE]
     copies = []
     lane = iota((CR, 2 * CAZ), 1)
     z = lane % CAZ
@@ -281,26 +280,26 @@
 
 
 def gas_body(
-    rad_ref, odd_ref, coef_ref, q_ref, first_ref, second_ref, rad_in, src_ref, cells_ref, _, sect_out, acc_ref
+    rad_ref, odd_ref, coef_ref, q_ref, first_ref, second_ref, az_prev, az_next, rad_in, src_ref, cells_ref, _,
+    sect_out, hot_ref, spread_ref,
 ):
-    width = 8
+    width = 4
+    zero = jnp.zeros((), BF16)
     for first in range(0, BLK_DEV, width):
+        cols = slice(first * BLK, (first + width) * BLK)
         hot, lanes = one_hot_rows(cells_ref, first, width)
-        mask = iota((CR, width * BLK), 0) == lanes
-        spread = [[], []]
+        hot_ref[:, cols] = hot
+        mask = equals(CR, lanes)
         for i in range(4):
             row = jnp.concatenate([src_ref[i, first + j : first + j + 1, :] for j in range(width)], axis=1)
-            high = row.astype(BF16).astype(F32)
-            spread[0].append(jnp.where(mask, high, 0.0).astype(BF16))
-            spread[1].append(jnp.where(mask, row - high, 0.0).astype(BF16))
-        total = sum(
-            lax.dot_general(hot, jnp.concatenate(part, axis=0), NT, preferred_element_type=F32)
-            for part in spread
-        )
-        if first == 0:
-            acc_ref[...] = total
-        else:
-            acc_ref[...] += total
+            high = row.astype(BF16)
+            low = (row - high.astype(F32)).astype(BF16)
+            spread_ref[i, 0:CR, cols] = jnp.where(mask, high, zero)
+            spread_ref[i, CR:, cols] = jnp.where(mask, low, zero)
+    added = []
+    for i in range(4):
+        total = lax.dot_general(hot_ref[...], spread_ref[i], NT, preferred_element_type=F32)
+        added.append(total[:, :CR] + total[:, CR:])
     rad = rad_ref[0]
     odd = odd_ref[0] == 1
     row = iota((CAZ, CR), 0)
@@ -310,14 +309,14 @@
     for f in range(FIELDS):
         c = [coef_ref[f, i] for i in range(6)]
         mid = (1.0 - c[1] - c[5]) - c[3] * metric
-        az_up = jnp.where(row == CAZ - 1, 0.0, (0.5 * (c[2] + c[3])) * metric)
-        az_down = jnp.where(row == 0, 0.0, (0.5 * (c[3] - c[2])) * metric)
+        az_up_edge, az_down_edge = (0.5 * (c[2] + c[3])) * metric, (0.5 * (c[3] - c[2])) * metric
+        az_up = jnp.where(row == CAZ - 1, 0.0, az_up_edge)
+        az_down = jnp.where(row == 0, 0.0, az_down_edge)
         ax_up, ax_down = 0.5 * (c[0] + c[1]), 0.5 * (c[1] - c[0])
         rad_up = jnp.where(lane == CR - 1, 0.0, 0.5 * (c[4] + c[5]))
         rad_down = jnp.where(lane == 0, 0.0, 0.5 * (c[5] - c[4]))
         across = 0.5 * jnp.where(rad == 0, c[4] + c[5], c[5] - c[4])
         across = jnp.where(lane == target, across, 0.0)
-        s = SOURCE_OF[f] * CR
         for a in range(CAX):
             q = q_ref[f, a]
             ahead = q_ref[f, a + 1] if a + 1 < CAX else jnp.where(odd, second_ref[f], first_ref[f])
@@ -331,8 +330,10 @@
                 + az_up * pltpu.roll(q, CAZ - 1, 0) + az_down * pltpu.roll(q, 1, 0)
                 + rad_up * pltpu.roll(q, CR - 1, 1) + rad_down * pltpu.roll(q, 1, 1)
                 + across * edge
-                + acc_ref[a * CAZ : (a + 1) * CAZ, s : s + CR]
+                + added[SOURCE_OF[f]][a * CAZ : (a + 1) * CAZ]
             )
+            sect_out[f, a, 0:1] += az_down_edge * az_prev[f, a : a + 1]
+            sect_out[f, a, CAZ - 1 : CAZ] += az_up_edge * az_next[f, a : a + 1]
 
 
 def lined(pieces, line_ref):
@@ -349,12 +350,6 @@
     send_out, onward_out, line_ref, ends_ref, piece_ref,
 ):
     onward_out[...] = moved_ref[1]
-    for home in range(N_AZ):
-        send_out[home, LINES:, :] = jnp.where(
-            az_ref[0] < N_AZ // 2,
-            got_ref[(home + 1) % N_AZ, LINES + 4 :, :],
-            got_ref[(home - 1) % N_AZ, LINES + 4 :, :],
-        )
     quad = az_ref[0] % QUADS
     low = iota((LINES, 2 * CAZ), 1) < CAZ
     line_ref[...] = jnp.zeros_like(line_ref)
@@ -396,8 +391,7 @@
 
 
 def merge_body(
-    rad_ref, odd_ref, coef_ref, sect_ref, got_ref, stay_ref, moved_ref, onward_ref,
-    gas_out, parcels_out, flip_ref, az_ref,
+    rad_ref, odd_ref, sect_ref, got_ref, stay_ref, moved_ref, onward_ref, gas_out, parcels_out, flip_ref
 ):
     odd = odd_ref[0] == 1
     parcels_out[:, 0:BLK_DEV, :] = stay_ref[...]
@@ -405,8 +399,6 @@
     parcels_out[:, BLK_DEV : BLK_DEV + MOVEB, :] = jnp.where(odd, first, second)
     parcels_out[:, BLK_DEV + MOVEB :, :] = jnp.where(odd, second, first)
     near = (iota((2 * CAZ, CR), 1) < CYCLES) & (rad_ref[0] == 0)
-    for owner in range(N_AZ):
-        az_ref[owner * SHARE : (owner + 1) * SHARE] = got_ref[owner, LINES:, :]
     tiles = []
     for pair in range(PAIRS):
         flip_ref[pair, FIELDS * CYCLES :, :] = jnp.zeros((CR - FIELDS * CYCLES, CR), F32)
@@ -415,28 +407,18 @@
                 first = f * CYCLES + quad * 4
                 flip_ref[pair, first : first + 4, :] = got_ref[pair * QUADS + quad, f * 4 : f * 4 + 4, :]
         tiles.append(flip_ref[pair].T)
-    lane = iota((1, CR), 1)
-    metric = 4.0 / ((rad_ref[0] * CR + lane).astype(F32) + 4.0)
-    metric = jnp.where((lane < CYCLES) & (rad_ref[0] == 0), 0.0, metric)
     for f in range(FIELDS):
         for pair in range(PAIRS):
             moved = pltpu.roll(tiles[pair], CR - f * CYCLES, 1) if f else tiles[pair]
             kept = sect_ref[f, 2 * pair : 2 * pair + 2].reshape(2 * CAZ, CR)
             gas_out[f, 2 * pair : 2 * pair + 2] = jnp.where(near, moved, kept).reshape(2, CAZ, CR)
-        az_up = (0.5 * (coef_ref[f, 2] + coef_ref[f, 3])) * metric
-        az_down = (0.5 * (coef_ref[f, 3] - coef_ref[f, 2])) * metric
-        after = az_up * az_ref[f * CAX : (f + 1) * CAX]
-        before = az_down * az_ref[(FIELDS + f) * CAX : (FIELDS + f + 1) * CAX]
-        for a in range(CAX):
-            gas_out[f, a, 0:1] += before[a : a + 1]
-            gas_out[f, a, CAZ - 1 : CAZ] += after[a : a + 1]
 
 
 def shards(fields, coeffs, parcels, cells, counts, moves, widths):
     rad_index = lax.axis_index("rad").astype(jnp.int32).reshape(1)
     az_index = lax.axis_index("az").astype(jnp.int32).reshape(1)
     odd = (lax.axis_index("ax").astype(jnp.int32) % 2).reshape(1)
-    n_ax, n_rad = lax.axis_size("ax"), lax.axis_size("rad")
+    n_ax, n_az, n_rad = (lax.axis_size(axis) for axis in ("ax", "az", "rad"))
     parcels = parcels.reshape(4, BLK_DEV, BLK)
     cells = cells.reshape(BLK_DEV, BLK)
     counts = counts.reshape(1)
@@ -444,14 +426,18 @@
     inner = [(i, i ^ 1) for i in range(n_ax)]
     outer = [(i, ((i + 1) ^ 1) - 1) for i in range(1, n_ax - 1)]
     along = [(i, i + 2) for i in range(0, n_ax - 2, 2)] + [(i, i - 2) for i in range(3, n_ax, 2)]
+    ahead = [(i, (i + 1) % n_az) for i in range(n_az)]
+    back = [((i + 1) % n_az, i) for i in range(n_az)]
     across = [(i, i ^ 1) for i in range(n_rad)]
     gas_shape = (FIELDS, CAX, CAZ, CR)
 
-    first, second = call(
-        edges_body, [(FIELDS, CAZ, CR)] * 2, [SMEM, VMEM], 10**6, 10**6, mib=4
+    first, second, az_lo, az_hi = call(
+        edges_body, [(FIELDS, CAZ, CR)] * 2 + [(FIELDS, CAX, CR)] * 2, [SMEM, VMEM], 10**6, 10**6, mib=4
     )(odd, fields)
     first = lax.ppermute(first, "ax", inner)
     second = lax.ppermute(second, "ax", outer)
+    az_prev = lax.ppermute(az_hi, "az", ahead)
+    az_next = lax.ppermute(az_lo, "az", back)
 
     tiles, near = call(
         near_parcels_body,
@@ -467,16 +453,15 @@
 
     (to_owner,) = call(
         near_body,
-        [(N_AZ, LINES + 4 + SHARE, 2 * CAZ)],
-        [SMEM, SMEM] + [VMEM] * 5, 10**7, 4 * 10**6,
+        [(N_AZ, LINES + 4, 2 * CAZ)],
+        [SMEM, SMEM] + [VMEM] * 4 + [ANY] * 2, 10**7, 4 * 10**6,
         [
-            pltpu.VMEM((2 * FIELDS * CAX, CR), F32),
-            pltpu.VMEM((N_AZ, LINES + 4 + SHARE, 2 * CAZ), F32),
+            pltpu.VMEM((N_AZ, LINES + 4, 2 * CAZ), F32),
             pltpu.SemaphoreType.DMA((PAIRS,)),
         ],
         mib=8,
         hbm_first=True,
-    )(odd, coeffs, fields, first, second, tiles, near)
+    )(odd, coeffs, first, second, tiles, near, az_prev, az_next)
     lines = lax.all_to_all(to_owner, "az", 0, 0, tiled=True)
 
     src, stay, leaving, rad_edge = call(
@@ -496,7 +481,7 @@
     basis, basis_turned = basis_parts()
     to_home, onward = call(
         filter_body,
-        [(N_AZ, LINES + SHARE, 2 * CAZ), (4, MOVEB, BLK)],
+        [(N_AZ, LINES, 2 * CAZ), (4, MOVEB, BLK)],
         [SMEM, SMEM] + [VMEM] * 4, 10**8, 10**6,
         [
             pltpu.VMEM((2 * BAND, NAZ), F32),
@@ -509,21 +494,18 @@
     onward = lax.ppermute(onward, "ax", along)
 
     (sect,) = call(
-        gas_body, [gas_shape], [SMEM, SMEM, SMEM] + [VMEM] * 6 + [ANY], 8 * 10**9, 4 * 10**6,
-        [pltpu.VMEM((ROWS, 4 * CR), F32)],
-        mib=16,
-    )(rad_index, odd, coeffs, fields, first, second, rad_got, src, cells, to_home)
+        gas_body, [gas_shape], [SMEM, SMEM, SMEM] + [VMEM] * 8 + [ANY], 8 * 10**9, 4 * 10**6,
+        [pltpu.VMEM((ROWS, PARCELS), BF16), pltpu.VMEM((4, 2 * CR, PARCELS), BF16)],
+        mib=24,
+    )(rad_index, odd, coeffs, fields, first, second, az_prev, az_next, rad_got, src, cells, to_home)
 
     gas_out, parcels_out = call(
         merge_body,
         [gas_shape, (4, BLK_DEV + 2 * MOVEB, BLK)],
-        [SMEM, SMEM, SMEM] + [VMEM] * 5, 10**6, 4 * 10**6,
-        [
-            pltpu.VMEM((PAIRS, CR, CR), F32),
-            pltpu.VMEM((2 * FIELDS * CAX, CR), F32),
-        ],
+        [SMEM, SMEM] + [VMEM] * 5, 10**6, 4 * 10**6,
+        [pltpu.VMEM((PAIRS, CR, CR), F32)],
         mib=8,
-    )(rad_index, odd, coeffs, sect, filtered, stay, moved, onward)
+    )(rad_index, odd, sect, filtered, stay, moved, onward)
     return gas_out, parcels_out.reshape(4, BLK_DEV + 2 * MOVEB, 1, BLK)
 
 

time: 59.7 us -> 58.7 us (0.983)
  starting transfers between devices: 23.1 us -> 26 us
  Pallas kernels: 20.6 us -> 18.3 us
  waiting for transfers between devices: 12 us -> 10.4 us
    ppermute x0 -> x2, starting transfers between devices: none -> 8.48 us  [the longest x1 5.38 us: shards(): az_next = lax.ppermute(az_lo, 'az', back)]
    all_to_all x1, starting transfers between devices: 9.31 us -> 6.17 us  [shards(): lines = lax.all_to_all(to_owner, 'az', 0, 0, tiled=True)]
    ppermute x1, starting transfers between devices: 4.18 us -> 2.46 us  [shards(): second = lax.ppermute(second, 'ax', outer)]
    all_to_all x1, waiting for transfers between devices: 4.76 us -> 3.5 us  [shards(): filtered = lax.all_to_all(to_home, 'az', 0, 0, tiled=True)]
    ppermute x1, starting transfers between devices: 4.25 us -> 3.25 us  [shards(): onward = lax.ppermute(onward, 'ax', along)]
    pallas_call x1, Pallas kernels: 3.52 us -> 2.61 us  [shards(): call(near_parcels_body, [(CR, ROWS), (4 * CYCLES, ROWS)], [SMEM] + [VMEM]...]
    pallas_call x5, Pallas kernels: 11.5 us -> 10.8 us  [the longest x1 5.42 us: shards(): call(gas_body, [gas_shape], [SMEM, SMEM, SMEM] + [VMEM] * 8 + [ANY], 8 *...]
    pallas_call x1, Pallas kernels: 5.55 us -> 4.9 us  [shards(): call(parcels_body, [(4, BLK_DEV, BLK), (4, BLK_DEV, BLK), (2, 4, MOVEB, B...]
  transfers between devices with their start and end apart: 7 -> 9, of which waited for: 3 -> 2; matrix products, arithmetic and copies ran while one was open for 0% -> 0% of each run, Pallas kernels for 28% -> 26%
where the time goes in v7:
time: 58.7 us; the launch traced here: 58.3 us
  starting transfers between devices  26 us (44%)
  Pallas kernels  18.3 us (31%)
  waiting for transfers between devices  10.4 us (18%)
  local copies, waits for them, and re-layouts  2.19 us (4%)
  between operations  1.52 us (3%)
    all_to_all x1, waiting for transfers between devices, shards(): lines = lax.all_to_all(to_owner, 'az', 0, 0, tiled=True)  6.88 us
    all_to_all x1, starting transfers between devices, shards(): lines = lax.all_to_all(to_owner, 'az', 0, 0, tiled=True)  6.17 us
    pallas_call x1, Pallas kernels, shards(): call(gas_body, [gas_shape], [SMEM, SMEM, SMEM] + [VMEM] * 8 + [ANY], 8 *...  5.42 us
    ppermute x1, starting transfers between devices, shards(): az_next = lax.ppermute(az_lo, 'az', back)  5.38 us
    pallas_call x1, Pallas kernels, shards(): call(parcels_body, [(4, BLK_DEV, BLK), (4, BLK_DEV, BLK), (2, 4, MOVEB, B...  4.9 us
    all_to_all x1, starting transfers between devices, shards(): filtered = lax.all_to_all(to_home, 'az', 0, 0, tiled=True)  3.52 us
    all_to_all x1, waiting for transfers between devices, shards(): filtered = lax.all_to_all(to_home, 'az', 0, 0, tiled=True)  3.5 us
    ppermute x1, starting transfers between devices, shards(): onward = lax.ppermute(onward, 'ax', along)  3.25 us
  transfers between devices with their start and end apart: 9, of which 2 were waited for; matrix products, arithmetic and copies ran while one was open for 0% of the time, Pallas kernels for 26%

profile of v7, /device:TPU:8, one launch (start us, length us, event | category | flops | bytes accessed | tf_op | source)
XLA Modules:
  0.0 58.3 jit_solution(16165522406886776549)
XLA Ops:
  0.6 0.0 copy-start.8
  0.7 0.0 copy-start
  0.7 1.3 %copy-done = f32[5,8,64,128]{3,2,1,0:T(8,128)S(1)} copy-done((f32[5,8,64,128]{3,2,1,0:T(8,128)S(1)}, f32[5,8,64,128]{3,2,1,0:T(8,128)}, u32[]{:S(2)}) %copy-start) | copy-done | bytes 1310744
  2.0 0.0 copy-start.1
  2.0 0.1 shard_map.104
  2.0 3.1 %collective-permute-start.2 = (f32[5,8,128]{2,1,0:T(8,128)S(1)}, f32[5,8,128]{2,1,0:T(8,128)S(1)}, u32[]{:S(2)}, u32[]{:S(2)}) collective-permute-start(f32[5,8,128]{2,1,0:T(8,128)S(1)} %get-tuple-element.18), channel_id=1, source_target_pairs={{0,16},{16,32},{32,48},{48,64},{64,80},{80,96},{96,112},{112,128},... | collective-permute-start | bytes 61448 | tf_op jit(solution)/shard_map/ppermute | solution.py:439
  5.1 5.4 %collective-permute-start.3 = (f32[5,8,128]{2,1,0:T(8,128)S(1)}, f32[5,8,128]{2,1,0:T(8,128)S(1)}, u32[]{:S(2)}, u32[]{:S(2)}) collective-permute-start(f32[5,8,128]{2,1,0:T(8,128)S(1)} %get-tuple-element.19), channel_id=1, source_target_pairs={{16,0},{32,16},{48,32},{64,48},{80,64},{96,80},{112,96},{128,112},... | collective-permute-start | bytes 61448 | tf_op jit(solution)/shard_map/ppermute | solution.py:440
  10.5 0.0 collective-permute-start
  10.5 2.5 %collective-permute-start.1 = (f32[5,64,128]{2,1,0:T(8,128)S(1)}, f32[5,64,128]{2,1,0:T(8,128)S(1)}, u32[]{:S(2)}, u32[]{:S(2)}) collective-permute-start(f32[5,64,128]{2,1,0:T(8,128)S(1)} %get-tuple-element.17), channel_id=1, source_target_pairs={{2,4},{4,2},{6,8},{8,6},{10,12},{12,10},{3,5},{5,3},{7,9},{9,7},{1... | collective-permute-start | bytes 491528 | tf_op jit(solution)/shard_map/ppermute | solution.py:438
  13.6 0.0 copy-done.8
  13.6 0.0 copy-done.1
  13.6 0.0 copy-start.6
  13.7 0.8 %copy-done.6 = f32[4,32,1,128]{3,2,1,0:T(1,128)S(1)} copy-done((f32[4,32,1,128]{3,2,1,0:T(1,128)S(1)}, f32[4,32,1,128]{3,2,1,0:T(1,128)}, u32[]{:S(2)}) %copy-start.6) | copy-done | bytes 65560
  14.5 0.0 copy-start.4
  14.5 2.6 %shard_map.106 = (f32[128,512]{1,0:T(8,128)S(1)}, f32[64,512]{1,0:T(8,128)S(1)}) custom-call(s32[1]{0:T(128)} %bitcast.11.count_ref, f32[5,8,64,128]{3,2,1,0:T(8,128)S(1)} %copy-done.1, f32[4,32,128]{2,1,0:T(8,128)S(1)} %bitcast.12, s32[32,128]{1,0:T(8,128)S(1)} %bitcast.14), custom_call_target="tpu_custom_call" | custom-call | flops 3000000000 | bytes 2000000 | tf_op jit(solution)/shard_map/pallas_call | solution.py:442
  17.1 0.0 copy-start.7
  17.1 0.0 copy-start.9
  17.1 0.0 collective-permute-done.2._.az_prev
  17.1 0.0 collective-permute-done.3.__.az_next
  17.2 0.0 collective-permute-done.first_ref
  17.2 0.0 collective-permute-done.1.second_ref
  17.2 0.0 copy-done.4
  17.2 1.7 %shard_map.107 = f32[16,24,128]{2,1,0:T(8,128)} custom-call(s32[1]{0:T(128)} %bitcast.1.odd_ref, f32[5,6]{1,0:T(8,128)S(1)} %copy-done.4, f32[5,64,128]{2,1,0:T(8,128)S(1)} %collective-permute-done.first_ref, f32[5,64,128]{2,1,0:T(8,128)S(1)} %collective-permute-done.1.second_ref, f32[128,512]{1,0:T(8,128)S(1)} %get-tuple-element.22.tiles_ref, ...), custom_call_target="tpu_custom_call" | custom-call | flops 10000000 | bytes 4000000 | tf_op jit(solution)/shard_map/pallas_call | solution.py:454
  18.9 6.2 %all-to-all-start = ((f32[16,24,128]{2,1,0:T(8,128)}), f32[16,24,128]{2,1,0:T(8,128)S(1)}, u32[]{:S(2)}, u32[]{:S(2)}) async-start(f32[16,24,128]{2,1,0:T(8,128)} %shard_map.107), calls=%async_computation | async-start | bytes 393216 | tf_op jit(solution)/shard_map/all_to_all | solution.py:465
  25.0 0.0 copy-done.7
  25.0 0.0 copy-done.9
  25.0 0.0 copy-start.2
  25.1 0.0 copy-start.3
  25.1 0.0 copy-start.5
  25.1 4.9 %shard_map.105 = (f32[4,32,128]{2,1,0:T(8,128)S(1)}, f32[4,32,128]{2,1,0:T(8,128)S(1)}, f32[2,4,4,128]{3,2,1,0:T(4,128)S(1)}, f32[32,128]{1,0:T(8,128)S(1)}) custom-call(s32[1]{0:T(128)} %bitcast.rad_ref, s32[1]{0:T(128)} %bitcast.1.odd_ref, s32[1]{0:T(128)} %bitcast.10.count_ref, s32[32]{0:T(128)S(1)} %bitcast.17, f32[5,8,64,128]{3,2,1,0:T(8,128)S(1)} %copy-done.1, ...), custom_call_target="tpu_custom_call" | custom-call | flops 6000000000 | bytes 2000000 | tf_op jit(solution)/shard_map/pallas_call | solution.py:467
  30.0 0.9 %collective-permute-start.5 = (f32[2,4,4,128]{3,2,1,0:T(4,128)S(1)}, f32[2,4,4,128]{3,2,1,0:T(4,128)S(1)}, u32[]{:S(2)}, u32[]{:S(2)}) collective-permute-start(f32[2,4,4,128]{3,2,1,0:T(4,128)S(1)} %get-tuple-element.24), channel_id=1, source_target_pairs={{0,2},{2,0},{4,6},{6,4},{8,10},{10,8},{12,14},{14,12},{1,3},{3,1},... | collective-permute-start | bytes 49160 | tf_op jit(solution)/shard_map/ppermute | solution.py:479
  30.9 1.1 %collective-permute-start.4 = (f32[32,128]{1,0:T(8,128)S(1)}, f32[32,128]{1,0:T(8,128)S(1)}, u32[]{:S(2)}, u32[]{:S(2)}) collective-permute-start(f32[32,128]{1,0:T(8,128)S(1)} %get-tuple-element.20), channel_id=1, source_target_pairs={{0,1},{1,0},{2,3},{3,2},{4,5},{5,4},{6,7},{7,6},{8,9},{9,8},{10,11... | collective-permute-start | bytes 49160 | tf_op jit(solution)/shard_map/ppermute | solution.py:478
  32.1 0.0 collective-permute-done.5.moved_ref
  32.1 6.9 %all-to-all-done.got_ref = f32[16,24,128]{2,1,0:T(8,128)S(1)} async-done(((f32[16,24,128]{2,1,0:T(8,128)}), f32[16,24,128]{2,1,0:T(8,128)S(1)}, u32[]{:S(2)}, u32[]{:S(2)}) %all-to-all-start) | async-done | bytes 196640 | tf_op jit(solution)/shard_map/all_to_all | solution.py:465
  38.9 0.0 copy-done.2
  38.9 0.0 copy-done.3
  38.9 0.0 copy-done.5
  39.0 2.1 %shard_map.108 = (f32[16,20,128]{2,1,0:T(8,128)}, f32[4,4,128]{2,1,0:T(4,128)S(1)}) custom-call(s32[1]{0:T(128)} %bitcast.6.az_ref, s32[16]{0:T(128)S(1)} %copy-done.5, bf16[256,1024]{1,0:T(8,128)(2,1)S(1)} %copy-done.3, bf16[1024,256]{1,0:T(8,128)(2,1)S(1)} %copy-done.2, f32[16,24,128]{2,1,0:T(8,128)S(1)} %all-to-all-done.got_ref, ...), custom_call_target="tpu_custom_call" | custom-call | flops 100000000 | bytes 1000000 | tf_op jit(solution)/shard_map/pallas_call | solution.py:482
  41.1 3.5 %all-to-all-start.1 = ((f32[16,20,128]{2,1,0:T(8,128)}), f32[16,20,128]{2,1,0:T(8,128)S(1)}, u32[]{:S(2)}, u32[]{:S(2)}) async-start(f32[16,20,128]{2,1,0:T(8,128)} %get-tuple-element.25._), calls=%async_computation.1 | async-start | bytes 393216 | tf_op jit(solution)/shard_map/all_to_all | solution.py:493
  44.6 3.3 %collective-permute-start.6 = (f32[4,4,128]{2,1,0:T(4,128)S(1)}, f32[4,4,128]{2,1,0:T(4,128)S(1)}, u32[]{:S(2)}, u32[]{:S(2)}) collective-permute-start(f32[4,4,128]{2,1,0:T(4,128)S(1)} %get-tuple-element.27), channel_id=1, source_target_pairs={{0,4},{4,8},{8,12},{6,2},{10,6},{14,10},{1,5},{5,9},{9,13},{7,3},{... | collective-permute-start | bytes 24584 | tf_op jit(solution)/shard_map/ppermute | solution.py:494
  47.9 0.0 collective-permute-done.4.rad_in
  47.9 5.4 %shard_map.109.sect_ref = f32[5,8,64,128]{3,2,1,0:T(8,128)S(1)} custom-call(s32[1]{0:T(128)} %bitcast.rad_ref, s32[1]{0:T(128)} %bitcast.1.odd_ref, f32[5,6]{1,0:T(8,128)S(1)} %copy-done.4, f32[5,8,64,128]{3,2,1,0:T(8,128)S(1)} %copy-done.1, f32[5,64,128]{2,1,0:T(8,128)S(1)} %collective-permute-done.first_ref, ...), custom_call_target="tpu_custom_call" | custom-call | flops 8000000000 | bytes 4000000 | tf_op jit(solution)/shard_map/pallas_call | solution.py:496
  53.3 0.0 collective-permute-done.6.onward_ref
  53.3 3.5 %all-to-all-done.1.got_ref = f32[16,20,128]{2,1,0:T(8,128)S(1)} async-done(((f32[16,20,128]{2,1,0:T(8,128)}), f32[16,20,128]{2,1,0:T(8,128)S(1)}, u32[]{:S(2)}, u32[]{:S(2)}) %all-to-all-start.1) | async-done | bytes 163872 | tf_op jit(solution)/shard_map/all_to_all | solution.py:493
  56.8 1.5 %shard_map.110 = (f32[5,8,64,128]{3,2,1,0:T(8,128)}, f32[4,40,128]{2,1,0:T(8,128)}) custom-call(s32[1]{0:T(128)} %bitcast.rad_ref, s32[1]{0:T(128)} %bitcast.1.odd_ref, f32[5,8,64,128]{3,2,1,0:T(8,128)S(1)} %shard_map.109.sect_ref, f32[16,20,128]{2,1,0:T(8,128)S(1)} %all-to-all-done.1.got_ref, f32[4,32,128]{2,1,0:T(8,128)S(1)} %get-tuple-element.26.stay_ref, ...), custom_call_target="tpu_custom_call" | custom-call | flops 1000000 | bytes 4000000 | tf_op jit(solution)/shard_map/pallas_call | solution.py:502
Async XLA Ops:
  0.6 13.0 %copy-start.8 = (s32[32,1,128]{2,1,0:T(1,128)S(1)}, s32[32,1,128]{2,1,0:T(1,128)}, u32[]{:S(2)}) copy-start(s32[32,1,128]{2,1,0:T(1,128)} %param.12) | copy-start | bytes 49156
  0.7 1.3 %copy-start = (f32[5,8,64,128]{3,2,1,0:T(8,128)S(1)}, f32[5,8,64,128]{3,2,1,0:T(8,128)}, u32[]{:S(2)}) copy-start(f32[5,8,64,128]{3,2,1,0:T(8,128)} %q_ref.7) | copy-start | bytes 3932164
  2.0 11.7 %copy-start.1 = (f32[5,8,64,128]{3,2,1,0:T(8,128)S(1)}, f32[5,8,64,128]{3,2,1,0:T(8,128)}, u32[]{:S(2)}) copy-start(f32[5,8,64,128]{3,2,1,0:T(8,128)} %q_ref.7) | copy-start | bytes 3932164
  2.0 15.1 %collective-permute-start.2 = (f32[5,8,128]{2,1,0:T(8,128)S(1)}, f32[5,8,128]{2,1,0:T(8,128)S(1)}, u32[]{:S(2)}, u32[]{:S(2)}) collective-permute-start(f32[5,8,128]{2,1,0:T(8,128)S(1)} %get-tuple-element.18), channel_id=1, source_target_pairs={{0,16},{16,32},{32,48},{48,64},{64,80},{80,96},{96,112},{112,128},... | collective-permute-start | bytes 61448 | tf_op jit(solution)/shard_map/ppermute | solution.py:439
  5.1 12.0 %collective-permute-start.3 = (f32[5,8,128]{2,1,0:T(8,128)S(1)}, f32[5,8,128]{2,1,0:T(8,128)S(1)}, u32[]{:S(2)}, u32[]{:S(2)}) collective-permute-start(f32[5,8,128]{2,1,0:T(8,128)S(1)} %get-tuple-element.19), channel_id=1, source_target_pairs={{16,0},{32,16},{48,32},{64,48},{80,64},{96,80},{112,96},{128,112},... | collective-permute-start | bytes 61448 | tf_op jit(solution)/shard_map/ppermute | solution.py:440
  10.5 6.7 %collective-permute-start = (f32[5,64,128]{2,1,0:T(8,128)S(1)}, f32[5,64,128]{2,1,0:T(8,128)S(1)}, u32[]{:S(2)}, u32[]{:S(2)}) collective-permute-start(f32[5,64,128]{2,1,0:T(8,128)S(1)} %get-tuple-element.16), channel_id=1, source_target_pairs={{0,2},{2,0},{4,6},{6,4},{8,10},{10,8},{12,14},{14,12},{1,3},{3,1},... | collective-permute-start | bytes 491528 | tf_op jit(solution)/shard_map/ppermute | solution.py:437
  10.5 6.7 %collective-permute-start.1 = (f32[5,64,128]{2,1,0:T(8,128)S(1)}, f32[5,64,128]{2,1,0:T(8,128)S(1)}, u32[]{:S(2)}, u32[]{:S(2)}) collective-permute-start(f32[5,64,128]{2,1,0:T(8,128)S(1)} %get-tuple-element.17), channel_id=1, source_target_pairs={{2,4},{4,2},{6,8},{8,6},{10,12},{12,10},{3,5},{5,3},{7,9},{9,7},{1... | collective-permute-start | bytes 491528 | tf_op jit(solution)/shard_map/ppermute | solution.py:438
  13.6 0.8 %copy-start.6 = (f32[4,32,1,128]{3,2,1,0:T(1,128)S(1)}, f32[4,32,1,128]{3,2,1,0:T(1,128)}, u32[]{:S(2)}) copy-start(f32[4,32,1,128]{3,2,1,0:T(1,128)} %param.11) | copy-start | bytes 196612
  14.5 2.7 %copy-start.4 = (f32[5,6]{1,0:T(8,128)S(1)}, f32[5,6]{1,0:T(8,128)}, u32[]{:S(2)}) copy-start(f32[5,6]{1,0:T(8,128)} %coef_ref.3) | copy-start | bytes 364
  17.1 7.9 %copy-start.7 = (f32[4,32,1,128]{3,2,1,0:T(1,128)S(1)}, f32[4,32,1,128]{3,2,1,0:T(1,128)}, u32[]{:S(2)}) copy-start(f32[4,32,1,128]{3,2,1,0:T(1,128)} %param.11) | copy-start | bytes 196612
  17.1 7.9 %copy-start.9 = (s32[32,1,1]{0,2,1:T(1,128)S(1)}, s32[32,1,1]{0,2,1:T(1,128)}, u32[]{:S(2)}) copy-start(s32[32,1,1]{0,2,1:T(1,128)} %param.14) | copy-start | bytes 388
  18.9 20.1 %all-to-all-start = ((f32[16,24,128]{2,1,0:T(8,128)}), f32[16,24,128]{2,1,0:T(8,128)S(1)}, u32[]{:S(2)}, u32[]{:S(2)}) async-start(f32[16,24,128]{2,1,0:T(8,128)} %shard_map.107), calls=%async_computation | async-start | bytes 393216 | tf_op jit(solution)/shard_map/all_to_all | solution.py:465
  25.0 13.9 %copy-start.2 = (bf16[1024,256]{1,0:T(8,128)(2,1)S(1)}, bf16[1024,256]{1,0:T(8,128)(2,1)}, u32[]{:S(2)}) copy-start(bf16[1024,256]{1,0:T(8,128)(2,1)} %constant.31.clone.turned_ref) | copy-start | bytes 1572868
  25.1 13.9 %copy-start.3 = (bf16[256,1024]{1,0:T(8,128)(2,1)S(1)}, bf16[256,1024]{1,0:T(8,128)(2,1)}, u32[]{:S(2)}) copy-start(bf16[256,1024]{1,0:T(8,128)(2,1)} %constant.30.clone.basis_ref) | copy-start | bytes 1572868
  25.1 13.9 %copy-start.5 = (s32[16]{0:T(128)S(1)}, s32[16]{0:T(128)}, u32[]{:S(2)}) copy-start(s32[16]{0:T(128)} %width_ref.1) | copy-start | bytes 196
  30.0 2.1 %collective-permute-start.5 = (f32[2,4,4,128]{3,2,1,0:T(4,128)S(1)}, f32[2,4,4,128]{3,2,1,0:T(4,128)S(1)}, u32[]{:S(2)}, u32[]{:S(2)}) collective-permute-start(f32[2,4,4,128]{3,2,1,0:T(4,128)S(1)} %get-tuple-element.24), channel_id=1, source_target_pairs={{0,2},{2,0},{4,6},{6,4},{8,10},{10,8},{12,14},{14,12},{1,3},{3,1},... | collective-permute-start | bytes 49160 | tf_op jit(solution)/shard_map/ppermute | solution.py:479
  30.9 17.0 %collective-permute-start.4 = (f32[32,128]{1,0:T(8,128)S(1)}, f32[32,128]{1,0:T(8,128)S(1)}, u32[]{:S(2)}, u32[]{:S(2)}) collective-permute-start(f32[32,128]{1,0:T(8,128)S(1)} %get-tuple-element.20), channel_id=1, source_target_pairs={{0,1},{1,0},{2,3},{3,2},{4,5},{5,4},{6,7},{7,6},{8,9},{9,8},{10,11... | collective-permute-start | bytes 49160 | tf_op jit(solution)/shard_map/ppermute | solution.py:478
  41.1 15.7 %all-to-all-start.1 = ((f32[16,20,128]{2,1,0:T(8,128)}), f32[16,20,128]{2,1,0:T(8,128)S(1)}, u32[]{:S(2)}, u32[]{:S(2)}) async-start(f32[16,20,128]{2,1,0:T(8,128)} %get-tuple-element.25._), calls=%async_computation.1 | async-start | bytes 393216 | tf_op jit(solution)/shard_map/all_to_all | solution.py:493
  44.6 8.7 %collective-permute-start.6 = (f32[4,4,128]{2,1,0:T(4,128)S(1)}, f32[4,4,128]{2,1,0:T(4,128)S(1)}, u32[]{:S(2)}, u32[]{:S(2)}) collective-permute-start(f32[4,4,128]{2,1,0:T(4,128)S(1)} %get-tuple-element.27), channel_id=1, source_target_pairs={{0,4},{4,8},{8,12},{6,2},{10,6},{14,10},{1,5},{5,9},{9,13},{7,3},{... | collective-permute-start | bytes 24584 | tf_op jit(solution)/shard_map/ppermute | solution.py:494

commit v8 on v7

--- a/solution.py
+++ b/solution.py
@@ -208,7 +208,7 @@
 
 
 def near_body(
-    odd_ref, coef_ref, first_ref, second_ref, tiles_ref, near_ref, _, __, send_hbm, send_out, sems
+    odd_ref, coef_ref, first_ref, second_ref, tiles_ref, near_ref, send_hbm, send_out, sems
 ):
     copies = []
     lane = iota((CR, 2 * CAZ), 1)
@@ -285,28 +285,31 @@
 ):
     width = 4
     zero = jnp.zeros((), BF16)
-    for first in range(0, BLK_DEV, width):
-        cols = slice(first * BLK, (first + width) * BLK)
-        hot, lanes = one_hot_rows(cells_ref, first, width)
-        hot_ref[:, cols] = hot
-        mask = equals(CR, lanes)
-        for i in range(4):
+
+    def scattered(i):
+        for first in range(0, BLK_DEV, width):
+            cols = slice(first * BLK, (first + width) * BLK)
+            if i == 0:
+                hot_ref[:, cols] = one_hot_rows(cells_ref, first, width)[0]
+            mask = equals(CR, lane_row(cells_ref, first, width) & (CR - 1))
             row = jnp.concatenate([src_ref[i, first + j : first + j + 1, :] for j in range(width)], axis=1)
             high = row.astype(BF16)
             low = (row - high.astype(F32)).astype(BF16)
             spread_ref[i, 0:CR, cols] = jnp.where(mask, high, zero)
             spread_ref[i, CR:, cols] = jnp.where(mask, low, zero)
-    added = []
-    for i in range(4):
         total = lax.dot_general(hot_ref[...], spread_ref[i], NT, preferred_element_type=F32)
-        added.append(total[:, :CR] + total[:, CR:])
+        return total[:, :CR] + total[:, CR:]
+
     rad = rad_ref[0]
     odd = odd_ref[0] == 1
     row = iota((CAZ, CR), 0)
     lane = iota((1, CR), 1)
     metric = 4.0 / ((rad * CR + lane).astype(F32) + 4.0)
     target = jnp.where(rad == 0, CR - 1, 0)
-    for f in range(FIELDS):
+    added = {0: scattered(0)}
+    for f in (0, 4, 1, 2, 3):
+        if f in (0, 1, 2):
+            added[f + 1] = scattered(f + 1)
         c = [coef_ref[f, i] for i in range(6)]
         mid = (1.0 - c[1] - c[5]) - c[3] * metric
         az_up_edge, az_down_edge = (0.5 * (c[2] + c[3])) * metric, (0.5 * (c[3] - c[2])) * metric
@@ -454,14 +457,14 @@
     (to_owner,) = call(
         near_body,
         [(N_AZ, LINES + 4, 2 * CAZ)],
-        [SMEM, SMEM] + [VMEM] * 4 + [ANY] * 2, 10**7, 4 * 10**6,
+        [SMEM, SMEM] + [VMEM] * 4, 10**7, 4 * 10**6,
         [
             pltpu.VMEM((N_AZ, LINES + 4, 2 * CAZ), F32),
             pltpu.SemaphoreType.DMA((PAIRS,)),
         ],
         mib=8,
         hbm_first=True,
-    )(odd, coeffs, first, second, tiles, near, az_prev, az_next)
+    )(odd, coeffs, first, second, tiles, near)
     lines = lax.all_to_all(to_owner, "az", 0, 0, tiled=True)
 
     src, stay, leaving, rad_edge = call(

time: 58.7 us -> 57.5 us (0.980)
  waiting for transfers between devices: 10.4 us -> 4.81 us
  starting transfers between devices: 26 us -> 30.4 us
    all_to_all x1, waiting for transfers between devices: 6.88 us -> 1.76 us  [shards(): lines = lax.all_to_all(to_owner, 'az', 0, 0, tiled=True)]
    all_to_all x1, starting transfers between devices: 6.17 us -> 9.44 us  [shards(): lines = lax.all_to_all(to_owner, 'az', 0, 0, tiled=True)]
    ppermute x1, starting transfers between devices: 5.38 us -> 2.5 us  [shards(): az_next = lax.ppermute(az_lo, 'az', back)]
    all_to_all x1, starting transfers between devices: 3.52 us -> 6.08 us  [shards(): filtered = lax.all_to_all(to_home, 'az', 0, 0, tiled=True)]
    ppermute x1, starting transfers between devices: 2.46 us -> 4.18 us  [shards(): second = lax.ppermute(second, 'ax', outer)]
where the time goes in v8:
time: 57.5 us; the launch traced here: 57.2 us
  starting transfers between devices  30.4 us (53%)
  Pallas kernels  18.3 us (32%)
  waiting for transfers between devices  4.81 us (8%)
  local copies, waits for them, and re-layouts  2.19 us (4%)
  between operations  1.52 us (3%)
    all_to_all x1, starting transfers between devices, shards(): lines = lax.all_to_all(to_owner, 'az', 0, 0, tiled=True)  9.44 us
    all_to_all x1, starting transfers between devices, shards(): filtered = lax.all_to_all(to_home, 'az', 0, 0, tiled=True)  6.08 us
    pallas_call x1, Pallas kernels, shards(): call(gas_body, [gas_shape], [SMEM, SMEM, SMEM] + [VMEM] * 8 + [ANY], 8 *...  5.43 us
    pallas_call x1, Pallas kernels, shards(): call(parcels_body, [(4, BLK_DEV, BLK), (4, BLK_DEV, BLK), (2, 4, MOVEB, B...  4.89 us
    ppermute x1, starting transfers between devices, shards(): second = lax.ppermute(second, 'ax', outer)  4.18 us
    ppermute x1, starting transfers between devices, shards(): onward = lax.ppermute(onward, 'ax', along)  3.37 us
    ppermute x1, starting transfers between devices, shards(): az_prev = lax.ppermute(az_hi, 'az', ahead)  3.14 us
    all_to_all x1, waiting for transfers between devices, shards(): filtered = lax.all_to_all(to_home, 'az', 0, 0, tiled=True)  3.03 us
  transfers between devices with their start and end apart: 9, of which 2 were waited for; matrix products, arithmetic and copies ran while one was open for 0% of the time, Pallas kernels for 26%

profile of v8, /device:TPU:8, one launch (start us, length us, event | category | flops | bytes accessed | tf_op | source)
XLA Modules:
  0.0 57.2 jit_solution(2754302792408204115)
XLA Ops:
  0.6 0.0 copy-start.8
  0.7 0.0 copy-start
  0.7 1.3 %copy-done = f32[5,8,64,128]{3,2,1,0:T(8,128)S(1)} copy-done((f32[5,8,64,128]{3,2,1,0:T(8,128)S(1)}, f32[5,8,64,128]{3,2,1,0:T(8,128)}, u32[]{:S(2)}) %copy-start) | copy-done | bytes 1310744
  2.0 0.0 copy-start.1
  2.0 0.1 shard_map.104
  2.0 0.1 collective-permute-start
  2.1 4.2 %collective-permute-start.1 = (f32[5,64,128]{2,1,0:T(8,128)S(1)}, f32[5,64,128]{2,1,0:T(8,128)S(1)}, u32[]{:S(2)}, u32[]{:S(2)}) collective-permute-start(f32[5,64,128]{2,1,0:T(8,128)S(1)} %get-tuple-element.17), channel_id=1, source_target_pairs={{2,4},{4,2},{6,8},{8,6},{10,12},{12,10},{3,5},{5,3},{7,9},{9,7},{1... | collective-permute-start | bytes 491528 | tf_op jit(solution)/shard_map/ppermute | solution.py:441
  7.0 0.0 copy-done.8
  7.0 0.0 copy-done.1
  7.0 0.0 copy-start.6
  7.0 0.8 %copy-done.6 = f32[4,32,1,128]{3,2,1,0:T(1,128)S(1)} copy-done((f32[4,32,1,128]{3,2,1,0:T(1,128)S(1)}, f32[4,32,1,128]{3,2,1,0:T(1,128)}, u32[]{:S(2)}) %copy-start.6) | copy-done | bytes 65560
  7.8 0.0 copy-start.4
  7.8 2.6 %shard_map.106 = (f32[128,512]{1,0:T(8,128)S(1)}, f32[64,512]{1,0:T(8,128)S(1)}) custom-call(s32[1]{0:T(128)} %bitcast.11.count_ref, f32[5,8,64,128]{3,2,1,0:T(8,128)S(1)} %copy-done.1, f32[4,32,128]{2,1,0:T(8,128)S(1)} %bitcast.12, s32[32,128]{1,0:T(8,128)S(1)} %bitcast.14), custom_call_target="tpu_custom_call" | custom-call | flops 3000000000 | bytes 2000000 | tf_op jit(solution)/shard_map/pallas_call | solution.py:445
  10.4 0.0 copy-start.7
  10.5 0.0 copy-start.9
  10.5 0.0 collective-permute-done.first_ref
  10.5 0.0 collective-permute-done.1.second_ref
  10.5 0.0 copy-done.4
  10.5 1.7 %shard_map.107 = f32[16,24,128]{2,1,0:T(8,128)} custom-call(s32[1]{0:T(128)} %bitcast.1.odd_ref, f32[5,6]{1,0:T(8,128)S(1)} %copy-done.4, f32[5,64,128]{2,1,0:T(8,128)S(1)} %collective-permute-done.first_ref, f32[5,64,128]{2,1,0:T(8,128)S(1)} %collective-permute-done.1.second_ref, f32[128,512]{1,0:T(8,128)S(1)} %get-tuple-element.22.tiles_ref, ...), custom_call_target="tpu_custom_call" | custom-call | flops 10000000 | bytes 4000000 | tf_op jit(solution)/shard_map/pallas_call | solution.py:457
  12.2 9.4 %all-to-all-start = ((f32[16,24,128]{2,1,0:T(8,128)}), f32[16,24,128]{2,1,0:T(8,128)S(1)}, u32[]{:S(2)}, u32[]{:S(2)}) async-start(f32[16,24,128]{2,1,0:T(8,128)} %shard_map.107), calls=%async_computation | async-start | bytes 393216 | tf_op jit(solution)/shard_map/all_to_all | solution.py:468
  21.6 0.0 copy-done.7
  21.6 0.0 copy-done.9
  21.6 0.0 copy-start.2
  21.6 0.0 copy-start.3
  21.7 0.0 copy-start.5
  21.7 4.9 %shard_map.105 = (f32[4,32,128]{2,1,0:T(8,128)S(1)}, f32[4,32,128]{2,1,0:T(8,128)S(1)}, f32[2,4,4,128]{3,2,1,0:T(4,128)S(1)}, f32[32,128]{1,0:T(8,128)S(1)}) custom-call(s32[1]{0:T(128)} %bitcast.rad_ref, s32[1]{0:T(128)} %bitcast.1.odd_ref, s32[1]{0:T(128)} %bitcast.10.count_ref, s32[32]{0:T(128)S(1)} %bitcast.17, f32[5,8,64,128]{3,2,1,0:T(8,128)S(1)} %copy-done.1, ...), custom_call_target="tpu_custom_call" | custom-call | flops 6000000000 | bytes 2000000 | tf_op jit(solution)/shard_map/pallas_call | solution.py:470
  26.6 1.0 %collective-permute-start.5 = (f32[2,4,4,128]{3,2,1,0:T(4,128)S(1)}, f32[2,4,4,128]{3,2,1,0:T(4,128)S(1)}, u32[]{:S(2)}, u32[]{:S(2)}) collective-permute-start(f32[2,4,4,128]{3,2,1,0:T(4,128)S(1)} %get-tuple-element.24), channel_id=1, source_target_pairs={{0,2},{2,0},{4,6},{6,4},{8,10},{10,8},{12,14},{14,12},{1,3},{3,1},... | collective-permute-start | bytes 49160 | tf_op jit(solution)/shard_map/ppermute | solution.py:482
  27.5 3.1 %collective-permute-start.2 = (f32[5,8,128]{2,1,0:T(8,128)S(1)}, f32[5,8,128]{2,1,0:T(8,128)S(1)}, u32[]{:S(2)}, u32[]{:S(2)}) collective-permute-start(f32[5,8,128]{2,1,0:T(8,128)S(1)} %get-tuple-element.18), channel_id=1, source_target_pairs={{0,16},{16,32},{32,48},{48,64},{64,80},{80,96},{96,112},{112,128},... | collective-permute-start | bytes 61448 | tf_op jit(solution)/shard_map/ppermute | solution.py:442
  30.7 2.5 %collective-permute-start.3 = (f32[5,8,128]{2,1,0:T(8,128)S(1)}, f32[5,8,128]{2,1,0:T(8,128)S(1)}, u32[]{:S(2)}, u32[]{:S(2)}) collective-permute-start(f32[5,8,128]{2,1,0:T(8,128)S(1)} %get-tuple-element.19), channel_id=1, source_target_pairs={{16,0},{32,16},{48,32},{64,48},{80,64},{96,80},{112,96},{128,112},... | collective-permute-start | bytes 61448 | tf_op jit(solution)/shard_map/ppermute | solution.py:443
  33.2 0.6 %collective-permute-start.4 = (f32[32,128]{1,0:T(8,128)S(1)}, f32[32,128]{1,0:T(8,128)S(1)}, u32[]{:S(2)}, u32[]{:S(2)}) collective-permute-start(f32[32,128]{1,0:T(8,128)S(1)} %get-tuple-element.20), channel_id=1, source_target_pairs={{0,1},{1,0},{2,3},{3,2},{4,5},{5,4},{6,7},{7,6},{8,9},{9,8},{10,11... | collective-permute-start | bytes 49160 | tf_op jit(solution)/shard_map/ppermute | solution.py:481
  33.8 0.0 collective-permute-done.5.moved_ref
  33.8 1.8 %all-to-all-done.got_ref = f32[16,24,128]{2,1,0:T(8,128)S(1)} async-done(((f32[16,24,128]{2,1,0:T(8,128)}), f32[16,24,128]{2,1,0:T(8,128)S(1)}, u32[]{:S(2)}, u32[]{:S(2)}) %all-to-all-start) | async-done | bytes 196640 | tf_op jit(solution)/shard_map/all_to_all | solution.py:468
  35.5 0.0 copy-done.2
  35.5 0.0 copy-done.3
  35.5 0.0 copy-done.5
  35.5 2.1 %shard_map.108 = (f32[16,20,128]{2,1,0:T(8,128)}, f32[4,4,128]{2,1,0:T(4,128)S(1)}) custom-call(s32[1]{0:T(128)} %bitcast.6.az_ref, s32[16]{0:T(128)S(1)} %copy-done.5, bf16[256,1024]{1,0:T(8,128)(2,1)S(1)} %copy-done.3, bf16[1024,256]{1,0:T(8,128)(2,1)S(1)} %copy-done.2, f32[16,24,128]{2,1,0:T(8,128)S(1)} %all-to-all-done.got_ref, ...), custom_call_target="tpu_custom_call" | custom-call | flops 100000000 | bytes 1000000 | tf_op jit(solution)/shard_map/pallas_call | solution.py:485
  37.7 6.1 %all-to-all-start.1 = ((f32[16,20,128]{2,1,0:T(8,128)}), f32[16,20,128]{2,1,0:T(8,128)S(1)}, u32[]{:S(2)}, u32[]{:S(2)}) async-start(f32[16,20,128]{2,1,0:T(8,128)} %get-tuple-element.25._), calls=%async_computation.1 | async-start | bytes 393216 | tf_op jit(solution)/shard_map/all_to_all | solution.py:496
  43.8 3.4 %collective-permute-start.6 = (f32[4,4,128]{2,1,0:T(4,128)S(1)}, f32[4,4,128]{2,1,0:T(4,128)S(1)}, u32[]{:S(2)}, u32[]{:S(2)}) collective-permute-start(f32[4,4,128]{2,1,0:T(4,128)S(1)} %get-tuple-element.27), channel_id=1, source_target_pairs={{0,4},{4,8},{8,12},{6,2},{10,6},{14,10},{1,5},{5,9},{9,13},{7,3},{... | collective-permute-start | bytes 24584 | tf_op jit(solution)/shard_map/ppermute | solution.py:497
  47.2 0.0 collective-permute-done.4.rad_in
  47.2 0.0 collective-permute-done.2.az_prev
  47.2 0.0 collective-permute-done.3.az_next
  47.2 5.4 %shard_map.109.sect_ref = f32[5,8,64,128]{3,2,1,0:T(8,128)S(1)} custom-call(s32[1]{0:T(128)} %bitcast.rad_ref, s32[1]{0:T(128)} %bitcast.1.odd_ref, f32[5,6]{1,0:T(8,128)S(1)} %copy-done.4, f32[5,8,64,128]{3,2,1,0:T(8,128)S(1)} %copy-done.1, f32[5,64,128]{2,1,0:T(8,128)S(1)} %collective-permute-done.first_ref, ...), custom_call_target="tpu_custom_call" | custom-call | flops 8000000000 | bytes 4000000 | tf_op jit(solution)/shard_map/pallas_call | solution.py:499
  52.6 0.0 collective-permute-done.6.onward_ref
  52.6 3.0 %all-to-all-done.1.got_ref = f32[16,20,128]{2,1,0:T(8,128)S(1)} async-done(((f32[16,20,128]{2,1,0:T(8,128)}), f32[16,20,128]{2,1,0:T(8,128)S(1)}, u32[]{:S(2)}, u32[]{:S(2)}) %all-to-all-start.1) | async-done | bytes 163872 | tf_op jit(solution)/shard_map/all_to_all | solution.py:496
  55.7 1.5 %shard_map.110 = (f32[5,8,64,128]{3,2,1,0:T(8,128)}, f32[4,40,128]{2,1,0:T(8,128)}) custom-call(s32[1]{0:T(128)} %bitcast.rad_ref, s32[1]{0:T(128)} %bitcast.1.odd_ref, f32[5,8,64,128]{3,2,1,0:T(8,128)S(1)} %shard_map.109.sect_ref, f32[16,20,128]{2,1,0:T(8,128)S(1)} %all-to-all-done.1.got_ref, f32[4,32,128]{2,1,0:T(8,128)S(1)} %get-tuple-element.26.stay_ref, ...), custom_call_target="tpu_custom_call" | custom-call | flops 1000000 | bytes 4000000 | tf_op jit(solution)/shard_map/pallas_call | solution.py:505
Async XLA Ops:
  0.6 6.3 %copy-start.8 = (s32[32,1,128]{2,1,0:T(1,128)S(1)}, s32[32,1,128]{2,1,0:T(1,128)}, u32[]{:S(2)}) copy-start(s32[32,1,128]{2,1,0:T(1,128)} %param.12) | copy-start | bytes 49156
  0.7 1.3 %copy-start = (f32[5,8,64,128]{3,2,1,0:T(8,128)S(1)}, f32[5,8,64,128]{3,2,1,0:T(8,128)}, u32[]{:S(2)}) copy-start(f32[5,8,64,128]{3,2,1,0:T(8,128)} %q_ref.7) | copy-start | bytes 3932164
  2.0 5.0 %copy-start.1 = (f32[5,8,64,128]{3,2,1,0:T(8,128)S(1)}, f32[5,8,64,128]{3,2,1,0:T(8,128)}, u32[]{:S(2)}) copy-start(f32[5,8,64,128]{3,2,1,0:T(8,128)} %q_ref.7) | copy-start | bytes 3932164
  2.0 8.4 %collective-permute-start = (f32[5,64,128]{2,1,0:T(8,128)S(1)}, f32[5,64,128]{2,1,0:T(8,128)S(1)}, u32[]{:S(2)}, u32[]{:S(2)}) collective-permute-start(f32[5,64,128]{2,1,0:T(8,128)S(1)} %get-tuple-element.16), channel_id=1, source_target_pairs={{0,2},{2,0},{4,6},{6,4},{8,10},{10,8},{12,14},{14,12},{1,3},{3,1},... | collective-permute-start | bytes 491528 | tf_op jit(solution)/shard_map/ppermute | solution.py:440
  2.1 8.4 %collective-permute-start.1 = (f32[5,64,128]{2,1,0:T(8,128)S(1)}, f32[5,64,128]{2,1,0:T(8,128)S(1)}, u32[]{:S(2)}, u32[]{:S(2)}) collective-permute-start(f32[5,64,128]{2,1,0:T(8,128)S(1)} %get-tuple-element.17), channel_id=1, source_target_pairs={{2,4},{4,2},{6,8},{8,6},{10,12},{12,10},{3,5},{5,3},{7,9},{9,7},{1... | collective-permute-start | bytes 491528 | tf_op jit(solution)/shard_map/ppermute | solution.py:441
  7.0 0.8 %copy-start.6 = (f32[4,32,1,128]{3,2,1,0:T(1,128)S(1)}, f32[4,32,1,128]{3,2,1,0:T(1,128)}, u32[]{:S(2)}) copy-start(f32[4,32,1,128]{3,2,1,0:T(1,128)} %param.11) | copy-start | bytes 196612
  7.8 2.7 %copy-start.4 = (f32[5,6]{1,0:T(8,128)S(1)}, f32[5,6]{1,0:T(8,128)}, u32[]{:S(2)}) copy-start(f32[5,6]{1,0:T(8,128)} %coef_ref.3) | copy-start | bytes 364
  10.4 11.2 %copy-start.7 = (f32[4,32,1,128]{3,2,1,0:T(1,128)S(1)}, f32[4,32,1,128]{3,2,1,0:T(1,128)}, u32[]{:S(2)}) copy-start(f32[4,32,1,128]{3,2,1,0:T(1,128)} %param.11) | copy-start | bytes 196612
  10.5 11.2 %copy-start.9 = (s32[32,1,1]{0,2,1:T(1,128)S(1)}, s32[32,1,1]{0,2,1:T(1,128)}, u32[]{:S(2)}) copy-start(s32[32,1,1]{0,2,1:T(1,128)} %param.14) | copy-start | bytes 388
  12.2 23.4 %all-to-all-start = ((f32[16,24,128]{2,1,0:T(8,128)}), f32[16,24,128]{2,1,0:T(8,128)S(1)}, u32[]{:S(2)}, u32[]{:S(2)}) async-start(f32[16,24,128]{2,1,0:T(8,128)} %shard_map.107), calls=%async_computation | async-start | bytes 393216 | tf_op jit(solution)/shard_map/all_to_all | solution.py:468
  21.6 13.9 %copy-start.2 = (bf16[1024,256]{1,0:T(8,128)(2,1)S(1)}, bf16[1024,256]{1,0:T(8,128)(2,1)}, u32[]{:S(2)}) copy-start(bf16[1024,256]{1,0:T(8,128)(2,1)} %constant.31.clone.turned_ref) | copy-start | bytes 1572868
  21.6 13.9 %copy-start.3 = (bf16[256,1024]{1,0:T(8,128)(2,1)S(1)}, bf16[256,1024]{1,0:T(8,128)(2,1)}, u32[]{:S(2)}) copy-start(bf16[256,1024]{1,0:T(8,128)(2,1)} %constant.30.clone.basis_ref) | copy-start | bytes 1572868
  21.7 13.9 %copy-start.5 = (s32[16]{0:T(128)S(1)}, s32[16]{0:T(128)}, u32[]{:S(2)}) copy-start(s32[16]{0:T(128)} %width_ref.1) | copy-start | bytes 196
  26.6 7.2 %collective-permute-start.5 = (f32[2,4,4,128]{3,2,1,0:T(4,128)S(1)}, f32[2,4,4,128]{3,2,1,0:T(4,128)S(1)}, u32[]{:S(2)}, u32[]{:S(2)}) collective-permute-start(f32[2,4,4,128]{3,2,1,0:T(4,128)S(1)} %get-tuple-element.24), channel_id=1, source_target_pairs={{0,2},{2,0},{4,6},{6,4},{8,10},{10,8},{12,14},{14,12},{1,3},{3,1},... | collective-permute-start | bytes 49160 | tf_op jit(solution)/shard_map/ppermute | solution.py:482
  27.5 19.6 %collective-permute-start.2 = (f32[5,8,128]{2,1,0:T(8,128)S(1)}, f32[5,8,128]{2,1,0:T(8,128)S(1)}, u32[]{:S(2)}, u32[]{:S(2)}) collective-permute-start(f32[5,8,128]{2,1,0:T(8,128)S(1)} %get-tuple-element.18), channel_id=1, source_target_pairs={{0,16},{16,32},{32,48},{48,64},{64,80},{80,96},{96,112},{112,128},... | collective-permute-start | bytes 61448 | tf_op jit(solution)/shard_map/ppermute | solution.py:442
  30.7 16.5 %collective-permute-start.3 = (f32[5,8,128]{2,1,0:T(8,128)S(1)}, f32[5,8,128]{2,1,0:T(8,128)S(1)}, u32[]{:S(2)}, u32[]{:S(2)}) collective-permute-start(f32[5,8,128]{2,1,0:T(8,128)S(1)} %get-tuple-element.19), channel_id=1, source_target_pairs={{16,0},{32,16},{48,32},{64,48},{80,64},{96,80},{112,96},{128,112},... | collective-permute-start | bytes 61448 | tf_op jit(solution)/shard_map/ppermute | solution.py:443
  33.2 14.0 %collective-permute-start.4 = (f32[32,128]{1,0:T(8,128)S(1)}, f32[32,128]{1,0:T(8,128)S(1)}, u32[]{:S(2)}, u32[]{:S(2)}) collective-permute-start(f32[32,128]{1,0:T(8,128)S(1)} %get-tuple-element.20), channel_id=1, source_target_pairs={{0,1},{1,0},{2,3},{3,2},{4,5},{5,4},{6,7},{7,6},{8,9},{9,8},{10,11... | collective-permute-start | bytes 49160 | tf_op jit(solution)/shard_map/ppermute | solution.py:481
  37.7 18.0 %all-to-all-start.1 = ((f32[16,20,128]{2,1,0:T(8,128)}), f32[16,20,128]{2,1,0:T(8,128)S(1)}, u32[]{:S(2)}, u32[]{:S(2)}) async-start(f32[16,20,128]{2,1,0:T(8,128)} %get-tuple-element.25._), calls=%async_computation.1 | async-start | bytes 393216 | tf_op jit(solution)/shard_map/all_to_all | solution.py:496
  43.8 8.8 %collective-permute-start.6 = (f32[4,4,128]{2,1,0:T(4,128)S(1)}, f32[4,4,128]{2,1,0:T(4,128)S(1)}, u32[]{:S(2)}, u32[]{:S(2)}) collective-permute-start(f32[4,4,128]{2,1,0:T(4,128)S(1)} %get-tuple-element.27), channel_id=1, source_target_pairs={{0,4},{4,8},{8,12},{6,2},{10,6},{14,10},{1,5},{5,9},{9,13},{7,3},{... | collective-permute-start | bytes 24584 | tf_op jit(solution)/shard_map/ppermute | solution.py:497

commit v9 on v8

--- a/solution.py
+++ b/solution.py
@@ -72,13 +72,14 @@
     )
 
 
-def edges_body(odd_ref, q_ref, first_out, second_out, az_lo, az_hi):
-    odd = odd_ref[0] == 1
+def edges_body(odd_ref, az_ref, q_ref, first_out, second_out, az_first, az_second):
+    odd, odd_az = odd_ref[0] == 1, az_ref[0] % 2 == 1
     low, high = q_ref[:, 0], q_ref[:, CAX - 1]
     first_out[...] = jnp.where(odd, low, high)
     second_out[...] = jnp.where(odd, high, low)
-    az_lo[...] = q_ref[:, :, 0, :]
-    az_hi[...] = q_ref[:, :, CAZ - 1, :]
+    low, high = q_ref[:, :, 0, :], q_ref[:, :, CAZ - 1, :]
+    az_first[...] = jnp.where(odd_az, low, high)
+    az_second[...] = jnp.where(odd_az, high, low)
 
 
 def lane_row(cells_ref, first, blocks):
@@ -131,35 +132,31 @@
         [jnp.concatenate(halves(q_ref[f + 1].reshape(ROWS, CR).T), axis=1) for f in range(3)], axis=0
     )
     spans = [(f * CR, (f + 1) * CR) for f in range(3)]
+    ready = one_hot_rows(cells_ref, 0, 4)
     for first in range(0, BLK_DEV, 4):
-        hot, lanes = one_hot_rows(cells_ref, first, 4)
+        hot, lanes = ready
         rows = jnp.dot(table, jnp.concatenate([hot, hot], axis=0), preferred_element_type=F32)
+        if first + 4 < BLK_DEV:
+            ready = one_hot_rows(cells_ref, first + 4, 4)
         pick(rows, first, spans, iota((CR, 4 * BLK), 0) == lanes, gas_ref)
     state, sources = step(count_ref, parcel_ref, gas_ref)
     for i in range(4):
         src_out[i] = sources[i]
         state_ref[i] = state[i]
     leave_ref[...] = jnp.zeros_like(leave_ref)
-
-    def place(block, ranks):
-        up, down = ranks
+    up, down, spare = jnp.int32(0), jnp.int32(0), 2 * MOVEB - 1
+    for block in range(BLK_DEV):
         move = move_ref[block]
-        row = state_ref[:, pl.ds(block, 1), :]
-        stay_out[:, pl.ds(block, 1), :] = jnp.where(move == 0, row, 0.0)
-
-        @pl.when(move == 1)
-        def _():
-            leave_ref[0, :, pl.ds(jnp.minimum(up, MOVEB - 1), 1), :] = row
-
-        @pl.when(move == -1)
-        def _():
-            leave_ref[1, :, pl.ds(jnp.minimum(down, MOVEB - 1), 1), :] = row
-
-        return up + (move == 1).astype(jnp.int32), down + (move == -1).astype(jnp.int32)
-
-    lax.fori_loop(0, BLK_DEV, place, (jnp.int32(0), jnp.int32(0)))
+        row = state_ref[:, block : block + 1, :]
+        stay_out[:, block : block + 1, :] = jnp.where(move == 0, row, 0.0)
+        to_up = jnp.where(move == 1, jnp.minimum(up, MOVEB - 1), spare)
+        to_down = jnp.where(move == -1, jnp.minimum(down, MOVEB - 1), spare)
+        leave_ref[0, :, pl.ds(to_up, 1), :] = row
+        leave_ref[1, :, pl.ds(to_down, 1), :] = row
+        up = up + jnp.where(move == 1, 1, 0)
+        down = down + jnp.where(move == -1, 1, 0)
     odd = odd_ref[0] == 1
-    up, down = leave_ref[0], leave_ref[1]
+    up, down = leave_ref[0, :, :MOVEB], leave_ref[1, :, :MOVEB]
     leave_out[0] = jnp.where(odd, down, up)
     leave_out[1] = jnp.where(odd, up, down)
 
@@ -280,7 +277,8 @@
 
 
 def gas_body(
-    rad_ref, odd_ref, coef_ref, q_ref, first_ref, second_ref, az_prev, az_next, rad_in, src_ref, cells_ref, _,
+    rad_ref, odd_ref, az_ref, coef_ref, q_ref, first_ref, second_ref, az_first, az_second, rad_in, src_ref,
+    cells_ref, _,
     sect_out, hot_ref, spread_ref,
 ):
     width = 4
@@ -306,6 +304,9 @@
     lane = iota((1, CR), 1)
     metric = 4.0 / ((rad * CR + lane).astype(F32) + 4.0)
     target = jnp.where(rad == 0, CR - 1, 0)
+    odd_az = az_ref[0] % 2 == 1
+    az_prev = jnp.where(odd_az, az_first[...], az_second[...])
+    az_next = jnp.where(odd_az, az_second[...], az_first[...])
     added = {0: scattered(0)}
     for f in (0, 4, 1, 2, 3):
         if f in (0, 1, 2):
@@ -429,18 +430,18 @@
     inner = [(i, i ^ 1) for i in range(n_ax)]
     outer = [(i, ((i + 1) ^ 1) - 1) for i in range(1, n_ax - 1)]
     along = [(i, i + 2) for i in range(0, n_ax - 2, 2)] + [(i, i - 2) for i in range(3, n_ax, 2)]
-    ahead = [(i, (i + 1) % n_az) for i in range(n_az)]
-    back = [((i + 1) % n_az, i) for i in range(n_az)]
+    inner_az = [(i, i ^ 1) for i in range(n_az)]
+    outer_az = [(i, (((i + 1) ^ 1) - 1) % n_az) for i in range(n_az)]
     across = [(i, i ^ 1) for i in range(n_rad)]
     gas_shape = (FIELDS, CAX, CAZ, CR)
 
-    first, second, az_lo, az_hi = call(
-        edges_body, [(FIELDS, CAZ, CR)] * 2 + [(FIELDS, CAX, CR)] * 2, [SMEM, VMEM], 10**6, 10**6, mib=4
-    )(odd, fields)
+    first, second, az_first, az_second = call(
+        edges_body, [(FIELDS, CAZ, CR)] * 2 + [(FIELDS, CAX, CR)] * 2, [SMEM, SMEM, VMEM], 10**6, 10**6, mib=4
+    )(odd, az_index, fields)
     first = lax.ppermute(first, "ax", inner)
     second = lax.ppermute(second, "ax", outer)
-    az_prev = lax.ppermute(az_hi, "az", ahead)
-    az_next = lax.ppermute(az_lo, "az", back)
+    az_first = lax.ppermute(az_first, "az", inner_az)
+    az_second = lax.ppermute(az_second, "az", outer_az)
 
     tiles, near = call(
         near_parcels_body,
@@ -474,7 +475,7 @@
         [
             pltpu.VMEM((3, BLK_DEV, BLK), F32),
             pltpu.VMEM((4, BLK_DEV, BLK), F32),
-            pltpu.VMEM((2, 4, MOVEB, BLK), F32),
+            pltpu.VMEM((2, 4, 2 * MOVEB, BLK), F32),
         ],
         mib=16,
     )(rad_index, odd, counts, moves, fields, parcels, cells)
@@ -497,10 +498,10 @@
     onward = lax.ppermute(onward, "ax", along)
 
     (sect,) = call(
-        gas_body, [gas_shape], [SMEM, SMEM, SMEM] + [VMEM] * 8 + [ANY], 8 * 10**9, 4 * 10**6,
+        gas_body, [gas_shape], [SMEM] * 4 + [VMEM] * 8 + [ANY], 8 * 10**9, 4 * 10**6,
         [pltpu.VMEM((ROWS, PARCELS), BF16), pltpu.VMEM((4, 2 * CR, PARCELS), BF16)],
         mib=24,
-    )(rad_index, odd, coeffs, fields, first, second, az_prev, az_next, rad_got, src, cells, to_home)
+    )(rad_index, odd, az_index, coeffs, fields, first, second, az_first, az_second, rad_got, src, cells, to_home)
 
     gas_out, parcels_out = call(
         merge_body,

time: 57.5 us -> 56.9 us (0.990)
  Pallas kernels: 18.3 us -> 17.7 us
where the time goes in v9:
time: 56.9 us; the launch traced here: 56.6 us
  starting transfers between devices  30 us (53%)
  Pallas kernels  17.7 us (31%)
  waiting for transfers between devices  5.11 us (9%)
  local copies, waits for them, and re-layouts  2.19 us (4%)
  between operations  1.52 us (3%)
    all_to_all x1, starting transfers between devices, shards(): lines = lax.all_to_all(to_owner, 'az', 0, 0, tiled=True)  9.43 us
    all_to_all x1, starting transfers between devices, shards(): filtered = lax.all_to_all(to_home, 'az', 0, 0, tiled=True)  5.52 us
    pallas_call x1, Pallas kernels, shards(): call(gas_body, [gas_shape], [SMEM] * 4 + [VMEM] * 8 + [ANY], 8 * 10 ** 9,...  5.45 us
    pallas_call x1, Pallas kernels, shards(): call(parcels_body, [(4, BLK_DEV, BLK), (4, BLK_DEV, BLK), (2, 4, MOVEB, B...  4.32 us
    ppermute x1, starting transfers between devices, shards(): second = lax.ppermute(second, 'ax', outer)  4.18 us
    ppermute x1, starting transfers between devices, shards(): onward = lax.ppermute(onward, 'ax', along)  3.38 us
    ppermute x1, starting transfers between devices, shards(): az_first = lax.ppermute(az_first, 'az', inner_az)  3.14 us
    all_to_all x1, waiting for transfers between devices, shards(): filtered = lax.all_to_all(to_home, 'az', 0, 0, tiled=True)  2.95 us
  transfers between devices with their start and end apart: 9, of which 2 were waited for; matrix products, arithmetic and copies ran while one was open for 0% of the time, Pallas kernels for 26%

profile of v9, /device:TPU:8, one launch (start us, length us, event | category | flops | bytes accessed | tf_op | source)
XLA Modules:
  0.0 56.6 jit_solution(10437605225169911276)
XLA Ops:
  0.6 0.0 copy-start.8
  0.7 0.0 copy-start
  0.7 1.3 %copy-done = f32[5,8,64,128]{3,2,1,0:T(8,128)S(1)} copy-done((f32[5,8,64,128]{3,2,1,0:T(8,128)S(1)}, f32[5,8,64,128]{3,2,1,0:T(8,128)}, u32[]{:S(2)}) %copy-start) | copy-done | bytes 1310744
  2.0 0.0 copy-start.1
  2.0 0.1 shard_map.104
  2.0 0.1 collective-permute-start
  2.1 4.2 %collective-permute-start.1 = (f32[5,64,128]{2,1,0:T(8,128)S(1)}, f32[5,64,128]{2,1,0:T(8,128)S(1)}, u32[]{:S(2)}, u32[]{:S(2)}) collective-permute-start(f32[5,64,128]{2,1,0:T(8,128)S(1)} %get-tuple-element.17), channel_id=1, source_target_pairs={{2,4},{4,2},{6,8},{8,6},{10,12},{12,10},{3,5},{5,3},{7,9},{9,7},{1... | collective-permute-start | bytes 491528 | tf_op jit(solution)/shard_map/ppermute | solution.py:442
  7.0 0.0 copy-done.8
  7.0 0.0 copy-done.1
  7.0 0.0 copy-start.6
  7.0 0.8 %copy-done.6 = f32[4,32,1,128]{3,2,1,0:T(1,128)S(1)} copy-done((f32[4,32,1,128]{3,2,1,0:T(1,128)S(1)}, f32[4,32,1,128]{3,2,1,0:T(1,128)}, u32[]{:S(2)}) %copy-start.6) | copy-done | bytes 65560
  7.8 0.0 copy-start.4
  7.8 2.6 %shard_map.106 = (f32[128,512]{1,0:T(8,128)S(1)}, f32[64,512]{1,0:T(8,128)S(1)}) custom-call(s32[1]{0:T(128)} %bitcast.11.count_ref, f32[5,8,64,128]{3,2,1,0:T(8,128)S(1)} %copy-done.1, f32[4,32,128]{2,1,0:T(8,128)S(1)} %bitcast.12, s32[32,128]{1,0:T(8,128)S(1)} %bitcast.14), custom_call_target="tpu_custom_call" | custom-call | flops 3000000000 | bytes 2000000 | tf_op jit(solution)/shard_map/pallas_call | solution.py:446
  10.5 0.0 copy-start.7
  10.5 0.0 copy-start.9
  10.5 0.0 collective-permute-done.first_ref
  10.5 0.0 collective-permute-done.1.second_ref
  10.5 0.0 copy-done.4
  10.5 1.7 %shard_map.107 = f32[16,24,128]{2,1,0:T(8,128)} custom-call(s32[1]{0:T(128)} %bitcast.1.odd_ref, f32[5,6]{1,0:T(8,128)S(1)} %copy-done.4, f32[5,64,128]{2,1,0:T(8,128)S(1)} %collective-permute-done.first_ref, f32[5,64,128]{2,1,0:T(8,128)S(1)} %collective-permute-done.1.second_ref, f32[128,512]{1,0:T(8,128)S(1)} %get-tuple-element.22.tiles_ref, ...), custom_call_target="tpu_custom_call" | custom-call | flops 10000000 | bytes 4000000 | tf_op jit(solution)/shard_map/pallas_call | solution.py:458
  12.2 9.4 %all-to-all-start = ((f32[16,24,128]{2,1,0:T(8,128)}), f32[16,24,128]{2,1,0:T(8,128)S(1)}, u32[]{:S(2)}, u32[]{:S(2)}) async-start(f32[16,24,128]{2,1,0:T(8,128)} %shard_map.107), calls=%async_computation | async-start | bytes 393216 | tf_op jit(solution)/shard_map/all_to_all | solution.py:469
  21.6 0.0 copy-done.7
  21.6 0.0 copy-done.9
  21.6 0.0 copy-start.2
  21.7 0.0 copy-start.3
  21.7 0.0 copy-start.5
  21.7 4.3 %shard_map.105 = (f32[4,32,128]{2,1,0:T(8,128)S(1)}, f32[4,32,128]{2,1,0:T(8,128)S(1)}, f32[2,4,4,128]{3,2,1,0:T(4,128)S(1)}, f32[32,128]{1,0:T(8,128)S(1)}) custom-call(s32[1]{0:T(128)} %bitcast.rad_ref, s32[1]{0:T(128)} %bitcast.1.odd_ref, s32[1]{0:T(128)} %bitcast.10.count_ref, s32[32]{0:T(128)S(1)} %bitcast.17, f32[5,8,64,128]{3,2,1,0:T(8,128)S(1)} %copy-done.1, ...), custom_call_target="tpu_custom_call" | custom-call | flops 6000000000 | bytes 2000000 | tf_op jit(solution)/shard_map/pallas_call | solution.py:471
  26.0 1.0 %collective-permute-start.5 = (f32[2,4,4,128]{3,2,1,0:T(4,128)S(1)}, f32[2,4,4,128]{3,2,1,0:T(4,128)S(1)}, u32[]{:S(2)}, u32[]{:S(2)}) collective-permute-start(f32[2,4,4,128]{3,2,1,0:T(4,128)S(1)} %get-tuple-element.24), channel_id=1, source_target_pairs={{0,2},{2,0},{4,6},{6,4},{8,10},{10,8},{12,14},{14,12},{1,3},{3,1},... | collective-permute-start | bytes 49160 | tf_op jit(solution)/shard_map/ppermute | solution.py:483
  27.0 3.1 %collective-permute-start.2 = (f32[5,8,128]{2,1,0:T(8,128)S(1)}, f32[5,8,128]{2,1,0:T(8,128)S(1)}, u32[]{:S(2)}, u32[]{:S(2)}) collective-permute-start(f32[5,8,128]{2,1,0:T(8,128)S(1)} %get-tuple-element.18), channel_id=1, source_target_pairs={{0,16},{16,0},{32,48},{48,32},{64,80},{80,64},{96,112},{112,96},{1... | collective-permute-start | bytes 61448 | tf_op jit(solution)/shard_map/ppermute | solution.py:443
  30.1 2.7 %collective-permute-start.3 = (f32[5,8,128]{2,1,0:T(8,128)S(1)}, f32[5,8,128]{2,1,0:T(8,128)S(1)}, u32[]{:S(2)}, u32[]{:S(2)}) collective-permute-start(f32[5,8,128]{2,1,0:T(8,128)S(1)} %get-tuple-element.19), channel_id=1, source_target_pairs={{0,240},{16,32},{32,16},{48,64},{64,48},{80,96},{96,80},{112,128},... | collective-permute-start | bytes 61448 | tf_op jit(solution)/shard_map/ppermute | solution.py:444
  32.8 0.6 %collective-permute-start.4 = (f32[32,128]{1,0:T(8,128)S(1)}, f32[32,128]{1,0:T(8,128)S(1)}, u32[]{:S(2)}, u32[]{:S(2)}) collective-permute-start(f32[32,128]{1,0:T(8,128)S(1)} %get-tuple-element.20), channel_id=1, source_target_pairs={{0,1},{1,0},{2,3},{3,2},{4,5},{5,4},{6,7},{7,6},{8,9},{9,8},{10,11... | collective-permute-start | bytes 49160 | tf_op jit(solution)/shard_map/ppermute | solution.py:482
  33.4 0.0 collective-permute-done.5.moved_ref
  33.4 2.1 %all-to-all-done.got_ref = f32[16,24,128]{2,1,0:T(8,128)S(1)} async-done(((f32[16,24,128]{2,1,0:T(8,128)}), f32[16,24,128]{2,1,0:T(8,128)S(1)}, u32[]{:S(2)}, u32[]{:S(2)}) %all-to-all-start) | async-done | bytes 196640 | tf_op jit(solution)/shard_map/all_to_all | solution.py:469
  35.5 0.0 copy-done.2
  35.5 0.0 copy-done.3
  35.5 0.0 copy-done.5
  35.5 2.1 %shard_map.108 = (f32[16,20,128]{2,1,0:T(8,128)}, f32[4,4,128]{2,1,0:T(4,128)S(1)}) custom-call(s32[1]{0:T(128)} %bitcast.2.az_ref, s32[16]{0:T(128)S(1)} %copy-done.5, bf16[256,1024]{1,0:T(8,128)(2,1)S(1)} %copy-done.3, bf16[1024,256]{1,0:T(8,128)(2,1)S(1)} %copy-done.2, f32[16,24,128]{2,1,0:T(8,128)S(1)} %all-to-all-done.got_ref, ...), custom_call_target="tpu_custom_call" | custom-call | flops 100000000 | bytes 1000000 | tf_op jit(solution)/shard_map/pallas_call | solution.py:486
  37.7 5.5 %all-to-all-start.1 = ((f32[16,20,128]{2,1,0:T(8,128)}), f32[16,20,128]{2,1,0:T(8,128)S(1)}, u32[]{:S(2)}, u32[]{:S(2)}) async-start(f32[16,20,128]{2,1,0:T(8,128)} %get-tuple-element.25._), calls=%async_computation.1 | async-start | bytes 393216 | tf_op jit(solution)/shard_map/all_to_all | solution.py:497
  43.2 3.4 %collective-permute-start.6 = (f32[4,4,128]{2,1,0:T(4,128)S(1)}, f32[4,4,128]{2,1,0:T(4,128)S(1)}, u32[]{:S(2)}, u32[]{:S(2)}) collective-permute-start(f32[4,4,128]{2,1,0:T(4,128)S(1)} %get-tuple-element.27), channel_id=1, source_target_pairs={{0,4},{4,8},{8,12},{6,2},{10,6},{14,10},{1,5},{5,9},{9,13},{7,3},{... | collective-permute-start | bytes 24584 | tf_op jit(solution)/shard_map/ppermute | solution.py:498
  46.6 0.0 collective-permute-done.4.rad_in
  46.6 0.0 collective-permute-done.2.az_first
  46.6 0.0 collective-permute-done.3.az_second
  46.6 5.4 %shard_map.109.sect_ref = f32[5,8,64,128]{3,2,1,0:T(8,128)S(1)} custom-call(s32[1]{0:T(128)} %bitcast.rad_ref, s32[1]{0:T(128)} %bitcast.1.odd_ref, s32[1]{0:T(128)} %bitcast.2.az_ref, f32[5,6]{1,0:T(8,128)S(1)} %copy-done.4, f32[5,8,64,128]{3,2,1,0:T(8,128)S(1)} %copy-done.1, f32[5,64,128]{2,1,0:T(8,128)S(1)} %collective-permute-done.first_ref, ...), custom_call_target="tpu_custom_call" | custom-call | flops 8000000000 | bytes 4000000 | tf_op jit(solution)/shard_map/pallas_call | solution.py:500
  52.1 0.0 collective-permute-done.6.onward_ref
  52.1 3.0 %all-to-all-done.1.got_ref = f32[16,20,128]{2,1,0:T(8,128)S(1)} async-done(((f32[16,20,128]{2,1,0:T(8,128)}), f32[16,20,128]{2,1,0:T(8,128)S(1)}, u32[]{:S(2)}, u32[]{:S(2)}) %all-to-all-start.1) | async-done | bytes 163872 | tf_op jit(solution)/shard_map/all_to_all | solution.py:497
  55.1 1.5 %shard_map.110 = (f32[5,8,64,128]{3,2,1,0:T(8,128)}, f32[4,40,128]{2,1,0:T(8,128)}) custom-call(s32[1]{0:T(128)} %bitcast.rad_ref, s32[1]{0:T(128)} %bitcast.1.odd_ref, f32[5,8,64,128]{3,2,1,0:T(8,128)S(1)} %shard_map.109.sect_ref, f32[16,20,128]{2,1,0:T(8,128)S(1)} %all-to-all-done.1.got_ref, f32[4,32,128]{2,1,0:T(8,128)S(1)} %get-tuple-element.26.stay_ref, ...), custom_call_target="tpu_custom_call" | custom-call | flops 1000000 | bytes 4000000 | tf_op jit(solution)/shard_map/pallas_call | solution.py:506
Async XLA Ops:
  0.6 6.4 %copy-start.8 = (s32[32,1,128]{2,1,0:T(1,128)S(1)}, s32[32,1,128]{2,1,0:T(1,128)}, u32[]{:S(2)}) copy-start(s32[32,1,128]{2,1,0:T(1,128)} %param.12) | copy-start | bytes 49156
  0.7 1.3 %copy-start = (f32[5,8,64,128]{3,2,1,0:T(8,128)S(1)}, f32[5,8,64,128]{3,2,1,0:T(8,128)}, u32[]{:S(2)}) copy-start(f32[5,8,64,128]{3,2,1,0:T(8,128)} %q_ref.7) | copy-start | bytes 3932164
  2.0 5.0 %copy-start.1 = (f32[5,8,64,128]{3,2,1,0:T(8,128)S(1)}, f32[5,8,64,128]{3,2,1,0:T(8,128)}, u32[]{:S(2)}) copy-start(f32[5,8,64,128]{3,2,1,0:T(8,128)} %q_ref.7) | copy-start | bytes 3932164
  2.0 8.5 %collective-permute-start = (f32[5,64,128]{2,1,0:T(8,128)S(1)}, f32[5,64,128]{2,1,0:T(8,128)S(1)}, u32[]{:S(2)}, u32[]{:S(2)}) collective-permute-start(f32[5,64,128]{2,1,0:T(8,128)S(1)} %get-tuple-element.16), channel_id=1, source_target_pairs={{0,2},{2,0},{4,6},{6,4},{8,10},{10,8},{12,14},{14,12},{1,3},{3,1},... | collective-permute-start | bytes 491528 | tf_op jit(solution)/shard_map/ppermute | solution.py:441
  2.1 8.4 %collective-permute-start.1 = (f32[5,64,128]{2,1,0:T(8,128)S(1)}, f32[5,64,128]{2,1,0:T(8,128)S(1)}, u32[]{:S(2)}, u32[]{:S(2)}) collective-permute-start(f32[5,64,128]{2,1,0:T(8,128)S(1)} %get-tuple-element.17), channel_id=1, source_target_pairs={{2,4},{4,2},{6,8},{8,6},{10,12},{12,10},{3,5},{5,3},{7,9},{9,7},{1... | collective-permute-start | bytes 491528 | tf_op jit(solution)/shard_map/ppermute | solution.py:442
  7.0 0.8 %copy-start.6 = (f32[4,32,1,128]{3,2,1,0:T(1,128)S(1)}, f32[4,32,1,128]{3,2,1,0:T(1,128)}, u32[]{:S(2)}) copy-start(f32[4,32,1,128]{3,2,1,0:T(1,128)} %param.11) | copy-start | bytes 196612
  7.8 2.7 %copy-start.4 = (f32[5,6]{1,0:T(8,128)S(1)}, f32[5,6]{1,0:T(8,128)}, u32[]{:S(2)}) copy-start(f32[5,6]{1,0:T(8,128)} %coef_ref.3) | copy-start | bytes 364
  10.5 11.2 %copy-start.7 = (f32[4,32,1,128]{3,2,1,0:T(1,128)S(1)}, f32[4,32,1,128]{3,2,1,0:T(1,128)}, u32[]{:S(2)}) copy-start(f32[4,32,1,128]{3,2,1,0:T(1,128)} %param.11) | copy-start | bytes 196612
  10.5 11.2 %copy-start.9 = (s32[32,1,1]{0,2,1:T(1,128)S(1)}, s32[32,1,1]{0,2,1:T(1,128)}, u32[]{:S(2)}) copy-start(s32[32,1,1]{0,2,1:T(1,128)} %param.14) | copy-start | bytes 388
  12.2 23.4 %all-to-all-start = ((f32[16,24,128]{2,1,0:T(8,128)}), f32[16,24,128]{2,1,0:T(8,128)S(1)}, u32[]{:S(2)}, u32[]{:S(2)}) async-start(f32[16,24,128]{2,1,0:T(8,128)} %shard_map.107), calls=%async_computation | async-start | bytes 393216 | tf_op jit(solution)/shard_map/all_to_all | solution.py:469
  21.6 13.9 %copy-start.2 = (bf16[1024,256]{1,0:T(8,128)(2,1)S(1)}, bf16[1024,256]{1,0:T(8,128)(2,1)}, u32[]{:S(2)}) copy-start(bf16[1024,256]{1,0:T(8,128)(2,1)} %constant.31.clone.turned_ref) | copy-start | bytes 1572868
  21.7 13.9 %copy-start.3 = (bf16[256,1024]{1,0:T(8,128)(2,1)S(1)}, bf16[256,1024]{1,0:T(8,128)(2,1)}, u32[]{:S(2)}) copy-start(bf16[256,1024]{1,0:T(8,128)(2,1)} %constant.30.clone.basis_ref) | copy-start | bytes 1572868
  21.7 13.9 %copy-start.5 = (s32[16]{0:T(128)S(1)}, s32[16]{0:T(128)}, u32[]{:S(2)}) copy-start(s32[16]{0:T(128)} %width_ref.1) | copy-start | bytes 196
  26.0 7.4 %collective-permute-start.5 = (f32[2,4,4,128]{3,2,1,0:T(4,128)S(1)}, f32[2,4,4,128]{3,2,1,0:T(4,128)S(1)}, u32[]{:S(2)}, u32[]{:S(2)}) collective-permute-start(f32[2,4,4,128]{3,2,1,0:T(4,128)S(1)} %get-tuple-element.24), channel_id=1, source_target_pairs={{0,2},{2,0},{4,6},{6,4},{8,10},{10,8},{12,14},{14,12},{1,3},{3,1},... | collective-permute-start | bytes 49160 | tf_op jit(solution)/shard_map/ppermute | solution.py:483
  27.0 19.6 %collective-permute-start.2 = (f32[5,8,128]{2,1,0:T(8,128)S(1)}, f32[5,8,128]{2,1,0:T(8,128)S(1)}, u32[]{:S(2)}, u32[]{:S(2)}) collective-permute-start(f32[5,8,128]{2,1,0:T(8,128)S(1)} %get-tuple-element.18), channel_id=1, source_target_pairs={{0,16},{16,0},{32,48},{48,32},{64,80},{80,64},{96,112},{112,96},{1... | collective-permute-start | bytes 61448 | tf_op jit(solution)/shard_map/ppermute | solution.py:443
  30.1 16.5 %collective-permute-start.3 = (f32[5,8,128]{2,1,0:T(8,128)S(1)}, f32[5,8,128]{2,1,0:T(8,128)S(1)}, u32[]{:S(2)}, u32[]{:S(2)}) collective-permute-start(f32[5,8,128]{2,1,0:T(8,128)S(1)} %get-tuple-element.19), channel_id=1, source_target_pairs={{0,240},{16,32},{32,16},{48,64},{64,48},{80,96},{96,80},{112,128},... | collective-permute-start | bytes 61448 | tf_op jit(solution)/shard_map/ppermute | solution.py:444
  32.8 13.8 %collective-permute-start.4 = (f32[32,128]{1,0:T(8,128)S(1)}, f32[32,128]{1,0:T(8,128)S(1)}, u32[]{:S(2)}, u32[]{:S(2)}) collective-permute-start(f32[32,128]{1,0:T(8,128)S(1)} %get-tuple-element.20), channel_id=1, source_target_pairs={{0,1},{1,0},{2,3},{3,2},{4,5},{5,4},{6,7},{7,6},{8,9},{9,8},{10,11... | collective-permute-start | bytes 49160 | tf_op jit(solution)/shard_map/ppermute | solution.py:482
  37.7 17.4 %all-to-all-start.1 = ((f32[16,20,128]{2,1,0:T(8,128)}), f32[16,20,128]{2,1,0:T(8,128)S(1)}, u32[]{:S(2)}, u32[]{:S(2)}) async-start(f32[16,20,128]{2,1,0:T(8,128)} %get-tuple-element.25._), calls=%async_computation.1 | async-start | bytes 393216 | tf_op jit(solution)/shard_map/all_to_all | solution.py:497
  43.2 8.9 %collective-permute-start.6 = (f32[4,4,128]{2,1,0:T(4,128)S(1)}, f32[4,4,128]{2,1,0:T(4,128)S(1)}, u32[]{:S(2)}, u32[]{:S(2)}) collective-permute-start(f32[4,4,128]{2,1,0:T(4,128)S(1)} %get-tuple-element.27), channel_id=1, source_target_pairs={{0,4},{4,8},{8,12},{6,2},{10,6},{14,10},{1,5},{5,9},{9,13},{7,3},{... | collective-permute-start | bytes 24584 | tf_op jit(solution)/shard_map/ppermute | solution.py:498

commit v10 on v9

--- a/solution.py
+++ b/solution.py
@@ -24,6 +24,7 @@
 PAIRS = CAX // 2
 QUADS = CYCLES // 4
 LINES = FIELDS * 4
+BAND = 24
 
 STEP_SIZE = 0.5
 EVAP_RATE = 0.5
@@ -72,7 +73,16 @@
     )
 
 
-def edges_body(odd_ref, az_ref, q_ref, first_out, second_out, az_first, az_second):
+def turned(parts):
+    lane = iota((2 * CAZ, CR), 1)
+    packed = jnp.zeros((2 * CAZ, CR), F32)
+    for f, part in enumerate(parts):
+        moved = pltpu.roll(part, f * BAND, 1) if f else part
+        packed = jnp.where((lane >= f * BAND) & (lane < (f + 1) * BAND), moved, packed)
+    return packed.T
+
+
+def edges_body(odd_ref, az_ref, q_ref, first_out, second_out, az_first, az_second, tiles_out):
     odd, odd_az = odd_ref[0] == 1, az_ref[0] % 2 == 1
     low, high = q_ref[:, 0], q_ref[:, CAX - 1]
     first_out[...] = jnp.where(odd, low, high)
@@ -80,6 +90,10 @@
     low, high = q_ref[:, :, 0, :], q_ref[:, :, CAZ - 1, :]
     az_first[...] = jnp.where(odd_az, low, high)
     az_second[...] = jnp.where(odd_az, high, low)
+    for p in range(PAIRS):
+        tiles_out[:, p * 2 * CAZ : (p + 1) * 2 * CAZ] = turned(
+            [q_ref[f, 2 * p : 2 * p + 2].reshape(2 * CAZ, CR) for f in range(FIELDS)]
+        )
 
 
 def lane_row(cells_ref, first, blocks):
@@ -164,25 +178,9 @@
 SOURCE_OF = (0, 1, 2, 3, 0)
 
 
-BAND = 24
-
-
-def turned(parts):
-    lane = iota((2 * CAZ, CR), 1)
-    packed = jnp.zeros((2 * CAZ, CR), F32)
-    for f, part in enumerate(parts):
-        moved = pltpu.roll(part, f * BAND, 1) if f else part
-        packed = jnp.where((lane >= f * BAND) & (lane < (f + 1) * BAND), moved, packed)
-    return packed.T
-
-
-def near_parcels_body(count_ref, q_ref, parcel_ref, cells_ref, tiles_out, near_out, gas_ref, hot_ref, spread_ref):
-    for p in range(PAIRS):
-        tiles_out[:, p * 2 * CAZ : (p + 1) * 2 * CAZ] = turned(
-            [q_ref[f, 2 * p : 2 * p + 2].reshape(2 * CAZ, CR) for f in range(FIELDS)]
-        )
+def near_parcels_body(count_ref, tiles_ref, parcel_ref, cells_ref, near_out, gas_ref, hot_ref, spread_ref):
     start = 16
-    table = jnp.concatenate(halves(tiles_out[start : 4 * BAND]), axis=0)
+    table = jnp.concatenate(halves(tiles_ref[start : 4 * BAND]), axis=0)
     depth = 4 * BAND - start
     spans = [((f + 1) * BAND - start, (f + 1) * BAND - start + CYCLES) for f in range(3)]
     for first in range(0, BLK_DEV, 4):
@@ -435,17 +433,17 @@
     across = [(i, i ^ 1) for i in range(n_rad)]
     gas_shape = (FIELDS, CAX, CAZ, CR)
 
-    first, second, az_first, az_second = call(
-        edges_body, [(FIELDS, CAZ, CR)] * 2 + [(FIELDS, CAX, CR)] * 2, [SMEM, SMEM, VMEM], 10**6, 10**6, mib=4
+    first, second, az_first, az_second, tiles = call(
+        edges_body, [(FIELDS, CAZ, CR)] * 2 + [(FIELDS, CAX, CR)] * 2 + [(CR, ROWS)], [SMEM, SMEM, VMEM], 10**6, 10**6, mib=4
     )(odd, az_index, fields)
     first = lax.ppermute(first, "ax", inner)
     second = lax.ppermute(second, "ax", outer)
     az_first = lax.ppermute(az_first, "az", inner_az)
     az_second = lax.ppermute(az_second, "az", outer_az)
 
-    tiles, near = call(
+    (near,) = call(
         near_parcels_body,
-        [(CR, ROWS), (4 * CYCLES, ROWS)],
+        [(4 * CYCLES, ROWS)],
         [SMEM] + [VMEM] * 3, 3 * 10**9, 2 * 10**6,
         [
             pltpu.VMEM((3, BLK_DEV, BLK), F32),
@@ -453,7 +451,7 @@
             pltpu.VMEM((8 * CYCLES, PARCELS), BF16),
         ],
         mib=16,
-    )(counts, fields, parcels, cells)
+    )(counts, tiles, parcels, cells)
 
     (to_owner,) = call(
         near_body,

time: 56.9 us -> 57.1 us (level)
  starting transfers between devices: 30 us -> 31.4 us
  local copies, waits for them, and re-layouts: 2.19 us -> 1.36 us
    all_to_all x1, starting transfers between devices: 9.43 us -> 10.5 us  [shards(): lines = lax.all_to_all(to_owner, 'az', 0, 0, tiled=True)]
    unnamed x20 -> x18, local copies, waits for them, and re-layouts: 2.19 us -> 1.36 us
    ppermute x1, starting transfers between devices: 0.98 us -> 0.3 us  [shards(): moved = lax.ppermute(leaving, 'ax', inner)]
  transfers between devices with their start and end apart: 9 -> 9, of which waited for: 2 -> 3; matrix products, arithmetic and copies ran while one was open for 0% -> 0% of each run, Pallas kernels for 26% -> 25%
where the time goes in v10:
time: 57.1 us; the launch traced here: 56.7 us
  starting transfers between devices  31.4 us (55%)
  Pallas kernels  17.8 us (31%)
  waiting for transfers between devices  4.67 us (8%)
  between operations  1.51 us (3%)
  local copies, waits for them, and re-layouts  1.36 us (2%)
    all_to_all x1, starting transfers between devices, shards(): lines = lax.all_to_all(to_owner, 'az', 0, 0, tiled=True)  10.5 us
    all_to_all x1, starting transfers between devices, shards(): filtered = lax.all_to_all(to_home, 'az', 0, 0, tiled=True)  6.04 us
    pallas_call x1, Pallas kernels, shards(): call(gas_body, [gas_shape], [SMEM] * 4 + [VMEM] * 8 + [ANY], 8 * 10 ** 9,...  5.44 us
    pallas_call x1, Pallas kernels, shards(): call(parcels_body, [(4, BLK_DEV, BLK), (4, BLK_DEV, BLK), (2, 4, MOVEB, B...  4.32 us
    ppermute x1, starting transfers between devices, shards(): second = lax.ppermute(second, 'ax', outer)  4.18 us
    ppermute x1, starting transfers between devices, shards(): onward = lax.ppermute(onward, 'ax', along)  3.67 us
    ppermute x1, starting transfers between devices, shards(): az_first = lax.ppermute(az_first, 'az', inner_az)  3.32 us
    all_to_all x1, waiting for transfers between devices, shards(): filtered = lax.all_to_all(to_home, 'az', 0, 0, tiled=True)  2.98 us
  transfers between devices with their start and end apart: 9, of which 3 were waited for; matrix products, arithmetic and copies ran while one was open for 0% of the time, Pallas kernels for 25%

profile of v10, /device:TPU:8, one launch (start us, length us, event | category | flops | bytes accessed | tf_op | source)
XLA Modules:
  0.0 56.7 jit_solution(2670042518018896932)
XLA Ops:
  0.6 0.0 copy-start.7
  0.7 0.0 copy-start
  0.7 1.3 %copy-done = f32[5,8,64,128]{3,2,1,0:T(8,128)S(1)} copy-done((f32[5,8,64,128]{3,2,1,0:T(8,128)S(1)}, f32[5,8,64,128]{3,2,1,0:T(8,128)}, u32[]{:S(2)}) %copy-start) | copy-done | bytes 1310744
  2.0 0.0 copy-start.6
  2.0 0.5 shard_map.104
  2.5 0.1 collective-permute-start
  2.6 4.2 %collective-permute-start.1 = (f32[5,64,128]{2,1,0:T(8,128)S(1)}, f32[5,64,128]{2,1,0:T(8,128)S(1)}, u32[]{:S(2)}, u32[]{:S(2)}) collective-permute-start(f32[5,64,128]{2,1,0:T(8,128)S(1)} %get-tuple-element.16), channel_id=1, source_target_pairs={{2,4},{4,2},{6,8},{8,6},{10,12},{12,10},{3,5},{5,3},{7,9},{9,7},{1... | collective-permute-start | bytes 491528 | tf_op jit(solution)/shard_map/ppermute | solution.py:440
  7.4 0.0 copy-done.7
  7.4 0.0 copy-done.6
  7.5 0.0 copy-start.4
  7.5 2.2 %shard_map.106.near_ref = f32[64,512]{1,0:T(8,128)S(1)} custom-call(s32[1]{0:T(128)} %bitcast.11.count_ref, f32[128,512]{1,0:T(8,128)S(1)} %get-tuple-element.21.tiles_ref, f32[4,32,128]{2,1,0:T(8,128)S(1)} %bitcast.12, s32[32,128]{1,0:T(8,128)S(1)} %bitcast.14), custom_call_target="tpu_custom_call" | custom-call | flops 3000000000 | bytes 2000000 | tf_op jit(solution)/shard_map/pallas_call | solution.py:444
  9.7 0.0 copy-start.1
  9.7 0.0 copy-start.8
  9.7 0.0 collective-permute-done.first_ref
  9.7 0.1 collective-permute-done.1.second_ref
  9.8 0.0 copy-done.4
  9.8 1.7 %shard_map.107 = f32[16,24,128]{2,1,0:T(8,128)} custom-call(s32[1]{0:T(128)} %bitcast.1.odd_ref, f32[5,6]{1,0:T(8,128)S(1)} %copy-done.4, f32[5,64,128]{2,1,0:T(8,128)S(1)} %collective-permute-done.first_ref, f32[5,64,128]{2,1,0:T(8,128)S(1)} %collective-permute-done.1.second_ref, f32[128,512]{1,0:T(8,128)S(1)} %get-tuple-element.21.tiles_ref, ...), custom_call_target="tpu_custom_call" | custom-call | flops 10000000 | bytes 4000000 | tf_op jit(solution)/shard_map/pallas_call | solution.py:456
  11.4 10.5 %all-to-all-start = ((f32[16,24,128]{2,1,0:T(8,128)}), f32[16,24,128]{2,1,0:T(8,128)S(1)}, u32[]{:S(2)}, u32[]{:S(2)}) async-start(f32[16,24,128]{2,1,0:T(8,128)} %shard_map.107), calls=%async_computation | async-start | bytes 393216 | tf_op jit(solution)/shard_map/all_to_all | solution.py:467
  21.9 0.0 copy-done.1
  22.0 0.0 copy-done.8
  22.0 0.0 copy-start.2
  22.0 0.0 copy-start.3
  22.0 0.0 copy-start.5
  22.0 4.3 %shard_map.105 = (f32[4,32,128]{2,1,0:T(8,128)S(1)}, f32[4,32,128]{2,1,0:T(8,128)S(1)}, f32[2,4,4,128]{3,2,1,0:T(4,128)S(1)}, f32[32,128]{1,0:T(8,128)S(1)}) custom-call(s32[1]{0:T(128)} %bitcast.rad_ref, s32[1]{0:T(128)} %bitcast.1.odd_ref, s32[1]{0:T(128)} %bitcast.10.count_ref, s32[32]{0:T(128)S(1)} %bitcast.17, f32[5,8,64,128]{3,2,1,0:T(8,128)S(1)} %copy-done.1, ...), custom_call_target="tpu_custom_call" | custom-call | flops 6000000000 | bytes 2000000 | tf_op jit(solution)/shard_map/pallas_call | solution.py:469
  26.3 0.3 collective-permute-start.5
  26.6 3.3 %collective-permute-start.2 = (f32[5,8,128]{2,1,0:T(8,128)S(1)}, f32[5,8,128]{2,1,0:T(8,128)S(1)}, u32[]{:S(2)}, u32[]{:S(2)}) collective-permute-start(f32[5,8,128]{2,1,0:T(8,128)S(1)} %get-tuple-element.17), channel_id=1, source_target_pairs={{0,16},{16,0},{32,48},{48,32},{64,80},{80,64},{96,112},{112,96},{1... | collective-permute-start | bytes 61448 | tf_op jit(solution)/shard_map/ppermute | solution.py:441
  29.9 2.7 %collective-permute-start.3 = (f32[5,8,128]{2,1,0:T(8,128)S(1)}, f32[5,8,128]{2,1,0:T(8,128)S(1)}, u32[]{:S(2)}, u32[]{:S(2)}) collective-permute-start(f32[5,8,128]{2,1,0:T(8,128)S(1)} %get-tuple-element.18), channel_id=1, source_target_pairs={{0,240},{16,32},{32,16},{48,64},{64,48},{80,96},{96,80},{112,128},... | collective-permute-start | bytes 61448 | tf_op jit(solution)/shard_map/ppermute | solution.py:442
  32.6 0.6 %collective-permute-start.4 = (f32[32,128]{1,0:T(8,128)S(1)}, f32[32,128]{1,0:T(8,128)S(1)}, u32[]{:S(2)}, u32[]{:S(2)}) collective-permute-start(f32[32,128]{1,0:T(8,128)S(1)} %get-tuple-element.19), channel_id=1, source_target_pairs={{0,1},{1,0},{2,3},{3,2},{4,5},{5,4},{6,7},{7,6},{8,9},{9,8},{10,11... | collective-permute-start | bytes 49160 | tf_op jit(solution)/shard_map/ppermute | solution.py:480
  33.2 0.0 collective-permute-done.5.moved_ref
  33.2 1.6 %all-to-all-done.got_ref = f32[16,24,128]{2,1,0:T(8,128)S(1)} async-done(((f32[16,24,128]{2,1,0:T(8,128)}), f32[16,24,128]{2,1,0:T(8,128)S(1)}, u32[]{:S(2)}, u32[]{:S(2)}) %all-to-all-start) | async-done | bytes 196640 | tf_op jit(solution)/shard_map/all_to_all | solution.py:467
  34.8 0.0 copy-done.2
  34.8 0.0 copy-done.3
  34.8 0.0 copy-done.5
  34.8 2.1 %shard_map.108 = (f32[16,20,128]{2,1,0:T(8,128)}, f32[4,4,128]{2,1,0:T(4,128)S(1)}) custom-call(s32[1]{0:T(128)} %bitcast.2.az_ref, s32[16]{0:T(128)S(1)} %copy-done.5, bf16[256,1024]{1,0:T(8,128)(2,1)S(1)} %copy-done.3, bf16[1024,256]{1,0:T(8,128)(2,1)S(1)} %copy-done.2, f32[16,24,128]{2,1,0:T(8,128)S(1)} %all-to-all-done.got_ref, ...), custom_call_target="tpu_custom_call" | custom-call | flops 100000000 | bytes 1000000 | tf_op jit(solution)/shard_map/pallas_call | solution.py:484
  37.0 6.0 %all-to-all-start.1 = ((f32[16,20,128]{2,1,0:T(8,128)}), f32[16,20,128]{2,1,0:T(8,128)S(1)}, u32[]{:S(2)}, u32[]{:S(2)}) async-start(f32[16,20,128]{2,1,0:T(8,128)} %get-tuple-element.23._), calls=%async_computation.1 | async-start | bytes 393216 | tf_op jit(solution)/shard_map/all_to_all | solution.py:495
  43.0 3.7 %collective-permute-start.6 = (f32[4,4,128]{2,1,0:T(4,128)S(1)}, f32[4,4,128]{2,1,0:T(4,128)S(1)}, u32[]{:S(2)}, u32[]{:S(2)}) collective-permute-start(f32[4,4,128]{2,1,0:T(4,128)S(1)} %get-tuple-element.25), channel_id=1, source_target_pairs={{0,4},{4,8},{8,12},{6,2},{10,6},{14,10},{1,5},{5,9},{9,13},{7,3},{... | collective-permute-start | bytes 24584 | tf_op jit(solution)/shard_map/ppermute | solution.py:496
  46.7 0.0 collective-permute-done.4.rad_in
  46.7 0.0 collective-permute-done.2.az_first
  46.7 0.0 collective-permute-done.3.az_second
  46.8 5.4 %shard_map.109.sect_ref = f32[5,8,64,128]{3,2,1,0:T(8,128)S(1)} custom-call(s32[1]{0:T(128)} %bitcast.rad_ref, s32[1]{0:T(128)} %bitcast.1.odd_ref, s32[1]{0:T(128)} %bitcast.2.az_ref, f32[5,6]{1,0:T(8,128)S(1)} %copy-done.4, f32[5,8,64,128]{3,2,1,0:T(8,128)S(1)} %copy-done.1, f32[5,64,128]{2,1,0:T(8,128)S(1)} %collective-permute-done.first_ref, ...), custom_call_target="tpu_custom_call" | custom-call | flops 8000000000 | bytes 4000000 | tf_op jit(solution)/shard_map/pallas_call | solution.py:498
  52.2 0.0 collective-permute-done.6.onward_ref
  52.2 3.0 %all-to-all-done.1.got_ref = f32[16,20,128]{2,1,0:T(8,128)S(1)} async-done(((f32[16,20,128]{2,1,0:T(8,128)}), f32[16,20,128]{2,1,0:T(8,128)S(1)}, u32[]{:S(2)}, u32[]{:S(2)}) %all-to-all-start.1) | async-done | bytes 163872 | tf_op jit(solution)/shard_map/all_to_all | solution.py:495
  55.2 1.5 %shard_map.110 = (f32[5,8,64,128]{3,2,1,0:T(8,128)}, f32[4,40,128]{2,1,0:T(8,128)}) custom-call(s32[1]{0:T(128)} %bitcast.rad_ref, s32[1]{0:T(128)} %bitcast.1.odd_ref, f32[5,8,64,128]{3,2,1,0:T(8,128)S(1)} %shard_map.109.sect_ref, f32[16,20,128]{2,1,0:T(8,128)S(1)} %all-to-all-done.1.got_ref, f32[4,32,128]{2,1,0:T(8,128)S(1)} %get-tuple-element.24.stay_ref, ...), custom_call_target="tpu_custom_call" | custom-call | flops 1000000 | bytes 4000000 | tf_op jit(solution)/shard_map/pallas_call | solution.py:504
Async XLA Ops:
  0.6 6.8 %copy-start.7 = (s32[32,1,128]{2,1,0:T(1,128)S(1)}, s32[32,1,128]{2,1,0:T(1,128)}, u32[]{:S(2)}) copy-start(s32[32,1,128]{2,1,0:T(1,128)} %param.12) | copy-start | bytes 49156
  0.7 1.3 %copy-start = (f32[5,8,64,128]{3,2,1,0:T(8,128)S(1)}, f32[5,8,64,128]{3,2,1,0:T(8,128)}, u32[]{:S(2)}) copy-start(f32[5,8,64,128]{3,2,1,0:T(8,128)} %q_ref.5) | copy-start | bytes 3932164
  2.0 5.5 %copy-start.6 = (f32[4,32,1,128]{3,2,1,0:T(1,128)S(1)}, f32[4,32,1,128]{3,2,1,0:T(1,128)}, u32[]{:S(2)}) copy-start(f32[4,32,1,128]{3,2,1,0:T(1,128)} %param.11) | copy-start | bytes 196612
  2.5 7.2 %collective-permute-start = (f32[5,64,128]{2,1,0:T(8,128)S(1)}, f32[5,64,128]{2,1,0:T(8,128)S(1)}, u32[]{:S(2)}, u32[]{:S(2)}) collective-permute-start(f32[5,64,128]{2,1,0:T(8,128)S(1)} %get-tuple-element.15), channel_id=1, source_target_pairs={{0,2},{2,0},{4,6},{6,4},{8,10},{10,8},{12,14},{14,12},{1,3},{3,1},... | collective-permute-start | bytes 491528 | tf_op jit(solution)/shard_map/ppermute | solution.py:439
  2.6 7.2 %collective-permute-start.1 = (f32[5,64,128]{2,1,0:T(8,128)S(1)}, f32[5,64,128]{2,1,0:T(8,128)S(1)}, u32[]{:S(2)}, u32[]{:S(2)}) collective-permute-start(f32[5,64,128]{2,1,0:T(8,128)S(1)} %get-tuple-element.16), channel_id=1, source_target_pairs={{2,4},{4,2},{6,8},{8,6},{10,12},{12,10},{3,5},{5,3},{7,9},{9,7},{1... | collective-permute-start | bytes 491528 | tf_op jit(solution)/shard_map/ppermute | solution.py:440
  7.5 2.3 %copy-start.4 = (f32[5,6]{1,0:T(8,128)S(1)}, f32[5,6]{1,0:T(8,128)}, u32[]{:S(2)}) copy-start(f32[5,6]{1,0:T(8,128)} %coef_ref.3) | copy-start | bytes 364
  9.7 12.3 %copy-start.1 = (f32[5,8,64,128]{3,2,1,0:T(8,128)S(1)}, f32[5,8,64,128]{3,2,1,0:T(8,128)}, u32[]{:S(2)}) copy-start(f32[5,8,64,128]{3,2,1,0:T(8,128)} %q_ref.5) | copy-start | bytes 3932164
  9.7 12.3 %copy-start.8 = (s32[32,1,1]{0,2,1:T(1,128)S(1)}, s32[32,1,1]{0,2,1:T(1,128)}, u32[]{:S(2)}) copy-start(s32[32,1,1]{0,2,1:T(1,128)} %param.14) | copy-start | bytes 388
  11.4 23.4 %all-to-all-start = ((f32[16,24,128]{2,1,0:T(8,128)}), f32[16,24,128]{2,1,0:T(8,128)S(1)}, u32[]{:S(2)}, u32[]{:S(2)}) async-start(f32[16,24,128]{2,1,0:T(8,128)} %shard_map.107), calls=%async_computation | async-start | bytes 393216 | tf_op jit(solution)/shard_map/all_to_all | solution.py:467
  22.0 12.9 %copy-start.2 = (bf16[1024,256]{1,0:T(8,128)(2,1)S(1)}, bf16[1024,256]{1,0:T(8,128)(2,1)}, u32[]{:S(2)}) copy-start(bf16[1024,256]{1,0:T(8,128)(2,1)} %constant.31.clone.turned_ref) | copy-start | bytes 1572868
  22.0 12.9 %copy-start.3 = (bf16[256,1024]{1,0:T(8,128)(2,1)S(1)}, bf16[256,1024]{1,0:T(8,128)(2,1)}, u32[]{:S(2)}) copy-start(bf16[256,1024]{1,0:T(8,128)(2,1)} %constant.30.clone.basis_ref) | copy-start | bytes 1572868
  22.0 12.9 %copy-start.5 = (s32[16]{0:T(128)S(1)}, s32[16]{0:T(128)}, u32[]{:S(2)}) copy-start(s32[16]{0:T(128)} %width_ref.1) | copy-start | bytes 196
  26.3 6.9 %collective-permute-start.5 = (f32[2,4,4,128]{3,2,1,0:T(4,128)S(1)}, f32[2,4,4,128]{3,2,1,0:T(4,128)S(1)}, u32[]{:S(2)}, u32[]{:S(2)}) collective-permute-start(f32[2,4,4,128]{3,2,1,0:T(4,128)S(1)} %get-tuple-element.22), channel_id=1, source_target_pairs={{0,2},{2,0},{4,6},{6,4},{8,10},{10,8},{12,14},{14,12},{1,3},{3,1},... | collective-permute-start | bytes 49160 | tf_op jit(solution)/shard_map/ppermute | solution.py:481
  26.6 20.1 %collective-permute-start.2 = (f32[5,8,128]{2,1,0:T(8,128)S(1)}, f32[5,8,128]{2,1,0:T(8,128)S(1)}, u32[]{:S(2)}, u32[]{:S(2)}) collective-permute-start(f32[5,8,128]{2,1,0:T(8,128)S(1)} %get-tuple-element.17), channel_id=1, source_target_pairs={{0,16},{16,0},{32,48},{48,32},{64,80},{80,64},{96,112},{112,96},{1... | collective-permute-start | bytes 61448 | tf_op jit(solution)/shard_map/ppermute | solution.py:441
  29.9 16.8 %collective-permute-start.3 = (f32[5,8,128]{2,1,0:T(8,128)S(1)}, f32[5,8,128]{2,1,0:T(8,128)S(1)}, u32[]{:S(2)}, u32[]{:S(2)}) collective-permute-start(f32[5,8,128]{2,1,0:T(8,128)S(1)} %get-tuple-element.18), channel_id=1, source_target_pairs={{0,240},{16,32},{32,16},{48,64},{64,48},{80,96},{96,80},{112,128},... | collective-permute-start | bytes 61448 | tf_op jit(solution)/shard_map/ppermute | solution.py:442
  32.6 14.1 %collective-permute-start.4 = (f32[32,128]{1,0:T(8,128)S(1)}, f32[32,128]{1,0:T(8,128)S(1)}, u32[]{:S(2)}, u32[]{:S(2)}) collective-permute-start(f32[32,128]{1,0:T(8,128)S(1)} %get-tuple-element.19), channel_id=1, source_target_pairs={{0,1},{1,0},{2,3},{3,2},{4,5},{5,4},{6,7},{7,6},{8,9},{9,8},{10,11... | collective-permute-start | bytes 49160 | tf_op jit(solution)/shard_map/ppermute | solution.py:480
  37.0 18.2 %all-to-all-start.1 = ((f32[16,20,128]{2,1,0:T(8,128)}), f32[16,20,128]{2,1,0:T(8,128)S(1)}, u32[]{:S(2)}, u32[]{:S(2)}) async-start(f32[16,20,128]{2,1,0:T(8,128)} %get-tuple-element.23._), calls=%async_computation.1 | async-start | bytes 393216 | tf_op jit(solution)/shard_map/all_to_all | solution.py:495
  43.0 9.2 %collective-permute-start.6 = (f32[4,4,128]{2,1,0:T(4,128)S(1)}, f32[4,4,128]{2,1,0:T(4,128)S(1)}, u32[]{:S(2)}, u32[]{:S(2)}) collective-permute-start(f32[4,4,128]{2,1,0:T(4,128)S(1)} %get-tuple-element.25), channel_id=1, source_target_pairs={{0,4},{4,8},{8,12},{6,2},{10,6},{14,10},{1,5},{5,9},{9,13},{7,3},{... | collective-permute-start | bytes 24584 | tf_op jit(solution)/shard_map/ppermute | solution.py:496

commit v11 on v10

--- a/solution.py
+++ b/solution.py
@@ -82,7 +82,22 @@
     return packed.T
 
 
-def edges_body(odd_ref, az_ref, q_ref, first_out, second_out, az_first, az_second, tiles_out):
+def rad_edges(rad, q_ref, rad_out):
+    extra = jnp.where(rad == 0, 1, 0)
+    lane = iota((32, CR), 1)
+    packed = jnp.zeros((32, CR), F32)
+    for f in range(FIELDS):
+        for g in range(16):
+            part = q_ref[f, g // 2, (g % 2) * 32 : (g % 2) * 32 + 32, :]
+            spot = g * 8 + f
+            packed = jnp.where(lane == spot, pltpu.roll(part, spot + extra, 1), packed)
+    rad_out[...] = packed
+
+
+def edges_body(
+    rad_ref, odd_ref, az_ref, q_ref, first_out, second_out, az_first, az_second, tiles_out, rad_out
+):
+    rad_edges(rad_ref[0], q_ref, rad_out)
     odd, odd_az = odd_ref[0] == 1, az_ref[0] % 2 == 1
     low, high = q_ref[:, 0], q_ref[:, CAX - 1]
     first_out[...] = jnp.where(odd, low, high)
@@ -115,7 +130,7 @@
 
 def step(count_ref, parcel_ref, gas_ref):
     slot = iota((BLK_DEV, BLK), 0) * BLK + iota((BLK_DEV, BLK), 1)
-    alive = slot < count_ref[0]
+    alive = slot < count_ref[0, 0, 0]
     diam = parcel_ref[3]
     vel = [parcel_ref[i] for i in range(3)]
     gas = [gas_ref[i] for i in range(3)]
@@ -138,10 +153,9 @@
 
 
 def parcels_body(
-    rad_ref, odd_ref, count_ref, move_ref, q_ref, parcel_ref, cells_ref,
-    src_out, stay_out, leave_out, rad_out, gas_ref, state_ref, leave_ref,
-):
-    rad_edges(rad_ref[0], q_ref, rad_out)
+    odd_ref, count_ref, move_ref, q_ref, parcel_ref, cells_ref,
+    src_out, stay_out, leave_out, gas_ref, state_ref, leave_ref,
+):
     table = jnp.concatenate(
         [jnp.concatenate(halves(q_ref[f + 1].reshape(ROWS, CR).T), axis=1) for f in range(3)], axis=0
     )
@@ -178,7 +192,10 @@
 SOURCE_OF = (0, 1, 2, 3, 0)
 
 
-def near_parcels_body(count_ref, tiles_ref, parcel_ref, cells_ref, near_out, gas_ref, hot_ref, spread_ref):
+def near_parcels_body(
+    count_ref, tiles_ref, parcel_ref, cells_ref, rad_ref, near_out, rad_out, gas_ref, hot_ref, spread_ref
+):
+    rad_out[...] = rad_ref[...]
     start = 16
     table = jnp.concatenate(halves(tiles_ref[start : 4 * BAND]), axis=0)
     depth = 4 * BAND - start
@@ -203,7 +220,7 @@
 
 
 def near_body(
-    odd_ref, coef_ref, first_ref, second_ref, tiles_ref, near_ref, send_hbm, send_out, sems
+    odd_ref, coef_ref, first_ref, second_ref, tiles_ref, near_ref, _, send_hbm, send_out, sems
 ):
     copies = []
     lane = iota((CR, 2 * CAZ), 1)
@@ -262,18 +279,6 @@
         copy.wait()
 
 
-def rad_edges(rad, q_ref, rad_out):
-    extra = jnp.where(rad == 0, 1, 0)
-    lane = iota((32, CR), 1)
-    packed = jnp.zeros((32, CR), F32)
-    for f in range(FIELDS):
-        for g in range(16):
-            part = q_ref[f, g // 2, (g % 2) * 32 : (g % 2) * 32 + 32, :]
-            spot = g * 8 + f
-            packed = jnp.where(lane == spot, pltpu.roll(part, spot + extra, 1), packed)
-    rad_out[...] = packed
-
-
 def gas_body(
     rad_ref, odd_ref, az_ref, coef_ref, q_ref, first_ref, second_ref, az_first, az_second, rad_in, src_ref,
     cells_ref, _,
@@ -423,7 +428,6 @@
     n_ax, n_az, n_rad = (lax.axis_size(axis) for axis in ("ax", "az", "rad"))
     parcels = parcels.reshape(4, BLK_DEV, BLK)
     cells = cells.reshape(BLK_DEV, BLK)
-    counts = counts.reshape(1)
     moves = moves.reshape(BLK_DEV)
     inner = [(i, i ^ 1) for i in range(n_ax)]
     outer = [(i, ((i + 1) ^ 1) - 1) for i in range(1, n_ax - 1)]
@@ -433,51 +437,54 @@
     across = [(i, i ^ 1) for i in range(n_rad)]
     gas_shape = (FIELDS, CAX, CAZ, CR)
 
-    first, second, az_first, az_second, tiles = call(
-        edges_body, [(FIELDS, CAZ, CR)] * 2 + [(FIELDS, CAX, CR)] * 2 + [(CR, ROWS)], [SMEM, SMEM, VMEM], 10**6, 10**6, mib=4
-    )(odd, az_index, fields)
+    first, second, az_first, az_second, tiles, rad_edge = call(
+        edges_body,
+        [(FIELDS, CAZ, CR)] * 2 + [(FIELDS, CAX, CR)] * 2 + [(CR, ROWS), (32, CR)],
+        [SMEM, SMEM, SMEM, VMEM], 10**6, 10**6,
+        mib=4,
+    )(rad_index, odd, az_index, fields)
+    second = lax.ppermute(second, "ax", outer)
     first = lax.ppermute(first, "ax", inner)
-    second = lax.ppermute(second, "ax", outer)
     az_first = lax.ppermute(az_first, "az", inner_az)
     az_second = lax.ppermute(az_second, "az", outer_az)
 
-    (near,) = call(
+    near, rad_edge = call(
         near_parcels_body,
-        [(4 * CYCLES, ROWS)],
-        [SMEM] + [VMEM] * 3, 3 * 10**9, 2 * 10**6,
+        [(4 * CYCLES, ROWS), (32, CR)],
+        [SMEM] + [VMEM] * 4, 3 * 10**9, 2 * 10**6,
         [
             pltpu.VMEM((3, BLK_DEV, BLK), F32),
             pltpu.VMEM((ROWS, PARCELS), BF16),
             pltpu.VMEM((8 * CYCLES, PARCELS), BF16),
         ],
         mib=16,
-    )(counts, tiles, parcels, cells)
+    )(counts, tiles, parcels, cells, rad_edge)
+    rad_got = lax.ppermute(rad_edge, "rad", across)
 
     (to_owner,) = call(
         near_body,
         [(N_AZ, LINES + 4, 2 * CAZ)],
-        [SMEM, SMEM] + [VMEM] * 4, 10**7, 4 * 10**6,
+        [SMEM, SMEM] + [VMEM] * 4 + [ANY], 10**7, 4 * 10**6,
         [
             pltpu.VMEM((N_AZ, LINES + 4, 2 * CAZ), F32),
             pltpu.SemaphoreType.DMA((PAIRS,)),
         ],
         mib=8,
         hbm_first=True,
-    )(odd, coeffs, first, second, tiles, near)
+    )(odd, coeffs, first, second, tiles, near, rad_got)
     lines = lax.all_to_all(to_owner, "az", 0, 0, tiled=True)
 
-    src, stay, leaving, rad_edge = call(
+    src, stay, leaving = call(
         parcels_body,
-        [(4, BLK_DEV, BLK), (4, BLK_DEV, BLK), (2, 4, MOVEB, BLK), (32, CR)],
-        [SMEM] * 4 + [VMEM] * 3, 6 * 10**9, 2 * 10**6,
+        [(4, BLK_DEV, BLK), (4, BLK_DEV, BLK), (2, 4, MOVEB, BLK)],
+        [SMEM] * 3 + [VMEM] * 3, 6 * 10**9, 2 * 10**6,
         [
             pltpu.VMEM((3, BLK_DEV, BLK), F32),
             pltpu.VMEM((4, BLK_DEV, BLK), F32),
             pltpu.VMEM((2, 4, 2 * MOVEB, BLK), F32),
         ],
         mib=16,
-    )(rad_index, odd, counts, moves, fields, parcels, cells)
-    rad_got = lax.ppermute(rad_edge, "rad", across)
+    )(odd, counts, moves, fields, parcels, cells)
     moved = lax.ppermute(leaving, "ax", inner)
 
     basis, basis_turned = basis_parts()

time: 57.1 us -> 59.3 us (1.039)
  waiting for transfers between devices: 4.67 us -> 8.92 us
  starting transfers between devices: 31.4 us -> 28.8 us
    ppermute x1, waiting for transfers between devices: 0.01 us -> 3.73 us  [shards(): rad_got = lax.ppermute(rad_edge, 'rad', across)]
    all_to_all x1, starting transfers between devices: 10.5 us -> 9.31 us  [shards(): lines = lax.all_to_all(to_owner, 'az', 0, 0, tiled=True)]
    all_to_all x1, starting transfers between devices: 6.04 us -> 5.11 us  [shards(): filtered = lax.all_to_all(to_home, 'az', 0, 0, tiled=True)]
  transfers between devices with their start and end apart: 9 -> 9, of which waited for: 3 -> 3; matrix products, arithmetic and copies ran while one was open for 0% -> 0% of each run, Pallas kernels for 25% -> 24%
where the time goes in v11:
time: 59.3 us; the launch traced here: 58.7 us
  starting transfers between devices  28.8 us (49%)
  Pallas kernels  18.1 us (31%)
  waiting for transfers between devices  8.92 us (15%)
  between operations  1.5 us (3%)
  local copies, waits for them, and re-layouts  1.36 us (2%)
    all_to_all x1, starting transfers between devices, shards(): lines = lax.all_to_all(to_owner, 'az', 0, 0, tiled=True)  9.31 us
    pallas_call x1, Pallas kernels, shards(): call(gas_body, [gas_shape], [SMEM] * 4 + [VMEM] * 8 + [ANY], 8 * 10 ** 9,...  5.41 us
    all_to_all x1, starting transfers between devices, shards(): filtered = lax.all_to_all(to_home, 'az', 0, 0, tiled=True)  5.11 us
    pallas_call x1, Pallas kernels, shards(): call(parcels_body, [(4, BLK_DEV, BLK), (4, BLK_DEV, BLK), (2, 4, MOVEB, B...  4.31 us
    ppermute x1, starting transfers between devices, shards(): second = lax.ppermute(second, 'ax', outer)  4.18 us
    ppermute x1, starting transfers between devices, shards(): onward = lax.ppermute(onward, 'ax', along)  3.73 us
    ppermute x1, waiting for transfers between devices, shards(): rad_got = lax.ppermute(rad_edge, 'rad', across)  3.73 us
    ppermute x1, starting transfers between devices, shards(): az_first = lax.ppermute(az_first, 'az', inner_az)  3.5 us
  transfers between devices with their start and end apart: 9, of which 3 were waited for; matrix products, arithmetic and copies ran while one was open for 0% of the time, Pallas kernels for 24%

profile of v11, /device:TPU:8, one launch (start us, length us, event | category | flops | bytes accessed | tf_op | source)
XLA Modules:
  0.0 58.7 jit_solution(14951861175673811520)
XLA Ops:
  0.6 0.0 copy-start.7
  0.7 0.0 copy-start
  0.7 1.3 %copy-done = f32[5,8,64,128]{3,2,1,0:T(8,128)S(1)} copy-done((f32[5,8,64,128]{3,2,1,0:T(8,128)S(1)}, f32[5,8,64,128]{3,2,1,0:T(8,128)}, u32[]{:S(2)}) %copy-start) | copy-done | bytes 1310744
  2.0 0.0 copy-start.6
  2.0 0.9 %shard_map.104 = (f32[5,64,128]{2,1,0:T(8,128)S(1)}, f32[5,64,128]{2,1,0:T(8,128)S(1)}, f32[5,8,128]{2,1,0:T(8,128)S(1)}, f32[5,8,128]{2,1,0:T(8,128)S(1)}, f32[...) custom-call(s32[1]{0:T(128)} %bitcast.rad_ref, s32[1]{0:T(128)} %bitcast.1.odd_ref, s32[1]{0:T(128)} %bitcast.2.az_ref, ...), custom_call_target="tpu_custom_call" | custom-call | flops 1000000 | bytes 1000000 | tf_op jit(solution)/shard_map/pallas_call | solution.py:440
  2.8 0.1 collective-permute-start
  2.9 4.2 %collective-permute-start.1 = (f32[5,64,128]{2,1,0:T(8,128)S(1)}, f32[5,64,128]{2,1,0:T(8,128)S(1)}, u32[]{:S(2)}, u32[]{:S(2)}) collective-permute-start(f32[5,64,128]{2,1,0:T(8,128)S(1)} %get-tuple-element.18), channel_id=1, source_target_pairs={{2,4},{4,2},{6,8},{8,6},{10,12},{12,10},{3,5},{5,3},{7,9},{9,7},{1... | collective-permute-start | bytes 491528 | tf_op jit(solution)/shard_map/ppermute | solution.py:446
  7.8 0.0 copy-done.7
  7.8 0.0 copy-done.6
  7.8 0.0 copy-start.4
  7.8 2.2 %shard_map.105 = (f32[64,512]{1,0:T(8,128)S(1)}, f32[32,128]{1,0:T(8,128)S(1)}) custom-call(s32[1,1,1]{2,1,0:T(1,128)S(6)} %copy.12.count_ref, f32[128,512]{1,0:T(8,128)S(1)} %get-tuple-element.21.tiles_ref, f32[4,32,128]{2,1,0:T(8,128)S(1)} %bitcast.9, s32[32,128]{1,0:T(8,128)S(1)} %bitcast.11, f32[32,128]{1,0:T(8,128)S(1)} %get-tuple-element.22.rad_ref), custom_call_target="tpu_custom_call" | custom-call | flops 3000000000 | bytes 2000000 | tf_op jit(solution)/shard_map/pallas_call | solution.py:451
  10.0 0.0 copy-start.1
  10.0 0.0 copy-start.8
  10.1 0.1 collective-permute-start.4
  10.2 3.7 %collective-permute-done.4._.rad_in = f32[32,128]{1,0:T(8,128)S(1)} collective-permute-done((f32[32,128]{1,0:T(8,128)S(1)}, f32[32,128]{1,0:T(8,128)S(1)}, u32[]{:S(2)}, u32[]{:S(2)}) %collective-permute-start.4) | collective-permute-done | bytes 16416 | tf_op jit(solution)/shard_map/ppermute | solution.py:462
  13.9 0.0 collective-permute-done.first_ref
  13.9 0.0 collective-permute-done.1.second_ref
  13.9 0.0 copy-done.4
  13.9 1.7 %shard_map.107 = f32[16,24,128]{2,1,0:T(8,128)} custom-call(s32[1]{0:T(128)} %bitcast.1.odd_ref, f32[5,6]{1,0:T(8,128)S(1)} %copy-done.4, f32[5,64,128]{2,1,0:T(8,128)S(1)} %collective-permute-done.first_ref, f32[5,64,128]{2,1,0:T(8,128)S(1)} %collective-permute-done.1.second_ref, f32[128,512]{1,0:T(8,128)S(1)} %get-tuple-element.21.tiles_ref, ...), custom_call_target="tpu_custom_call" | custom-call | flops 10000000 | bytes 4000000 | tf_op jit(solution)/shard_map/pallas_call | solution.py:464
  15.6 9.3 %all-to-all-start = ((f32[16,24,128]{2,1,0:T(8,128)}), f32[16,24,128]{2,1,0:T(8,128)S(1)}, u32[]{:S(2)}, u32[]{:S(2)}) async-start(f32[16,24,128]{2,1,0:T(8,128)} %shard_map.107), calls=%async_computation | async-start | bytes 393216 | tf_op jit(solution)/shard_map/all_to_all | solution.py:475
  24.9 0.0 copy-done.1
  24.9 0.0 copy-done.8
  24.9 0.0 copy-start.2
  24.9 0.0 copy-start.3
  24.9 0.0 copy-start.5
  24.9 4.3 %shard_map.106 = (f32[4,32,128]{2,1,0:T(8,128)S(1)}, f32[4,32,128]{2,1,0:T(8,128)S(1)}, f32[2,4,4,128]{3,2,1,0:T(4,128)S(1)}) custom-call(s32[1]{0:T(128)} %bitcast.1.odd_ref, s32[1,1,1]{2,1,0:T(1,128)S(6)} %copy.12.count_ref, s32[32]{0:T(128)S(1)} %bitcast.14, f32[5,8,64,128]{3,2,1,0:T(8,128)S(1)} %copy-done.1, f32[4,32,128]{2,1,0:T(8,128)S(1)} %bitcast.10, ...), custom_call_target="tpu_custom_call" | custom-call | flops 6000000000 | bytes 2000000 | tf_op jit(solution)/shard_map/pallas_call | solution.py:477
  29.2 0.1 collective-permute-start.5
  29.3 3.5 %collective-permute-start.2 = (f32[5,8,128]{2,1,0:T(8,128)S(1)}, f32[5,8,128]{2,1,0:T(8,128)S(1)}, u32[]{:S(2)}, u32[]{:S(2)}) collective-permute-start(f32[5,8,128]{2,1,0:T(8,128)S(1)} %get-tuple-element.19), channel_id=1, source_target_pairs={{0,16},{16,0},{32,48},{48,32},{64,80},{80,64},{96,112},{112,96},{1... | collective-permute-start | bytes 61448 | tf_op jit(solution)/shard_map/ppermute | solution.py:448
  32.8 2.7 %collective-permute-start.3 = (f32[5,8,128]{2,1,0:T(8,128)S(1)}, f32[5,8,128]{2,1,0:T(8,128)S(1)}, u32[]{:S(2)}, u32[]{:S(2)}) collective-permute-start(f32[5,8,128]{2,1,0:T(8,128)S(1)} %get-tuple-element.20), channel_id=1, source_target_pairs={{0,240},{16,32},{32,16},{48,64},{64,48},{80,96},{96,80},{112,128},... | collective-permute-start | bytes 61448 | tf_op jit(solution)/shard_map/ppermute | solution.py:449
  35.5 0.0 collective-permute-done.5.moved_ref
  35.5 1.9 %all-to-all-done.got_ref = f32[16,24,128]{2,1,0:T(8,128)S(1)} async-done(((f32[16,24,128]{2,1,0:T(8,128)}), f32[16,24,128]{2,1,0:T(8,128)S(1)}, u32[]{:S(2)}, u32[]{:S(2)}) %all-to-all-start) | async-done | bytes 196640 | tf_op jit(solution)/shard_map/all_to_all | solution.py:475
  37.5 0.0 copy-done.2
  37.5 0.0 copy-done.3
  37.5 0.0 copy-done.5
  37.5 2.1 %shard_map.108 = (f32[16,20,128]{2,1,0:T(8,128)}, f32[4,4,128]{2,1,0:T(4,128)S(1)}) custom-call(s32[1]{0:T(128)} %bitcast.2.az_ref, s32[16]{0:T(128)S(1)} %copy-done.5, bf16[256,1024]{1,0:T(8,128)(2,1)S(1)} %copy-done.3, bf16[1024,256]{1,0:T(8,128)(2,1)S(1)} %copy-done.2, f32[16,24,128]{2,1,0:T(8,128)S(1)} %all-to-all-done.got_ref, ...), custom_call_target="tpu_custom_call" | custom-call | flops 100000000 | bytes 1000000 | tf_op jit(solution)/shard_map/pallas_call | solution.py:491
  39.6 5.1 %all-to-all-start.1 = ((f32[16,20,128]{2,1,0:T(8,128)}), f32[16,20,128]{2,1,0:T(8,128)S(1)}, u32[]{:S(2)}, u32[]{:S(2)}) async-start(f32[16,20,128]{2,1,0:T(8,128)} %get-tuple-element.27._), calls=%async_computation.1 | async-start | bytes 393216 | tf_op jit(solution)/shard_map/all_to_all | solution.py:502
  44.8 3.7 %collective-permute-start.6 = (f32[4,4,128]{2,1,0:T(4,128)S(1)}, f32[4,4,128]{2,1,0:T(4,128)S(1)}, u32[]{:S(2)}, u32[]{:S(2)}) collective-permute-start(f32[4,4,128]{2,1,0:T(4,128)S(1)} %get-tuple-element.29), channel_id=1, source_target_pairs={{0,4},{4,8},{8,12},{6,2},{10,6},{14,10},{1,5},{5,9},{9,13},{7,3},{... | collective-permute-start | bytes 24584 | tf_op jit(solution)/shard_map/ppermute | solution.py:503
  48.5 0.0 collective-permute-done.2.az_first
  48.5 0.0 collective-permute-done.3.az_second
  48.5 5.4 %shard_map.109.sect_ref = f32[5,8,64,128]{3,2,1,0:T(8,128)S(1)} custom-call(s32[1]{0:T(128)} %bitcast.rad_ref, s32[1]{0:T(128)} %bitcast.1.odd_ref, s32[1]{0:T(128)} %bitcast.2.az_ref, f32[5,6]{1,0:T(8,128)S(1)} %copy-done.4, f32[5,8,64,128]{3,2,1,0:T(8,128)S(1)} %copy-done.1, f32[5,64,128]{2,1,0:T(8,128)S(1)} %collective-permute-done.first_ref, ...), custom_call_target="tpu_custom_call" | custom-call | flops 8000000000 | bytes 4000000 | tf_op jit(solution)/shard_map/pallas_call | solution.py:505
  53.9 0.0 collective-permute-done.6.onward_ref
  53.9 3.2 %all-to-all-done.1.got_ref = f32[16,20,128]{2,1,0:T(8,128)S(1)} async-done(((f32[16,20,128]{2,1,0:T(8,128)}), f32[16,20,128]{2,1,0:T(8,128)S(1)}, u32[]{:S(2)}, u32[]{:S(2)}) %all-to-all-start.1) | async-done | bytes 163872 | tf_op jit(solution)/shard_map/all_to_all | solution.py:502
  57.2 1.5 %shard_map.110 = (f32[5,8,64,128]{3,2,1,0:T(8,128)}, f32[4,40,128]{2,1,0:T(8,128)}) custom-call(s32[1]{0:T(128)} %bitcast.rad_ref, s32[1]{0:T(128)} %bitcast.1.odd_ref, f32[5,8,64,128]{3,2,1,0:T(8,128)S(1)} %shard_map.109.sect_ref, f32[16,20,128]{2,1,0:T(8,128)S(1)} %all-to-all-done.1.got_ref, f32[4,32,128]{2,1,0:T(8,128)S(1)} %get-tuple-element.28.stay_ref, ...), custom_call_target="tpu_custom_call" | custom-call | flops 1000000 | bytes 4000000 | tf_op jit(solution)/shard_map/pallas_call | solution.py:511
Async XLA Ops:
  0.6 7.2 %copy-start.7 = (s32[32,1,128]{2,1,0:T(1,128)S(1)}, s32[32,1,128]{2,1,0:T(1,128)}, u32[]{:S(2)}) copy-start(s32[32,1,128]{2,1,0:T(1,128)} %param.12) | copy-start | bytes 49156
  0.7 1.3 %copy-start = (f32[5,8,64,128]{3,2,1,0:T(8,128)S(1)}, f32[5,8,64,128]{3,2,1,0:T(8,128)}, u32[]{:S(2)}) copy-start(f32[5,8,64,128]{3,2,1,0:T(8,128)} %q_ref.5) | copy-start | bytes 3932164
  2.0 5.8 %copy-start.6 = (f32[4,32,1,128]{3,2,1,0:T(1,128)S(1)}, f32[4,32,1,128]{3,2,1,0:T(1,128)}, u32[]{:S(2)}) copy-start(f32[4,32,1,128]{3,2,1,0:T(1,128)} %param.11) | copy-start | bytes 196612
  2.8 11.0 %collective-permute-start = (f32[5,64,128]{2,1,0:T(8,128)S(1)}, f32[5,64,128]{2,1,0:T(8,128)S(1)}, u32[]{:S(2)}, u32[]{:S(2)}) collective-permute-start(f32[5,64,128]{2,1,0:T(8,128)S(1)} %get-tuple-element.17), channel_id=1, source_target_pairs={{0,2},{2,0},{4,6},{6,4},{8,10},{10,8},{12,14},{14,12},{1,3},{3,1},... | collective-permute-start | bytes 491528 | tf_op jit(solution)/shard_map/ppermute | solution.py:447
  2.9 10.9 %collective-permute-start.1 = (f32[5,64,128]{2,1,0:T(8,128)S(1)}, f32[5,64,128]{2,1,0:T(8,128)S(1)}, u32[]{:S(2)}, u32[]{:S(2)}) collective-permute-start(f32[5,64,128]{2,1,0:T(8,128)S(1)} %get-tuple-element.18), channel_id=1, source_target_pairs={{2,4},{4,2},{6,8},{8,6},{10,12},{12,10},{3,5},{5,3},{7,9},{9,7},{1... | collective-permute-start | bytes 491528 | tf_op jit(solution)/shard_map/ppermute | solution.py:446
  7.8 6.1 %copy-start.4 = (f32[5,6]{1,0:T(8,128)S(1)}, f32[5,6]{1,0:T(8,128)}, u32[]{:S(2)}) copy-start(f32[5,6]{1,0:T(8,128)} %coef_ref.3) | copy-start | bytes 364
  10.0 14.8 %copy-start.1 = (f32[5,8,64,128]{3,2,1,0:T(8,128)S(1)}, f32[5,8,64,128]{3,2,1,0:T(8,128)}, u32[]{:S(2)}) copy-start(f32[5,8,64,128]{3,2,1,0:T(8,128)} %q_ref.5) | copy-start | bytes 3932164
  10.0 14.8 %copy-start.8 = (s32[32,1,1]{0,2,1:T(1,128)S(1)}, s32[32,1,1]{0,2,1:T(1,128)}, u32[]{:S(2)}) copy-start(s32[32,1,1]{0,2,1:T(1,128)} %param.14) | copy-start | bytes 388
  10.1 3.8 %collective-permute-start.4 = (f32[32,128]{1,0:T(8,128)S(1)}, f32[32,128]{1,0:T(8,128)S(1)}, u32[]{:S(2)}, u32[]{:S(2)}) collective-permute-start(f32[32,128]{1,0:T(8,128)S(1)} %get-tuple-element.23), channel_id=1, source_target_pairs={{0,1},{1,0},{2,3},{3,2},{4,5},{5,4},{6,7},{7,6},{8,9},{9,8},{10,11... | collective-permute-start | bytes 49160 | tf_op jit(solution)/shard_map/ppermute | solution.py:462
  15.6 21.9 %all-to-all-start = ((f32[16,24,128]{2,1,0:T(8,128)}), f32[16,24,128]{2,1,0:T(8,128)S(1)}, u32[]{:S(2)}, u32[]{:S(2)}) async-start(f32[16,24,128]{2,1,0:T(8,128)} %shard_map.107), calls=%async_computation | async-start | bytes 393216 | tf_op jit(solution)/shard_map/all_to_all | solution.py:475
  24.9 12.6 %copy-start.2 = (bf16[1024,256]{1,0:T(8,128)(2,1)S(1)}, bf16[1024,256]{1,0:T(8,128)(2,1)}, u32[]{:S(2)}) copy-start(bf16[1024,256]{1,0:T(8,128)(2,1)} %constant.31.clone.turned_ref) | copy-start | bytes 1572868
  24.9 12.6 %copy-start.3 = (bf16[256,1024]{1,0:T(8,128)(2,1)S(1)}, bf16[256,1024]{1,0:T(8,128)(2,1)}, u32[]{:S(2)}) copy-start(bf16[256,1024]{1,0:T(8,128)(2,1)} %constant.30.clone.basis_ref) | copy-start | bytes 1572868
  24.9 12.6 %copy-start.5 = (s32[16]{0:T(128)S(1)}, s32[16]{0:T(128)}, u32[]{:S(2)}) copy-start(s32[16]{0:T(128)} %width_ref.1) | copy-start | bytes 196
  29.2 6.3 %collective-permute-start.5 = (f32[2,4,4,128]{3,2,1,0:T(4,128)S(1)}, f32[2,4,4,128]{3,2,1,0:T(4,128)S(1)}, u32[]{:S(2)}, u32[]{:S(2)}) collective-permute-start(f32[2,4,4,128]{3,2,1,0:T(4,128)S(1)} %get-tuple-element.26), channel_id=1, source_target_pairs={{0,2},{2,0},{4,6},{6,4},{8,10},{10,8},{12,14},{14,12},{1,3},{3,1},... | collective-permute-start | bytes 49160 | tf_op jit(solution)/shard_map/ppermute | solution.py:488
  29.3 19.2 %collective-permute-start.2 = (f32[5,8,128]{2,1,0:T(8,128)S(1)}, f32[5,8,128]{2,1,0:T(8,128)S(1)}, u32[]{:S(2)}, u32[]{:S(2)}) collective-permute-start(f32[5,8,128]{2,1,0:T(8,128)S(1)} %get-tuple-element.19), channel_id=1, source_target_pairs={{0,16},{16,0},{32,48},{48,32},{64,80},{80,64},{96,112},{112,96},{1... | collective-permute-start | bytes 61448 | tf_op jit(solution)/shard_map/ppermute | solution.py:448
  32.8 15.7 %collective-permute-start.3 = (f32[5,8,128]{2,1,0:T(8,128)S(1)}, f32[5,8,128]{2,1,0:T(8,128)S(1)}, u32[]{:S(2)}, u32[]{:S(2)}) collective-permute-start(f32[5,8,128]{2,1,0:T(8,128)S(1)} %get-tuple-element.20), channel_id=1, source_target_pairs={{0,240},{16,32},{32,16},{48,64},{64,48},{80,96},{96,80},{112,128},... | collective-permute-start | bytes 61448 | tf_op jit(solution)/shard_map/ppermute | solution.py:449
  39.6 17.5 %all-to-all-start.1 = ((f32[16,20,128]{2,1,0:T(8,128)}), f32[16,20,128]{2,1,0:T(8,128)S(1)}, u32[]{:S(2)}, u32[]{:S(2)}) async-start(f32[16,20,128]{2,1,0:T(8,128)} %get-tuple-element.27._), calls=%async_computation.1 | async-start | bytes 393216 | tf_op jit(solution)/shard_map/all_to_all | solution.py:502
  44.8 9.2 %collective-permute-start.6 = (f32[4,4,128]{2,1,0:T(4,128)S(1)}, f32[4,4,128]{2,1,0:T(4,128)S(1)}, u32[]{:S(2)}, u32[]{:S(2)}) collective-permute-start(f32[4,4,128]{2,1,0:T(4,128)S(1)} %get-tuple-element.29), channel_id=1, source_target_pairs={{0,4},{4,8},{8,12},{6,2},{10,6},{14,10},{1,5},{5,9},{9,13},{7,3},{... | collective-permute-start | bytes 24584 | tf_op jit(solution)/shard_map/ppermute | solution.py:503

commit v12 on v9

--- a/solution.py
+++ b/solution.py
@@ -285,17 +285,23 @@
     zero = jnp.zeros((), BF16)
 
     def scattered(i):
-        for first in range(0, BLK_DEV, width):
-            cols = slice(first * BLK, (first + width) * BLK)
-            if i == 0:
-                hot_ref[:, cols] = one_hot_rows(cells_ref, first, width)[0]
-            mask = equals(CR, lane_row(cells_ref, first, width) & (CR - 1))
-            row = jnp.concatenate([src_ref[i, first + j : first + j + 1, :] for j in range(width)], axis=1)
-            high = row.astype(BF16)
-            low = (row - high.astype(F32)).astype(BF16)
-            spread_ref[i, 0:CR, cols] = jnp.where(mask, high, zero)
-            spread_ref[i, CR:, cols] = jnp.where(mask, low, zero)
-        total = lax.dot_general(hot_ref[...], spread_ref[i], NT, preferred_element_type=F32)
+        parts = 2 if i == 0 else 1
+        blocks = BLK_DEV // parts
+        total = None
+        for start in range(0, BLK_DEV, blocks):
+            for first in range(start, start + blocks, width):
+                cols = slice(first * BLK, (first + width) * BLK)
+                if i == 0:
+                    hot_ref[:, cols] = one_hot_rows(cells_ref, first, width)[0]
+                mask = equals(CR, lane_row(cells_ref, first, width) & (CR - 1))
+                row = jnp.concatenate([src_ref[i, first + j : first + j + 1, :] for j in range(width)], axis=1)
+                high = row.astype(BF16)
+                low = (row - high.astype(F32)).astype(BF16)
+                spread_ref[i, 0:CR, cols] = jnp.where(mask, high, zero)
+                spread_ref[i, CR:, cols] = jnp.where(mask, low, zero)
+            cols = slice(start * BLK, (start + blocks) * BLK)
+            part = lax.dot_general(hot_ref[:, cols], spread_ref[i, :, cols], NT, preferred_element_type=F32)
+            total = part if total is None else total + part
         return total[:, :CR] + total[:, CR:]
 
     rad = rad_ref[0]

time: 56.9 us -> 57 us (level)
  no operation moved by 1% of the time
where the time goes in v12:
time: 57 us; the launch traced here: 56.6 us
  starting transfers between devices  30 us (53%)
  Pallas kernels  17.7 us (31%)
  waiting for transfers between devices  5.16 us (9%)
  local copies, waits for them, and re-layouts  2.19 us (4%)
  between operations  1.52 us (3%)
    all_to_all x1, starting transfers between devices, shards(): lines = lax.all_to_all(to_owner, 'az', 0, 0, tiled=True)  9.43 us
    all_to_all x1, starting transfers between devices, shards(): filtered = lax.all_to_all(to_home, 'az', 0, 0, tiled=True)  5.54 us
    pallas_call x1, Pallas kernels, shards(): call(gas_body, [gas_shape], [SMEM] * 4 + [VMEM] * 8 + [ANY], 8 * 10 ** 9,...  5.43 us
    pallas_call x1, Pallas kernels, shards(): call(parcels_body, [(4, BLK_DEV, BLK), (4, BLK_DEV, BLK), (2, 4, MOVEB, B...  4.32 us
    ppermute x1, starting transfers between devices, shards(): second = lax.ppermute(second, 'ax', outer)  4.18 us
    ppermute x1, starting transfers between devices, shards(): onward = lax.ppermute(onward, 'ax', along)  3.37 us
    ppermute x1, starting transfers between devices, shards(): az_first = lax.ppermute(az_first, 'az', inner_az)  3.14 us
    all_to_all x1, waiting for transfers between devices, shards(): filtered = lax.all_to_all(to_home, 'az', 0, 0, tiled=True)  2.99 us
  transfers between devices with their start and end apart: 9, of which 2 were waited for; matrix products, arithmetic and copies ran while one was open for 0% of the time, Pallas kernels for 26%

profile of v12, /device:TPU:8, one launch (start us, length us, event | category | flops | bytes accessed | tf_op | source)
XLA Modules:
  0.0 56.6 jit_solution(17716900881705831306)
XLA Ops:
  0.6 0.0 copy-start.8
  0.7 0.0 copy-start
  0.7 1.3 %copy-done = f32[5,8,64,128]{3,2,1,0:T(8,128)S(1)} copy-done((f32[5,8,64,128]{3,2,1,0:T(8,128)S(1)}, f32[5,8,64,128]{3,2,1,0:T(8,128)}, u32[]{:S(2)}) %copy-start) | copy-done | bytes 1310744
  2.0 0.0 copy-start.1
  2.0 0.1 shard_map.104
  2.0 0.1 collective-permute-start
  2.1 4.2 %collective-permute-start.1 = (f32[5,64,128]{2,1,0:T(8,128)S(1)}, f32[5,64,128]{2,1,0:T(8,128)S(1)}, u32[]{:S(2)}, u32[]{:S(2)}) collective-permute-start(f32[5,64,128]{2,1,0:T(8,128)S(1)} %get-tuple-element.17), channel_id=1, source_target_pairs={{2,4},{4,2},{6,8},{8,6},{10,12},{12,10},{3,5},{5,3},{7,9},{9,7},{1... | collective-permute-start | bytes 491528 | tf_op jit(solution)/shard_map/ppermute | solution.py:448
  7.0 0.0 copy-done.8
  7.0 0.0 copy-done.1
  7.0 0.0 copy-start.6
  7.0 0.8 %copy-done.6 = f32[4,32,1,128]{3,2,1,0:T(1,128)S(1)} copy-done((f32[4,32,1,128]{3,2,1,0:T(1,128)S(1)}, f32[4,32,1,128]{3,2,1,0:T(1,128)}, u32[]{:S(2)}) %copy-start.6) | copy-done | bytes 65560
  7.8 0.0 copy-start.4
  7.8 2.6 %shard_map.106 = (f32[128,512]{1,0:T(8,128)S(1)}, f32[64,512]{1,0:T(8,128)S(1)}) custom-call(s32[1]{0:T(128)} %bitcast.11.count_ref, f32[5,8,64,128]{3,2,1,0:T(8,128)S(1)} %copy-done.1, f32[4,32,128]{2,1,0:T(8,128)S(1)} %bitcast.12, s32[32,128]{1,0:T(8,128)S(1)} %bitcast.14), custom_call_target="tpu_custom_call" | custom-call | flops 3000000000 | bytes 2000000 | tf_op jit(solution)/shard_map/pallas_call | solution.py:452
  10.5 0.0 copy-start.7
  10.5 0.0 copy-start.9
  10.5 0.0 collective-permute-done.first_ref
  10.5 0.0 collective-permute-done.1.second_ref
  10.5 0.0 copy-done.4
  10.5 1.7 %shard_map.107 = f32[16,24,128]{2,1,0:T(8,128)} custom-call(s32[1]{0:T(128)} %bitcast.1.odd_ref, f32[5,6]{1,0:T(8,128)S(1)} %copy-done.4, f32[5,64,128]{2,1,0:T(8,128)S(1)} %collective-permute-done.first_ref, f32[5,64,128]{2,1,0:T(8,128)S(1)} %collective-permute-done.1.second_ref, f32[128,512]{1,0:T(8,128)S(1)} %get-tuple-element.22.tiles_ref, ...), custom_call_target="tpu_custom_call" | custom-call | flops 10000000 | bytes 4000000 | tf_op jit(solution)/shard_map/pallas_call | solution.py:464
  12.2 9.4 %all-to-all-start = ((f32[16,24,128]{2,1,0:T(8,128)}), f32[16,24,128]{2,1,0:T(8,128)S(1)}, u32[]{:S(2)}, u32[]{:S(2)}) async-start(f32[16,24,128]{2,1,0:T(8,128)} %shard_map.107), calls=%async_computation | async-start | bytes 393216 | tf_op jit(solution)/shard_map/all_to_all | solution.py:475
  21.6 0.0 copy-done.7
  21.6 0.0 copy-done.9
  21.6 0.0 copy-start.2
  21.7 0.0 copy-start.3
  21.7 0.0 copy-start.5
  21.7 4.3 %shard_map.105 = (f32[4,32,128]{2,1,0:T(8,128)S(1)}, f32[4,32,128]{2,1,0:T(8,128)S(1)}, f32[2,4,4,128]{3,2,1,0:T(4,128)S(1)}, f32[32,128]{1,0:T(8,128)S(1)}) custom-call(s32[1]{0:T(128)} %bitcast.rad_ref, s32[1]{0:T(128)} %bitcast.1.odd_ref, s32[1]{0:T(128)} %bitcast.10.count_ref, s32[32]{0:T(128)S(1)} %bitcast.17, f32[5,8,64,128]{3,2,1,0:T(8,128)S(1)} %copy-done.1, ...), custom_call_target="tpu_custom_call" | custom-call | flops 6000000000 | bytes 2000000 | tf_op jit(solution)/shard_map/pallas_call | solution.py:477
  26.0 1.0 %collective-permute-start.5 = (f32[2,4,4,128]{3,2,1,0:T(4,128)S(1)}, f32[2,4,4,128]{3,2,1,0:T(4,128)S(1)}, u32[]{:S(2)}, u32[]{:S(2)}) collective-permute-start(f32[2,4,4,128]{3,2,1,0:T(4,128)S(1)} %get-tuple-element.24), channel_id=1, source_target_pairs={{0,2},{2,0},{4,6},{6,4},{8,10},{10,8},{12,14},{14,12},{1,3},{3,1},... | collective-permute-start | bytes 49160 | tf_op jit(solution)/shard_map/ppermute | solution.py:489
  27.0 3.1 %collective-permute-start.2 = (f32[5,8,128]{2,1,0:T(8,128)S(1)}, f32[5,8,128]{2,1,0:T(8,128)S(1)}, u32[]{:S(2)}, u32[]{:S(2)}) collective-permute-start(f32[5,8,128]{2,1,0:T(8,128)S(1)} %get-tuple-element.18), channel_id=1, source_target_pairs={{0,16},{16,0},{32,48},{48,32},{64,80},{80,64},{96,112},{112,96},{1... | collective-permute-start | bytes 61448 | tf_op jit(solution)/shard_map/ppermute | solution.py:449
  30.1 2.7 %collective-permute-start.3 = (f32[5,8,128]{2,1,0:T(8,128)S(1)}, f32[5,8,128]{2,1,0:T(8,128)S(1)}, u32[]{:S(2)}, u32[]{:S(2)}) collective-permute-start(f32[5,8,128]{2,1,0:T(8,128)S(1)} %get-tuple-element.19), channel_id=1, source_target_pairs={{0,240},{16,32},{32,16},{48,64},{64,48},{80,96},{96,80},{112,128},... | collective-permute-start | bytes 61448 | tf_op jit(solution)/shard_map/ppermute | solution.py:450
  32.8 0.6 %collective-permute-start.4 = (f32[32,128]{1,0:T(8,128)S(1)}, f32[32,128]{1,0:T(8,128)S(1)}, u32[]{:S(2)}, u32[]{:S(2)}) collective-permute-start(f32[32,128]{1,0:T(8,128)S(1)} %get-tuple-element.20), channel_id=1, source_target_pairs={{0,1},{1,0},{2,3},{3,2},{4,5},{5,4},{6,7},{7,6},{8,9},{9,8},{10,11... | collective-permute-start | bytes 49160 | tf_op jit(solution)/shard_map/ppermute | solution.py:488
  33.4 0.0 collective-permute-done.5.moved_ref
  33.4 2.2 %all-to-all-done.got_ref = f32[16,24,128]{2,1,0:T(8,128)S(1)} async-done(((f32[16,24,128]{2,1,0:T(8,128)}), f32[16,24,128]{2,1,0:T(8,128)S(1)}, u32[]{:S(2)}, u32[]{:S(2)}) %all-to-all-start) | async-done | bytes 196640 | tf_op jit(solution)/shard_map/all_to_all | solution.py:475
  35.5 0.0 copy-done.2
  35.5 0.0 copy-done.3
  35.5 0.0 copy-done.5
  35.5 2.1 %shard_map.108 = (f32[16,20,128]{2,1,0:T(8,128)}, f32[4,4,128]{2,1,0:T(4,128)S(1)}) custom-call(s32[1]{0:T(128)} %bitcast.2.az_ref, s32[16]{0:T(128)S(1)} %copy-done.5, bf16[256,1024]{1,0:T(8,128)(2,1)S(1)} %copy-done.3, bf16[1024,256]{1,0:T(8,128)(2,1)S(1)} %copy-done.2, f32[16,24,128]{2,1,0:T(8,128)S(1)} %all-to-all-done.got_ref, ...), custom_call_target="tpu_custom_call" | custom-call | flops 100000000 | bytes 1000000 | tf_op jit(solution)/shard_map/pallas_call | solution.py:492
  37.7 5.5 %all-to-all-start.1 = ((f32[16,20,128]{2,1,0:T(8,128)}), f32[16,20,128]{2,1,0:T(8,128)S(1)}, u32[]{:S(2)}, u32[]{:S(2)}) async-start(f32[16,20,128]{2,1,0:T(8,128)} %get-tuple-element.25._), calls=%async_computation.1 | async-start | bytes 393216 | tf_op jit(solution)/shard_map/all_to_all | solution.py:503
  43.2 3.4 %collective-permute-start.6 = (f32[4,4,128]{2,1,0:T(4,128)S(1)}, f32[4,4,128]{2,1,0:T(4,128)S(1)}, u32[]{:S(2)}, u32[]{:S(2)}) collective-permute-start(f32[4,4,128]{2,1,0:T(4,128)S(1)} %get-tuple-element.27), channel_id=1, source_target_pairs={{0,4},{4,8},{8,12},{6,2},{10,6},{14,10},{1,5},{5,9},{9,13},{7,3},{... | collective-permute-start | bytes 24584 | tf_op jit(solution)/shard_map/ppermute | solution.py:504
  46.6 0.0 collective-permute-done.4.rad_in
  46.6 0.0 collective-permute-done.2.az_first
  46.6 0.0 collective-permute-done.3.az_second
  46.6 5.4 %shard_map.109.sect_ref = f32[5,8,64,128]{3,2,1,0:T(8,128)S(1)} custom-call(s32[1]{0:T(128)} %bitcast.rad_ref, s32[1]{0:T(128)} %bitcast.1.odd_ref, s32[1]{0:T(128)} %bitcast.2.az_ref, f32[5,6]{1,0:T(8,128)S(1)} %copy-done.4, f32[5,8,64,128]{3,2,1,0:T(8,128)S(1)} %copy-done.1, f32[5,64,128]{2,1,0:T(8,128)S(1)} %collective-permute-done.first_ref, ...), custom_call_target="tpu_custom_call" | custom-call | flops 8000000000 | bytes 4000000 | tf_op jit(solution)/shard_map/pallas_call | solution.py:506
  52.1 0.0 collective-permute-done.6.onward_ref
  52.1 3.0 %all-to-all-done.1.got_ref = f32[16,20,128]{2,1,0:T(8,128)S(1)} async-done(((f32[16,20,128]{2,1,0:T(8,128)}), f32[16,20,128]{2,1,0:T(8,128)S(1)}, u32[]{:S(2)}, u32[]{:S(2)}) %all-to-all-start.1) | async-done | bytes 163872 | tf_op jit(solution)/shard_map/all_to_all | solution.py:503
  55.1 1.5 %shard_map.110 = (f32[5,8,64,128]{3,2,1,0:T(8,128)}, f32[4,40,128]{2,1,0:T(8,128)}) custom-call(s32[1]{0:T(128)} %bitcast.rad_ref, s32[1]{0:T(128)} %bitcast.1.odd_ref, f32[5,8,64,128]{3,2,1,0:T(8,128)S(1)} %shard_map.109.sect_ref, f32[16,20,128]{2,1,0:T(8,128)S(1)} %all-to-all-done.1.got_ref, f32[4,32,128]{2,1,0:T(8,128)S(1)} %get-tuple-element.26.stay_ref, ...), custom_call_target="tpu_custom_call" | custom-call | flops 1000000 | bytes 4000000 | tf_op jit(solution)/shard_map/pallas_call | solution.py:512
Async XLA Ops:
  0.6 6.4 %copy-start.8 = (s32[32,1,128]{2,1,0:T(1,128)S(1)}, s32[32,1,128]{2,1,0:T(1,128)}, u32[]{:S(2)}) copy-start(s32[32,1,128]{2,1,0:T(1,128)} %param.12) | copy-start | bytes 49156
  0.7 1.3 %copy-start = (f32[5,8,64,128]{3,2,1,0:T(8,128)S(1)}, f32[5,8,64,128]{3,2,1,0:T(8,128)}, u32[]{:S(2)}) copy-start(f32[5,8,64,128]{3,2,1,0:T(8,128)} %q_ref.7) | copy-start | bytes 3932164
  2.0 5.0 %copy-start.1 = (f32[5,8,64,128]{3,2,1,0:T(8,128)S(1)}, f32[5,8,64,128]{3,2,1,0:T(8,128)}, u32[]{:S(2)}) copy-start(f32[5,8,64,128]{3,2,1,0:T(8,128)} %q_ref.7) | copy-start | bytes 3932164
  2.0 8.5 %collective-permute-start = (f32[5,64,128]{2,1,0:T(8,128)S(1)}, f32[5,64,128]{2,1,0:T(8,128)S(1)}, u32[]{:S(2)}, u32[]{:S(2)}) collective-permute-start(f32[5,64,128]{2,1,0:T(8,128)S(1)} %get-tuple-element.16), channel_id=1, source_target_pairs={{0,2},{2,0},{4,6},{6,4},{8,10},{10,8},{12,14},{14,12},{1,3},{3,1},... | collective-permute-start | bytes 491528 | tf_op jit(solution)/shard_map/ppermute | solution.py:447
  2.1 8.4 %collective-permute-start.1 = (f32[5,64,128]{2,1,0:T(8,128)S(1)}, f32[5,64,128]{2,1,0:T(8,128)S(1)}, u32[]{:S(2)}, u32[]{:S(2)}) collective-permute-start(f32[5,64,128]{2,1,0:T(8,128)S(1)} %get-tuple-element.17), channel_id=1, source_target_pairs={{2,4},{4,2},{6,8},{8,6},{10,12},{12,10},{3,5},{5,3},{7,9},{9,7},{1... | collective-permute-start | bytes 491528 | tf_op jit(solution)/shard_map/ppermute | solution.py:448
  7.0 0.8 %copy-start.6 = (f32[4,32,1,128]{3,2,1,0:T(1,128)S(1)}, f32[4,32,1,128]{3,2,1,0:T(1,128)}, u32[]{:S(2)}) copy-start(f32[4,32,1,128]{3,2,1,0:T(1,128)} %param.11) | copy-start | bytes 196612
  7.8 2.7 %copy-start.4 = (f32[5,6]{1,0:T(8,128)S(1)}, f32[5,6]{1,0:T(8,128)}, u32[]{:S(2)}) copy-start(f32[5,6]{1,0:T(8,128)} %coef_ref.3) | copy-start | bytes 364
  10.5 11.2 %copy-start.7 = (f32[4,32,1,128]{3,2,1,0:T(1,128)S(1)}, f32[4,32,1,128]{3,2,1,0:T(1,128)}, u32[]{:S(2)}) copy-start(f32[4,32,1,128]{3,2,1,0:T(1,128)} %param.11) | copy-start | bytes 196612
  10.5 11.2 %copy-start.9 = (s32[32,1,1]{0,2,1:T(1,128)S(1)}, s32[32,1,1]{0,2,1:T(1,128)}, u32[]{:S(2)}) copy-start(s32[32,1,1]{0,2,1:T(1,128)} %param.14) | copy-start | bytes 388
  12.2 23.4 %all-to-all-start = ((f32[16,24,128]{2,1,0:T(8,128)}), f32[16,24,128]{2,1,0:T(8,128)S(1)}, u32[]{:S(2)}, u32[]{:S(2)}) async-start(f32[16,24,128]{2,1,0:T(8,128)} %shard_map.107), calls=%async_computation | async-start | bytes 393216 | tf_op jit(solution)/shard_map/all_to_all | solution.py:475
  21.6 13.9 %copy-start.2 = (bf16[1024,256]{1,0:T(8,128)(2,1)S(1)}, bf16[1024,256]{1,0:T(8,128)(2,1)}, u32[]{:S(2)}) copy-start(bf16[1024,256]{1,0:T(8,128)(2,1)} %constant.31.clone.turned_ref) | copy-start | bytes 1572868
  21.7 13.9 %copy-start.3 = (bf16[256,1024]{1,0:T(8,128)(2,1)S(1)}, bf16[256,1024]{1,0:T(8,128)(2,1)}, u32[]{:S(2)}) copy-start(bf16[256,1024]{1,0:T(8,128)(2,1)} %constant.30.clone.basis_ref) | copy-start | bytes 1572868
  21.7 13.9 %copy-start.5 = (s32[16]{0:T(128)S(1)}, s32[16]{0:T(128)}, u32[]{:S(2)}) copy-start(s32[16]{0:T(128)} %width_ref.1) | copy-start | bytes 196
  26.0 7.4 %collective-permute-start.5 = (f32[2,4,4,128]{3,2,1,0:T(4,128)S(1)}, f32[2,4,4,128]{3,2,1,0:T(4,128)S(1)}, u32[]{:S(2)}, u32[]{:S(2)}) collective-permute-start(f32[2,4,4,128]{3,2,1,0:T(4,128)S(1)} %get-tuple-element.24), channel_id=1, source_target_pairs={{0,2},{2,0},{4,6},{6,4},{8,10},{10,8},{12,14},{14,12},{1,3},{3,1},... | collective-permute-start | bytes 49160 | tf_op jit(solution)/shard_map/ppermute | solution.py:489
  27.0 19.6 %collective-permute-start.2 = (f32[5,8,128]{2,1,0:T(8,128)S(1)}, f32[5,8,128]{2,1,0:T(8,128)S(1)}, u32[]{:S(2)}, u32[]{:S(2)}) collective-permute-start(f32[5,8,128]{2,1,0:T(8,128)S(1)} %get-tuple-element.18), channel_id=1, source_target_pairs={{0,16},{16,0},{32,48},{48,32},{64,80},{80,64},{96,112},{112,96},{1... | collective-permute-start | bytes 61448 | tf_op jit(solution)/shard_map/ppermute | solution.py:449
  30.1 16.5 %collective-permute-start.3 = (f32[5,8,128]{2,1,0:T(8,128)S(1)}, f32[5,8,128]{2,1,0:T(8,128)S(1)}, u32[]{:S(2)}, u32[]{:S(2)}) collective-permute-start(f32[5,8,128]{2,1,0:T(8,128)S(1)} %get-tuple-element.19), channel_id=1, source_target_pairs={{0,240},{16,32},{32,16},{48,64},{64,48},{80,96},{96,80},{112,128},... | collective-permute-start | bytes 61448 | tf_op jit(solution)/shard_map/ppermute | solution.py:450
  32.8 13.8 %collective-permute-start.4 = (f32[32,128]{1,0:T(8,128)S(1)}, f32[32,128]{1,0:T(8,128)S(1)}, u32[]{:S(2)}, u32[]{:S(2)}) collective-permute-start(f32[32,128]{1,0:T(8,128)S(1)} %get-tuple-element.20), channel_id=1, source_target_pairs={{0,1},{1,0},{2,3},{3,2},{4,5},{5,4},{6,7},{7,6},{8,9},{9,8},{10,11... | collective-permute-start | bytes 49160 | tf_op jit(solution)/shard_map/ppermute | solution.py:488
  37.7 17.4 %all-to-all-start.1 = ((f32[16,20,128]{2,1,0:T(8,128)}), f32[16,20,128]{2,1,0:T(8,128)S(1)}, u32[]{:S(2)}, u32[]{:S(2)}) async-start(f32[16,20,128]{2,1,0:T(8,128)} %get-tuple-element.25._), calls=%async_computation.1 | async-start | bytes 393216 | tf_op jit(solution)/shard_map/all_to_all | solution.py:503
  43.2 8.8 %collective-permute-start.6 = (f32[4,4,128]{2,1,0:T(4,128)S(1)}, f32[4,4,128]{2,1,0:T(4,128)S(1)}, u32[]{:S(2)}, u32[]{:S(2)}) collective-permute-start(f32[4,4,128]{2,1,0:T(4,128)S(1)} %get-tuple-element.27), channel_id=1, source_target_pairs={{0,4},{4,8},{8,12},{6,2},{10,6},{14,10},{1,5},{5,9},{9,13},{7,3},{... | collective-permute-start | bytes 24584 | tf_op jit(solution)/shard_map/ppermute | solution.py:504

commit v13 on v10

--- a/solution.py
+++ b/solution.py
@@ -82,7 +82,7 @@
     return packed.T
 
 
-def edges_body(odd_ref, az_ref, q_ref, first_out, second_out, az_first, az_second, tiles_out):
+def edges_body(odd_ref, az_ref, q_ref, first_out, second_out, az_first, az_second):
     odd, odd_az = odd_ref[0] == 1, az_ref[0] % 2 == 1
     low, high = q_ref[:, 0], q_ref[:, CAX - 1]
     first_out[...] = jnp.where(odd, low, high)
@@ -90,6 +90,9 @@
     low, high = q_ref[:, :, 0, :], q_ref[:, :, CAZ - 1, :]
     az_first[...] = jnp.where(odd_az, low, high)
     az_second[...] = jnp.where(odd_az, high, low)
+
+
+def tiles_body(q_ref, tiles_out):
     for p in range(PAIRS):
         tiles_out[:, p * 2 * CAZ : (p + 1) * 2 * CAZ] = turned(
             [q_ref[f, 2 * p : 2 * p + 2].reshape(2 * CAZ, CR) for f in range(FIELDS)]
@@ -433,14 +436,15 @@
     across = [(i, i ^ 1) for i in range(n_rad)]
     gas_shape = (FIELDS, CAX, CAZ, CR)
 
-    first, second, az_first, az_second, tiles = call(
-        edges_body, [(FIELDS, CAZ, CR)] * 2 + [(FIELDS, CAX, CR)] * 2 + [(CR, ROWS)], [SMEM, SMEM, VMEM], 10**6, 10**6, mib=4
+    first, second, az_first, az_second = call(
+        edges_body, [(FIELDS, CAZ, CR)] * 2 + [(FIELDS, CAX, CR)] * 2, [SMEM, SMEM, VMEM], 10**6, 10**6, mib=4
     )(odd, az_index, fields)
     first = lax.ppermute(first, "ax", inner)
     second = lax.ppermute(second, "ax", outer)
     az_first = lax.ppermute(az_first, "az", inner_az)
     az_second = lax.ppermute(az_second, "az", outer_az)
 
+    (tiles,) = call(tiles_body, [(CR, ROWS)], [VMEM], 10**6, 10**6, mib=4)(fields)
     (near,) = call(
         near_parcels_body,
         [(4 * CYCLES, ROWS)],

time: 57.1 us -> 56.8 us (level)
  transfers between devices with their start and end apart: 9 -> 9, of which waited for: 3 -> 2; matrix products, arithmetic and copies ran while one was open for 0% -> 0% of each run, Pallas kernels for 25% -> 26%
where the time goes in v13:
time: 56.8 us; the launch traced here: 56.4 us
  starting transfers between devices  31.1 us (55%)
  Pallas kernels  17.8 us (31%)
  waiting for transfers between devices  4.59 us (8%)
  between operations  1.52 us (3%)
  local copies, waits for them, and re-layouts  1.35 us (2%)
    all_to_all x1, starting transfers between devices, shards(): lines = lax.all_to_all(to_owner, 'az', 0, 0, tiled=True)  10.2 us
    all_to_all x1, starting transfers between devices, shards(): filtered = lax.all_to_all(to_home, 'az', 0, 0, tiled=True)  6.09 us
    pallas_call x1, Pallas kernels, shards(): call(gas_body, [gas_shape], [SMEM] * 4 + [VMEM] * 8 + [ANY], 8 * 10 ** 9,...  5.44 us
    pallas_call x1, Pallas kernels, shards(): call(parcels_body, [(4, BLK_DEV, BLK), (4, BLK_DEV, BLK), (2, 4, MOVEB, B...  4.32 us
    ppermute x1, starting transfers between devices, shards(): second = lax.ppermute(second, 'ax', outer)  4.18 us
    ppermute x1, starting transfers between devices, shards(): onward = lax.ppermute(onward, 'ax', along)  3.66 us
    ppermute x1, starting transfers between devices, shards(): az_first = lax.ppermute(az_first, 'az', inner_az)  3.38 us
    all_to_all x1, waiting for transfers between devices, shards(): filtered = lax.all_to_all(to_home, 'az', 0, 0, tiled=True)  2.99 us
  transfers between devices with their start and end apart: 9, of which 2 were waited for; matrix products, arithmetic and copies ran while one was open for 0% of the time, Pallas kernels for 26%

profile of v13, /device:TPU:8, one launch (start us, length us, event | category | flops | bytes accessed | tf_op | source)
XLA Modules:
  0.0 56.4 jit_solution(3458288075069296491)
XLA Ops:
  0.6 0.0 copy-start
  0.7 1.3 %copy-done = f32[5,8,64,128]{3,2,1,0:T(8,128)S(1)} copy-done((f32[5,8,64,128]{3,2,1,0:T(8,128)S(1)}, f32[5,8,64,128]{3,2,1,0:T(8,128)}, u32[]{:S(2)}) %copy-start) | copy-done | bytes 1310744
  2.0 0.0 copy-start.1
  2.0 0.0 copy-start.6
  2.0 0.0 copy-start.7
  2.0 0.1 shard_map.104
  2.0 0.1 collective-permute-start
  2.1 4.2 %collective-permute-start.1 = (f32[5,64,128]{2,1,0:T(8,128)S(1)}, f32[5,64,128]{2,1,0:T(8,128)S(1)}, u32[]{:S(2)}, u32[]{:S(2)}) collective-permute-start(f32[5,64,128]{2,1,0:T(8,128)S(1)} %get-tuple-element.15), channel_id=1, source_target_pairs={{2,4},{4,2},{6,8},{8,6},{10,12},{12,10},{3,5},{5,3},{7,9},{9,7},{1... | collective-permute-start | bytes 491528 | tf_op jit(solution)/shard_map/ppermute | solution.py:443
  6.3 0.0 copy-done.1
  6.3 0.5 shard_map.106.tiles_ref
  7.5 0.0 copy-done.6
  7.5 0.0 copy-done.7
  7.5 0.0 copy-start.4
  7.5 2.2 %shard_map.107.near_ref = f32[64,512]{1,0:T(8,128)S(1)} custom-call(s32[1]{0:T(128)} %bitcast.11.count_ref, f32[128,512]{1,0:T(8,128)S(1)} %shard_map.106.tiles_ref, f32[4,32,128]{2,1,0:T(8,128)S(1)} %bitcast.12, s32[32,128]{1,0:T(8,128)S(1)} %bitcast.14), custom_call_target="tpu_custom_call" | custom-call | flops 3000000000 | bytes 2000000 | tf_op jit(solution)/shard_map/pallas_call | solution.py:448
  9.7 0.0 copy-start.8
  9.8 0.0 collective-permute-done.first_ref
  9.8 0.0 collective-permute-done.1.second_ref
  9.8 0.0 copy-done.4
  9.8 1.7 %shard_map.108 = f32[16,24,128]{2,1,0:T(8,128)} custom-call(s32[1]{0:T(128)} %bitcast.1.odd_ref, f32[5,6]{1,0:T(8,128)S(1)} %copy-done.4, f32[5,64,128]{2,1,0:T(8,128)S(1)} %collective-permute-done.first_ref, f32[5,64,128]{2,1,0:T(8,128)S(1)} %collective-permute-done.1.second_ref, f32[128,512]{1,0:T(8,128)S(1)} %shard_map.106.tiles_ref, ...), custom_call_target="tpu_custom_call" | custom-call | flops 10000000 | bytes 4000000 | tf_op jit(solution)/shard_map/pallas_call | solution.py:460
  11.4 10.2 %all-to-all-start = ((f32[16,24,128]{2,1,0:T(8,128)}), f32[16,24,128]{2,1,0:T(8,128)S(1)}, u32[]{:S(2)}, u32[]{:S(2)}) async-start(f32[16,24,128]{2,1,0:T(8,128)} %shard_map.108), calls=%async_computation | async-start | bytes 393216 | tf_op jit(solution)/shard_map/all_to_all | solution.py:471
  21.6 0.0 copy-done.8
  21.6 0.0 copy-start.2
  21.6 0.0 copy-start.3
  21.7 0.0 copy-start.5
  21.7 4.3 %shard_map.105 = (f32[4,32,128]{2,1,0:T(8,128)S(1)}, f32[4,32,128]{2,1,0:T(8,128)S(1)}, f32[2,4,4,128]{3,2,1,0:T(4,128)S(1)}, f32[32,128]{1,0:T(8,128)S(1)}) custom-call(s32[1]{0:T(128)} %bitcast.rad_ref, s32[1]{0:T(128)} %bitcast.1.odd_ref, s32[1]{0:T(128)} %bitcast.10.count_ref, s32[32]{0:T(128)S(1)} %bitcast.17, f32[5,8,64,128]{3,2,1,0:T(8,128)S(1)} %copy-done.1, ...), custom_call_target="tpu_custom_call" | custom-call | flops 6000000000 | bytes 2000000 | tf_op jit(solution)/shard_map/pallas_call | solution.py:473
  26.0 0.2 collective-permute-start.5
  26.2 3.4 %collective-permute-start.2 = (f32[5,8,128]{2,1,0:T(8,128)S(1)}, f32[5,8,128]{2,1,0:T(8,128)S(1)}, u32[]{:S(2)}, u32[]{:S(2)}) collective-permute-start(f32[5,8,128]{2,1,0:T(8,128)S(1)} %get-tuple-element.16), channel_id=1, source_target_pairs={{0,16},{16,0},{32,48},{48,32},{64,80},{80,64},{96,112},{112,96},{1... | collective-permute-start | bytes 61448 | tf_op jit(solution)/shard_map/ppermute | solution.py:444
  29.6 2.7 %collective-permute-start.3 = (f32[5,8,128]{2,1,0:T(8,128)S(1)}, f32[5,8,128]{2,1,0:T(8,128)S(1)}, u32[]{:S(2)}, u32[]{:S(2)}) collective-permute-start(f32[5,8,128]{2,1,0:T(8,128)S(1)} %get-tuple-element.17), channel_id=1, source_target_pairs={{0,240},{16,32},{32,16},{48,64},{64,48},{80,96},{96,80},{112,128},... | collective-permute-start | bytes 61448 | tf_op jit(solution)/shard_map/ppermute | solution.py:445
  32.3 0.6 %collective-permute-start.4 = (f32[32,128]{1,0:T(8,128)S(1)}, f32[32,128]{1,0:T(8,128)S(1)}, u32[]{:S(2)}, u32[]{:S(2)}) collective-permute-start(f32[32,128]{1,0:T(8,128)S(1)} %get-tuple-element.18), channel_id=1, source_target_pairs={{0,1},{1,0},{2,3},{3,2},{4,5},{5,4},{6,7},{7,6},{8,9},{9,8},{10,11... | collective-permute-start | bytes 49160 | tf_op jit(solution)/shard_map/ppermute | solution.py:484
  32.9 0.0 collective-permute-done.5.moved_ref
  32.9 1.6 %all-to-all-done.got_ref = f32[16,24,128]{2,1,0:T(8,128)S(1)} async-done(((f32[16,24,128]{2,1,0:T(8,128)}), f32[16,24,128]{2,1,0:T(8,128)S(1)}, u32[]{:S(2)}, u32[]{:S(2)}) %all-to-all-start) | async-done | bytes 196640 | tf_op jit(solution)/shard_map/all_to_all | solution.py:471
  34.5 0.0 copy-done.2
  34.5 0.0 copy-done.3
  34.5 0.0 copy-done.5
  34.5 2.1 %shard_map.109 = (f32[16,20,128]{2,1,0:T(8,128)}, f32[4,4,128]{2,1,0:T(4,128)S(1)}) custom-call(s32[1]{0:T(128)} %bitcast.2.az_ref, s32[16]{0:T(128)S(1)} %copy-done.5, bf16[256,1024]{1,0:T(8,128)(2,1)S(1)} %copy-done.3, bf16[1024,256]{1,0:T(8,128)(2,1)S(1)} %copy-done.2, f32[16,24,128]{2,1,0:T(8,128)S(1)} %all-to-all-done.got_ref, ...), custom_call_target="tpu_custom_call" | custom-call | flops 100000000 | bytes 1000000 | tf_op jit(solution)/shard_map/pallas_call | solution.py:488
  36.6 6.1 %all-to-all-start.1 = ((f32[16,20,128]{2,1,0:T(8,128)}), f32[16,20,128]{2,1,0:T(8,128)S(1)}, u32[]{:S(2)}, u32[]{:S(2)}) async-start(f32[16,20,128]{2,1,0:T(8,128)} %get-tuple-element.21._), calls=%async_computation.1 | async-start | bytes 393216 | tf_op jit(solution)/shard_map/all_to_all | solution.py:499
  42.7 3.7 %collective-permute-start.6 = (f32[4,4,128]{2,1,0:T(4,128)S(1)}, f32[4,4,128]{2,1,0:T(4,128)S(1)}, u32[]{:S(2)}, u32[]{:S(2)}) collective-permute-start(f32[4,4,128]{2,1,0:T(4,128)S(1)} %get-tuple-element.23), channel_id=1, source_target_pairs={{0,4},{4,8},{8,12},{6,2},{10,6},{14,10},{1,5},{5,9},{9,13},{7,3},{... | collective-permute-start | bytes 24584 | tf_op jit(solution)/shard_map/ppermute | solution.py:500
  46.4 0.0 collective-permute-done.4.rad_in
  46.4 0.0 collective-permute-done.2.az_first
  46.4 0.0 collective-permute-done.3.az_second
  46.4 5.4 %shard_map.110.sect_ref = f32[5,8,64,128]{3,2,1,0:T(8,128)S(1)} custom-call(s32[1]{0:T(128)} %bitcast.rad_ref, s32[1]{0:T(128)} %bitcast.1.odd_ref, s32[1]{0:T(128)} %bitcast.2.az_ref, f32[5,6]{1,0:T(8,128)S(1)} %copy-done.4, f32[5,8,64,128]{3,2,1,0:T(8,128)S(1)} %copy-done.1, f32[5,64,128]{2,1,0:T(8,128)S(1)} %collective-permute-done.first_ref, ...), custom_call_target="tpu_custom_call" | custom-call | flops 8000000000 | bytes 4000000 | tf_op jit(solution)/shard_map/pallas_call | solution.py:502
  51.9 0.0 collective-permute-done.6.onward_ref
  51.9 3.0 %all-to-all-done.1.got_ref = f32[16,20,128]{2,1,0:T(8,128)S(1)} async-done(((f32[16,20,128]{2,1,0:T(8,128)}), f32[16,20,128]{2,1,0:T(8,128)S(1)}, u32[]{:S(2)}, u32[]{:S(2)}) %all-to-all-start.1) | async-done | bytes 163872 | tf_op jit(solution)/shard_map/all_to_all | solution.py:499
  54.9 1.5 %shard_map.111 = (f32[5,8,64,128]{3,2,1,0:T(8,128)}, f32[4,40,128]{2,1,0:T(8,128)}) custom-call(s32[1]{0:T(128)} %bitcast.rad_ref, s32[1]{0:T(128)} %bitcast.1.odd_ref, f32[5,8,64,128]{3,2,1,0:T(8,128)S(1)} %shard_map.110.sect_ref, f32[16,20,128]{2,1,0:T(8,128)S(1)} %all-to-all-done.1.got_ref, f32[4,32,128]{2,1,0:T(8,128)S(1)} %get-tuple-element.22.stay_ref, ...), custom_call_target="tpu_custom_call" | custom-call | flops 1000000 | bytes 4000000 | tf_op jit(solution)/shard_map/pallas_call | solution.py:508
Async XLA Ops:
  0.6 1.3 %copy-start = (f32[5,8,64,128]{3,2,1,0:T(8,128)S(1)}, f32[5,8,64,128]{3,2,1,0:T(8,128)}, u32[]{:S(2)}) copy-start(f32[5,8,64,128]{3,2,1,0:T(8,128)} %q_ref.7) | copy-start | bytes 3932164
  2.0 4.4 %copy-start.1 = (f32[5,8,64,128]{3,2,1,0:T(8,128)S(1)}, f32[5,8,64,128]{3,2,1,0:T(8,128)}, u32[]{:S(2)}) copy-start(f32[5,8,64,128]{3,2,1,0:T(8,128)} %q_ref.7) | copy-start | bytes 3932164
  2.0 5.5 %copy-start.6 = (f32[4,32,1,128]{3,2,1,0:T(1,128)S(1)}, f32[4,32,1,128]{3,2,1,0:T(1,128)}, u32[]{:S(2)}) copy-start(f32[4,32,1,128]{3,2,1,0:T(1,128)} %param.11) | copy-start | bytes 196612
  2.0 5.5 %copy-start.7 = (s32[32,1,128]{2,1,0:T(1,128)S(1)}, s32[32,1,128]{2,1,0:T(1,128)}, u32[]{:S(2)}) copy-start(s32[32,1,128]{2,1,0:T(1,128)} %param.12) | copy-start | bytes 49156
  2.0 7.7 %collective-permute-start = (f32[5,64,128]{2,1,0:T(8,128)S(1)}, f32[5,64,128]{2,1,0:T(8,128)S(1)}, u32[]{:S(2)}, u32[]{:S(2)}) collective-permute-start(f32[5,64,128]{2,1,0:T(8,128)S(1)} %get-tuple-element.14), channel_id=1, source_target_pairs={{0,2},{2,0},{4,6},{6,4},{8,10},{10,8},{12,14},{14,12},{1,3},{3,1},... | collective-permute-start | bytes 491528 | tf_op jit(solution)/shard_map/ppermute | solution.py:442
  2.1 7.6 %collective-permute-start.1 = (f32[5,64,128]{2,1,0:T(8,128)S(1)}, f32[5,64,128]{2,1,0:T(8,128)S(1)}, u32[]{:S(2)}, u32[]{:S(2)}) collective-permute-start(f32[5,64,128]{2,1,0:T(8,128)S(1)} %get-tuple-element.15), channel_id=1, source_target_pairs={{2,4},{4,2},{6,8},{8,6},{10,12},{12,10},{3,5},{5,3},{7,9},{9,7},{1... | collective-permute-start | bytes 491528 | tf_op jit(solution)/shard_map/ppermute | solution.py:443
  7.5 2.3 %copy-start.4 = (f32[5,6]{1,0:T(8,128)S(1)}, f32[5,6]{1,0:T(8,128)}, u32[]{:S(2)}) copy-start(f32[5,6]{1,0:T(8,128)} %coef_ref.3) | copy-start | bytes 364
  9.7 11.9 %copy-start.8 = (s32[32,1,1]{0,2,1:T(1,128)S(1)}, s32[32,1,1]{0,2,1:T(1,128)}, u32[]{:S(2)}) copy-start(s32[32,1,1]{0,2,1:T(1,128)} %param.14) | copy-start | bytes 388
  11.4 23.0 %all-to-all-start = ((f32[16,24,128]{2,1,0:T(8,128)}), f32[16,24,128]{2,1,0:T(8,128)S(1)}, u32[]{:S(2)}, u32[]{:S(2)}) async-start(f32[16,24,128]{2,1,0:T(8,128)} %shard_map.108), calls=%async_computation | async-start | bytes 393216 | tf_op jit(solution)/shard_map/all_to_all | solution.py:471
  21.6 12.8 %copy-start.2 = (bf16[1024,256]{1,0:T(8,128)(2,1)S(1)}, bf16[1024,256]{1,0:T(8,128)(2,1)}, u32[]{:S(2)}) copy-start(bf16[1024,256]{1,0:T(8,128)(2,1)} %constant.31.clone.turned_ref) | copy-start | bytes 1572868
  21.6 12.8 %copy-start.3 = (bf16[256,1024]{1,0:T(8,128)(2,1)S(1)}, bf16[256,1024]{1,0:T(8,128)(2,1)}, u32[]{:S(2)}) copy-start(bf16[256,1024]{1,0:T(8,128)(2,1)} %constant.30.clone.basis_ref) | copy-start | bytes 1572868
  21.7 12.8 %copy-start.5 = (s32[16]{0:T(128)S(1)}, s32[16]{0:T(128)}, u32[]{:S(2)}) copy-start(s32[16]{0:T(128)} %width_ref.1) | copy-start | bytes 196
  26.0 6.9 %collective-permute-start.5 = (f32[2,4,4,128]{3,2,1,0:T(4,128)S(1)}, f32[2,4,4,128]{3,2,1,0:T(4,128)S(1)}, u32[]{:S(2)}, u32[]{:S(2)}) collective-permute-start(f32[2,4,4,128]{3,2,1,0:T(4,128)S(1)} %get-tuple-element.20), channel_id=1, source_target_pairs={{0,2},{2,0},{4,6},{6,4},{8,10},{10,8},{12,14},{14,12},{1,3},{3,1},... | collective-permute-start | bytes 49160 | tf_op jit(solution)/shard_map/ppermute | solution.py:485
  26.2 20.2 %collective-permute-start.2 = (f32[5,8,128]{2,1,0:T(8,128)S(1)}, f32[5,8,128]{2,1,0:T(8,128)S(1)}, u32[]{:S(2)}, u32[]{:S(2)}) collective-permute-start(f32[5,8,128]{2,1,0:T(8,128)S(1)} %get-tuple-element.16), channel_id=1, source_target_pairs={{0,16},{16,0},{32,48},{48,32},{64,80},{80,64},{96,112},{112,96},{1... | collective-permute-start | bytes 61448 | tf_op jit(solution)/shard_map/ppermute | solution.py:444
  29.6 16.8 %collective-permute-start.3 = (f32[5,8,128]{2,1,0:T(8,128)S(1)}, f32[5,8,128]{2,1,0:T(8,128)S(1)}, u32[]{:S(2)}, u32[]{:S(2)}) collective-permute-start(f32[5,8,128]{2,1,0:T(8,128)S(1)} %get-tuple-element.17), channel_id=1, source_target_pairs={{0,240},{16,32},{32,16},{48,64},{64,48},{80,96},{96,80},{112,128},... | collective-permute-start | bytes 61448 | tf_op jit(solution)/shard_map/ppermute | solution.py:445
  32.3 14.1 %collective-permute-start.4 = (f32[32,128]{1,0:T(8,128)S(1)}, f32[32,128]{1,0:T(8,128)S(1)}, u32[]{:S(2)}, u32[]{:S(2)}) collective-permute-start(f32[32,128]{1,0:T(8,128)S(1)} %get-tuple-element.18), channel_id=1, source_target_pairs={{0,1},{1,0},{2,3},{3,2},{4,5},{5,4},{6,7},{7,6},{8,9},{9,8},{10,11... | collective-permute-start | bytes 49160 | tf_op jit(solution)/shard_map/ppermute | solution.py:484
  36.6 18.2 %all-to-all-start.1 = ((f32[16,20,128]{2,1,0:T(8,128)}), f32[16,20,128]{2,1,0:T(8,128)S(1)}, u32[]{:S(2)}, u32[]{:S(2)}) async-start(f32[16,20,128]{2,1,0:T(8,128)} %get-tuple-element.21._), calls=%async_computation.1 | async-start | bytes 393216 | tf_op jit(solution)/shard_map/all_to_all | solution.py:499
  42.7 9.1 %collective-permute-start.6 = (f32[4,4,128]{2,1,0:T(4,128)S(1)}, f32[4,4,128]{2,1,0:T(4,128)S(1)}, u32[]{:S(2)}, u32[]{:S(2)}) collective-permute-start(f32[4,4,128]{2,1,0:T(4,128)S(1)} %get-tuple-element.23), channel_id=1, source_target_pairs={{0,4},{4,8},{8,12},{6,2},{10,6},{14,10},{1,5},{5,9},{9,13},{7,3},{... | collective-permute-start | bytes 24584 | tf_op jit(solution)/shard_map/ppermute | solution.py:500
